TPU v7x, 32 devices: a whole 2x2x4 slice. The times are simulated.
32 devices in a mesh: groups: 2 (over y), dp: 8 (over z, x), tensor: 2 (over core).
Axes of the slice: x: 2, y: 2, z: 4, core: 2. Of those that a mesh axis runs over, the one named last changes fastest.
Arguments:
- activations: bfloat16 [16, 384, 5120], P(('groups', 'dp'), None, 'tensor'), parts along dimension 0, may hold values from -6 to 6
- out_grads: bfloat16 [16, 384, 5120], P(('groups', 'dp'), None, 'tensor'), parts along dimension 0, may hold values from -6 to 6
- projections: bfloat16 [5120, 128], P('tensor'), may hold values from -0.078125 to 0.078125
- sample_index: int32 [16, 256], P(('groups', 'dp')), parts along dimension 0, may hold values from 0 to 383
- queries: bfloat16 [512, 4096], P(('groups', 'dp'), 'tensor'), parts along dimension 0, may hold values from -0.005859375 to 0.005859375
Outputs:
- scores: float32 [16, 256], P(('groups', 'dp'), 'tensor'), parts along dimension 0
There are 2 independent parts, one for each index of `groups`. A program takes and returns all parts, laid end to end along the dimension named above; an argument that names none is the same for every part. Nothing has to cross between parts.
All inputs are finite; a program needn't handle non-finite values.
Results may differ from a plain program's by a relative error of at most 0.003.
Values may be sent and summed in bfloat16 or wider, within the bound.
No kernel may reach another device: no remote copies, remote signals or barrier semaphores. Data moves between devices by JAX's collectives and lax.ppermute only.
A program may use at most 64 MiB of HBM per device.

v0:
```python
import jax
import jax.numpy as jnp
from jax import lax
from jax.sharding import PartitionSpec as P


def on_device(activations, out_grads, projections, sample_index, queries):
    picks = sample_index[0]
    picked_in = jnp.take(activations[0], picks, axis=0)
    picked_grad = jnp.take(out_grads[0], picks, axis=0)
    rank = projections.shape[1] // 2
    partial_proj = jnp.concatenate(
        [
            jnp.dot(picked_in, projections[:, 0:rank], preferred_element_type=jnp.float32),
            jnp.dot(
                picked_grad, projections[:, rank : 2 * rank], preferred_element_type=jnp.float32
            ),
        ],
        axis=1,
    )
    own_rows = rank // lax.axis_size("tensor")
    summed = lax.psum(partial_proj, "tensor")
    left = summed[:, 0:rank]
    right = summed[:, rank : 2 * rank]
    right_own = lax.dynamic_slice_in_dim(right, lax.axis_index("tensor") * own_rows, own_rows, 1)
    sketch = jnp.dot(right_own.T, left, precision=lax.Precision.HIGHEST)
    flat_sketch = sketch.astype(jnp.bfloat16).reshape(1, own_rows * rank)
    contract = (((1,), (1,)), ((), ()))
    partial_scores = lax.dot_general(
        flat_sketch,
        lax.all_gather(queries, "dp", axis=0, tiled=True),
        contract,
        preferred_element_type=jnp.float32,
    )
    return lax.psum_scatter(partial_scores, "tensor", scatter_dimension=1, tiled=True)


def solution(mesh):
    in_specs = (
        P(("groups", "dp"), None, "tensor"),
        P(("groups", "dp"), None, "tensor"),
        P("tensor", None),
        P(("groups", "dp"), None),
        P(("groups", "dp"), "tensor"),
    )
    out_specs = P(("groups", "dp"), "tensor")
    return jax.shard_map(
        on_device, mesh=mesh, in_specs=in_specs, out_specs=out_specs, check_vma=False
    )
```

profile of v0, /device:TPU:0, one launch (start us, length us, event | category | flops | bytes accessed | tf_op | source)
XLA Modules:
  0.0 82.8 jit_solution(8266184391114368025)
XLA Ops:
  7.4 0.0 copy-start
  7.4 0.0 all-reduce.2.cloned.1.call-start
  7.4 0.8 compare_select_fusion
  8.2 0.7 compare_and_fusion
  8.9 0.0 copy-done
  8.9 2.5 %gather_fusion.1 = bf16[256,2560]{1,0:T(8,128)(2,1)} fusion(bf16[384,2560]{1,0:T(8,128)(2,1)S(1)} %bitcast.9, s32[1024]{0:T(1024)S(1)} %pad_clamp_fusion), kind=kCustom, calls=%fused_computation.1.clone | custom fusion | bytes 2622464 | tf_op jit(solution)/shard_map/jit(_take)/gather | solution.py:10
  11.4 4.5 %gather_fusion = bf16[256,2560]{1,0:T(8,128)(2,1)S(1)} fusion(bf16[384,2560]{1,0:T(8,128)(2,1)} %bitcast.10, s32[1024]{0:T(1024)S(1)} %pad_clamp_fusion), kind=kCustom, calls=%fused_computation.clone | custom fusion | bytes 2622464 | tf_op jit(solution)/shard_map/jit(_take)/gather | solution.py:9
  16.0 0.0 copy-start.1
  16.0 2.4 %fusion = f32[256,64]{0,1:T(8,128)S(1)} fusion(bf16[256,2560]{1,0:T(8,128)(2,1)} %gather_fusion.1, pred[256]{0:T(512)(128)(4,1)S(1)} %compare_and_fusion, bf16[2560,128]{1,0:T(8,128)(2,1)} %param.9), kind=kOutput, calls=%fused_computation.2 | convolution fusion | flops 84541440 | bytes 2031872 | tf_op jit(solution)/shard_map/dot_general | solution.py:15
  18.4 0.6 fusion.2
  19.0 0.7 pad_maximum_fusion
  19.7 0.0 all-reduce.2.cloned.1.call-update
  19.7 0.0 all-gather.2.cloned.1.call-start
  19.7 0.5 all-gather.2.cloned.1.call-update
  20.3 0.0 reduce-scatter.4.cloned.1.call-start
  20.3 20.1 %all-reduce.2.cloned.1.call-done = f32[256,128]{0,1:T(8,128)} async-done(((f32[256,128]{0,1:T(8,128)}), f32[256,128]{0,1:T(8,128)}) %all-reduce.2.cloned.1.call-update) | async-done | bytes 131088 | tf_op jit(solution)/shard_map/psum | solution.py:22
  40.4 0.8 %slice.20 = f32[256,64]{0,1:T(8,128)S(1)} slice(f32[256,128]{0,1:T(8,128)} %all-reduce.2.cloned.1.call-done), slice={[0:256], [64:128]} | slice | bytes 131072 | tf_op jit(solution)/shard_map/slice | solution.py:24
  41.3 1.0 %convolution_convert_fusion = bf16[32,64]{1,0:T(8,128)(2,1)S(1)} fusion(f32[256,128]{0,1:T(8,128)} %all-reduce.2.cloned.1.call-done, f32[256,64]{0,1:T(8,128)S(1)} %slice.20, s32[]{:T(128)S(6)} %select_n.10), kind=kOutput, calls=%fused_computation.9 | convolution fusion | flops 6293504 | bytes 102404 | tf_op jit(solution)/shard_map/dot_general | solution.py:26
  42.3 0.1 reshape.34
  42.4 23.0 %all-gather.2.cloned.1.call-done = bf16[256,2048]{1,0:T(8,128)(2,1)} async-done(((bf16[32,2048]{1,0:T(8,128)(2,1)}), bf16[256,2048]{1,0:T(8,128)(2,1)}) %all-gather.2.cloned.1.call-update) | async-done | bytes 1048592 | tf_op jit(solution)/shard_map/all_gather | solution.py:31
  65.4 2.3 %convolution_bitcast_fusion = f32[256,1]{1,0:T(8,128)} fusion(bf16[2048,1]{0,1:T(2,128)(2,1)S(1)} %reshape.34, bf16[256,2048]{1,0:T(8,128)(2,1)} %all-gather.2.cloned.1.call-done), kind=kOutput, calls=%fused_computation.8 | convolution fusion | flops 1048576 | bytes 1053696
  67.7 0.0 reduce-scatter.4.cloned.1.call-update
  67.7 6.2 %reduce-scatter.4.cloned.1.call-done = f32[128,1]{1,0:T(8,128)} async-done(((f32[256,1]{1,0:T(8,128)}), f32[128,1]{1,0:T(8,128)}) %reduce-scatter.4.cloned.1.call-update) | async-done | bytes 528
  73.9 1.4 %copy.7 = f32[1,128]{1,0:T(1,128)} copy(f32[1,128]{0,1:T(8,128)} %bitcast.11) | data formatting | bytes 1024
  (2 shorter events, 0.0 us)
Async XLA Ops:
  7.4 1.6 %copy-start = (bf16[1,384,2560]{2,1,0:T(8,128)(2,1)S(1)}, bf16[1,384,2560]{2,1,0:T(8,128)(2,1)}, u32[]{:S(2)}) copy-start(bf16[1,384,2560]{2,1,0:T(8,128)(2,1)} %param.8) | copy-start | bytes 5898244
  7.4 33.1 %all-reduce.2.cloned.1.call-start = ((), (), s32[]{:S(2)}) async-start(), calls=%async_computation.1 | async-start | bytes 262144 | tf_op jit(solution)/shard_map/psum | solution.py:22
  16.0 2.4 %copy-start.1 = (bf16[2560,128]{1,0:T(8,128)(2,1)S(1)}, bf16[2560,128]{1,0:T(8,128)(2,1)}, u32[]{:S(2)}) copy-start(bf16[2560,128]{1,0:T(8,128)(2,1)} %param.9) | copy-start | bytes 1966084
  19.7 45.7 %all-gather.2.cloned.1.call-start = ((), (), s32[]{:S(2)}) async-start(), calls=%async_computation.2 | async-start | bytes 1179648 | tf_op jit(solution)/shard_map/all_gather | solution.py:31
  20.3 53.6 %reduce-scatter.4.cloned.1.call-start = ((), (), s32[]{:S(2)}) async-start(), calls=%async_computation.3 | async-start | bytes 196608
Sparse Core Ops, SparseCore 0:
  19.8 20.5 all-reduce.1
  67.8 6.0 reduce-scatter.3
Sparse Core Ops, SparseCore 1:
  22.3 43.1 all-gather.1
where the time goes:
time: 83.1 us; the launch traced here: 82.8 us
  waiting for transfers between devices  49.9 us (60%)
  between operations  14.9 us (18%)
  local copies, waits for them, and re-layouts  9.43 us (11%)
  matrix products  6.29 us (8%)
  other arithmetic  2.17 us (3%)
    all_gather x1, waiting for transfers between devices, on_device(): lax.all_gather(queries, 'dp', axis=0, tiled=True)  23 us
    psum x1, waiting for transfers between devices, on_device(): summed = lax.psum(partial_proj, 'tensor')  20.1 us
    unnamed x4, waiting for transfers between devices  6.76 us
    gather x1, local copies, waits for them, and re-layouts, on_device(): picked_in = jnp.take(activations[0], picks, axis=0)  4.53 us
    gather x1, local copies, waits for them, and re-layouts, on_device(): picked_grad = jnp.take(out_grads[0], picks, axis=0)  2.5 us
    dot_general x1, matrix products, on_device(): jnp.dot(picked_grad, projections[:, rank:2 * rank], preferred_element_typ...  2.4 us
    unnamed x1, matrix products  2.28 us
  transfers between devices with their start and end apart: 3, of which 3 were waited for; matrix products, arithmetic and copies ran while one was open for 2% of the time, Pallas kernels for 0%

commit v1 on v0

v1 whole, which is shorter than its diff:
```python
import functools

import jax
import jax.numpy as jnp
from jax import lax
from jax.experimental import pallas as pl
from jax.experimental.pallas import tpu as pltpu
from jax.sharding import PartitionSpec as P

F32 = jnp.float32
BF16 = jnp.bfloat16
LANES = 128


def project_kernel(rank, picks_ref, acts_ref, grads_ref, proj_ref, out_ref):
    rows = acts_ref.shape[0]
    samples = picks_ref.shape[1]
    token = lax.broadcasted_iota(jnp.int32, (rows, samples), 0) + pl.program_id(0) * rows
    hits = jnp.where(token == picks_ref[...], 1.0, 0.0).astype(BF16)
    count = jnp.dot(hits, jnp.ones((samples, 2 * rank), BF16), preferred_element_type=F32)
    left = jnp.dot(acts_ref[...], proj_ref[...], preferred_element_type=F32)
    right = jnp.dot(grads_ref[...], proj_ref[...], preferred_element_type=F32)
    column = lax.broadcasted_iota(jnp.int32, (rows, 2 * rank), 1)
    out_ref[...] = jnp.where(column < rank, left * count, right)


def sketch_kernel(rank, place_ref, own_ref, other_ref, out_ref, held):
    total = own_ref[...] + other_ref[...]
    held[...] = lax.dot_general(
        total[:, rank : 2 * rank],
        total[:, 0:rank],
        (((0,), (0,)), ((), ())),
        precision=lax.Precision.HIGHEST,
        preferred_element_type=F32,
    )
    pairs = out_ref.shape[1]
    start = place_ref[0] * (2 * pairs)
    even = held[pl.ds(start, pairs, stride=2), :]
    odd = held[pl.ds(start + 1, pairs, stride=2), :]
    rows = jnp.concatenate([even, odd], axis=1).astype(BF16)
    out_ref[...] = jnp.broadcast_to(rows[None], out_ref.shape)


def score_kernel(place_ref, sketches_ref, queries_ref, out_ref, wide, padded):
    clips, pairs, _ = sketches_ref.shape
    queries = queries_ref.shape[0]
    wide[...] = sketches_ref[...].astype(F32).reshape(clips * pairs, LANES)
    padded[...] = jnp.zeros_like(padded)
    first = pl.multiple_of(place_ref[1] * queries, queries)
    padded[pl.ds(first, queries), :] = queries_ref[...]
    flat = jnp.concatenate(
        [wide[pl.ds(j, clips, stride=pairs), :] for j in range(pairs)], axis=1
    ).astype(BF16)
    scores = lax.dot_general(
        flat, padded[...], (((1,), (1,)), ((), ())), preferred_element_type=F32
    )
    for half in range(2):
        out_ref[:, half, :] = jnp.where(place_ref[2] == half, scores, 0.0)


def on_device(activations, out_grads, projections, sample_index, queries):
    clips = lax.axis_size("dp")
    tokens, units = activations.shape[1:]
    rank = projections.shape[1] // 2
    samples = sample_index.shape[1]
    own_queries, entries = queries.shape
    pairs = entries // LANES
    per_row = LANES // own_queries
    out_rows = clips // 2 // per_row
    spot = lax.axis_index("dp")
    half = lax.axis_index("tensor")
    place = jnp.stack([half, spot % per_row, spot // (clips // 2)]).astype(jnp.int32)
    smem = pl.BlockSpec(memory_space=pltpu.SMEM)
    vmem = pl.BlockSpec(memory_space=pltpu.VMEM)

    tile = LANES
    partial = pl.pallas_call(
        functools.partial(project_kernel, rank),
        grid=(tokens // tile,),
        in_specs=[
            pl.BlockSpec((1, samples), lambda i: (0, 0)),
            pl.BlockSpec((None, tile, units), lambda i: (0, i, 0)),
            pl.BlockSpec((None, tile, units), lambda i: (0, i, 0)),
            pl.BlockSpec((units, 2 * rank), lambda i: (0, 0)),
        ],
        out_specs=pl.BlockSpec((tile, 2 * rank), lambda i: (i, 0)),
        out_shape=jax.ShapeDtypeStruct((tokens, 2 * rank), F32),
        name="project",
    )(sample_index, activations, out_grads, projections)

    other = lax.ppermute(partial, "tensor", [(0, 1), (1, 0)])
    sketch = pl.pallas_call(
        functools.partial(sketch_kernel, rank),
        in_specs=[smem, vmem, vmem],
        out_specs=vmem,
        out_shape=jax.ShapeDtypeStruct((clips, pairs, LANES), BF16),
        scratch_shapes=[pltpu.VMEM((rank, rank), F32)],
        name="sketch",
    )(place, partial, other)

    sketches = lax.all_to_all(sketch, "dp", split_axis=0, concat_axis=0, tiled=True)
    scored = pl.pallas_call(
        score_kernel,
        in_specs=[smem, vmem, vmem],
        out_specs=vmem,
        out_shape=jax.ShapeDtypeStruct((clips, 2, LANES), F32),
        scratch_shapes=[
            pltpu.VMEM((clips * pairs, LANES), F32),
            pltpu.VMEM((LANES, entries), BF16),
        ],
        name="score",
    )(place, sketches, queries)

    back = lax.all_to_all(
        scored.reshape(2 * clips, LANES), ("dp", "tensor"), split_axis=0, concat_axis=0, tiled=True
    )
    summed = back.reshape(2, out_rows, 2 * per_row, LANES).sum(axis=(0, 2))
    return summed.reshape(1, out_rows * LANES)


def solution(mesh):
    in_specs = (
        P(("groups", "dp"), None, "tensor"),
        P(("groups", "dp"), None, "tensor"),
        P("tensor", None),
        P(("groups", "dp"), None),
        P(("groups", "dp"), "tensor"),
    )
    out_specs = P(("groups", "dp"), "tensor")
    return jax.shard_map(
        on_device, mesh=mesh, in_specs=in_specs, out_specs=out_specs, check_vma=False
    )
```

time: 83.1 us -> 35.4 us (0.43)
  waiting for transfers between devices: 49.9 us -> 0.61 us
  blocking collectives: 0 us -> 23.7 us
  between operations: 14.9 us -> 0.01 us
  local copies, waits for them, and re-layouts: 9.43 us -> 0.68 us
  Pallas kernels: 0 us -> 8.37 us
  matrix products: 6.29 us -> 0 us
  other arithmetic: 2.17 us -> 1.21 us
    all_to_all x0 -> x2, blocking collectives: none -> 23.7 us  [the longest x1 14 us: on_device(): lax.all_to_all(sketch, 'dp', split_axis=0, concat_axis=0, tiled=True)]
    all_gather x1 -> x0, waiting for transfers between devices: 23 us -> none  [on_device(): lax.all_gather(queries, 'dp', axis=0, tiled=True)]
    psum x1 -> x0, waiting for transfers between devices: 20.1 us -> none  [on_device(): summed = lax.psum(partial_proj, 'tensor')]
    pallas_call x0 -> x3, Pallas kernels: none -> 8.37 us  [the longest x1 4.46 us: on_device(): pl.pallas_call(functools.partial(project_kernel, rank), grid=(tokens // t...]
    gather x2 -> x0, local copies, waits for them, and re-layouts: 7.03 us -> none  [the longest x1 4.53 us: on_device(): picked_in = jnp.take(activations[0], picks, axis=0)]
    unnamed x4 -> x0, waiting for transfers between devices: 6.76 us -> none
    dot_general x3 -> x0, matrix products: 4.02 us -> none  [the longest x1 2.4 us: on_device(): jnp.dot(picked_grad, projections[:, rank:2 * rank], preferred_element_typ...]
    unnamed x1 -> x0, matrix products: 2.28 us -> none
  transfers between devices with their start and end apart: 3 -> 1, of which waited for: 3 -> 1; matrix products, arithmetic and copies ran while one was open for 2% -> 2% of each run, Pallas kernels for 0% -> 0%
where the time goes in v1:
time: 35.4 us; the launch traced here: 35.1 us
  blocking collectives  23.7 us (67%)
  Pallas kernels  8.37 us (24%)
  other arithmetic  1.21 us (3%)
  local copies, waits for them, and re-layouts  0.68 us (2%)
  waiting for transfers between devices  0.61 us (2%)
  starting transfers between devices  0.46 us (1%)
    all_to_all x1, blocking collectives, on_device(): lax.all_to_all(sketch, 'dp', split_axis=0, concat_axis=0, tiled=True)  14 us
    all_to_all x1, blocking collectives, on_device(): lax.all_to_all(scored.reshape(2 * clips, LANES), ('dp', 'tensor'), split_...  9.79 us
    pallas_call x1, Pallas kernels, on_device(): pl.pallas_call(functools.partial(project_kernel, rank), grid=(tokens // t...  4.46 us
    pallas_call x1, Pallas kernels, on_device(): pl.pallas_call(functools.partial(sketch_kernel, rank), in_specs=[smem, vm...  2.08 us
    pallas_call x1, Pallas kernels, on_device(): pl.pallas_call(score_kernel, in_specs=[smem, vmem, vmem], out_specs=vmem,...  1.83 us
  transfers between devices with their start and end apart: 1, of which 1 were waited for; matrix products, arithmetic and copies ran while one was open for 2% of the time, Pallas kernels for 0%

profile of v1, /device:TPU:0, one launch (start us, length us, event | category | flops | bytes accessed | tf_op | source)
XLA Modules:
  0.0 35.1 jit_solution(1293903168133535516)
XLA Ops:
  0.0 4.5 %project.1.own_ref = f32[384,128]{1,0:T(8,128)} custom-call(s32[1,256]{1,0:T(1,128)} %picks_ref.1, bf16[1,384,2560]{2,1,0:T(8,128)(2,1)} %acts_ref.1, bf16[1,384,2560]{2,1,0:T(8,128)(2,1)} %grads_ref.1, bf16[2560,128]{1,0:T(8,128)(2,1)} %proj_ref.1), custom_call_target="tpu_custom_call" | custom-call | tf_op jit(solution)/shard_map/project/pallas_call | solution.py:77
  4.5 0.5 %collective-permute-start = (f32[384,128]{1,0:T(8,128)}, f32[384,128]{1,0:T(8,128)S(1)}, u32[]{:S(2)}, u32[]{:S(2)}) collective-permute-start(f32[384,128]{1,0:T(8,128)} %project.1.own_ref), channel_id=1, source_target_pairs={{0,1},{1,0},{2,3},{3,2},{4,5},{5,4},{6,7},{7,6},{8,9},{9,8},{10,11... | collective-permute-start | bytes 589832 | tf_op jit(solution)/shard_map/ppermute | solution.py:91
  4.9 0.7 %pad_add_fusion.place_ref = s32[3]{0:T(128)} fusion(s32[1]{0:T(128)} %bitcast.2, s32[1]{0:T(128)} %bitcast.1, s32[1]{0:T(128)} %bitcast), kind=kLoop, calls=%fused_computation | loop fusion | flops 6 | bytes 24 | tf_op jit(solution)/shard_map/stack | solution.py:72
  5.6 0.6 %collective-permute-done.other_ref = f32[384,128]{1,0:T(8,128)S(1)} collective-permute-done((f32[384,128]{1,0:T(8,128)}, f32[384,128]{1,0:T(8,128)S(1)}, u32[]{:S(2)}, u32[]{:S(2)}) %collective-permute-start) | collective-permute-done | bytes 196640 | tf_op jit(solution)/shard_map/ppermute | solution.py:91
  6.2 0.0 copy-start
  6.2 0.7 %copy-done = f32[384,128]{1,0:T(8,128)} copy-done((f32[384,128]{1,0:T(8,128)}, f32[384,128]{1,0:T(8,128)S(1)}, u32[]{:S(2)}) %copy-start) | copy-done | bytes 196632
  6.9 2.1 %sketch.1 = bf16[8,16,128]{2,1,0:T(8,128)(2,1)} custom-call(s32[3]{0:T(128)} %pad_add_fusion.place_ref, f32[384,128]{1,0:T(8,128)} %project.1.own_ref, f32[384,128]{1,0:T(8,128)} %copy-done), custom_call_target="tpu_custom_call" | custom-call | tf_op jit(solution)/shard_map/sketch/pallas_call | solution.py:92
  9.0 14.0 %all_to_all.14.sketches_ref = bf16[8,16,128]{2,1,0:T(8,128)(2,1)} all-to-all(bf16[8,16,128]{2,1,0:T(8,128)(2,1)} %sketch.1), channel_id=1, replica_groups=mesh['groups'=2,'dp'=8,'tensor'=2] {'dp'}, dimensions={0} | all-to-all | bytes 65536 | tf_op jit(solution)/shard_map/all_to_all | solution.py:101
  22.9 1.8 %score.1 = f32[8,2,128]{2,1,0:T(2,128)} custom-call(s32[3]{0:T(128)} %pad_add_fusion.place_ref, bf16[8,16,128]{2,1,0:T(8,128)(2,1)} %all_to_all.14.sketches_ref, bf16[32,2048]{1,0:T(8,128)(2,1)} %queries_ref.1), custom_call_target="tpu_custom_call" | custom-call | tf_op jit(solution)/shard_map/score/pallas_call | solution.py:102
  24.7 9.8 %all_to_all.15 = f32[16,1,128]{2,1,0:T(1,128)S(1)} all-to-all(f32[16,1,128]{2,1,0:T(1,128)} %bitcast.7), channel_id=1, replica_groups=mesh['groups'=2,'dp'=8,'tensor'=2] {'dp','tensor'}, dimensions={0} | all-to-all | bytes 16384 | tf_op jit(solution)/shard_map/all_to_all | solution.py:114
  34.5 0.5 %reduce_sum.11 = f32[128]{0:T(128)} reduce(f32[16,1,128]{2,1,0:T(1,128)S(1)} %all_to_all.15, f32[]{:T(128)} %constant.35.clone.1), dimensions={0,1}, to_apply=%region_0.1 | reduce | flops 1920 | bytes 8708 | tf_op jit(solution)/shard_map/reduce_sum | solution.py:117
Async XLA Ops:
  4.5 1.7 %collective-permute-start = (f32[384,128]{1,0:T(8,128)}, f32[384,128]{1,0:T(8,128)S(1)}, u32[]{:S(2)}, u32[]{:S(2)}) collective-permute-start(f32[384,128]{1,0:T(8,128)} %project.1.own_ref), channel_id=1, source_target_pairs={{0,1},{1,0},{2,3},{3,2},{4,5},{5,4},{6,7},{7,6},{8,9},{9,8},{10,11... | collective-permute-start | bytes 589832 | tf_op jit(solution)/shard_map/ppermute | solution.py:91
  6.2 0.7 %copy-start = (f32[384,128]{1,0:T(8,128)}, f32[384,128]{1,0:T(8,128)S(1)}, u32[]{:S(2)}) copy-start(f32[384,128]{1,0:T(8,128)S(1)} %collective-permute-done.other_ref) | copy-start | bytes 589828

commit v2 on v0

v2 whole, which is shorter than its diff:
```python
import functools

import jax
import jax.numpy as jnp
from jax import lax
from jax.experimental import pallas as pl
from jax.experimental.pallas import tpu as pltpu
from jax.sharding import PartitionSpec as P

F32 = jnp.float32
BF16 = jnp.bfloat16
LANES = 128
CHUNK = 512


def project_kernel(rank, picks_ref, acts_ref, grads_ref, proj_ref, out_ref, acts, grads, proj, sems):
    tokens, units = acts.shape
    samples = picks_ref.shape[1]
    copies = []
    for i in range(units // CHUNK):
        part = pl.ds(i * CHUNK, CHUNK)
        three = (
            pltpu.make_async_copy(proj_ref.at[part, :], proj.at[part, :], sems.at[i, 0]),
            pltpu.make_async_copy(acts_ref.at[0, :, part], acts.at[:, part], sems.at[i, 1]),
            pltpu.make_async_copy(grads_ref.at[0, :, part], grads.at[:, part], sems.at[i, 2]),
        )
        for copy in three:
            copy.start()
        copies.append(three)

    token = lax.broadcasted_iota(jnp.int32, (tokens, samples), 0)
    hits = jnp.where(token == picks_ref[...], 1.0, 0.0).astype(BF16)
    count = jnp.dot(hits, jnp.ones((samples, 2 * rank), BF16), preferred_element_type=F32)
    column = lax.broadcasted_iota(jnp.int32, (tokens, 2 * rank), 1)
    count = jnp.where(column < rank, count, 1.0)

    is_left = lax.broadcasted_iota(jnp.int32, (CHUNK, 2 * rank), 1) < rank
    total = None
    for i, three in enumerate(copies):
        for copy in three:
            copy.wait()
        part = pl.ds(i * CHUNK, CHUNK)
        weights = proj[part, :]
        zero = jnp.zeros_like(weights)
        both = jnp.concatenate(
            [jnp.where(is_left, weights, zero), jnp.where(is_left, zero, weights)], axis=0
        )
        term = jnp.dot(
            jnp.concatenate([acts[:, part], grads[:, part]], axis=1), both, preferred_element_type=F32
        )
        total = term if total is None else total + term
    out_ref[...] = total * count


def sketch_kernel(rank, own_ref, other_ref, out_ref, held):
    total = own_ref[...] + other_ref[...]
    held[...] = lax.dot_general(
        total[:, rank : 2 * rank],
        total[:, 0:rank],
        (((0,), (0,)), ((), ())),
        precision=lax.Precision.HIGHEST,
        preferred_element_type=F32,
    )
    pairs = out_ref.shape[0]
    even = held[pl.ds(0, pairs, stride=2), :]
    odd = held[pl.ds(1, pairs, stride=2), :]
    out_ref[...] = jnp.concatenate([even, odd], axis=1).astype(BF16)


def score_kernel(rounds, *refs):
    sketches, (own_ref, other_ref), outs, wide = (
        refs[:rounds],
        refs[rounds : rounds + 2],
        refs[rounds + 2 : -1],
        refs[-1],
    )
    pairs = sketches[0].shape[0]
    queries = own_ref.shape[0]
    slots = wide.shape[0] // pairs
    wide[...] = jnp.zeros_like(wide)
    for r in range(rounds):
        wide[pl.ds(r, pairs, stride=slots), :] = sketches[r][...].astype(F32)
    half = lax.axis_index("tensor")
    scores = None
    for side, ref in ((half, own_ref), (1 - half, other_ref)):
        start = side * (slots * pairs // 2)
        flat = jnp.concatenate(
            [
                wide[pl.ds(pl.multiple_of(start + j * slots, slots), slots), :]
                for j in range(pairs // 2)
            ],
            axis=1,
        ).astype(BF16)
        term = lax.dot_general(
            flat, ref[...], (((1,), (1,)), ((), ())), preferred_element_type=F32
        )
        scores = term if scores is None else scores + term
    low = lax.rem(lax.axis_index("dp"), rounds)
    spread = jnp.concatenate([scores] * rounds, axis=1)
    block = lax.broadcasted_iota(jnp.int32, spread.shape, 1) // queries
    spread = jnp.where(block == low, spread, 0.0)
    for r in range(rounds):
        outs[r][...] = spread[r : r + 1, :]


def on_device(activations, out_grads, projections, sample_index, queries):
    clips = lax.axis_size("dp")
    tokens, units = activations.shape[1:]
    rank = projections.shape[1] // 2
    own_queries, entries = queries.shape
    pairs = 2 * entries // LANES
    rounds = clips // 2
    slots = -(-rounds // 8) * 8
    vmem = pl.BlockSpec(memory_space=pltpu.VMEM)
    hbm = pl.BlockSpec(memory_space=pl.ANY)
    swap = [(0, 1), (1, 0)]

    def place(a, l, t):
        return (a * rounds + l) * 2 + t

    there = [
        [
            (place(a, l, t), place(t, (l + r) % rounds, a))
            for a in range(2)
            for l in range(rounds)
            for t in range(2)
        ]
        for r in range(rounds)
    ]
    back = [[(dst, src) for src, dst in perm] for perm in there]

    other_queries = lax.ppermute(queries, "tensor", swap)
    partial = pl.pallas_call(
        functools.partial(project_kernel, rank),
        in_specs=[vmem, hbm, hbm, hbm],
        out_specs=vmem,
        out_shape=jax.ShapeDtypeStruct((tokens, 2 * rank), F32),
        scratch_shapes=[
            pltpu.VMEM((tokens, units), BF16),
            pltpu.VMEM((tokens, units), BF16),
            pltpu.VMEM((units, 2 * rank), BF16),
            pltpu.SemaphoreType.DMA((units // CHUNK, 3)),
        ],
        compiler_params=pltpu.CompilerParams(vmem_limit_bytes=16 << 20),
        name="project",
    )(sample_index, activations, out_grads, projections)

    other = lax.ppermute(partial, "tensor", swap)
    sketch = pl.pallas_call(
        functools.partial(sketch_kernel, rank),
        in_specs=[vmem, vmem],
        out_specs=vmem,
        out_shape=jax.ShapeDtypeStruct((pairs, LANES), BF16),
        scratch_shapes=[pltpu.VMEM((rank, rank), F32)],
        compiler_params=pltpu.CompilerParams(vmem_limit_bytes=8 << 20),
        name="sketch",
    )(partial, other)

    sketches = [lax.ppermute(sketch, ("dp", "tensor"), perm) for perm in there]
    width = rounds * own_queries
    scored = pl.pallas_call(
        functools.partial(score_kernel, rounds),
        in_specs=[vmem] * (rounds + 2),
        out_specs=[vmem] * rounds,
        out_shape=[jax.ShapeDtypeStruct((1, width), F32)] * rounds,
        scratch_shapes=[pltpu.VMEM((pairs * slots, LANES), F32)],
        compiler_params=pltpu.CompilerParams(vmem_limit_bytes=16 << 20),
        name="score",
    )(*sketches, queries, other_queries)

    parts = [lax.ppermute(s, ("dp", "tensor"), perm) for s, perm in zip(scored, back)]
    return functools.reduce(jnp.add, parts)


def solution(mesh):
    in_specs = (
        P(("groups", "dp"), None, "tensor"),
        P(("groups", "dp"), None, "tensor"),
        P("tensor", None),
        P(("groups", "dp"), None),
        P(("groups", "dp"), "tensor"),
    )
    out_specs = P(("groups", "dp"), "tensor")
    return jax.shard_map(
        on_device, mesh=mesh, in_specs=in_specs, out_specs=out_specs, check_vma=False
    )
```

time: 83.1 us -> 38.7 us (0.47)
  the two profiles are of different devices: /device:TPU:0 before, /device:TPU:1 now
where the time goes in v2:
time: 38.7 us; the launch traced here: 38.4 us
  starting transfers between devices  18 us (47%)
  waiting for transfers between devices  10.5 us (27%)
  local copies, waits for them, and re-layouts  4.86 us (13%)
  Pallas kernels  4.46 us (12%)
  other arithmetic  0.52 us (1%)
    ppermute x4, starting transfers between devices, on_device(): sketches = [lax.ppermute(sketch, ('dp', 'tensor'), perm) for perm in there]  11.2 us
    ppermute x4, starting transfers between devices, on_device(): lax.ppermute(s, ('dp', 'tensor'), perm)  6.28 us
    ppermute x4, waiting for transfers between devices, on_device(): lax.ppermute(s, ('dp', 'tensor'), perm)  5.66 us
    unnamed x10, local copies, waits for them, and re-layouts  4.86 us
    ppermute x4, waiting for transfers between devices, on_device(): sketches = [lax.ppermute(sketch, ('dp', 'tensor'), perm) for perm in there]  3.92 us
    pallas_call x1, Pallas kernels, on_device(): pl.pallas_call(functools.partial(project_kernel, rank), in_specs=[vmem, h...  3.74 us
    ppermute x1, waiting for transfers between devices, on_device(): other = lax.ppermute(partial, 'tensor', swap)  0.93 us
  transfers between devices with their start and end apart: 10, of which 7 were waited for; matrix products, arithmetic and copies ran while one was open for 0% of the time, Pallas kernels for 1%

profile of v2, /device:TPU:1, one launch (start us, length us, event | category | flops | bytes accessed | tf_op | source)
XLA Modules:
  0.0 38.4 jit_solution(17518417218575311158)
XLA Ops:
  0.0 1.5 %copy-done = bf16[1,384,2560]{2,1,0:T(8,128)(2,1)S(1)} copy-done((bf16[1,384,2560]{2,1,0:T(8,128)(2,1)S(1)}, bf16[1,384,2560]{2,1,0:T(8,128)(2,1)}, u32[]{:S(2)}) %copy-start) | copy-done | bytes 1966104
  1.5 1.5 %copy-done.1 = bf16[1,384,2560]{2,1,0:T(8,128)(2,1)S(1)} copy-done((bf16[1,384,2560]{2,1,0:T(8,128)(2,1)S(1)}, bf16[1,384,2560]{2,1,0:T(8,128)(2,1)}, u32[]{:S(2)}) %copy-start.1) | copy-done | bytes 1966104
  3.1 1.1 %copy-done.2 = bf16[2560,128]{1,0:T(8,128)(2,1)S(1)} copy-done((bf16[2560,128]{1,0:T(8,128)(2,1)S(1)}, bf16[2560,128]{1,0:T(8,128)(2,1)}, u32[]{:S(2)}) %copy-start.2) | copy-done | bytes 655384
  4.2 0.7 %copy-done.4 = s32[1,256]{1,0:T(1,128)S(1)} copy-done((s32[1,256]{1,0:T(1,128)S(1)}, s32[1,256]{1,0:T(1,128)}, u32[]{:S(2)}) %copy-start.4) | copy-done | bytes 1048
  4.9 3.7 %project.1.own_ref = f32[384,128]{1,0:T(8,128)S(1)} custom-call(s32[1,256]{1,0:T(1,128)S(1)} %copy-done.4, bf16[1,384,2560]{2,1,0:T(8,128)(2,1)S(1)} %copy-done, bf16[1,384,2560]{2,1,0:T(8,128)(2,1)S(1)} %copy-done.1, bf16[2560,128]{1,0:T(8,128)(2,1)S(1)} %copy-done.2), custom_call_target="tpu_custom_call" | custom-call | tf_op jit(solution)/shard_map/project/pallas_call | solution.py:133
  8.6 0.1 collective-permute-start
  8.7 0.5 %collective-permute-start.5 = (bf16[32,2048]{1,0:T(8,128)(2,1)S(1)}, bf16[32,2048]{1,0:T(8,128)(2,1)S(1)}, u32[]{:S(2)}, u32[]{:S(2)}) collective-permute-start(bf16[32,2048]{1,0:T(8,128)(2,1)S(1)} %copy-done.3), channel_id=1, source_target_pairs={{0,1},{1,0},{2,3},{3,2},{4,5},{5,4},{6,7},{7,6},{8,9},{9,8},{10,11... | collective-permute-start | bytes 393224 | tf_op jit(solution)/shard_map/ppermute | solution.py:132
  9.2 0.9 %collective-permute-done.other_ref = f32[384,128]{1,0:T(8,128)S(1)} collective-permute-done((f32[384,128]{1,0:T(8,128)S(1)}, f32[384,128]{1,0:T(8,128)S(1)}, u32[]{:S(2)}, u32[]{:S(2)}) %collective-permute-start) | collective-permute-done | bytes 196640 | tf_op jit(solution)/shard_map/ppermute | solution.py:148
  10.1 0.5 %sketch.1 = bf16[32,128]{1,0:T(8,128)(2,1)S(1)} custom-call(f32[384,128]{1,0:T(8,128)S(1)} %project.1.own_ref, f32[384,128]{1,0:T(8,128)S(1)} %collective-permute-done.other_ref), custom_call_target="tpu_custom_call" | custom-call | tf_op jit(solution)/shard_map/sketch/pallas_call | solution.py:149
  10.6 5.6 %collective-permute-start.1 = (bf16[32,128]{1,0:T(8,128)(2,1)S(1)}, bf16[32,128]{1,0:T(8,128)(2,1)S(1)}, u32[]{:S(2)}, u32[]{:S(2)}) collective-permute-start(bf16[32,128]{1,0:T(8,128)(2,1)S(1)} %sketch.1), channel_id=1, source_target_pairs={{0,0},{1,8},{2,2},{3,10},{4,4},{5,12},{6,6},{7,14},{8,1},{9,9},{10... | collective-permute-start | bytes 24584 | tf_op jit(solution)/shard_map/ppermute | solution.py:159
  16.2 1.1 %collective-permute-start.2 = (bf16[32,128]{1,0:T(8,128)(2,1)S(1)}, bf16[32,128]{1,0:T(8,128)(2,1)S(1)}, u32[]{:S(2)}, u32[]{:S(2)}) collective-permute-start(bf16[32,128]{1,0:T(8,128)(2,1)S(1)} %sketch.1), channel_id=1, source_target_pairs={{0,2},{1,10},{2,4},{3,12},{4,6},{5,14},{6,0},{7,8},{8,3},{9,11},{1... | collective-permute-start | bytes 24584 | tf_op jit(solution)/shard_map/ppermute | solution.py:159
  17.2 3.6 %collective-permute-start.3 = (bf16[32,128]{1,0:T(8,128)(2,1)S(1)}, bf16[32,128]{1,0:T(8,128)(2,1)S(1)}, u32[]{:S(2)}, u32[]{:S(2)}) collective-permute-start(bf16[32,128]{1,0:T(8,128)(2,1)S(1)} %sketch.1), channel_id=1, source_target_pairs={{0,4},{1,12},{2,6},{3,14},{4,0},{5,8},{6,2},{7,10},{8,5},{9,13},{1... | collective-permute-start | bytes 24584 | tf_op jit(solution)/shard_map/ppermute | solution.py:159
  20.8 0.9 %collective-permute-start.4 = (bf16[32,128]{1,0:T(8,128)(2,1)S(1)}, bf16[32,128]{1,0:T(8,128)(2,1)S(1)}, u32[]{:S(2)}, u32[]{:S(2)}) collective-permute-start(bf16[32,128]{1,0:T(8,128)(2,1)S(1)} %sketch.1), channel_id=1, source_target_pairs={{0,6},{1,14},{2,0},{3,8},{4,2},{5,10},{6,4},{7,12},{8,7},{9,15},{1... | collective-permute-start | bytes 24584 | tf_op jit(solution)/shard_map/ppermute | solution.py:159
  21.8 0.2 collective-permute-done.2.refs_1_
  22.0 0.2 collective-permute-done.3.refs_2_
  22.2 3.5 %collective-permute-done.4.refs_3_ = bf16[32,128]{1,0:T(8,128)(2,1)S(1)} collective-permute-done((bf16[32,128]{1,0:T(8,128)(2,1)S(1)}, bf16[32,128]{1,0:T(8,128)(2,1)S(1)}, u32[]{:S(2)}, u32[]{:S(2)}) %collective-permute-start.4) | collective-permute-done | bytes 8224 | tf_op jit(solution)/shard_map/ppermute | solution.py:159
  25.7 0.3 score.1
  26.0 1.9 %collective-permute-start.6 = (f32[1,128]{1,0:T(1,128)S(1)}, f32[1,128]{1,0:T(1,128)S(1)}, u32[]{:S(2)}, u32[]{:S(2)}) collective-permute-start(f32[1,128]{1,0:T(1,128)S(1)} %get-tuple-element.9), channel_id=1, source_target_pairs={{0,0},{8,1},{2,2},{10,3},{4,4},{12,5},{6,6},{14,7},{1,8},{9,9},{3,... | collective-permute-start | bytes 1544 | tf_op jit(solution)/shard_map/ppermute | solution.py:171
  27.9 1.9 %collective-permute-start.7 = (f32[1,128]{1,0:T(1,128)S(1)}, f32[1,128]{1,0:T(1,128)S(1)}, u32[]{:S(2)}, u32[]{:S(2)}) collective-permute-start(f32[1,128]{1,0:T(1,128)S(1)} %get-tuple-element.10), channel_id=1, source_target_pairs={{2,0},{10,1},{4,2},{12,3},{6,4},{14,5},{0,6},{8,7},{3,8},{11,9},{5... | collective-permute-start | bytes 1544 | tf_op jit(solution)/shard_map/ppermute | solution.py:171
  29.8 2.5 %collective-permute-start.8 = (f32[1,128]{1,0:T(1,128)S(1)}, f32[1,128]{1,0:T(1,128)S(1)}, u32[]{:S(2)}, u32[]{:S(2)}) collective-permute-start(f32[1,128]{1,0:T(1,128)S(1)} %get-tuple-element.11), channel_id=1, source_target_pairs={{4,0},{12,1},{6,2},{14,3},{0,4},{8,5},{2,6},{10,7},{5,8},{13,9},{7... | collective-permute-start | bytes 1544 | tf_op jit(solution)/shard_map/ppermute | solution.py:171
  32.3 0.5 %collective-permute-done.7 = f32[1,128]{1,0:T(1,128)S(1)} collective-permute-done((f32[1,128]{1,0:T(1,128)S(1)}, f32[1,128]{1,0:T(1,128)S(1)}, u32[]{:S(2)}, u32[]{:S(2)}) %collective-permute-start.7) | collective-permute-done | bytes 544 | tf_op jit(solution)/shard_map/ppermute | solution.py:171
  32.7 1.8 %collective-permute-done.8 = f32[1,128]{1,0:T(1,128)S(1)} collective-permute-done((f32[1,128]{1,0:T(1,128)S(1)}, f32[1,128]{1,0:T(1,128)S(1)}, u32[]{:S(2)}, u32[]{:S(2)}) %collective-permute-start.8) | collective-permute-done | bytes 544 | tf_op jit(solution)/shard_map/ppermute | solution.py:171
  34.6 3.4 %collective-permute-done.9 = f32[1,128]{1,0:T(1,128)S(1)} collective-permute-done((f32[1,128]{1,0:T(1,128)S(1)}, f32[1,128]{1,0:T(1,128)S(1)}, u32[]{:S(2)}, u32[]{:S(2)}) %collective-permute-start.9) | collective-permute-done | bytes 544 | tf_op jit(solution)/shard_map/ppermute | solution.py:171
  37.9 0.5 %add_add_fusion = f32[1,128]{1,0:T(1,128)} fusion(f32[1,128]{1,0:T(1,128)S(1)} %collective-permute-done.9, f32[1,128]{1,0:T(1,128)S(1)} %collective-permute-done.8, f32[1,128]{1,0:T(1,128)S(1)} %collective-permute-done.6, f32[1,128]{1,0:T(1,128)S(1)} %collective-permute-done.7), kind=kLoop, calls=%fused_computation | loop fusion | flops 384 | bytes 2560 | tf_op jit(solution)/shard_map/add | solution.py:172
  (10 shorter events, 0.0 us)
Async XLA Ops:
  0.0 1.5 %copy-start = (bf16[1,384,2560]{2,1,0:T(8,128)(2,1)S(1)}, bf16[1,384,2560]{2,1,0:T(8,128)(2,1)}, u32[]{:S(2)}) copy-start(bf16[1,384,2560]{2,1,0:T(8,128)(2,1)} %acts_ref.1) | copy-start | bytes 5898244
  1.5 1.5 %copy-start.1 = (bf16[1,384,2560]{2,1,0:T(8,128)(2,1)S(1)}, bf16[1,384,2560]{2,1,0:T(8,128)(2,1)}, u32[]{:S(2)}) copy-start(bf16[1,384,2560]{2,1,0:T(8,128)(2,1)} %grads_ref.1) | copy-start | bytes 5898244
  3.1 1.1 %copy-start.2 = (bf16[2560,128]{1,0:T(8,128)(2,1)S(1)}, bf16[2560,128]{1,0:T(8,128)(2,1)}, u32[]{:S(2)}) copy-start(bf16[2560,128]{1,0:T(8,128)(2,1)} %proj_ref.1) | copy-start | bytes 1966084
  4.2 0.7 %copy-start.4 = (s32[1,256]{1,0:T(1,128)S(1)}, s32[1,256]{1,0:T(1,128)}, u32[]{:S(2)}) copy-start(s32[1,256]{1,0:T(1,128)} %picks_ref.1) | copy-start | bytes 3076
  4.9 3.9 %copy-start.3 = (bf16[32,2048]{1,0:T(8,128)(2,1)S(1)}, bf16[32,2048]{1,0:T(8,128)(2,1)}, u32[]{:S(2)}) copy-start(bf16[32,2048]{1,0:T(8,128)(2,1)} %refs_4_.1) | copy-start | bytes 393220
  8.6 1.5 %collective-permute-start = (f32[384,128]{1,0:T(8,128)S(1)}, f32[384,128]{1,0:T(8,128)S(1)}, u32[]{:S(2)}, u32[]{:S(2)}) collective-permute-start(f32[384,128]{1,0:T(8,128)S(1)} %project.1.own_ref), channel_id=1, source_target_pairs={{0,1},{1,0},{2,3},{3,2},{4,5},{5,4},{6,7},{7,6},{8,9},{9,8},{10,11... | collective-permute-start | bytes 589832 | tf_op jit(solution)/shard_map/ppermute | solution.py:148
  8.7 13.0 %collective-permute-start.5 = (bf16[32,2048]{1,0:T(8,128)(2,1)S(1)}, bf16[32,2048]{1,0:T(8,128)(2,1)S(1)}, u32[]{:S(2)}, u32[]{:S(2)}) collective-permute-start(bf16[32,2048]{1,0:T(8,128)(2,1)S(1)} %copy-done.3), channel_id=1, source_target_pairs={{0,1},{1,0},{2,3},{3,2},{4,5},{5,4},{6,7},{7,6},{8,9},{9,8},{10,11... | collective-permute-start | bytes 393224 | tf_op jit(solution)/shard_map/ppermute | solution.py:132
  10.6 11.2 %collective-permute-start.1 = (bf16[32,128]{1,0:T(8,128)(2,1)S(1)}, bf16[32,128]{1,0:T(8,128)(2,1)S(1)}, u32[]{:S(2)}, u32[]{:S(2)}) collective-permute-start(bf16[32,128]{1,0:T(8,128)(2,1)S(1)} %sketch.1), channel_id=1, source_target_pairs={{0,0},{1,8},{2,2},{3,10},{4,4},{5,12},{6,6},{7,14},{8,1},{9,9},{10... | collective-permute-start | bytes 24584 | tf_op jit(solution)/shard_map/ppermute | solution.py:159
  16.2 5.8 %collective-permute-start.2 = (bf16[32,128]{1,0:T(8,128)(2,1)S(1)}, bf16[32,128]{1,0:T(8,128)(2,1)S(1)}, u32[]{:S(2)}, u32[]{:S(2)}) collective-permute-start(bf16[32,128]{1,0:T(8,128)(2,1)S(1)} %sketch.1), channel_id=1, source_target_pairs={{0,2},{1,10},{2,4},{3,12},{4,6},{5,14},{6,0},{7,8},{8,3},{9,11},{1... | collective-permute-start | bytes 24584 | tf_op jit(solution)/shard_map/ppermute | solution.py:159
  17.2 5.0 %collective-permute-start.3 = (bf16[32,128]{1,0:T(8,128)(2,1)S(1)}, bf16[32,128]{1,0:T(8,128)(2,1)S(1)}, u32[]{:S(2)}, u32[]{:S(2)}) collective-permute-start(bf16[32,128]{1,0:T(8,128)(2,1)S(1)} %sketch.1), channel_id=1, source_target_pairs={{0,4},{1,12},{2,6},{3,14},{4,0},{5,8},{6,2},{7,10},{8,5},{9,13},{1... | collective-permute-start | bytes 24584 | tf_op jit(solution)/shard_map/ppermute | solution.py:159
  20.8 4.9 %collective-permute-start.4 = (bf16[32,128]{1,0:T(8,128)(2,1)S(1)}, bf16[32,128]{1,0:T(8,128)(2,1)S(1)}, u32[]{:S(2)}, u32[]{:S(2)}) collective-permute-start(bf16[32,128]{1,0:T(8,128)(2,1)S(1)} %sketch.1), channel_id=1, source_target_pairs={{0,6},{1,14},{2,0},{3,8},{4,2},{5,10},{6,4},{7,12},{8,7},{9,15},{1... | collective-permute-start | bytes 24584 | tf_op jit(solution)/shard_map/ppermute | solution.py:159
  26.0 6.3 %collective-permute-start.6 = (f32[1,128]{1,0:T(1,128)S(1)}, f32[1,128]{1,0:T(1,128)S(1)}, u32[]{:S(2)}, u32[]{:S(2)}) collective-permute-start(f32[1,128]{1,0:T(1,128)S(1)} %get-tuple-element.9), channel_id=1, source_target_pairs={{0,0},{8,1},{2,2},{10,3},{4,4},{12,5},{6,6},{14,7},{1,8},{9,9},{3,... | collective-permute-start | bytes 1544 | tf_op jit(solution)/shard_map/ppermute | solution.py:171
  27.9 4.8 %collective-permute-start.7 = (f32[1,128]{1,0:T(1,128)S(1)}, f32[1,128]{1,0:T(1,128)S(1)}, u32[]{:S(2)}, u32[]{:S(2)}) collective-permute-start(f32[1,128]{1,0:T(1,128)S(1)} %get-tuple-element.10), channel_id=1, source_target_pairs={{2,0},{10,1},{4,2},{12,3},{6,4},{14,5},{0,6},{8,7},{3,8},{11,9},{5... | collective-permute-start | bytes 1544 | tf_op jit(solution)/shard_map/ppermute | solution.py:171
  29.8 4.8 %collective-permute-start.8 = (f32[1,128]{1,0:T(1,128)S(1)}, f32[1,128]{1,0:T(1,128)S(1)}, u32[]{:S(2)}, u32[]{:S(2)}) collective-permute-start(f32[1,128]{1,0:T(1,128)S(1)} %get-tuple-element.11), channel_id=1, source_target_pairs={{4,0},{12,1},{6,2},{14,3},{0,4},{8,5},{2,6},{10,7},{5,8},{13,9},{7... | collective-permute-start | bytes 1544 | tf_op jit(solution)/shard_map/ppermute | solution.py:171
  32.2 5.7 %collective-permute-start.9 = (f32[1,128]{1,0:T(1,128)S(1)}, f32[1,128]{1,0:T(1,128)S(1)}, u32[]{:S(2)}, u32[]{:S(2)}) collective-permute-start(f32[1,128]{1,0:T(1,128)S(1)} %get-tuple-element.12), channel_id=1, source_target_pairs={{6,0},{14,1},{0,2},{8,3},{2,4},{10,5},{4,6},{12,7},{7,8},{15,9},{1... | collective-permute-start | bytes 1544 | tf_op jit(solution)/shard_map/ppermute | solution.py:171

commit v3 on v2

v3 whole, which is shorter than its diff:
```python
import functools

import jax
import jax.numpy as jnp
from jax import lax
from jax.experimental import pallas as pl
from jax.experimental.pallas import tpu as pltpu
from jax.sharding import PartitionSpec as P

F32 = jnp.float32
BF16 = jnp.bfloat16
LANES = 128
CHUNK = 512


def project_kernel(rank, acts_ref, grads_ref, proj_ref, out_ref, both, proj, sems):
    tokens, units = acts_ref.shape[1:]
    copies = []
    for i in range(units // CHUNK):
        part = pl.ds(i * CHUNK, CHUNK)
        three = (
            pltpu.make_async_copy(proj_ref.at[part, :], proj.at[part, :], sems.at[i, 0]),
            pltpu.make_async_copy(
                acts_ref.at[0, :, part], both.at[pl.ds(0, tokens), part], sems.at[i, 1]
            ),
            pltpu.make_async_copy(
                grads_ref.at[0, :, part], both.at[pl.ds(tokens, tokens), part], sems.at[i, 2]
            ),
        )
        for copy in three:
            copy.start()
        copies.append(three)

    total = None
    for i, three in enumerate(copies):
        for copy in three:
            copy.wait()
        part = pl.ds(i * CHUNK, CHUNK)
        term = jnp.dot(both[:, part], proj[part, :], preferred_element_type=F32)
        total = term if total is None else total + term
    column = lax.broadcasted_iota(jnp.int32, (tokens, 2 * rank), 1)
    out_ref[...] = jnp.where(column < rank, total[0:tokens], total[tokens:])


def count_kernel(picks_ref, out_ref):
    tokens, width = out_ref.shape
    samples = picks_ref.shape[1]
    token = lax.broadcasted_iota(jnp.int32, (tokens, samples), 0)
    hits = jnp.where(token == picks_ref[...], 1.0, 0.0).astype(BF16)
    out_ref[...] = jnp.dot(hits, jnp.ones((samples, width), BF16), preferred_element_type=F32)


def sketch_kernel(rank, count_ref, own_ref, other_ref, out_ref, held):
    total = own_ref[...] + other_ref[...]
    held[...] = lax.dot_general(
        total[:, rank : 2 * rank],
        total[:, 0:rank] * count_ref[...],
        (((0,), (0,)), ((), ())),
        precision=lax.Precision.HIGHEST,
        preferred_element_type=F32,
    )
    pairs = out_ref.shape[0]
    even = held[pl.ds(0, pairs, stride=2), :]
    odd = held[pl.ds(1, pairs, stride=2), :]
    out_ref[...] = jnp.concatenate([even, odd], axis=1).astype(BF16)


def score_kernel(rounds, *refs):
    sketches, queries, outs, wide = refs[:rounds], refs[rounds : rounds + 4], refs[rounds + 4 : -1], refs[-1]
    pairs = sketches[0].shape[0]
    own_queries = queries[0].shape[0]
    slots = wide.shape[0] // pairs
    wide[...] = jnp.zeros_like(wide)
    for r in range(rounds):
        wide[pl.ds(r, pairs, stride=slots), :] = sketches[r][...].astype(F32)
    half = lax.axis_index("tensor")
    flats = []
    for side in (half, 1 - half):
        start = side * (slots * pairs // 2)
        flats.append(
            jnp.concatenate(
                [
                    wide[pl.ds(pl.multiple_of(start + j * slots, slots), slots), :]
                    for j in range(pairs // 2)
                ],
                axis=1,
            ).astype(BF16)
        )
    spot = lax.axis_index("dp")
    block = lax.broadcasted_iota(jnp.int32, (slots, 2 * rounds * own_queries), 1) // own_queries
    spread = jnp.zeros(block.shape, F32)
    for k, member in ((0, spot), (1, spot + 1 - 2 * lax.rem(spot, 2))):
        scores = sum(
            lax.dot_general(
                flat, queries[2 * k + i][...], (((1,), (1,)), ((), ())), preferred_element_type=F32
            )
            for i, flat in enumerate(flats)
        )
        here = block == lax.rem(member, 2 * rounds)
        spread = jnp.where(here, jnp.concatenate([scores] * (2 * rounds), axis=1), spread)
    for r in range(rounds):
        outs[r][...] = spread[r : r + 1, :]


def on_device(activations, out_grads, projections, sample_index, queries):
    clips = lax.axis_size("dp")
    tokens, units = activations.shape[1:]
    rank = projections.shape[1] // 2
    own_queries, entries = queries.shape
    pairs = 2 * entries // LANES
    rounds = clips // 4
    slots = -(-rounds // 8) * 8
    vmem = pl.BlockSpec(memory_space=pltpu.VMEM)
    hbm = pl.BlockSpec(memory_space=pl.ANY)
    swap = [(0, 1), (1, 0)]

    def place(a, l, b, t):
        return ((a * rounds + l) * 2 + b) * 2 + t

    there = [
        [
            (place(a, l, b, t), place(t, (l + r) % rounds, b, a))
            for a in range(2)
            for l in range(rounds)
            for b in range(2)
            for t in range(2)
        ]
        for r in range(rounds)
    ]
    back = [[(dst, src) for src, dst in perm] for perm in there]

    pair_queries = lax.ppermute(queries, "dp", [(d, d ^ 1) for d in range(clips)])
    other_queries = lax.ppermute(queries, "tensor", swap)
    other_pair_queries = lax.ppermute(pair_queries, "tensor", swap)
    partial = pl.pallas_call(
        functools.partial(project_kernel, rank),
        in_specs=[hbm] * 3,
        out_specs=vmem,
        out_shape=jax.ShapeDtypeStruct((tokens, 2 * rank), F32),
        scratch_shapes=[
            pltpu.VMEM((2 * tokens, units), BF16),
            pltpu.VMEM((units, 2 * rank), BF16),
            pltpu.SemaphoreType.DMA((units // CHUNK, 3)),
        ],
        compiler_params=pltpu.CompilerParams(vmem_limit_bytes=55000 << 10),
        cost_estimate=pl.CostEstimate(
            flops=8 * tokens * units * rank, bytes_accessed=4 * tokens * units, transcendentals=0
        ),
        name="project",
    )(activations, out_grads, projections)

    other = lax.ppermute(partial, "tensor", swap)
    count = pl.pallas_call(
        count_kernel,
        in_specs=[vmem],
        out_specs=vmem,
        out_shape=jax.ShapeDtypeStruct((tokens, rank), F32),
        compiler_params=pltpu.CompilerParams(vmem_limit_bytes=8 << 20),
        name="count",
    )(sample_index)
    sketch = pl.pallas_call(
        functools.partial(sketch_kernel, rank),
        in_specs=[vmem] * 3,
        out_specs=vmem,
        out_shape=jax.ShapeDtypeStruct((pairs, LANES), BF16),
        scratch_shapes=[pltpu.VMEM((rank, rank), F32)],
        compiler_params=pltpu.CompilerParams(vmem_limit_bytes=8 << 20),
        name="sketch",
    )(count, partial, other)

    sketches = [lax.ppermute(sketch, ("dp", "tensor"), perm) for perm in there]
    width = 2 * rounds * own_queries
    scored = pl.pallas_call(
        functools.partial(score_kernel, rounds),
        in_specs=[vmem] * (rounds + 4),
        out_specs=[vmem] * rounds,
        out_shape=[jax.ShapeDtypeStruct((1, width), F32)] * rounds,
        scratch_shapes=[pltpu.VMEM((pairs * slots, LANES), F32)],
        compiler_params=pltpu.CompilerParams(vmem_limit_bytes=16 << 20),
        name="score",
    )(*sketches, queries, other_queries, pair_queries, other_pair_queries)

    parts = [lax.ppermute(s, ("dp", "tensor"), perm) for s, perm in zip(scored, back)]
    return functools.reduce(jnp.add, parts)


def solution(mesh):
    in_specs = (
        P(("groups", "dp"), None, "tensor"),
        P(("groups", "dp"), None, "tensor"),
        P("tensor", None),
        P(("groups", "dp"), None),
        P(("groups", "dp"), "tensor"),
    )
    out_specs = P(("groups", "dp"), "tensor")
    return jax.shard_map(
        on_device, mesh=mesh, in_specs=in_specs, out_specs=out_specs, check_vma=False
    )
```

time: 38.7 us -> 25.6 us (0.66)
  starting transfers between devices: 18 us -> 13 us
  local copies, waits for them, and re-layouts: 4.86 us -> 0.01 us
  waiting for transfers between devices: 10.5 us -> 7.05 us
    ppermute x4 -> x2, starting transfers between devices: 11.2 us -> 5.63 us  [on_device(): sketches = [lax.ppermute(sketch, ('dp', 'tensor'), perm) for perm in there]]
    unnamed x10 -> x4, local copies, waits for them, and re-layouts: 4.86 us -> 0.01 us
    ppermute x4 -> x2, waiting for transfers between devices: 5.66 us -> 2.91 us  [on_device(): lax.ppermute(s, ('dp', 'tensor'), perm)]
    ppermute x0 -> x2, starting transfers between devices: none -> 2.47 us  [the longest x1 2.04 us: on_device(): lax.ppermute(queries, 'dp', [(d, d ^ 1) for d in range(clips)])]
    ppermute x4 -> x2, starting transfers between devices: 6.28 us -> 3.85 us  [on_device(): lax.ppermute(s, ('dp', 'tensor'), perm)]
    ppermute x1, starting transfers between devices: 0.12 us -> 1.02 us  [on_device(): other = lax.ppermute(partial, 'tensor', swap)]
    ppermute x1, waiting for transfers between devices: 0.93 us -> 0.35 us  [on_device(): other = lax.ppermute(partial, 'tensor', swap)]
    pallas_call x2 -> x3, Pallas kernels: 4.19 us -> 4.45 us  [the longest x1 3.81 us: on_device(): pl.pallas_call(functools.partial(project_kernel, rank), in_specs=[hbm] *...]
  transfers between devices with their start and end apart: 10 -> 8, of which waited for: 7 -> 5; matrix products, arithmetic and copies ran while one was open for 0% -> 0% of each run, Pallas kernels for 1% -> 18%
where the time goes in v3:
time: 25.6 us; the launch traced here: 25.4 us
  starting transfers between devices  13 us (51%)
  waiting for transfers between devices  7.05 us (28%)
  Pallas kernels  4.77 us (19%)
  other arithmetic  0.51 us (2%)
    ppermute x2, starting transfers between devices, on_device(): sketches = [lax.ppermute(sketch, ('dp', 'tensor'), perm) for perm in there]  5.63 us
    ppermute x2, starting transfers between devices, on_device(): lax.ppermute(s, ('dp', 'tensor'), perm)  3.85 us
    pallas_call x1, Pallas kernels, on_device(): pl.pallas_call(functools.partial(project_kernel, rank), in_specs=[hbm] *...  3.81 us
    ppermute x2, waiting for transfers between devices, on_device(): sketches = [lax.ppermute(sketch, ('dp', 'tensor'), perm) for perm in there]  3.78 us
    ppermute x2, waiting for transfers between devices, on_device(): lax.ppermute(s, ('dp', 'tensor'), perm)  2.91 us
    ppermute x1, starting transfers between devices, on_device(): lax.ppermute(queries, 'dp', [(d, d ^ 1) for d in range(clips)])  2.04 us
    ppermute x1, starting transfers between devices, on_device(): other = lax.ppermute(partial, 'tensor', swap)  1.02 us
    add x1, other arithmetic, on_device(): return functools.reduce(jnp.add, parts)  0.51 us
  transfers between devices with their start and end apart: 8, of which 5 were waited for; matrix products, arithmetic and copies ran while one was open for 0% of the time, Pallas kernels for 18%

profile of v3, /device:TPU:1, one launch (start us, length us, event | category | flops | bytes accessed | tf_op | source)
XLA Modules:
  0.0 25.4 jit_solution(10048307039897211891)
XLA Ops:
  0.0 0.0 copy-start
  0.0 2.0 %collective-permute-start.4 = (bf16[32,2048]{1,0:T(8,128)(2,1)}, bf16[32,2048]{1,0:T(8,128)(2,1)S(1)}, u32[]{:S(2)}, u32[]{:S(2)}) collective-permute-start(bf16[32,2048]{1,0:T(8,128)(2,1)} %refs_2_.1), channel_id=1, source_target_pairs={{0,2},{2,0},{4,6},{6,4},{8,10},{10,8},{12,14},{14,12},{1,3},{3,1},... | collective-permute-start | bytes 393224 | tf_op jit(solution)/shard_map/ppermute | solution.py:132
  2.0 3.8 %project.1.own_ref = f32[384,128]{1,0:T(8,128)S(1)} custom-call(bf16[1,384,2560]{2,1,0:T(8,128)(2,1)} %acts_ref.1, bf16[1,384,2560]{2,1,0:T(8,128)(2,1)} %grads_ref.1, bf16[2560,128]{1,0:T(8,128)(2,1)} %proj_ref.1), custom_call_target="tpu_custom_call" | custom-call | flops 503316480 | bytes 3932160 | tf_op jit(solution)/shard_map/project/pallas_call | solution.py:135
  5.9 1.0 %collective-permute-start = (f32[384,128]{1,0:T(8,128)S(1)}, f32[384,128]{1,0:T(8,128)S(1)}, u32[]{:S(2)}, u32[]{:S(2)}) collective-permute-start(f32[384,128]{1,0:T(8,128)S(1)} %project.1.own_ref), channel_id=1, source_target_pairs={{0,1},{1,0},{2,3},{3,2},{4,5},{5,4},{6,7},{7,6},{8,9},{9,8},{10,11... | collective-permute-start | bytes 589832 | tf_op jit(solution)/shard_map/ppermute | solution.py:152
  6.9 0.0 copy-done
  6.9 0.1 collective-permute-start.3
  7.0 0.0 collective-permute-done.4.refs_4_
  7.0 0.4 %collective-permute-start.5 = (bf16[32,2048]{1,0:T(8,128)(2,1)S(1)}, bf16[32,2048]{1,0:T(8,128)(2,1)S(1)}, u32[]{:S(2)}, u32[]{:S(2)}) collective-permute-start(bf16[32,2048]{1,0:T(8,128)(2,1)S(1)} %collective-permute-done.4.refs_4_), channel_id=1, source_target_pairs={{0,1},{1,0},{2,3},{3,2},{4,5},{5,4},{6,7},{7,6},{8,9},{9,8},{10,11... | collective-permute-start | bytes 393224 | tf_op jit(solution)/shard_map/ppermute | solution.py:134
  7.4 0.0 copy-done.1
  7.4 0.2 count.1.count_ref
  7.6 0.3 %collective-permute-done.other_ref = f32[384,128]{1,0:T(8,128)S(1)} collective-permute-done((f32[384,128]{1,0:T(8,128)S(1)}, f32[384,128]{1,0:T(8,128)S(1)}, u32[]{:S(2)}, u32[]{:S(2)}) %collective-permute-start) | collective-permute-done | bytes 196640 | tf_op jit(solution)/shard_map/ppermute | solution.py:152
  7.9 0.5 %sketch.1 = bf16[32,128]{1,0:T(8,128)(2,1)S(1)} custom-call(f32[384,64]{1,0:T(8,128)S(1)} %count.1.count_ref, f32[384,128]{1,0:T(8,128)S(1)} %project.1.own_ref, f32[384,128]{1,0:T(8,128)S(1)} %collective-permute-done.other_ref), custom_call_target="tpu_custom_call" | custom-call | tf_op jit(solution)/shard_map/sketch/pallas_call | solution.py:161
  8.4 4.5 %collective-permute-start.1 = (bf16[32,128]{1,0:T(8,128)(2,1)S(1)}, bf16[32,128]{1,0:T(8,128)(2,1)S(1)}, u32[]{:S(2)}, u32[]{:S(2)}) collective-permute-start(bf16[32,128]{1,0:T(8,128)(2,1)S(1)} %sketch.1), channel_id=1, source_target_pairs={{0,0},{1,8},{2,2},{3,10},{4,4},{5,12},{6,6},{7,14},{8,1},{9,9},{10... | collective-permute-start | bytes 24584 | tf_op jit(solution)/shard_map/ppermute | solution.py:171
  12.9 1.2 %collective-permute-start.2 = (bf16[32,128]{1,0:T(8,128)(2,1)S(1)}, bf16[32,128]{1,0:T(8,128)(2,1)S(1)}, u32[]{:S(2)}, u32[]{:S(2)}) collective-permute-start(bf16[32,128]{1,0:T(8,128)(2,1)S(1)} %sketch.1), channel_id=1, source_target_pairs={{0,4},{1,12},{2,6},{3,14},{4,0},{5,8},{6,2},{7,10},{8,5},{9,13},{1... | collective-permute-start | bytes 24584 | tf_op jit(solution)/shard_map/ppermute | solution.py:171
  14.0 0.0 collective-permute-done.3.refs_3_
  14.0 0.2 collective-permute-done.1.refs_0_
  14.3 3.6 %collective-permute-done.2.refs_1_ = bf16[32,128]{1,0:T(8,128)(2,1)S(1)} collective-permute-done((bf16[32,128]{1,0:T(8,128)(2,1)S(1)}, bf16[32,128]{1,0:T(8,128)(2,1)S(1)}, u32[]{:S(2)}, u32[]{:S(2)}) %collective-permute-start.2) | collective-permute-done | bytes 8224 | tf_op jit(solution)/shard_map/ppermute | solution.py:171
  17.8 0.0 collective-permute-done.5.refs_5_
  17.8 0.3 %score.1 = (f32[1,128]{1,0:T(1,128)S(1)}, f32[1,128]{1,0:T(1,128)S(1)}) custom-call(bf16[32,128]{1,0:T(8,128)(2,1)S(1)} %collective-permute-done.1.refs_0_, bf16[32,128]{1,0:T(8,128)(2,1)S(1)} %collective-permute-done.2.refs_1_, bf16[32,2048]{1,0:T(8,128)(2,1)S(1)} %copy-done, bf16[32,2048]{1,0:T(8,128)(2,1)S(1)} %collective-permute-done.3.refs_3_, ...), custom_call_target="tpu_custom_call" | custom-call | tf_op jit(solution)/shard_map/score/pallas_call | solution.py:173
  18.1 1.9 %collective-permute-start.6 = (f32[1,128]{1,0:T(1,128)S(1)}, f32[1,128]{1,0:T(1,128)S(1)}, u32[]{:S(2)}, u32[]{:S(2)}) collective-permute-start(f32[1,128]{1,0:T(1,128)S(1)} %get-tuple-element.7), channel_id=1, source_target_pairs={{0,0},{8,1},{2,2},{10,3},{4,4},{12,5},{6,6},{14,7},{1,8},{9,9},{3,... | collective-permute-start | bytes 1544 | tf_op jit(solution)/shard_map/ppermute | solution.py:183
  20.1 1.9 %collective-permute-start.7 = (f32[1,128]{1,0:T(1,128)S(1)}, f32[1,128]{1,0:T(1,128)S(1)}, u32[]{:S(2)}, u32[]{:S(2)}) collective-permute-start(f32[1,128]{1,0:T(1,128)S(1)} %get-tuple-element.8), channel_id=1, source_target_pairs={{4,0},{12,1},{6,2},{14,3},{0,4},{8,5},{2,6},{10,7},{5,8},{13,9},{7... | collective-permute-start | bytes 1544 | tf_op jit(solution)/shard_map/ppermute | solution.py:183
  22.0 1.9 %collective-permute-done.6 = f32[1,128]{1,0:T(1,128)S(1)} collective-permute-done((f32[1,128]{1,0:T(1,128)S(1)}, f32[1,128]{1,0:T(1,128)S(1)}, u32[]{:S(2)}, u32[]{:S(2)}) %collective-permute-start.6) | collective-permute-done | bytes 544 | tf_op jit(solution)/shard_map/ppermute | solution.py:183
  23.9 1.0 %collective-permute-done.7 = f32[1,128]{1,0:T(1,128)S(1)} collective-permute-done((f32[1,128]{1,0:T(1,128)S(1)}, f32[1,128]{1,0:T(1,128)S(1)}, u32[]{:S(2)}, u32[]{:S(2)}) %collective-permute-start.7) | collective-permute-done | bytes 544 | tf_op jit(solution)/shard_map/ppermute | solution.py:183
  24.9 0.5 %add.3 = f32[1,128]{1,0:T(1,128)} add(f32[1,128]{1,0:T(1,128)S(1)} %collective-permute-done.6, f32[1,128]{1,0:T(1,128)S(1)} %collective-permute-done.7) | non-fusion elementwise | flops 128 | bytes 1536 | tf_op jit(solution)/shard_map/add | solution.py:184
  (1 shorter events, 0.0 us)
Async XLA Ops:
  0.0 6.9 %copy-start = (bf16[32,2048]{1,0:T(8,128)(2,1)S(1)}, bf16[32,2048]{1,0:T(8,128)(2,1)}, u32[]{:S(2)}) copy-start(bf16[32,2048]{1,0:T(8,128)(2,1)} %refs_2_.1) | copy-start | bytes 393220
  0.0 7.4 %copy-start.1 = (s32[1,256]{1,0:T(1,128)S(1)}, s32[1,256]{1,0:T(1,128)}, u32[]{:S(2)}) copy-start(s32[1,256]{1,0:T(1,128)} %picks_ref.1) | copy-start | bytes 3076
  0.0 7.0 %collective-permute-start.4 = (bf16[32,2048]{1,0:T(8,128)(2,1)}, bf16[32,2048]{1,0:T(8,128)(2,1)S(1)}, u32[]{:S(2)}, u32[]{:S(2)}) collective-permute-start(bf16[32,2048]{1,0:T(8,128)(2,1)} %refs_2_.1), channel_id=1, source_target_pairs={{0,2},{2,0},{4,6},{6,4},{8,10},{10,8},{12,14},{14,12},{1,3},{3,1},... | collective-permute-start | bytes 393224 | tf_op jit(solution)/shard_map/ppermute | solution.py:132
  5.9 2.1 %collective-permute-start = (f32[384,128]{1,0:T(8,128)S(1)}, f32[384,128]{1,0:T(8,128)S(1)}, u32[]{:S(2)}, u32[]{:S(2)}) collective-permute-start(f32[384,128]{1,0:T(8,128)S(1)} %project.1.own_ref), channel_id=1, source_target_pairs={{0,1},{1,0},{2,3},{3,2},{4,5},{5,4},{6,7},{7,6},{8,9},{9,8},{10,11... | collective-permute-start | bytes 589832 | tf_op jit(solution)/shard_map/ppermute | solution.py:152
  6.9 7.2 %collective-permute-start.3 = (bf16[32,2048]{1,0:T(8,128)(2,1)S(1)}, bf16[32,2048]{1,0:T(8,128)(2,1)S(1)}, u32[]{:S(2)}, u32[]{:S(2)}) collective-permute-start(bf16[32,2048]{1,0:T(8,128)(2,1)S(1)} %copy-done), channel_id=1, source_target_pairs={{0,1},{1,0},{2,3},{3,2},{4,5},{5,4},{6,7},{7,6},{8,9},{9,8},{10,11... | collective-permute-start | bytes 393224 | tf_op jit(solution)/shard_map/ppermute | solution.py:133
  7.0 10.9 %collective-permute-start.5 = (bf16[32,2048]{1,0:T(8,128)(2,1)S(1)}, bf16[32,2048]{1,0:T(8,128)(2,1)S(1)}, u32[]{:S(2)}, u32[]{:S(2)}) collective-permute-start(bf16[32,2048]{1,0:T(8,128)(2,1)S(1)} %collective-permute-done.4.refs_4_), channel_id=1, source_target_pairs={{0,1},{1,0},{2,3},{3,2},{4,5},{5,4},{6,7},{7,6},{8,9},{9,8},{10,11... | collective-permute-start | bytes 393224 | tf_op jit(solution)/shard_map/ppermute | solution.py:134
  8.4 5.9 %collective-permute-start.1 = (bf16[32,128]{1,0:T(8,128)(2,1)S(1)}, bf16[32,128]{1,0:T(8,128)(2,1)S(1)}, u32[]{:S(2)}, u32[]{:S(2)}) collective-permute-start(bf16[32,128]{1,0:T(8,128)(2,1)S(1)} %sketch.1), channel_id=1, source_target_pairs={{0,0},{1,8},{2,2},{3,10},{4,4},{5,12},{6,6},{7,14},{8,1},{9,9},{10... | collective-permute-start | bytes 24584 | tf_op jit(solution)/shard_map/ppermute | solution.py:171
  12.9 4.9 %collective-permute-start.2 = (bf16[32,128]{1,0:T(8,128)(2,1)S(1)}, bf16[32,128]{1,0:T(8,128)(2,1)S(1)}, u32[]{:S(2)}, u32[]{:S(2)}) collective-permute-start(bf16[32,128]{1,0:T(8,128)(2,1)S(1)} %sketch.1), channel_id=1, source_target_pairs={{0,4},{1,12},{2,6},{3,14},{4,0},{5,8},{6,2},{7,10},{8,5},{9,13},{1... | collective-permute-start | bytes 24584 | tf_op jit(solution)/shard_map/ppermute | solution.py:171
  18.1 5.8 %collective-permute-start.6 = (f32[1,128]{1,0:T(1,128)S(1)}, f32[1,128]{1,0:T(1,128)S(1)}, u32[]{:S(2)}, u32[]{:S(2)}) collective-permute-start(f32[1,128]{1,0:T(1,128)S(1)} %get-tuple-element.7), channel_id=1, source_target_pairs={{0,0},{8,1},{2,2},{10,3},{4,4},{12,5},{6,6},{14,7},{1,8},{9,9},{3,... | collective-permute-start | bytes 1544 | tf_op jit(solution)/shard_map/ppermute | solution.py:183
  20.1 4.8 %collective-permute-start.7 = (f32[1,128]{1,0:T(1,128)S(1)}, f32[1,128]{1,0:T(1,128)S(1)}, u32[]{:S(2)}, u32[]{:S(2)}) collective-permute-start(f32[1,128]{1,0:T(1,128)S(1)} %get-tuple-element.8), channel_id=1, source_target_pairs={{4,0},{12,1},{6,2},{14,3},{0,4},{8,5},{2,6},{10,7},{5,8},{13,9},{7... | collective-permute-start | bytes 1544 | tf_op jit(solution)/shard_map/ppermute | solution.py:183

commit v4 on v3

--- a/solution.py
+++ b/solution.py
@@ -27,8 +27,8 @@
                 grads_ref.at[0, :, part], both.at[pl.ds(tokens, tokens), part], sems.at[i, 2]
             ),
         )
-        for copy in three:
-            copy.start()
+        for k, copy in enumerate(three):
+            copy.start(priority=(i + k) % 2)
         copies.append(three)
 
     total = None
@@ -66,38 +66,32 @@
 
 
 def score_kernel(rounds, *refs):
-    sketches, queries, outs, wide = refs[:rounds], refs[rounds : rounds + 4], refs[rounds + 4 : -1], refs[-1]
+    sketches, queries, outs, wide = refs[:rounds], refs[rounds : rounds + 2], refs[rounds + 2 : -1], refs[-1]
     pairs = sketches[0].shape[0]
     own_queries = queries[0].shape[0]
     slots = wide.shape[0] // pairs
     wide[...] = jnp.zeros_like(wide)
     for r in range(rounds):
         wide[pl.ds(r, pairs, stride=slots), :] = sketches[r][...].astype(F32)
-    half = lax.axis_index("tensor")
-    flats = []
-    for side in (half, 1 - half):
-        start = side * (slots * pairs // 2)
-        flats.append(
-            jnp.concatenate(
-                [
-                    wide[pl.ds(pl.multiple_of(start + j * slots, slots), slots), :]
-                    for j in range(pairs // 2)
-                ],
-                axis=1,
-            ).astype(BF16)
+    spot = lax.axis_index("dp")
+    upper = spot // rounds
+    scores = None
+    for ref, half in zip(queries, (upper, 1 - upper)):
+        start = half * (slots * pairs // 2)
+        flat = jnp.concatenate(
+            [
+                wide[pl.ds(pl.multiple_of(start + j * slots, slots), slots), :]
+                for j in range(pairs // 2)
+            ],
+            axis=1,
+        ).astype(BF16)
+        term = lax.dot_general(
+            flat, ref[...], (((1,), (1,)), ((), ())), preferred_element_type=F32
         )
-    spot = lax.axis_index("dp")
-    block = lax.broadcasted_iota(jnp.int32, (slots, 2 * rounds * own_queries), 1) // own_queries
-    spread = jnp.zeros(block.shape, F32)
-    for k, member in ((0, spot), (1, spot + 1 - 2 * lax.rem(spot, 2))):
-        scores = sum(
-            lax.dot_general(
-                flat, queries[2 * k + i][...], (((1,), (1,)), ((), ())), preferred_element_type=F32
-            )
-            for i, flat in enumerate(flats)
-        )
-        here = block == lax.rem(member, 2 * rounds)
-        spread = jnp.where(here, jnp.concatenate([scores] * (2 * rounds), axis=1), spread)
+        scores = term if scores is None else scores + term
+    spread = jnp.concatenate([scores] * rounds, axis=1)
+    block = lax.broadcasted_iota(jnp.int32, spread.shape, 1) // own_queries
+    spread = jnp.where(block == lax.rem(spot, rounds), spread, 0.0)
     for r in range(rounds):
         outs[r][...] = spread[r : r + 1, :]
 
@@ -108,30 +102,32 @@
     rank = projections.shape[1] // 2
     own_queries, entries = queries.shape
     pairs = 2 * entries // LANES
-    rounds = clips // 4
+    rounds = clips // 2
     slots = -(-rounds // 8) * 8
     vmem = pl.BlockSpec(memory_space=pltpu.VMEM)
     hbm = pl.BlockSpec(memory_space=pl.ANY)
     swap = [(0, 1), (1, 0)]
 
-    def place(a, l, b, t):
-        return ((a * rounds + l) * 2 + b) * 2 + t
+    def place(a, m, t):
+        return (a * rounds + m) * 2 + t
 
-    there = [
-        [
-            (place(a, l, b, t), place(t, (l + r) % rounds, b, a))
-            for a in range(2)
-            for l in range(rounds)
-            for b in range(2)
-            for t in range(2)
-        ]
-        for r in range(rounds)
+    taken = [
+        lax.ppermute(
+            queries,
+            ("dp", "tensor"),
+            [
+                (place(t, m, a ^ j), place(a, m, t))
+                for a in range(2)
+                for m in range(rounds)
+                for t in range(2)
+            ],
+        )
+        for j in range(2)
     ]
-    back = [[(dst, src) for src, dst in perm] for perm in there]
-
-    pair_queries = lax.ppermute(queries, "dp", [(d, d ^ 1) for d in range(clips)])
-    other_queries = lax.ppermute(queries, "tensor", swap)
-    other_pair_queries = lax.ppermute(pair_queries, "tensor", swap)
+    across = [
+        [(a * rounds + m, a * rounds + (m ^ r)) for a in range(2) for m in range(rounds)]
+        for r in range(1, rounds)
+    ]
     partial = pl.pallas_call(
         functools.partial(project_kernel, rank),
         in_specs=[hbm] * 3,
@@ -168,20 +164,20 @@
         name="sketch",
     )(count, partial, other)
 
-    sketches = [lax.ppermute(sketch, ("dp", "tensor"), perm) for perm in there]
-    width = 2 * rounds * own_queries
+    sketches = [sketch] + [lax.ppermute(sketch, "dp", perm) for perm in across]
+    width = rounds * own_queries
     scored = pl.pallas_call(
         functools.partial(score_kernel, rounds),
-        in_specs=[vmem] * (rounds + 4),
+        in_specs=[vmem] * (rounds + 2),
         out_specs=[vmem] * rounds,
         out_shape=[jax.ShapeDtypeStruct((1, width), F32)] * rounds,
         scratch_shapes=[pltpu.VMEM((pairs * slots, LANES), F32)],
         compiler_params=pltpu.CompilerParams(vmem_limit_bytes=16 << 20),
         name="score",
-    )(*sketches, queries, other_queries, pair_queries, other_pair_queries)
+    )(*sketches, *taken)
 
-    parts = [lax.ppermute(s, ("dp", "tensor"), perm) for s, perm in zip(scored, back)]
-    return functools.reduce(jnp.add, parts)
+    parts = [lax.ppermute(s, "dp", perm) for s, perm in zip(scored[1:], across)]
+    return functools.reduce(jnp.add, parts, scored[0])
 
 
 def solution(mesh):

time: 25.6 us -> 25.2 us (0.984)
  the two profiles are of different devices: /device:TPU:1 before, /device:TPU:0 now
where the time goes in v4:
time: 25.2 us; the launch traced here: 25 us
  starting transfers between devices  13.1 us (52%)
  waiting for transfers between devices  6.14 us (24%)
  Pallas kernels  5.22 us (21%)
  other arithmetic  0.52 us (2%)
    ppermute x2, starting transfers between devices, on_device(): lax.ppermute(queries, ('dp', 'tensor'), [(place(t, m, a ^ j), place(a, m,...  5.58 us
    ppermute x3, waiting for transfers between devices, on_device(): sketches = [sketch] + [lax.ppermute(sketch, 'dp', perm) for perm in across]  4.53 us
    pallas_call x1, Pallas kernels, on_device(): pl.pallas_call(functools.partial(project_kernel, rank), in_specs=[hbm] *...  4.3 us
    ppermute x3, starting transfers between devices, on_device(): parts = [lax.ppermute(s, 'dp', perm) for s, perm in zip(scored[1:], across)]  3.5 us
    ppermute x3, starting transfers between devices, on_device(): sketches = [sketch] + [lax.ppermute(sketch, 'dp', perm) for perm in across]  3.49 us
    ppermute x3, waiting for transfers between devices, on_device(): parts = [lax.ppermute(s, 'dp', perm) for s, perm in zip(scored[1:], across)]  1.6 us
    ppermute x1, starting transfers between devices, on_device(): other = lax.ppermute(partial, 'tensor', swap)  0.52 us
    add x1, other arithmetic, on_device(): return functools.reduce(jnp.add, parts, scored[0])  0.52 us
  transfers between devices with their start and end apart: 9, of which 6 were waited for; matrix products, arithmetic and copies ran while one was open for 0% of the time, Pallas kernels for 3%

profile of v4, /device:TPU:0, one launch (start us, length us, event | category | flops | bytes accessed | tf_op | source)
XLA Modules:
  0.0 25.0 jit_solution(8207791539574477959)
XLA Ops:
  0.0 4.3 %project.1.own_ref = f32[384,128]{1,0:T(8,128)S(1)} custom-call(bf16[1,384,2560]{2,1,0:T(8,128)(2,1)} %acts_ref.1, bf16[1,384,2560]{2,1,0:T(8,128)(2,1)} %grads_ref.1, bf16[2560,128]{1,0:T(8,128)(2,1)} %proj_ref.1), custom_call_target="tpu_custom_call" | custom-call | flops 503316480 | bytes 3932160 | tf_op jit(solution)/shard_map/project/pallas_call | solution.py:131
  4.3 0.5 %collective-permute-start = (f32[384,128]{1,0:T(8,128)S(1)}, f32[384,128]{1,0:T(8,128)S(1)}, u32[]{:S(2)}, u32[]{:S(2)}) collective-permute-start(f32[384,128]{1,0:T(8,128)S(1)} %project.1.own_ref), channel_id=1, source_target_pairs={{0,1},{1,0},{2,3},{3,2},{4,5},{5,4},{6,7},{7,6},{8,9},{9,8},{10,11... | collective-permute-start | bytes 589832 | tf_op jit(solution)/shard_map/ppermute | solution.py:148
  4.8 0.0 copy-done.1
  4.8 0.7 %collective-permute-start.4 = (bf16[32,2048]{1,0:T(8,128)(2,1)S(1)}, bf16[32,2048]{1,0:T(8,128)(2,1)S(1)}, u32[]{:S(2)}, u32[]{:S(2)}) collective-permute-start(bf16[32,2048]{1,0:T(8,128)(2,1)S(1)} %copy-done.1), channel_id=1, source_target_pairs={{0,0},{8,1},{2,2},{10,3},{4,4},{12,5},{6,6},{14,7},{1,8},{9,9},{3,... | collective-permute-start | bytes 393224 | tf_op jit(solution)/shard_map/ppermute | solution.py:115
  5.5 4.9 %collective-permute-start.5 = (bf16[32,2048]{1,0:T(8,128)(2,1)S(1)}, bf16[32,2048]{1,0:T(8,128)(2,1)S(1)}, u32[]{:S(2)}, u32[]{:S(2)}) collective-permute-start(bf16[32,2048]{1,0:T(8,128)(2,1)S(1)} %copy-done.1), channel_id=1, source_target_pairs={{1,0},{9,1},{3,2},{11,3},{5,4},{13,5},{7,6},{15,7},{0,8},{8,9},{2,... | collective-permute-start | bytes 393224 | tf_op jit(solution)/shard_map/ppermute | solution.py:115
  10.4 0.2 count.1.count_ref
  10.6 0.0 collective-permute-done.other_ref
  10.6 0.5 %sketch.1.refs_0_ = bf16[32,128]{1,0:T(8,128)(2,1)S(1)} custom-call(f32[384,64]{1,0:T(8,128)S(1)} %count.1.count_ref, f32[384,128]{1,0:T(8,128)S(1)} %project.1.own_ref, f32[384,128]{1,0:T(8,128)S(1)} %collective-permute-done.other_ref), custom_call_target="tpu_custom_call" | custom-call | tf_op jit(solution)/shard_map/sketch/pallas_call | solution.py:157
  11.1 1.9 %collective-permute-start.1 = (bf16[32,128]{1,0:T(8,128)(2,1)S(1)}, bf16[32,128]{1,0:T(8,128)(2,1)S(1)}, u32[]{:S(2)}, u32[]{:S(2)}) collective-permute-start(bf16[32,128]{1,0:T(8,128)(2,1)S(1)} %sketch.1.refs_0_), channel_id=1, source_target_pairs={{0,2},{2,0},{4,6},{6,4},{8,10},{10,8},{12,14},{14,12},{1,3},{3,1},... | collective-permute-start | bytes 24584 | tf_op jit(solution)/shard_map/ppermute | solution.py:167
  13.0 1.6 %collective-permute-start.2 = (bf16[32,128]{1,0:T(8,128)(2,1)S(1)}, bf16[32,128]{1,0:T(8,128)(2,1)S(1)}, u32[]{:S(2)}, u32[]{:S(2)}) collective-permute-start(bf16[32,128]{1,0:T(8,128)(2,1)S(1)} %sketch.1.refs_0_), channel_id=1, source_target_pairs={{0,4},{2,6},{4,0},{6,2},{8,12},{10,14},{12,8},{14,10},{1,5},{3,7},... | collective-permute-start | bytes 24584 | tf_op jit(solution)/shard_map/ppermute | solution.py:167
  14.6 0.0 collective-permute-start.3
  14.6 0.0 collective-permute-done.4.refs_4_
  14.6 0.0 collective-permute-done.5.refs_5_
  14.6 0.2 collective-permute-done.1.refs_1_
  14.8 2.7 %collective-permute-done.2.refs_2_ = bf16[32,128]{1,0:T(8,128)(2,1)S(1)} collective-permute-done((bf16[32,128]{1,0:T(8,128)(2,1)S(1)}, bf16[32,128]{1,0:T(8,128)(2,1)S(1)}, u32[]{:S(2)}, u32[]{:S(2)}) %collective-permute-start.2) | collective-permute-done | bytes 8224 | tf_op jit(solution)/shard_map/ppermute | solution.py:167
  17.5 1.7 %collective-permute-done.3.refs_3_ = bf16[32,128]{1,0:T(8,128)(2,1)S(1)} collective-permute-done((bf16[32,128]{1,0:T(8,128)(2,1)S(1)}, bf16[32,128]{1,0:T(8,128)(2,1)S(1)}, u32[]{:S(2)}, u32[]{:S(2)}) %collective-permute-start.3) | collective-permute-done | bytes 8224 | tf_op jit(solution)/shard_map/ppermute | solution.py:167
  19.1 0.3 %score.1 = (f32[1,128]{1,0:T(1,128)S(1)}, f32[1,128]{1,0:T(1,128)S(1)}, f32[1,128]{1,0:T(1,128)S(1)}, f32[1,128]{1,0:T(1,128)S(1)}) custom-call(bf16[32,128]{1,0:T(8,128)(2,1)S(1)} %sketch.1.refs_0_, bf16[32,128]{1,0:T(8,128)(2,1)S(1)} %collective-permute-done.1.refs_1_, bf16[32,128]{1,0:T(8,128)(2,1)S(1)} %collective-permute-done.2.refs_2_, ...), custom_call_target="tpu_custom_call" | custom-call | tf_op jit(solution)/shard_map/score/pallas_call | solution.py:169
  19.4 0.5 %collective-permute-start.6 = (f32[1,128]{1,0:T(1,128)S(1)}, f32[1,128]{1,0:T(1,128)S(1)}, u32[]{:S(2)}, u32[]{:S(2)}) collective-permute-start(f32[1,128]{1,0:T(1,128)S(1)} %get-tuple-element.10), channel_id=1, source_target_pairs={{0,2},{2,0},{4,6},{6,4},{8,10},{10,8},{12,14},{14,12},{1,3},{3,1},... | collective-permute-start | bytes 1544 | tf_op jit(solution)/shard_map/ppermute | solution.py:179
  19.9 0.1 collective-permute-start.7
  20.1 2.8 %collective-permute-start.8 = (f32[1,128]{1,0:T(1,128)S(1)}, f32[1,128]{1,0:T(1,128)S(1)}, u32[]{:S(2)}, u32[]{:S(2)}) collective-permute-start(f32[1,128]{1,0:T(1,128)S(1)} %get-tuple-element.12), channel_id=1, source_target_pairs={{0,6},{2,4},{4,2},{6,0},{8,14},{10,12},{12,10},{14,8},{1,7},{3,5},... | collective-permute-start | bytes 1544 | tf_op jit(solution)/shard_map/ppermute | solution.py:179
  22.9 0.1 collective-permute-done.6
  23.0 0.5 %collective-permute-done.7 = f32[1,128]{1,0:T(1,128)S(1)} collective-permute-done((f32[1,128]{1,0:T(1,128)S(1)}, f32[1,128]{1,0:T(1,128)S(1)}, u32[]{:S(2)}, u32[]{:S(2)}) %collective-permute-start.7) | collective-permute-done | bytes 544 | tf_op jit(solution)/shard_map/ppermute | solution.py:179
  23.5 1.0 %collective-permute-done.8 = f32[1,128]{1,0:T(1,128)S(1)} collective-permute-done((f32[1,128]{1,0:T(1,128)S(1)}, f32[1,128]{1,0:T(1,128)S(1)}, u32[]{:S(2)}, u32[]{:S(2)}) %collective-permute-start.8) | collective-permute-done | bytes 544 | tf_op jit(solution)/shard_map/ppermute | solution.py:179
  24.5 0.5 %add_add_fusion = f32[1,128]{1,0:T(1,128)} fusion(f32[1,128]{1,0:T(1,128)S(1)} %collective-permute-done.8, f32[1,128]{1,0:T(1,128)S(1)} %collective-permute-done.7, f32[1,128]{1,0:T(1,128)S(1)} %get-tuple-element.9, f32[1,128]{1,0:T(1,128)S(1)} %collective-permute-done.6), kind=kLoop, calls=%fused_computation | loop fusion | flops 384 | bytes 2560 | tf_op jit(solution)/shard_map/add | solution.py:180
  (3 shorter events, 0.0 us)
Async XLA Ops:
  0.0 4.8 %copy-start.1 = (bf16[32,2048]{1,0:T(8,128)(2,1)S(1)}, bf16[32,2048]{1,0:T(8,128)(2,1)}, u32[]{:S(2)}) copy-start(bf16[32,2048]{1,0:T(8,128)(2,1)} %param.9) | copy-start | bytes 393220
  0.0 10.4 %copy-start = (s32[1,256]{1,0:T(1,128)S(1)}, s32[1,256]{1,0:T(1,128)}, u32[]{:S(2)}) copy-start(s32[1,256]{1,0:T(1,128)} %picks_ref.1) | copy-start | bytes 3076
  4.3 6.3 %collective-permute-start = (f32[384,128]{1,0:T(8,128)S(1)}, f32[384,128]{1,0:T(8,128)S(1)}, u32[]{:S(2)}, u32[]{:S(2)}) collective-permute-start(f32[384,128]{1,0:T(8,128)S(1)} %project.1.own_ref), channel_id=1, source_target_pairs={{0,1},{1,0},{2,3},{3,2},{4,5},{5,4},{6,7},{7,6},{8,9},{9,8},{10,11... | collective-permute-start | bytes 589832 | tf_op jit(solution)/shard_map/ppermute | solution.py:148
  4.8 9.8 %collective-permute-start.4 = (bf16[32,2048]{1,0:T(8,128)(2,1)S(1)}, bf16[32,2048]{1,0:T(8,128)(2,1)S(1)}, u32[]{:S(2)}, u32[]{:S(2)}) collective-permute-start(bf16[32,2048]{1,0:T(8,128)(2,1)S(1)} %copy-done.1), channel_id=1, source_target_pairs={{0,0},{8,1},{2,2},{10,3},{4,4},{12,5},{6,6},{14,7},{1,8},{9,9},{3,... | collective-permute-start | bytes 393224 | tf_op jit(solution)/shard_map/ppermute | solution.py:115
  5.5 9.1 %collective-permute-start.5 = (bf16[32,2048]{1,0:T(8,128)(2,1)S(1)}, bf16[32,2048]{1,0:T(8,128)(2,1)S(1)}, u32[]{:S(2)}, u32[]{:S(2)}) collective-permute-start(bf16[32,2048]{1,0:T(8,128)(2,1)S(1)} %copy-done.1), channel_id=1, source_target_pairs={{1,0},{9,1},{3,2},{11,3},{5,4},{13,5},{7,6},{15,7},{0,8},{8,9},{2,... | collective-permute-start | bytes 393224 | tf_op jit(solution)/shard_map/ppermute | solution.py:115
  11.1 3.7 %collective-permute-start.1 = (bf16[32,128]{1,0:T(8,128)(2,1)S(1)}, bf16[32,128]{1,0:T(8,128)(2,1)S(1)}, u32[]{:S(2)}, u32[]{:S(2)}) collective-permute-start(bf16[32,128]{1,0:T(8,128)(2,1)S(1)} %sketch.1.refs_0_), channel_id=1, source_target_pairs={{0,2},{2,0},{4,6},{6,4},{8,10},{10,8},{12,14},{14,12},{1,3},{3,1},... | collective-permute-start | bytes 24584 | tf_op jit(solution)/shard_map/ppermute | solution.py:167
  13.0 4.5 %collective-permute-start.2 = (bf16[32,128]{1,0:T(8,128)(2,1)S(1)}, bf16[32,128]{1,0:T(8,128)(2,1)S(1)}, u32[]{:S(2)}, u32[]{:S(2)}) collective-permute-start(bf16[32,128]{1,0:T(8,128)(2,1)S(1)} %sketch.1.refs_0_), channel_id=1, source_target_pairs={{0,4},{2,6},{4,0},{6,2},{8,12},{10,14},{12,8},{14,10},{1,5},{3,7},... | collective-permute-start | bytes 24584 | tf_op jit(solution)/shard_map/ppermute | solution.py:167
  14.6 4.5 %collective-permute-start.3 = (bf16[32,128]{1,0:T(8,128)(2,1)S(1)}, bf16[32,128]{1,0:T(8,128)(2,1)S(1)}, u32[]{:S(2)}, u32[]{:S(2)}) collective-permute-start(bf16[32,128]{1,0:T(8,128)(2,1)S(1)} %sketch.1.refs_0_), channel_id=1, source_target_pairs={{0,6},{2,4},{4,2},{6,0},{8,14},{10,12},{12,10},{14,8},{1,7},{3,5},... | collective-permute-start | bytes 24584 | tf_op jit(solution)/shard_map/ppermute | solution.py:167
  19.4 3.6 %collective-permute-start.6 = (f32[1,128]{1,0:T(1,128)S(1)}, f32[1,128]{1,0:T(1,128)S(1)}, u32[]{:S(2)}, u32[]{:S(2)}) collective-permute-start(f32[1,128]{1,0:T(1,128)S(1)} %get-tuple-element.10), channel_id=1, source_target_pairs={{0,2},{2,0},{4,6},{6,4},{8,10},{10,8},{12,14},{14,12},{1,3},{3,1},... | collective-permute-start | bytes 1544 | tf_op jit(solution)/shard_map/ppermute | solution.py:179
  19.9 3.5 %collective-permute-start.7 = (f32[1,128]{1,0:T(1,128)S(1)}, f32[1,128]{1,0:T(1,128)S(1)}, u32[]{:S(2)}, u32[]{:S(2)}) collective-permute-start(f32[1,128]{1,0:T(1,128)S(1)} %get-tuple-element.11), channel_id=1, source_target_pairs={{0,4},{2,6},{4,0},{6,2},{8,12},{10,14},{12,8},{14,10},{1,5},{3,7},... | collective-permute-start | bytes 1544 | tf_op jit(solution)/shard_map/ppermute | solution.py:179
  20.1 4.4 %collective-permute-start.8 = (f32[1,128]{1,0:T(1,128)S(1)}, f32[1,128]{1,0:T(1,128)S(1)}, u32[]{:S(2)}, u32[]{:S(2)}) collective-permute-start(f32[1,128]{1,0:T(1,128)S(1)} %get-tuple-element.12), channel_id=1, source_target_pairs={{0,6},{2,4},{4,2},{6,0},{8,14},{10,12},{12,10},{14,8},{1,7},{3,5},... | collective-permute-start | bytes 1544 | tf_op jit(solution)/shard_map/ppermute | solution.py:179

commit v5 on v4

--- a/solution.py
+++ b/solution.py
@@ -27,8 +27,8 @@
                 grads_ref.at[0, :, part], both.at[pl.ds(tokens, tokens), part], sems.at[i, 2]
             ),
         )
-        for k, copy in enumerate(three):
-            copy.start(priority=(i + k) % 2)
+        for copy in three:
+            copy.start()
         copies.append(three)
 
     total = None
@@ -66,7 +66,7 @@
 
 
 def score_kernel(rounds, *refs):
-    sketches, queries, outs, wide = refs[:rounds], refs[rounds : rounds + 2], refs[rounds + 2 : -1], refs[-1]
+    sketches, queries, outs, wide = refs[:rounds], refs[rounds : rounds + 4], refs[rounds + 4 : -1], refs[-1]
     pairs = sketches[0].shape[0]
     own_queries = queries[0].shape[0]
     slots = wide.shape[0] // pairs
@@ -74,9 +74,11 @@
     for r in range(rounds):
         wide[pl.ds(r, pairs, stride=slots), :] = sketches[r][...].astype(F32)
     spot = lax.axis_index("dp")
-    upper = spot // rounds
+    core = lax.axis_index("tensor")
+    near = spot // rounds == core
     scores = None
-    for ref, half in zip(queries, (upper, 1 - upper)):
+    for i, half in enumerate((core, 1 - core)):
+        entries = jnp.where(near, queries[2 * i][...], queries[2 * i + 1][...])
         start = half * (slots * pairs // 2)
         flat = jnp.concatenate(
             [
@@ -86,7 +88,7 @@
             axis=1,
         ).astype(BF16)
         term = lax.dot_general(
-            flat, ref[...], (((1,), (1,)), ((), ())), preferred_element_type=F32
+            flat, entries, (((1,), (1,)), ((), ())), preferred_element_type=F32
         )
         scores = term if scores is None else scores + term
     spread = jnp.concatenate([scores] * rounds, axis=1)
@@ -108,22 +110,9 @@
     hbm = pl.BlockSpec(memory_space=pl.ANY)
     swap = [(0, 1), (1, 0)]
 
-    def place(a, m, t):
-        return (a * rounds + m) * 2 + t
-
-    taken = [
-        lax.ppermute(
-            queries,
-            ("dp", "tensor"),
-            [
-                (place(t, m, a ^ j), place(a, m, t))
-                for a in range(2)
-                for m in range(rounds)
-                for t in range(2)
-            ],
-        )
-        for j in range(2)
-    ]
+    far = lax.ppermute(queries, "dp", [(d, (d + rounds) % clips) for d in range(clips)])
+    core_own = lax.ppermute(queries, "tensor", swap)
+    core_far = lax.ppermute(far, "tensor", swap)
     across = [
         [(a * rounds + m, a * rounds + (m ^ r)) for a in range(2) for m in range(rounds)]
         for r in range(1, rounds)
@@ -168,13 +157,13 @@
     width = rounds * own_queries
     scored = pl.pallas_call(
         functools.partial(score_kernel, rounds),
-        in_specs=[vmem] * (rounds + 2),
+        in_specs=[vmem] * (rounds + 4),
         out_specs=[vmem] * rounds,
         out_shape=[jax.ShapeDtypeStruct((1, width), F32)] * rounds,
         scratch_shapes=[pltpu.VMEM((pairs * slots, LANES), F32)],
         compiler_params=pltpu.CompilerParams(vmem_limit_bytes=16 << 20),
         name="score",
-    )(*sketches, *taken)
+    )(*sketches, queries, far, core_own, core_far)
 
     parts = [lax.ppermute(s, "dp", perm) for s, perm in zip(scored[1:], across)]
     return functools.reduce(jnp.add, parts, scored[0])

time: 25.2 us -> 25.3 us (level)
  waiting for transfers between devices: 6.14 us -> 8.25 us
  starting transfers between devices: 13.1 us -> 11.6 us
  Pallas kernels: 5.22 us -> 4.74 us
    ppermute x2 -> x3, waiting for transfers between devices: 0.01 us -> 2.19 us  [the longest x1 2.19 us: on_device(): lax.ppermute(queries, 'dp', [(d, (d + rounds) % clips) for d in range(cli...]
    ppermute x3, waiting for transfers between devices: 4.53 us -> 3.32 us  [on_device(): sketches = [sketch] + [lax.ppermute(sketch, 'dp', perm) for perm in across]]
    ppermute x3, waiting for transfers between devices: 1.6 us -> 2.74 us  [on_device(): parts = [lax.ppermute(s, 'dp', perm) for s, perm in zip(scored[1:], across)]]
    ppermute x2 -> x3, starting transfers between devices: 5.58 us -> 4.53 us  [the longest x1 4.04 us: on_device(): lax.ppermute(queries, 'dp', [(d, (d + rounds) % clips) for d in range(cli...]
    pallas_call x1, Pallas kernels: 4.3 us -> 3.81 us  [on_device(): pl.pallas_call(functools.partial(project_kernel, rank), in_specs=[hbm] *...]
    ppermute x1, starting transfers between devices: 0.52 us -> 0.07 us  [on_device(): other = lax.ppermute(partial, 'tensor', swap)]
  transfers between devices with their start and end apart: 9 -> 10, of which waited for: 6 -> 7; matrix products, arithmetic and copies ran while one was open for 0% -> 0% of each run, Pallas kernels for 3% -> 18%
where the time goes in v5:
time: 25.3 us; the launch traced here: 25.2 us
  starting transfers between devices  11.6 us (46%)
  waiting for transfers between devices  8.25 us (33%)
  Pallas kernels  4.74 us (19%)
  other arithmetic  0.52 us (2%)
    ppermute x1, starting transfers between devices, on_device(): lax.ppermute(queries, 'dp', [(d, (d + rounds) % clips) for d in range(cli...  4.04 us
    pallas_call x1, Pallas kernels, on_device(): pl.pallas_call(functools.partial(project_kernel, rank), in_specs=[hbm] *...  3.81 us
    ppermute x3, starting transfers between devices, on_device(): parts = [lax.ppermute(s, 'dp', perm) for s, perm in zip(scored[1:], across)]  3.51 us
    ppermute x3, starting transfers between devices, on_device(): sketches = [sketch] + [lax.ppermute(sketch, 'dp', perm) for perm in across]  3.49 us
    ppermute x3, waiting for transfers between devices, on_device(): sketches = [sketch] + [lax.ppermute(sketch, 'dp', perm) for perm in across]  3.32 us
    ppermute x3, waiting for transfers between devices, on_device(): parts = [lax.ppermute(s, 'dp', perm) for s, perm in zip(scored[1:], across)]  2.74 us
    ppermute x1, waiting for transfers between devices, on_device(): lax.ppermute(queries, 'dp', [(d, (d + rounds) % clips) for d in range(cli...  2.19 us
    add x1, other arithmetic, on_device(): return functools.reduce(jnp.add, parts, scored[0])  0.52 us
  transfers between devices with their start and end apart: 10, of which 7 were waited for; matrix products, arithmetic and copies ran while one was open for 0% of the time, Pallas kernels for 18%

profile of v5, /device:TPU:0, one launch (start us, length us, event | category | flops | bytes accessed | tf_op | source)
XLA Modules:
  0.0 25.2 jit_solution(15307909089035940485)
XLA Ops:
  0.0 4.0 %collective-permute-start.4 = (bf16[32,2048]{1,0:T(8,128)(2,1)}, bf16[32,2048]{1,0:T(8,128)(2,1)S(1)}, u32[]{:S(2)}, u32[]{:S(2)}) collective-permute-start(bf16[32,2048]{1,0:T(8,128)(2,1)} %refs_4_.1), channel_id=1, source_target_pairs={{0,8},{2,10},{4,12},{6,14},{8,0},{10,2},{12,4},{14,6},{1,9},{3,11}... | collective-permute-start | bytes 393224 | tf_op jit(solution)/shard_map/ppermute | solution.py:113
  4.0 3.8 %project.1.own_ref = f32[384,128]{1,0:T(8,128)S(1)} custom-call(bf16[1,384,2560]{2,1,0:T(8,128)(2,1)} %acts_ref.1, bf16[1,384,2560]{2,1,0:T(8,128)(2,1)} %grads_ref.1, bf16[2560,128]{1,0:T(8,128)(2,1)} %proj_ref.1), custom_call_target="tpu_custom_call" | custom-call | flops 503316480 | bytes 3932160 | tf_op jit(solution)/shard_map/project/pallas_call | solution.py:120
  7.9 0.1 collective-permute-start
  7.9 0.5 %collective-permute-start.5 = (bf16[32,2048]{1,0:T(8,128)(2,1)S(1)}, bf16[32,2048]{1,0:T(8,128)(2,1)S(1)}, u32[]{:S(2)}, u32[]{:S(2)}) collective-permute-start(bf16[32,2048]{1,0:T(8,128)(2,1)S(1)} %copy-done), channel_id=1, source_target_pairs={{0,1},{1,0},{2,3},{3,2},{4,5},{5,4},{6,7},{7,6},{8,9},{9,8},{10,11... | collective-permute-start | bytes 393224 | tf_op jit(solution)/shard_map/ppermute | solution.py:114
  8.4 2.2 %collective-permute-done.4.refs_5_ = bf16[32,2048]{1,0:T(8,128)(2,1)S(1)} collective-permute-done((bf16[32,2048]{1,0:T(8,128)(2,1)}, bf16[32,2048]{1,0:T(8,128)(2,1)S(1)}, u32[]{:S(2)}, u32[]{:S(2)}) %collective-permute-start.4) | collective-permute-done | bytes 131104 | tf_op jit(solution)/shard_map/ppermute | solution.py:113
  10.6 0.0 collective-permute-start.6
  10.6 0.2 count.1.count_ref
  10.8 0.5 %sketch.1.refs_0_ = bf16[32,128]{1,0:T(8,128)(2,1)S(1)} custom-call(f32[384,64]{1,0:T(8,128)S(1)} %count.1.count_ref, f32[384,128]{1,0:T(8,128)S(1)} %project.1.own_ref, f32[384,128]{1,0:T(8,128)S(1)} %collective-permute-done.other_ref), custom_call_target="tpu_custom_call" | custom-call | tf_op jit(solution)/shard_map/sketch/pallas_call | solution.py:146
  11.3 1.5 %collective-permute-start.1 = (bf16[32,128]{1,0:T(8,128)(2,1)S(1)}, bf16[32,128]{1,0:T(8,128)(2,1)S(1)}, u32[]{:S(2)}, u32[]{:S(2)}) collective-permute-start(bf16[32,128]{1,0:T(8,128)(2,1)S(1)} %sketch.1.refs_0_), channel_id=1, source_target_pairs={{0,2},{2,0},{4,6},{6,4},{8,10},{10,8},{12,14},{14,12},{1,3},{3,1},... | collective-permute-start | bytes 24584 | tf_op jit(solution)/shard_map/ppermute | solution.py:156
  12.8 0.8 %collective-permute-start.2 = (bf16[32,128]{1,0:T(8,128)(2,1)S(1)}, bf16[32,128]{1,0:T(8,128)(2,1)S(1)}, u32[]{:S(2)}, u32[]{:S(2)}) collective-permute-start(bf16[32,128]{1,0:T(8,128)(2,1)S(1)} %sketch.1.refs_0_), channel_id=1, source_target_pairs={{0,4},{2,6},{4,0},{6,2},{8,12},{10,14},{12,8},{14,10},{1,5},{3,7},... | collective-permute-start | bytes 24584 | tf_op jit(solution)/shard_map/ppermute | solution.py:156
  13.6 1.2 %collective-permute-start.3 = (bf16[32,128]{1,0:T(8,128)(2,1)S(1)}, bf16[32,128]{1,0:T(8,128)(2,1)S(1)}, u32[]{:S(2)}, u32[]{:S(2)}) collective-permute-start(bf16[32,128]{1,0:T(8,128)(2,1)S(1)} %sketch.1.refs_0_), channel_id=1, source_target_pairs={{0,6},{2,4},{4,2},{6,0},{8,14},{10,12},{12,10},{14,8},{1,7},{3,5},... | collective-permute-start | bytes 24584 | tf_op jit(solution)/shard_map/ppermute | solution.py:156
  14.8 0.0 collective-permute-done.5.refs_6_
  14.8 0.2 collective-permute-done.1.refs_1_
  15.0 1.5 %collective-permute-done.2.refs_2_ = bf16[32,128]{1,0:T(8,128)(2,1)S(1)} collective-permute-done((bf16[32,128]{1,0:T(8,128)(2,1)S(1)}, bf16[32,128]{1,0:T(8,128)(2,1)S(1)}, u32[]{:S(2)}, u32[]{:S(2)}) %collective-permute-start.2) | collective-permute-done | bytes 8224 | tf_op jit(solution)/shard_map/ppermute | solution.py:156
  16.4 1.7 %collective-permute-done.3.refs_3_ = bf16[32,128]{1,0:T(8,128)(2,1)S(1)} collective-permute-done((bf16[32,128]{1,0:T(8,128)(2,1)S(1)}, bf16[32,128]{1,0:T(8,128)(2,1)S(1)}, u32[]{:S(2)}, u32[]{:S(2)}) %collective-permute-start.3) | collective-permute-done | bytes 8224 | tf_op jit(solution)/shard_map/ppermute | solution.py:156
  18.1 0.0 collective-permute-done.6.refs_7_
  18.1 0.3 %score.1 = (f32[1,128]{1,0:T(1,128)S(1)}, f32[1,128]{1,0:T(1,128)S(1)}, f32[1,128]{1,0:T(1,128)S(1)}, f32[1,128]{1,0:T(1,128)S(1)}) custom-call(bf16[32,128]{1,0:T(8,128)(2,1)S(1)} %sketch.1.refs_0_, bf16[32,128]{1,0:T(8,128)(2,1)S(1)} %collective-permute-done.1.refs_1_, bf16[32,128]{1,0:T(8,128)(2,1)S(1)} %collective-permute-done.2.refs_2_, ...), custom_call_target="tpu_custom_call" | custom-call | tf_op jit(solution)/shard_map/score/pallas_call | solution.py:158
  18.4 0.6 %collective-permute-start.7 = (f32[1,128]{1,0:T(1,128)S(1)}, f32[1,128]{1,0:T(1,128)S(1)}, u32[]{:S(2)}, u32[]{:S(2)}) collective-permute-start(f32[1,128]{1,0:T(1,128)S(1)} %get-tuple-element.10), channel_id=1, source_target_pairs={{0,2},{2,0},{4,6},{6,4},{8,10},{10,8},{12,14},{14,12},{1,3},{3,1},... | collective-permute-start | bytes 1544 | tf_op jit(solution)/shard_map/ppermute | solution.py:168
  19.0 1.2 %collective-permute-start.8 = (f32[1,128]{1,0:T(1,128)S(1)}, f32[1,128]{1,0:T(1,128)S(1)}, u32[]{:S(2)}, u32[]{:S(2)}) collective-permute-start(f32[1,128]{1,0:T(1,128)S(1)} %get-tuple-element.11), channel_id=1, source_target_pairs={{0,4},{2,6},{4,0},{6,2},{8,12},{10,14},{12,8},{14,10},{1,5},{3,7},... | collective-permute-start | bytes 1544 | tf_op jit(solution)/shard_map/ppermute | solution.py:168
  20.2 1.7 %collective-permute-start.9 = (f32[1,128]{1,0:T(1,128)S(1)}, f32[1,128]{1,0:T(1,128)S(1)}, u32[]{:S(2)}, u32[]{:S(2)}) collective-permute-start(f32[1,128]{1,0:T(1,128)S(1)} %get-tuple-element.12), channel_id=1, source_target_pairs={{0,6},{2,4},{4,2},{6,0},{8,14},{10,12},{12,10},{14,8},{1,7},{3,5},... | collective-permute-start | bytes 1544 | tf_op jit(solution)/shard_map/ppermute | solution.py:168
  21.9 0.1 collective-permute-done.7
  22.0 0.5 %collective-permute-done.8 = f32[1,128]{1,0:T(1,128)S(1)} collective-permute-done((f32[1,128]{1,0:T(1,128)S(1)}, f32[1,128]{1,0:T(1,128)S(1)}, u32[]{:S(2)}, u32[]{:S(2)}) %collective-permute-start.8) | collective-permute-done | bytes 544 | tf_op jit(solution)/shard_map/ppermute | solution.py:168
  22.5 2.1 %collective-permute-done.9 = f32[1,128]{1,0:T(1,128)S(1)} collective-permute-done((f32[1,128]{1,0:T(1,128)S(1)}, f32[1,128]{1,0:T(1,128)S(1)}, u32[]{:S(2)}, u32[]{:S(2)}) %collective-permute-start.9) | collective-permute-done | bytes 544 | tf_op jit(solution)/shard_map/ppermute | solution.py:168
  24.7 0.5 %add_add_fusion = f32[1,128]{1,0:T(1,128)} fusion(f32[1,128]{1,0:T(1,128)S(1)} %collective-permute-done.9, f32[1,128]{1,0:T(1,128)S(1)} %collective-permute-done.8, f32[1,128]{1,0:T(1,128)S(1)} %get-tuple-element.9, f32[1,128]{1,0:T(1,128)S(1)} %collective-permute-done.7), kind=kLoop, calls=%fused_computation | loop fusion | flops 384 | bytes 2560 | tf_op jit(solution)/shard_map/add | solution.py:169
  (5 shorter events, 0.0 us)
Async XLA Ops:
  0.0 7.9 %copy-start = (bf16[32,2048]{1,0:T(8,128)(2,1)S(1)}, bf16[32,2048]{1,0:T(8,128)(2,1)}, u32[]{:S(2)}) copy-start(bf16[32,2048]{1,0:T(8,128)(2,1)} %refs_4_.1) | copy-start | bytes 393220
  0.0 10.6 %copy-start.1 = (s32[1,256]{1,0:T(1,128)S(1)}, s32[1,256]{1,0:T(1,128)}, u32[]{:S(2)}) copy-start(s32[1,256]{1,0:T(1,128)} %picks_ref.1) | copy-start | bytes 3076
  0.0 10.6 %collective-permute-start.4 = (bf16[32,2048]{1,0:T(8,128)(2,1)}, bf16[32,2048]{1,0:T(8,128)(2,1)S(1)}, u32[]{:S(2)}, u32[]{:S(2)}) collective-permute-start(bf16[32,2048]{1,0:T(8,128)(2,1)} %refs_4_.1), channel_id=1, source_target_pairs={{0,8},{2,10},{4,12},{6,14},{8,0},{10,2},{12,4},{14,6},{1,9},{3,11}... | collective-permute-start | bytes 393224 | tf_op jit(solution)/shard_map/ppermute | solution.py:113
  7.9 3.0 %collective-permute-start = (f32[384,128]{1,0:T(8,128)S(1)}, f32[384,128]{1,0:T(8,128)S(1)}, u32[]{:S(2)}, u32[]{:S(2)}) collective-permute-start(f32[384,128]{1,0:T(8,128)S(1)} %project.1.own_ref), channel_id=1, source_target_pairs={{0,1},{1,0},{2,3},{3,2},{4,5},{5,4},{6,7},{7,6},{8,9},{9,8},{10,11... | collective-permute-start | bytes 589832 | tf_op jit(solution)/shard_map/ppermute | solution.py:137
  7.9 6.9 %collective-permute-start.5 = (bf16[32,2048]{1,0:T(8,128)(2,1)S(1)}, bf16[32,2048]{1,0:T(8,128)(2,1)S(1)}, u32[]{:S(2)}, u32[]{:S(2)}) collective-permute-start(bf16[32,2048]{1,0:T(8,128)(2,1)S(1)} %copy-done), channel_id=1, source_target_pairs={{0,1},{1,0},{2,3},{3,2},{4,5},{5,4},{6,7},{7,6},{8,9},{9,8},{10,11... | collective-permute-start | bytes 393224 | tf_op jit(solution)/shard_map/ppermute | solution.py:114
  10.6 7.5 %collective-permute-start.6 = (bf16[32,2048]{1,0:T(8,128)(2,1)S(1)}, bf16[32,2048]{1,0:T(8,128)(2,1)S(1)}, u32[]{:S(2)}, u32[]{:S(2)}) collective-permute-start(bf16[32,2048]{1,0:T(8,128)(2,1)S(1)} %collective-permute-done.4.refs_5_), channel_id=1, source_target_pairs={{0,1},{1,0},{2,3},{3,2},{4,5},{5,4},{6,7},{7,6},{8,9},{9,8},{10,11... | collective-permute-start | bytes 393224 | tf_op jit(solution)/shard_map/ppermute | solution.py:115
  11.3 3.7 %collective-permute-start.1 = (bf16[32,128]{1,0:T(8,128)(2,1)S(1)}, bf16[32,128]{1,0:T(8,128)(2,1)S(1)}, u32[]{:S(2)}, u32[]{:S(2)}) collective-permute-start(bf16[32,128]{1,0:T(8,128)(2,1)S(1)} %sketch.1.refs_0_), channel_id=1, source_target_pairs={{0,2},{2,0},{4,6},{6,4},{8,10},{10,8},{12,14},{14,12},{1,3},{3,1},... | collective-permute-start | bytes 24584 | tf_op jit(solution)/shard_map/ppermute | solution.py:156
  12.8 3.7 %collective-permute-start.2 = (bf16[32,128]{1,0:T(8,128)(2,1)S(1)}, bf16[32,128]{1,0:T(8,128)(2,1)S(1)}, u32[]{:S(2)}, u32[]{:S(2)}) collective-permute-start(bf16[32,128]{1,0:T(8,128)(2,1)S(1)} %sketch.1.refs_0_), channel_id=1, source_target_pairs={{0,4},{2,6},{4,0},{6,2},{8,12},{10,14},{12,8},{14,10},{1,5},{3,7},... | collective-permute-start | bytes 24584 | tf_op jit(solution)/shard_map/ppermute | solution.py:156
  13.6 4.5 %collective-permute-start.3 = (bf16[32,128]{1,0:T(8,128)(2,1)S(1)}, bf16[32,128]{1,0:T(8,128)(2,1)S(1)}, u32[]{:S(2)}, u32[]{:S(2)}) collective-permute-start(bf16[32,128]{1,0:T(8,128)(2,1)S(1)} %sketch.1.refs_0_), channel_id=1, source_target_pairs={{0,6},{2,4},{4,2},{6,0},{8,14},{10,12},{12,10},{14,8},{1,7},{3,5},... | collective-permute-start | bytes 24584 | tf_op jit(solution)/shard_map/ppermute | solution.py:156
  18.4 3.6 %collective-permute-start.7 = (f32[1,128]{1,0:T(1,128)S(1)}, f32[1,128]{1,0:T(1,128)S(1)}, u32[]{:S(2)}, u32[]{:S(2)}) collective-permute-start(f32[1,128]{1,0:T(1,128)S(1)} %get-tuple-element.10), channel_id=1, source_target_pairs={{0,2},{2,0},{4,6},{6,4},{8,10},{10,8},{12,14},{14,12},{1,3},{3,1},... | collective-permute-start | bytes 1544 | tf_op jit(solution)/shard_map/ppermute | solution.py:168
  19.0 3.5 %collective-permute-start.8 = (f32[1,128]{1,0:T(1,128)S(1)}, f32[1,128]{1,0:T(1,128)S(1)}, u32[]{:S(2)}, u32[]{:S(2)}) collective-permute-start(f32[1,128]{1,0:T(1,128)S(1)} %get-tuple-element.11), channel_id=1, source_target_pairs={{0,4},{2,6},{4,0},{6,2},{8,12},{10,14},{12,8},{14,10},{1,5},{3,7},... | collective-permute-start | bytes 1544 | tf_op jit(solution)/shard_map/ppermute | solution.py:168
  20.2 4.4 %collective-permute-start.9 = (f32[1,128]{1,0:T(1,128)S(1)}, f32[1,128]{1,0:T(1,128)S(1)}, u32[]{:S(2)}, u32[]{:S(2)}) collective-permute-start(f32[1,128]{1,0:T(1,128)S(1)} %get-tuple-element.12), channel_id=1, source_target_pairs={{0,6},{2,4},{4,2},{6,0},{8,14},{10,12},{12,10},{14,8},{1,7},{3,5},... | collective-permute-start | bytes 1544 | tf_op jit(solution)/shard_map/ppermute | solution.py:168

commit v6 on v5

--- a/solution.py
+++ b/solution.py
@@ -59,20 +59,21 @@
         precision=lax.Precision.HIGHEST,
         preferred_element_type=F32,
     )
-    pairs = out_ref.shape[0]
+    pairs = out_ref.shape[1]
     even = held[pl.ds(0, pairs, stride=2), :]
     odd = held[pl.ds(1, pairs, stride=2), :]
-    out_ref[...] = jnp.concatenate([even, odd], axis=1).astype(BF16)
+    rows = jnp.concatenate([even, odd], axis=1).astype(BF16)
+    out_ref[...] = jnp.broadcast_to(rows[None], out_ref.shape)
 
 
-def score_kernel(rounds, *refs):
-    sketches, queries, outs, wide = refs[:rounds], refs[rounds : rounds + 4], refs[rounds + 4 : -1], refs[-1]
-    pairs = sketches[0].shape[0]
+def score_kernel(sketches_ref, *refs):
+    queries, out_ref, wide = refs[:4], refs[4], refs[5]
+    rounds, pairs, _ = sketches_ref.shape
     own_queries = queries[0].shape[0]
     slots = wide.shape[0] // pairs
     wide[...] = jnp.zeros_like(wide)
     for r in range(rounds):
-        wide[pl.ds(r, pairs, stride=slots), :] = sketches[r][...].astype(F32)
+        wide[pl.ds(r, pairs, stride=slots), :] = sketches_ref[r].astype(F32)
     spot = lax.axis_index("dp")
     core = lax.axis_index("tensor")
     near = spot // rounds == core
@@ -94,8 +95,7 @@
     spread = jnp.concatenate([scores] * rounds, axis=1)
     block = lax.broadcasted_iota(jnp.int32, spread.shape, 1) // own_queries
     spread = jnp.where(block == lax.rem(spot, rounds), spread, 0.0)
-    for r in range(rounds):
-        outs[r][...] = spread[r : r + 1, :]
+    out_ref[...] = spread[0:rounds]
 
 
 def on_device(activations, out_grads, projections, sample_index, queries):
@@ -113,10 +113,7 @@
     far = lax.ppermute(queries, "dp", [(d, (d + rounds) % clips) for d in range(clips)])
     core_own = lax.ppermute(queries, "tensor", swap)
     core_far = lax.ppermute(far, "tensor", swap)
-    across = [
-        [(a * rounds + m, a * rounds + (m ^ r)) for a in range(2) for m in range(rounds)]
-        for r in range(1, rounds)
-    ]
+    halves = [list(range(a * rounds, (a + 1) * rounds)) for a in range(2)]
     partial = pl.pallas_call(
         functools.partial(project_kernel, rank),
         in_specs=[hbm] * 3,
@@ -147,26 +144,26 @@
         functools.partial(sketch_kernel, rank),
         in_specs=[vmem] * 3,
         out_specs=vmem,
-        out_shape=jax.ShapeDtypeStruct((pairs, LANES), BF16),
+        out_shape=jax.ShapeDtypeStruct((rounds, pairs, LANES), BF16),
         scratch_shapes=[pltpu.VMEM((rank, rank), F32)],
         compiler_params=pltpu.CompilerParams(vmem_limit_bytes=8 << 20),
         name="sketch",
     )(count, partial, other)
 
-    sketches = [sketch] + [lax.ppermute(sketch, "dp", perm) for perm in across]
+    sketches = lax.all_to_all(sketch, "dp", 0, 0, axis_index_groups=halves, tiled=True)
     width = rounds * own_queries
     scored = pl.pallas_call(
-        functools.partial(score_kernel, rounds),
-        in_specs=[vmem] * (rounds + 4),
-        out_specs=[vmem] * rounds,
-        out_shape=[jax.ShapeDtypeStruct((1, width), F32)] * rounds,
+        score_kernel,
+        in_specs=[vmem] * 5,
+        out_specs=vmem,
+        out_shape=jax.ShapeDtypeStruct((rounds, width), F32),
         scratch_shapes=[pltpu.VMEM((pairs * slots, LANES), F32)],
         compiler_params=pltpu.CompilerParams(vmem_limit_bytes=16 << 20),
         name="score",
-    )(*sketches, queries, far, core_own, core_far)
+    )(sketches, queries, far, core_own, core_far)
 
-    parts = [lax.ppermute(s, "dp", perm) for s, perm in zip(scored[1:], across)]
-    return functools.reduce(jnp.add, parts, scored[0])
+    parts = lax.all_to_all(scored, "dp", 0, 0, axis_index_groups=halves, tiled=True)
+    return parts.sum(axis=0, keepdims=True)
 
 
 def solution(mesh):

time: 25.3 us -> 28 us (1.11)
  blocking collectives: 0 us -> 7 us
  starting transfers between devices: 11.6 us -> 7.86 us
  waiting for transfers between devices: 8.25 us -> 6.91 us
  Pallas kernels: 4.74 us -> 5.35 us
    ppermute x6 -> x0, starting transfers between devices: 7 us -> none  [the longest x3 3.51 us: on_device(): parts = [lax.ppermute(s, 'dp', perm) for s, perm in zip(scored[1:], across)]]
    all_to_all x0 -> x1, blocking collectives: none -> 7 us  [on_device(): lax.all_to_all(scored, 'dp', 0, 0, axis_index_groups=halves, tiled=True)]
    ppermute x6 -> x0, waiting for transfers between devices: 6.06 us -> none  [the longest x3 3.32 us: on_device(): sketches = [sketch] + [lax.ppermute(sketch, 'dp', perm) for perm in across]]
    all_to_all x0 -> x1, waiting for transfers between devices: none -> 4.71 us  [on_device(): lax.all_to_all(sketch, 'dp', 0, 0, axis_index_groups=halves, tiled=True)]
    all_to_all x0 -> x1, starting transfers between devices: none -> 3.26 us  [on_device(): lax.all_to_all(sketch, 'dp', 0, 0, axis_index_groups=halves, tiled=True)]
    pallas_call x1, Pallas kernels: 0.46 us -> 1.07 us  [on_device(): pl.pallas_call(functools.partial(sketch_kernel, rank), in_specs=[vmem] *...]
    reduce_sum x0 -> x1, other arithmetic: none -> 0.53 us  [on_device(): return parts.sum(axis=0, keepdims=True)]
    add x1 -> x0, other arithmetic: 0.52 us -> none  [on_device(): return functools.reduce(jnp.add, parts, scored[0])]
  transfers between devices with their start and end apart: 10 -> 5, of which waited for: 7 -> 2; matrix products, arithmetic and copies ran while one was open for 0% -> 0% of each run, Pallas kernels for 18% -> 18%
where the time goes in v6:
time: 28 us; the launch traced here: 27.7 us
  starting transfers between devices  7.86 us (28%)
  blocking collectives  7 us (25%)
  waiting for transfers between devices  6.91 us (25%)
  Pallas kernels  5.35 us (19%)
  other arithmetic  0.53 us (2%)
    all_to_all x1, blocking collectives, on_device(): lax.all_to_all(scored, 'dp', 0, 0, axis_index_groups=halves, tiled=True)  7 us
    all_to_all x1, waiting for transfers between devices, on_device(): lax.all_to_all(sketch, 'dp', 0, 0, axis_index_groups=halves, tiled=True)  4.71 us
    ppermute x1, starting transfers between devices, on_device(): lax.ppermute(queries, 'dp', [(d, (d + rounds) % clips) for d in range(cli...  4.04 us
    pallas_call x1, Pallas kernels, on_device(): pl.pallas_call(functools.partial(project_kernel, rank), in_specs=[hbm] *...  3.81 us
    all_to_all x1, starting transfers between devices, on_device(): lax.all_to_all(sketch, 'dp', 0, 0, axis_index_groups=halves, tiled=True)  3.26 us
    ppermute x1, waiting for transfers between devices, on_device(): lax.ppermute(queries, 'dp', [(d, (d + rounds) % clips) for d in range(cli...  2.19 us
    pallas_call x1, Pallas kernels, on_device(): pl.pallas_call(functools.partial(sketch_kernel, rank), in_specs=[vmem] *...  1.07 us
  transfers between devices with their start and end apart: 5, of which 2 were waited for; matrix products, arithmetic and copies ran while one was open for 0% of the time, Pallas kernels for 18%

profile of v6, /device:TPU:0, one launch (start us, length us, event | category | flops | bytes accessed | tf_op | source)
XLA Modules:
  0.0 27.7 jit_solution(3321908081121402853)
XLA Ops:
  0.0 0.0 copy-start
  0.0 0.0 copy-start.1
  0.0 4.0 %collective-permute-start.1 = (bf16[32,2048]{1,0:T(8,128)(2,1)}, bf16[32,2048]{1,0:T(8,128)(2,1)S(1)}, u32[]{:S(2)}, u32[]{:S(2)}) collective-permute-start(bf16[32,2048]{1,0:T(8,128)(2,1)} %refs_0_.1), channel_id=1, source_target_pairs={{0,8},{2,10},{4,12},{6,14},{8,0},{10,2},{12,4},{14,6},{1,9},{3,11}... | collective-permute-start | bytes 393224 | tf_op jit(solution)/shard_map/ppermute | solution.py:113
  4.0 3.8 %project.1.own_ref = f32[384,128]{1,0:T(8,128)S(1)} custom-call(bf16[1,384,2560]{2,1,0:T(8,128)(2,1)} %acts_ref.1, bf16[1,384,2560]{2,1,0:T(8,128)(2,1)} %grads_ref.1, bf16[2560,128]{1,0:T(8,128)(2,1)} %proj_ref.1), custom_call_target="tpu_custom_call" | custom-call | flops 503316480 | bytes 3932160 | tf_op jit(solution)/shard_map/project/pallas_call | solution.py:117
  7.9 0.1 collective-permute-start
  7.9 0.0 copy-done
  7.9 0.5 %collective-permute-start.2 = (bf16[32,2048]{1,0:T(8,128)(2,1)S(1)}, bf16[32,2048]{1,0:T(8,128)(2,1)S(1)}, u32[]{:S(2)}, u32[]{:S(2)}) collective-permute-start(bf16[32,2048]{1,0:T(8,128)(2,1)S(1)} %copy-done), channel_id=1, source_target_pairs={{0,1},{1,0},{2,3},{3,2},{4,5},{5,4},{6,7},{7,6},{8,9},{9,8},{10,11... | collective-permute-start | bytes 393224 | tf_op jit(solution)/shard_map/ppermute | solution.py:114
  8.4 2.2 %collective-permute-done.1.refs_1_ = bf16[32,2048]{1,0:T(8,128)(2,1)S(1)} collective-permute-done((bf16[32,2048]{1,0:T(8,128)(2,1)}, bf16[32,2048]{1,0:T(8,128)(2,1)S(1)}, u32[]{:S(2)}, u32[]{:S(2)}) %collective-permute-start.1) | collective-permute-done | bytes 131104 | tf_op jit(solution)/shard_map/ppermute | solution.py:113
  10.6 0.0 collective-permute-start.3
  10.6 0.0 copy-done.1
  10.6 0.2 count.1.count_ref
  10.8 0.0 collective-permute-done.other_ref
  10.8 1.1 %sketch.1 = bf16[4,32,128]{2,1,0:T(8,128)(2,1)} custom-call(f32[384,64]{1,0:T(8,128)S(1)} %count.1.count_ref, f32[384,128]{1,0:T(8,128)S(1)} %project.1.own_ref, f32[384,128]{1,0:T(8,128)S(1)} %collective-permute-done.other_ref), custom_call_target="tpu_custom_call" | custom-call | tf_op jit(solution)/shard_map/sketch/pallas_call | solution.py:143
  11.9 3.3 %all-to-all-start = ((bf16[4,32,128]{2,1,0:T(8,128)(2,1)}), bf16[4,32,128]{2,1,0:T(8,128)(2,1)S(1)}, u32[]{:S(2)}, u32[]{:S(2)}) async-start(bf16[4,32,128]{2,1,0:T(8,128)(2,1)} %sketch.1), calls=%async_computation | async-start | bytes 65536 | tf_op jit(solution)/shard_map/all_to_all | solution.py:153
  15.2 0.0 collective-permute-done.2.refs_2_
  15.2 4.7 %all-to-all-done.sketches_ref = bf16[4,32,128]{2,1,0:T(8,128)(2,1)S(1)} async-done(((bf16[4,32,128]{2,1,0:T(8,128)(2,1)}), bf16[4,32,128]{2,1,0:T(8,128)(2,1)S(1)}, u32[]{:S(2)}, u32[]{:S(2)}) %all-to-all-start) | async-done | bytes 32800 | tf_op jit(solution)/shard_map/all_to_all | solution.py:153
  19.9 0.0 collective-permute-done.3.refs_3_
  19.9 0.3 score.1
  20.2 7.0 %all_to_all.14 = f32[4,1,128]{2,1,0:T(1,128)S(1)} all-to-all(f32[4,1,128]{2,1,0:T(1,128)S(1)} %bitcast.4), channel_id=1, replica_groups={{0,2,4,6},{8,10,12,14},{1,3,5,7},{9,11,13,15},{16,18,20,22},{24,26,28,3..., dimensions={0} | all-to-all | bytes 4096 | tf_op jit(solution)/shard_map/all_to_all | solution.py:165
  27.2 0.5 %reduce_sum.9 = f32[128]{0:T(128)} reduce(f32[4,1,128]{2,1,0:T(1,128)S(1)} %all_to_all.14, f32[]{:T(128)} %constant.0.clone.1), dimensions={0,1}, to_apply=%region_0.0 | reduce | flops 384 | bytes 2564 | tf_op jit(solution)/shard_map/reduce_sum | solution.py:166
Async XLA Ops:
  0.0 7.9 %copy-start = (bf16[32,2048]{1,0:T(8,128)(2,1)S(1)}, bf16[32,2048]{1,0:T(8,128)(2,1)}, u32[]{:S(2)}) copy-start(bf16[32,2048]{1,0:T(8,128)(2,1)} %refs_0_.1) | copy-start | bytes 393220
  0.0 10.6 %copy-start.1 = (s32[1,256]{1,0:T(1,128)S(1)}, s32[1,256]{1,0:T(1,128)}, u32[]{:S(2)}) copy-start(s32[1,256]{1,0:T(1,128)} %picks_ref.1) | copy-start | bytes 3076
  0.0 10.6 %collective-permute-start.1 = (bf16[32,2048]{1,0:T(8,128)(2,1)}, bf16[32,2048]{1,0:T(8,128)(2,1)S(1)}, u32[]{:S(2)}, u32[]{:S(2)}) collective-permute-start(bf16[32,2048]{1,0:T(8,128)(2,1)} %refs_0_.1), channel_id=1, source_target_pairs={{0,8},{2,10},{4,12},{6,14},{8,0},{10,2},{12,4},{14,6},{1,9},{3,11}... | collective-permute-start | bytes 393224 | tf_op jit(solution)/shard_map/ppermute | solution.py:113
  7.9 3.0 %collective-permute-start = (f32[384,128]{1,0:T(8,128)S(1)}, f32[384,128]{1,0:T(8,128)S(1)}, u32[]{:S(2)}, u32[]{:S(2)}) collective-permute-start(f32[384,128]{1,0:T(8,128)S(1)} %project.1.own_ref), channel_id=1, source_target_pairs={{0,1},{1,0},{2,3},{3,2},{4,5},{5,4},{6,7},{7,6},{8,9},{9,8},{10,11... | collective-permute-start | bytes 589832 | tf_op jit(solution)/shard_map/ppermute | solution.py:134
  7.9 7.2 %collective-permute-start.2 = (bf16[32,2048]{1,0:T(8,128)(2,1)S(1)}, bf16[32,2048]{1,0:T(8,128)(2,1)S(1)}, u32[]{:S(2)}, u32[]{:S(2)}) collective-permute-start(bf16[32,2048]{1,0:T(8,128)(2,1)S(1)} %copy-done), channel_id=1, source_target_pairs={{0,1},{1,0},{2,3},{3,2},{4,5},{5,4},{6,7},{7,6},{8,9},{9,8},{10,11... | collective-permute-start | bytes 393224 | tf_op jit(solution)/shard_map/ppermute | solution.py:114
  10.6 9.3 %collective-permute-start.3 = (bf16[32,2048]{1,0:T(8,128)(2,1)S(1)}, bf16[32,2048]{1,0:T(8,128)(2,1)S(1)}, u32[]{:S(2)}, u32[]{:S(2)}) collective-permute-start(bf16[32,2048]{1,0:T(8,128)(2,1)S(1)} %collective-permute-done.1.refs_1_), channel_id=1, source_target_pairs={{0,1},{1,0},{2,3},{3,2},{4,5},{5,4},{6,7},{7,6},{8,9},{9,8},{10,11... | collective-permute-start | bytes 393224 | tf_op jit(solution)/shard_map/ppermute | solution.py:115
  11.9 8.0 %all-to-all-start = ((bf16[4,32,128]{2,1,0:T(8,128)(2,1)}), bf16[4,32,128]{2,1,0:T(8,128)(2,1)S(1)}, u32[]{:S(2)}, u32[]{:S(2)}) async-start(bf16[4,32,128]{2,1,0:T(8,128)(2,1)} %sketch.1), calls=%async_computation | async-start | bytes 65536 | tf_op jit(solution)/shard_map/all_to_all | solution.py:153

commit v7 on v3

v7 whole, which is shorter than its diff:
```python
import functools

import jax
import jax.numpy as jnp
from jax import lax
from jax.experimental import pallas as pl
from jax.experimental.pallas import tpu as pltpu
from jax.sharding import PartitionSpec as P

F32 = jnp.float32
BF16 = jnp.bfloat16
LANES = 128
CHUNK = 128


def project_kernel(rank, acts_ref, grads_ref, proj_ref, out_ref, both, proj, sems):
    chunks = both.shape[0]
    weights = pltpu.make_async_copy(proj_ref, proj, sems.at[chunks, 0])
    weights.start()
    copies = []
    for i in range(chunks):
        part = pl.ds(i * CHUNK, CHUNK)
        two = (
            pltpu.make_async_copy(
                acts_ref.at[0, part, :], both.at[i, pl.ds(0, CHUNK), :], sems.at[i, 0]
            ),
            pltpu.make_async_copy(
                grads_ref.at[0, part, :], both.at[i, pl.ds(CHUNK, CHUNK), :], sems.at[i, 1]
            ),
        )
        for copy in two:
            copy.start()
        copies.append(two)

    weights.wait()
    column = lax.broadcasted_iota(jnp.int32, (CHUNK, 2 * rank), 1)
    for i, two in enumerate(copies):
        for copy in two:
            copy.wait()
        term = jnp.dot(both[i], proj[...], preferred_element_type=F32)
        out_ref[pl.ds(i * CHUNK, CHUNK), :] = jnp.where(column < rank, term[0:CHUNK], term[CHUNK:])


def count_kernel(picks_ref, out_ref):
    tokens, width = out_ref.shape
    samples = picks_ref.shape[1]
    token = lax.broadcasted_iota(jnp.int32, (tokens, samples), 0)
    hits = jnp.where(token == picks_ref[...], 1.0, 0.0).astype(BF16)
    out_ref[...] = jnp.dot(hits, jnp.ones((samples, width), BF16), preferred_element_type=F32)


def sketch_kernel(rank, count_ref, own_ref, other_ref, out_ref, held):
    total = own_ref[...] + other_ref[...]
    held[...] = lax.dot_general(
        total[:, rank : 2 * rank],
        total[:, 0:rank] * count_ref[...],
        (((0,), (0,)), ((), ())),
        precision=lax.Precision.HIGHEST,
        preferred_element_type=F32,
    )
    pairs = out_ref.shape[0]
    even = held[pl.ds(0, pairs, stride=2), :]
    odd = held[pl.ds(1, pairs, stride=2), :]
    out_ref[...] = jnp.concatenate([even, odd], axis=1).astype(BF16)


def score_kernel(clips, *refs):
    sketches, queries, outs, wide = refs[:clips], refs[clips : clips + 4], refs[clips + 4 : -1], refs[-1]
    pairs = sketches[0].shape[0]
    own_queries = queries[0].shape[0]
    blocks = outs[0].shape[1] // own_queries
    slots = wide.shape[0] // pairs
    wide[...] = jnp.zeros_like(wide)
    for r in range(clips):
        wide[pl.ds(r, pairs, stride=slots), :] = sketches[r][...].astype(F32)
    spot = lax.axis_index("dp")
    core = lax.axis_index("tensor")
    flats = []
    for half in (core, 1 - core):
        start = half * (slots * pairs // 2)
        flats.append(
            jnp.concatenate(
                [
                    wide[pl.ds(pl.multiple_of(start + j * slots, slots), slots), :]
                    for j in range(pairs // 2)
                ],
                axis=1,
            ).astype(BF16)
        )
    block = lax.broadcasted_iota(jnp.int32, (slots, blocks * own_queries), 1) // own_queries
    spread = jnp.zeros(block.shape, F32)
    for k, member in ((0, spot), (1, spot + 1 - 2 * lax.rem(spot, 2))):
        scores = sum(
            lax.dot_general(
                flat, queries[2 * k + i][...], (((1,), (1,)), ((), ())), preferred_element_type=F32
            )
            for i, flat in enumerate(flats)
        )
        here = block == lax.rem(member, blocks)
        spread = jnp.where(here, jnp.concatenate([scores] * blocks, axis=1), spread)
    spread = jnp.where(spot // blocks == core, spread, 0.0)
    for r in range(clips):
        outs[r][...] = spread[r : r + 1, :]


def on_device(activations, out_grads, projections, sample_index, queries):
    clips = lax.axis_size("dp")
    tokens, units = activations.shape[1:]
    rank = projections.shape[1] // 2
    own_queries, entries = queries.shape
    pairs = 2 * entries // LANES
    rounds = clips // 4
    slots = -(-2 * rounds // 8) * 8
    vmem = pl.BlockSpec(memory_space=pltpu.VMEM)
    hbm = pl.BlockSpec(memory_space=pl.ANY)
    swap = [(0, 1), (1, 0)]
    both = ("dp", "tensor")

    def place(a, l, b, t):
        return ((a * rounds + l) * 2 + b) * 2 + t

    spots = [(a, l, b) for a in range(2) for l in range(rounds) for b in range(2)]
    far = [
        [(place(a, l, b, 1 - a), place(1 - a, (l + r) % rounds, b, 1 - a)) for a, l, b in spots]
        for r in range(rounds)
    ]
    near = [
        [(place(a, l, b, a), place(a, (l + r) % rounds, b, a)) for a, l, b in spots]
        for r in range(1, rounds)
    ]
    moves = far + near
    returns = [[(dst, src) for src, dst in perm] for perm in moves]
    to_worker = [(place(a, l, b, 1 - a), place(a, l, b, a)) for a, l, b in spots]

    pair_queries = lax.ppermute(queries, "dp", [(d, d ^ 1) for d in range(clips)])
    other_queries = lax.ppermute(queries, both, to_worker)
    other_pair_queries = lax.ppermute(pair_queries, both, to_worker)
    partial = pl.pallas_call(
        functools.partial(project_kernel, rank),
        in_specs=[hbm] * 3,
        out_specs=vmem,
        out_shape=jax.ShapeDtypeStruct((tokens, 2 * rank), F32),
        scratch_shapes=[
            pltpu.VMEM((tokens // CHUNK, 2 * CHUNK, units), BF16),
            pltpu.VMEM((units, 2 * rank), BF16),
            pltpu.SemaphoreType.DMA((tokens // CHUNK + 1, 2)),
        ],
        compiler_params=pltpu.CompilerParams(vmem_limit_bytes=55000 << 10),
        cost_estimate=pl.CostEstimate(
            flops=8 * tokens * units * rank, bytes_accessed=4 * tokens * units, transcendentals=0
        ),
        name="project",
    )(activations, out_grads, projections)

    other = lax.ppermute(partial, "tensor", swap)
    count = pl.pallas_call(
        count_kernel,
        in_specs=[vmem],
        out_specs=vmem,
        out_shape=jax.ShapeDtypeStruct((tokens, rank), F32),
        compiler_params=pltpu.CompilerParams(vmem_limit_bytes=8 << 20),
        name="count",
    )(sample_index)
    sketch = pl.pallas_call(
        functools.partial(sketch_kernel, rank),
        in_specs=[vmem] * 3,
        out_specs=vmem,
        out_shape=jax.ShapeDtypeStruct((pairs, LANES), BF16),
        scratch_shapes=[pltpu.VMEM((rank, rank), F32)],
        compiler_params=pltpu.CompilerParams(vmem_limit_bytes=8 << 20),
        name="sketch",
    )(count, partial, other)

    sketches = [sketch] + [lax.ppermute(sketch, both, perm) for perm in moves]
    width = 2 * rounds * own_queries
    scored = pl.pallas_call(
        functools.partial(score_kernel, 2 * rounds),
        in_specs=[vmem] * (2 * rounds + 4),
        out_specs=[vmem] * (2 * rounds),
        out_shape=[jax.ShapeDtypeStruct((1, width), F32)] * (2 * rounds),
        scratch_shapes=[pltpu.VMEM((pairs * slots, LANES), F32)],
        compiler_params=pltpu.CompilerParams(vmem_limit_bytes=16 << 20),
        name="score",
    )(*sketches, queries, other_queries, pair_queries, other_pair_queries)

    parts = [lax.ppermute(s, both, perm) for s, perm in zip(scored[1:], returns)]
    return functools.reduce(jnp.add, parts, scored[0])


def solution(mesh):
    in_specs = (
        P(("groups", "dp"), None, "tensor"),
        P(("groups", "dp"), None, "tensor"),
        P("tensor", None),
        P(("groups", "dp"), None),
        P(("groups", "dp"), "tensor"),
    )
    out_specs = P(("groups", "dp"), "tensor")
    return jax.shard_map(
        on_device, mesh=mesh, in_specs=in_specs, out_specs=out_specs, check_vma=False
    )
```

time: 25.6 us -> 27.8 us (1.086)
  the two profiles are of different devices: /device:TPU:1 before, /device:TPU:0 now
where the time goes in v7:
time: 27.8 us; the launch traced here: 27.5 us
  starting transfers between devices  17.1 us (62%)
  waiting for transfers between devices  5.76 us (21%)
  Pallas kernels  4.01 us (14%)
  other arithmetic  0.52 us (2%)
    ppermute x3, starting transfers between devices, on_device(): sketches = [sketch] + [lax.ppermute(sketch, both, perm) for perm in moves]  6.06 us
    ppermute x3, starting transfers between devices, on_device(): lax.ppermute(s, both, perm)  5.42 us
    pallas_call x1, Pallas kernels, on_device(): pl.pallas_call(functools.partial(project_kernel, rank), in_specs=[hbm] *...  3.04 us
    ppermute x3, waiting for transfers between devices, on_device(): lax.ppermute(s, both, perm)  2.94 us
    ppermute x1, starting transfers between devices, on_device(): lax.ppermute(queries, 'dp', [(d, d ^ 1) for d in range(clips)])  2.94 us
    ppermute x3, waiting for transfers between devices, on_device(): sketches = [sketch] + [lax.ppermute(sketch, both, perm) for perm in moves]  2.81 us
    ppermute x1, starting transfers between devices, on_device(): other_queries = lax.ppermute(queries, both, to_worker)  1.29 us
    ppermute x1, starting transfers between devices, on_device(): other_pair_queries = lax.ppermute(pair_queries, both, to_worker)  1.29 us
  transfers between devices with their start and end apart: 10, of which 3 were waited for; matrix products, arithmetic and copies ran while one was open for 0% of the time, Pallas kernels for 13%

profile of v7, /device:TPU:0, one launch (start us, length us, event | category | flops | bytes accessed | tf_op | source)
XLA Modules:
  0.0 27.5 jit_solution(16838456490905326519)
XLA Ops:
  0.0 2.9 %collective-permute-start.5 = (bf16[32,2048]{1,0:T(8,128)(2,1)}, bf16[32,2048]{1,0:T(8,128)(2,1)S(1)}, u32[]{:S(2)}, u32[]{:S(2)}) collective-permute-start(bf16[32,2048]{1,0:T(8,128)(2,1)} %refs_4_.1), channel_id=1, source_target_pairs={{0,2},{2,0},{4,6},{6,4},{8,10},{10,8},{12,14},{14,12},{1,3},{3,1},... | collective-permute-start | bytes 393224 | tf_op jit(solution)/shard_map/ppermute | solution.py:135
  2.9 3.0 %project.1.own_ref = f32[384,128]{1,0:T(8,128)S(1)} custom-call(bf16[1,384,2560]{2,1,0:T(8,128)(2,1)} %acts_ref.1, bf16[1,384,2560]{2,1,0:T(8,128)(2,1)} %grads_ref.1, bf16[2560,128]{1,0:T(8,128)(2,1)} %proj_ref.1), custom_call_target="tpu_custom_call" | custom-call | flops 503316480 | bytes 3932160 | tf_op jit(solution)/shard_map/project/pallas_call | solution.py:138
  6.0 0.1 collective-permute-start
  6.1 1.3 %collective-permute-start.4 = (bf16[32,2048]{1,0:T(8,128)(2,1)S(1)}, bf16[32,2048]{1,0:T(8,128)(2,1)S(1)}, u32[]{:S(2)}, u32[]{:S(2)}) collective-permute-start(bf16[32,2048]{1,0:T(8,128)(2,1)S(1)} %copy-done), channel_id=1, source_target_pairs={{1,0},{3,2},{5,4},{7,6},{8,9},{10,11},{12,13},{14,15},{17,16},{19,... | collective-permute-start | bytes 393224 | tf_op jit(solution)/shard_map/ppermute | solution.py:136
  7.4 0.0 collective-permute-done.5.refs_6_
  7.4 1.3 %collective-permute-start.6 = (bf16[32,2048]{1,0:T(8,128)(2,1)S(1)}, bf16[32,2048]{1,0:T(8,128)(2,1)S(1)}, u32[]{:S(2)}, u32[]{:S(2)}) collective-permute-start(bf16[32,2048]{1,0:T(8,128)(2,1)S(1)} %collective-permute-done.5.refs_6_), channel_id=1, source_target_pairs={{1,0},{3,2},{5,4},{7,6},{8,9},{10,11},{12,13},{14,15},{17,16},{19,... | collective-permute-start | bytes 393224 | tf_op jit(solution)/shard_map/ppermute | solution.py:137
  8.7 0.2 count.1.count_ref
  8.9 0.0 collective-permute-done.other_ref
  8.9 0.5 %sketch.1.refs_0_ = bf16[32,128]{1,0:T(8,128)(2,1)S(1)} custom-call(f32[384,64]{1,0:T(8,128)S(1)} %count.1.count_ref, f32[384,128]{1,0:T(8,128)S(1)} %project.1.own_ref, f32[384,128]{1,0:T(8,128)S(1)} %collective-permute-done.other_ref), custom_call_target="tpu_custom_call" | custom-call | tf_op jit(solution)/shard_map/sketch/pallas_call | solution.py:164
  9.4 1.3 %collective-permute-start.1 = (bf16[32,128]{1,0:T(8,128)(2,1)S(1)}, bf16[32,128]{1,0:T(8,128)(2,1)S(1)}, u32[]{:S(2)}, u32[]{:S(2)}) collective-permute-start(bf16[32,128]{1,0:T(8,128)(2,1)S(1)} %sketch.1.refs_0_), channel_id=1, source_target_pairs={{1,9},{3,11},{5,13},{7,15},{8,0},{10,2},{12,4},{14,6},{17,25},{19,... | collective-permute-start | bytes 24584 | tf_op jit(solution)/shard_map/ppermute | solution.py:174
  10.7 1.3 %collective-permute-start.2 = (bf16[32,128]{1,0:T(8,128)(2,1)S(1)}, bf16[32,128]{1,0:T(8,128)(2,1)S(1)}, u32[]{:S(2)}, u32[]{:S(2)}) collective-permute-start(bf16[32,128]{1,0:T(8,128)(2,1)S(1)} %sketch.1.refs_0_), channel_id=1, source_target_pairs={{1,13},{3,15},{5,9},{7,11},{8,4},{10,6},{12,0},{14,2},{17,29},{19,... | collective-permute-start | bytes 24584 | tf_op jit(solution)/shard_map/ppermute | solution.py:174
  12.0 3.5 %collective-permute-start.3 = (bf16[32,128]{1,0:T(8,128)(2,1)S(1)}, bf16[32,128]{1,0:T(8,128)(2,1)S(1)}, u32[]{:S(2)}, u32[]{:S(2)}) collective-permute-start(bf16[32,128]{1,0:T(8,128)(2,1)S(1)} %sketch.1.refs_0_), channel_id=1, source_target_pairs={{0,4},{2,6},{4,0},{6,2},{9,13},{11,15},{13,9},{15,11},{16,20},{18,... | collective-permute-start | bytes 24584 | tf_op jit(solution)/shard_map/ppermute | solution.py:174
  15.5 0.0 collective-permute-done.4.refs_5_
  15.5 0.5 %collective-permute-done.1.refs_1_ = bf16[32,128]{1,0:T(8,128)(2,1)S(1)} collective-permute-done((bf16[32,128]{1,0:T(8,128)(2,1)S(1)}, bf16[32,128]{1,0:T(8,128)(2,1)S(1)}, u32[]{:S(2)}, u32[]{:S(2)}) %collective-permute-start.1) | collective-permute-done | bytes 8224 | tf_op jit(solution)/shard_map/ppermute | solution.py:174
  16.0 2.3 %collective-permute-done.2.refs_2_ = bf16[32,128]{1,0:T(8,128)(2,1)S(1)} collective-permute-done((bf16[32,128]{1,0:T(8,128)(2,1)S(1)}, bf16[32,128]{1,0:T(8,128)(2,1)S(1)}, u32[]{:S(2)}, u32[]{:S(2)}) %collective-permute-start.2) | collective-permute-done | bytes 8224 | tf_op jit(solution)/shard_map/ppermute | solution.py:174
  18.3 0.0 collective-permute-done.3.refs_3_
  18.3 0.0 collective-permute-done.6.refs_7_
  18.3 0.3 %score.1 = (f32[1,128]{1,0:T(1,128)S(1)}, f32[1,128]{1,0:T(1,128)S(1)}, f32[1,128]{1,0:T(1,128)S(1)}, f32[1,128]{1,0:T(1,128)S(1)}) custom-call(bf16[32,128]{1,0:T(8,128)(2,1)S(1)} %sketch.1.refs_0_, bf16[32,128]{1,0:T(8,128)(2,1)S(1)} %collective-permute-done.1.refs_1_, bf16[32,128]{1,0:T(8,128)(2,1)S(1)} %collective-permute-done.2.refs_2_, ...), custom_call_target="tpu_custom_call" | custom-call | tf_op jit(solution)/shard_map/score/pallas_call | solution.py:176
  18.6 1.3 %collective-permute-start.7 = (f32[1,128]{1,0:T(1,128)S(1)}, f32[1,128]{1,0:T(1,128)S(1)}, u32[]{:S(2)}, u32[]{:S(2)}) collective-permute-start(f32[1,128]{1,0:T(1,128)S(1)} %get-tuple-element.10), channel_id=1, source_target_pairs={{9,1},{11,3},{13,5},{15,7},{0,8},{2,10},{4,12},{6,14},{25,17},{27,... | collective-permute-start | bytes 1544 | tf_op jit(solution)/shard_map/ppermute | solution.py:186
  19.9 1.6 %collective-permute-start.8 = (f32[1,128]{1,0:T(1,128)S(1)}, f32[1,128]{1,0:T(1,128)S(1)}, u32[]{:S(2)}, u32[]{:S(2)}) collective-permute-start(f32[1,128]{1,0:T(1,128)S(1)} %get-tuple-element.11), channel_id=1, source_target_pairs={{13,1},{15,3},{9,5},{11,7},{4,8},{6,10},{0,12},{2,14},{29,17},{31,... | collective-permute-start | bytes 1544 | tf_op jit(solution)/shard_map/ppermute | solution.py:186
  21.6 2.5 %collective-permute-start.9 = (f32[1,128]{1,0:T(1,128)S(1)}, f32[1,128]{1,0:T(1,128)S(1)}, u32[]{:S(2)}, u32[]{:S(2)}) collective-permute-start(f32[1,128]{1,0:T(1,128)S(1)} %get-tuple-element.12), channel_id=1, source_target_pairs={{4,0},{6,2},{0,4},{2,6},{13,9},{15,11},{9,13},{11,15},{20,16},{22,... | collective-permute-start | bytes 1544 | tf_op jit(solution)/shard_map/ppermute | solution.py:186
  24.1 0.0 collective-permute-done.8
  24.1 2.9 %collective-permute-done.9 = f32[1,128]{1,0:T(1,128)S(1)} collective-permute-done((f32[1,128]{1,0:T(1,128)S(1)}, f32[1,128]{1,0:T(1,128)S(1)}, u32[]{:S(2)}, u32[]{:S(2)}) %collective-permute-start.9) | collective-permute-done | bytes 544 | tf_op jit(solution)/shard_map/ppermute | solution.py:186
  27.0 0.5 %add_add_fusion = f32[1,128]{1,0:T(1,128)} fusion(f32[1,128]{1,0:T(1,128)S(1)} %collective-permute-done.9, f32[1,128]{1,0:T(1,128)S(1)} %collective-permute-done.8, f32[1,128]{1,0:T(1,128)S(1)} %get-tuple-element.9, f32[1,128]{1,0:T(1,128)S(1)} %collective-permute-done.7), kind=kLoop, calls=%fused_computation | loop fusion | flops 384 | bytes 2560 | tf_op jit(solution)/shard_map/add | solution.py:187
  (5 shorter events, 0.0 us)
Async XLA Ops:
  0.0 6.1 %copy-start = (bf16[32,2048]{1,0:T(8,128)(2,1)S(1)}, bf16[32,2048]{1,0:T(8,128)(2,1)}, u32[]{:S(2)}) copy-start(bf16[32,2048]{1,0:T(8,128)(2,1)} %refs_4_.1) | copy-start | bytes 393220
  0.0 8.7 %copy-start.1 = (s32[1,256]{1,0:T(1,128)S(1)}, s32[1,256]{1,0:T(1,128)}, u32[]{:S(2)}) copy-start(s32[1,256]{1,0:T(1,128)} %picks_ref.1) | copy-start | bytes 3076
  0.0 7.4 %collective-permute-start.5 = (bf16[32,2048]{1,0:T(8,128)(2,1)}, bf16[32,2048]{1,0:T(8,128)(2,1)S(1)}, u32[]{:S(2)}, u32[]{:S(2)}) collective-permute-start(bf16[32,2048]{1,0:T(8,128)(2,1)} %refs_4_.1), channel_id=1, source_target_pairs={{0,2},{2,0},{4,6},{6,4},{8,10},{10,8},{12,14},{14,12},{1,3},{3,1},... | collective-permute-start | bytes 393224 | tf_op jit(solution)/shard_map/ppermute | solution.py:135
  6.0 2.9 %collective-permute-start = (f32[384,128]{1,0:T(8,128)S(1)}, f32[384,128]{1,0:T(8,128)S(1)}, u32[]{:S(2)}, u32[]{:S(2)}) collective-permute-start(f32[384,128]{1,0:T(8,128)S(1)} %project.1.own_ref), channel_id=1, source_target_pairs={{0,1},{1,0},{2,3},{3,2},{4,5},{5,4},{6,7},{7,6},{8,9},{9,8},{10,11... | collective-permute-start | bytes 589832 | tf_op jit(solution)/shard_map/ppermute | solution.py:155
  6.1 9.4 %collective-permute-start.4 = (bf16[32,2048]{1,0:T(8,128)(2,1)S(1)}, bf16[32,2048]{1,0:T(8,128)(2,1)S(1)}, u32[]{:S(2)}, u32[]{:S(2)}) collective-permute-start(bf16[32,2048]{1,0:T(8,128)(2,1)S(1)} %copy-done), channel_id=1, source_target_pairs={{1,0},{3,2},{5,4},{7,6},{8,9},{10,11},{12,13},{14,15},{17,16},{19,... | collective-permute-start | bytes 393224 | tf_op jit(solution)/shard_map/ppermute | solution.py:136
  7.4 10.9 %collective-permute-start.6 = (bf16[32,2048]{1,0:T(8,128)(2,1)S(1)}, bf16[32,2048]{1,0:T(8,128)(2,1)S(1)}, u32[]{:S(2)}, u32[]{:S(2)}) collective-permute-start(bf16[32,2048]{1,0:T(8,128)(2,1)S(1)} %collective-permute-done.5.refs_6_), channel_id=1, source_target_pairs={{1,0},{3,2},{5,4},{7,6},{8,9},{10,11},{12,13},{14,15},{17,16},{19,... | collective-permute-start | bytes 393224 | tf_op jit(solution)/shard_map/ppermute | solution.py:137
  9.4 6.6 %collective-permute-start.1 = (bf16[32,128]{1,0:T(8,128)(2,1)S(1)}, bf16[32,128]{1,0:T(8,128)(2,1)S(1)}, u32[]{:S(2)}, u32[]{:S(2)}) collective-permute-start(bf16[32,128]{1,0:T(8,128)(2,1)S(1)} %sketch.1.refs_0_), channel_id=1, source_target_pairs={{1,9},{3,11},{5,13},{7,15},{8,0},{10,2},{12,4},{14,6},{17,25},{19,... | collective-permute-start | bytes 24584 | tf_op jit(solution)/shard_map/ppermute | solution.py:174
  10.7 7.6 %collective-permute-start.2 = (bf16[32,128]{1,0:T(8,128)(2,1)S(1)}, bf16[32,128]{1,0:T(8,128)(2,1)S(1)}, u32[]{:S(2)}, u32[]{:S(2)}) collective-permute-start(bf16[32,128]{1,0:T(8,128)(2,1)S(1)} %sketch.1.refs_0_), channel_id=1, source_target_pairs={{1,13},{3,15},{5,9},{7,11},{8,4},{10,6},{12,0},{14,2},{17,29},{19,... | collective-permute-start | bytes 24584 | tf_op jit(solution)/shard_map/ppermute | solution.py:174
  12.0 6.3 %collective-permute-start.3 = (bf16[32,128]{1,0:T(8,128)(2,1)S(1)}, bf16[32,128]{1,0:T(8,128)(2,1)S(1)}, u32[]{:S(2)}, u32[]{:S(2)}) collective-permute-start(bf16[32,128]{1,0:T(8,128)(2,1)S(1)} %sketch.1.refs_0_), channel_id=1, source_target_pairs={{0,4},{2,6},{4,0},{6,2},{9,13},{11,15},{13,9},{15,11},{16,20},{18,... | collective-permute-start | bytes 24584 | tf_op jit(solution)/shard_map/ppermute | solution.py:174
  18.6 5.4 %collective-permute-start.7 = (f32[1,128]{1,0:T(1,128)S(1)}, f32[1,128]{1,0:T(1,128)S(1)}, u32[]{:S(2)}, u32[]{:S(2)}) collective-permute-start(f32[1,128]{1,0:T(1,128)S(1)} %get-tuple-element.10), channel_id=1, source_target_pairs={{9,1},{11,3},{13,5},{15,7},{0,8},{2,10},{4,12},{6,14},{25,17},{27,... | collective-permute-start | bytes 1544 | tf_op jit(solution)/shard_map/ppermute | solution.py:186
  19.9 4.1 %collective-permute-start.8 = (f32[1,128]{1,0:T(1,128)S(1)}, f32[1,128]{1,0:T(1,128)S(1)}, u32[]{:S(2)}, u32[]{:S(2)}) collective-permute-start(f32[1,128]{1,0:T(1,128)S(1)} %get-tuple-element.11), channel_id=1, source_target_pairs={{13,1},{15,3},{9,5},{11,7},{4,8},{6,10},{0,12},{2,14},{29,17},{31,... | collective-permute-start | bytes 1544 | tf_op jit(solution)/shard_map/ppermute | solution.py:186
  21.6 5.4 %collective-permute-start.9 = (f32[1,128]{1,0:T(1,128)S(1)}, f32[1,128]{1,0:T(1,128)S(1)}, u32[]{:S(2)}, u32[]{:S(2)}) collective-permute-start(f32[1,128]{1,0:T(1,128)S(1)} %get-tuple-element.12), channel_id=1, source_target_pairs={{4,0},{6,2},{0,4},{2,6},{13,9},{15,11},{9,13},{11,15},{20,16},{22,... | collective-permute-start | bytes 1544 | tf_op jit(solution)/shard_map/ppermute | solution.py:186

commit v8 on v7

--- a/solution.py
+++ b/solution.py
@@ -10,7 +10,7 @@
 F32 = jnp.float32
 BF16 = jnp.bfloat16
 LANES = 128
-CHUNK = 128
+CHUNK = 64
 
 
 def project_kernel(rank, acts_ref, grads_ref, proj_ref, out_ref, both, proj, sems):
@@ -64,15 +64,14 @@
     out_ref[...] = jnp.concatenate([even, odd], axis=1).astype(BF16)
 
 
-def score_kernel(clips, *refs):
-    sketches, queries, outs, wide = refs[:clips], refs[clips : clips + 4], refs[clips + 4 : -1], refs[-1]
-    pairs = sketches[0].shape[0]
+def score_kernel(mates, own_ref, far_ref, *refs):
+    queries, (out_ref, back_ref, wide) = refs[: 2 * mates], refs[2 * mates :]
+    pairs = own_ref.shape[0]
     own_queries = queries[0].shape[0]
-    blocks = outs[0].shape[1] // own_queries
     slots = wide.shape[0] // pairs
     wide[...] = jnp.zeros_like(wide)
-    for r in range(clips):
-        wide[pl.ds(r, pairs, stride=slots), :] = sketches[r][...].astype(F32)
+    wide[pl.ds(0, pairs, stride=slots), :] = own_ref[...].astype(F32)
+    wide[pl.ds(1, pairs, stride=slots), :] = far_ref[...].astype(F32)
     spot = lax.axis_index("dp")
     core = lax.axis_index("tensor")
     flats = []
@@ -87,20 +86,20 @@
                 axis=1,
             ).astype(BF16)
         )
-    block = lax.broadcasted_iota(jnp.int32, (slots, blocks * own_queries), 1) // own_queries
+    block = lax.broadcasted_iota(jnp.int32, (slots, mates * own_queries), 1) // own_queries
     spread = jnp.zeros(block.shape, F32)
-    for k, member in ((0, spot), (1, spot + 1 - 2 * lax.rem(spot, 2))):
+    for r in range(mates):
         scores = sum(
             lax.dot_general(
-                flat, queries[2 * k + i][...], (((1,), (1,)), ((), ())), preferred_element_type=F32
+                flat, queries[2 * r + i][...], (((1,), (1,)), ((), ())), preferred_element_type=F32
             )
             for i, flat in enumerate(flats)
         )
-        here = block == lax.rem(member, blocks)
-        spread = jnp.where(here, jnp.concatenate([scores] * blocks, axis=1), spread)
-    spread = jnp.where(spot // blocks == core, spread, 0.0)
-    for r in range(clips):
-        outs[r][...] = spread[r : r + 1, :]
+        here = block == lax.rem(spot, mates) ^ r
+        spread = jnp.where(here, jnp.concatenate([scores] * mates, axis=1), spread)
+    spread = jnp.where(spot // mates == core, spread, 0.0)
+    out_ref[...] = spread[0:1, :]
+    back_ref[...] = spread[1:2, :]
 
 
 def on_device(activations, out_grads, projections, sample_index, queries):
@@ -109,32 +108,25 @@
     rank = projections.shape[1] // 2
     own_queries, entries = queries.shape
     pairs = 2 * entries // LANES
-    rounds = clips // 4
-    slots = -(-2 * rounds // 8) * 8
+    mates = clips // 2
+    slots = 8
     vmem = pl.BlockSpec(memory_space=pltpu.VMEM)
     hbm = pl.BlockSpec(memory_space=pl.ANY)
     swap = [(0, 1), (1, 0)]
     both = ("dp", "tensor")
 
-    def place(a, l, b, t):
-        return ((a * rounds + l) * 2 + b) * 2 + t
+    def place(a, m, t):
+        return (a * mates + m) * 2 + t
 
-    spots = [(a, l, b) for a in range(2) for l in range(rounds) for b in range(2)]
-    far = [
-        [(place(a, l, b, 1 - a), place(1 - a, (l + r) % rounds, b, 1 - a)) for a, l, b in spots]
-        for r in range(rounds)
-    ]
-    near = [
-        [(place(a, l, b, a), place(a, (l + r) % rounds, b, a)) for a, l, b in spots]
-        for r in range(1, rounds)
-    ]
-    moves = far + near
-    returns = [[(dst, src) for src, dst in perm] for perm in moves]
-    to_worker = [(place(a, l, b, 1 - a), place(a, l, b, a)) for a, l, b in spots]
+    spots = [(a, m) for a in range(2) for m in range(mates)]
+    there = [(place(a, m, 1 - a), place(1 - a, m, 1 - a)) for a, m in spots]
+    there += [(place(a, m, a), place(a, m, 1 - a)) for a, m in spots]
+    back = [(dst, src) for src, dst in there]
 
-    pair_queries = lax.ppermute(queries, "dp", [(d, d ^ 1) for d in range(clips)])
-    other_queries = lax.ppermute(queries, both, to_worker)
-    other_pair_queries = lax.ppermute(pair_queries, both, to_worker)
+    taken = []
+    for r in range(mates):
+        half = lax.ppermute(queries, "dp", [(d, d ^ r) for d in range(clips)]) if r else queries
+        taken += [half, lax.ppermute(half, "tensor", swap)]
     partial = pl.pallas_call(
         functools.partial(project_kernel, rank),
         in_specs=[hbm] * 3,
@@ -171,20 +163,19 @@
         name="sketch",
     )(count, partial, other)
 
-    sketches = [sketch] + [lax.ppermute(sketch, both, perm) for perm in moves]
-    width = 2 * rounds * own_queries
-    scored = pl.pallas_call(
-        functools.partial(score_kernel, 2 * rounds),
-        in_specs=[vmem] * (2 * rounds + 4),
-        out_specs=[vmem] * (2 * rounds),
-        out_shape=[jax.ShapeDtypeStruct((1, width), F32)] * (2 * rounds),
+    far_sketch = lax.ppermute(sketch, both, there)
+    width = mates * own_queries
+    near_scores, far_scores = pl.pallas_call(
+        functools.partial(score_kernel, mates),
+        in_specs=[vmem] * (2 * mates + 2),
+        out_specs=[vmem] * 2,
+        out_shape=[jax.ShapeDtypeStruct((1, width), F32)] * 2,
         scratch_shapes=[pltpu.VMEM((pairs * slots, LANES), F32)],
-        compiler_params=pltpu.CompilerParams(vmem_limit_bytes=16 << 20),
+        compiler_params=pltpu.CompilerParams(vmem_limit_bytes=(16 + mates // 2) << 20),
         name="score",
-    )(*sketches, queries, other_queries, pair_queries, other_pair_queries)
+    )(sketch, far_sketch, *taken)
 
-    parts = [lax.ppermute(s, both, perm) for s, perm in zip(scored[1:], returns)]
-    return functools.reduce(jnp.add, parts, scored[0])
+    return near_scores + lax.ppermute(far_scores, both, back)
 
 
 def solution(mesh):

time: 27.8 us -> 19.4 us (0.70)
  the two profiles are of different devices: /device:TPU:0 before, /device:TPU:1 now
where the time goes in v8:
time: 19.4 us; the launch traced here: 19.3 us
  starting transfers between devices  11.2 us (58%)
  Pallas kernels  4.45 us (23%)
  waiting for transfers between devices  3.04 us (16%)
  other arithmetic  0.51 us (3%)
    ppermute x3, starting transfers between devices, on_device(): lax.ppermute(queries, 'dp', [(d, d ^ r) for d in range(clips)])  3.34 us
    pallas_call x1, Pallas kernels, on_device(): pl.pallas_call(functools.partial(project_kernel, rank), in_specs=[hbm] *...  3.34 us
    ppermute x4, starting transfers between devices, on_device(): taken += [half, lax.ppermute(half, 'tensor', swap)]  2.81 us
    ppermute x1, starting transfers between devices, on_device(): far_sketch = lax.ppermute(sketch, both, there)  2.46 us
    ppermute x1, waiting for transfers between devices, on_device(): return near_scores + lax.ppermute(far_scores, both, back)  2.22 us
    ppermute x1, starting transfers between devices, on_device(): return near_scores + lax.ppermute(far_scores, both, back)  1.33 us
    ppermute x1, starting transfers between devices, on_device(): other = lax.ppermute(partial, 'tensor', swap)  1.3 us
    ppermute x1, waiting for transfers between devices, on_device(): far_sketch = lax.ppermute(sketch, both, there)  0.79 us
  transfers between devices with their start and end apart: 10, of which 2 were waited for; matrix products, arithmetic and copies ran while one was open for 0% of the time, Pallas kernels for 21%

profile of v8, /device:TPU:1, one launch (start us, length us, event | category | flops | bytes accessed | tf_op | source)
XLA Modules:
  0.0 19.3 jit_solution(399770424252796094)
XLA Ops:
  0.0 2.0 %collective-permute-start.3 = (bf16[32,2048]{1,0:T(8,128)(2,1)}, bf16[32,2048]{1,0:T(8,128)(2,1)S(1)}, u32[]{:S(2)}, u32[]{:S(2)}) collective-permute-start(bf16[32,2048]{1,0:T(8,128)(2,1)} %refs_0_.1), channel_id=1, source_target_pairs={{0,2},{2,0},{4,6},{6,4},{8,10},{10,8},{12,14},{14,12},{1,3},{3,1},... | collective-permute-start | bytes 393224 | tf_op jit(solution)/shard_map/ppermute | solution.py:128
  2.0 1.3 %collective-permute-start.5 = (bf16[32,2048]{1,0:T(8,128)(2,1)}, bf16[32,2048]{1,0:T(8,128)(2,1)S(1)}, u32[]{:S(2)}, u32[]{:S(2)}) collective-permute-start(bf16[32,2048]{1,0:T(8,128)(2,1)} %refs_0_.1), channel_id=1, source_target_pairs={{0,4},{2,6},{4,0},{6,2},{8,12},{10,14},{12,8},{14,10},{1,5},{3,7},... | collective-permute-start | bytes 393224 | tf_op jit(solution)/shard_map/ppermute | solution.py:128
  3.3 0.0 collective-permute-start.7
  3.3 3.3 %project.1.own_ref = f32[384,128]{1,0:T(8,128)S(1)} custom-call(bf16[1,384,2560]{2,1,0:T(8,128)(2,1)} %acts_ref.1, bf16[1,384,2560]{2,1,0:T(8,128)(2,1)} %grads_ref.1, bf16[2560,128]{1,0:T(8,128)(2,1)} %proj_ref.1), custom_call_target="tpu_custom_call" | custom-call | flops 503316480 | bytes 3932160 | tf_op jit(solution)/shard_map/project/pallas_call | solution.py:130
  6.7 1.3 %collective-permute-start = (f32[384,128]{1,0:T(8,128)S(1)}, f32[384,128]{1,0:T(8,128)S(1)}, u32[]{:S(2)}, u32[]{:S(2)}) collective-permute-start(f32[384,128]{1,0:T(8,128)S(1)} %project.1.own_ref), channel_id=1, source_target_pairs={{0,1},{1,0},{2,3},{3,2},{4,5},{5,4},{6,7},{7,6},{8,9},{9,8},{10,11... | collective-permute-start | bytes 589832 | tf_op jit(solution)/shard_map/ppermute | solution.py:147
  8.0 0.1 collective-permute-start.2
  8.1 0.0 collective-permute-done.3.refs_2_
  8.1 0.4 %collective-permute-start.4 = (bf16[32,2048]{1,0:T(8,128)(2,1)S(1)}, bf16[32,2048]{1,0:T(8,128)(2,1)S(1)}, u32[]{:S(2)}, u32[]{:S(2)}) collective-permute-start(bf16[32,2048]{1,0:T(8,128)(2,1)S(1)} %collective-permute-done.3.refs_2_), channel_id=1, source_target_pairs={{0,1},{1,0},{2,3},{3,2},{4,5},{5,4},{6,7},{7,6},{8,9},{9,8},{10,11... | collective-permute-start | bytes 393224 | tf_op jit(solution)/shard_map/ppermute | solution.py:129
  8.5 0.0 collective-permute-done.5.refs_4_
  8.5 1.1 %collective-permute-start.6 = (bf16[32,2048]{1,0:T(8,128)(2,1)S(1)}, bf16[32,2048]{1,0:T(8,128)(2,1)S(1)}, u32[]{:S(2)}, u32[]{:S(2)}) collective-permute-start(bf16[32,2048]{1,0:T(8,128)(2,1)S(1)} %collective-permute-done.5.refs_4_), channel_id=1, source_target_pairs={{0,1},{1,0},{2,3},{3,2},{4,5},{5,4},{6,7},{7,6},{8,9},{9,8},{10,11... | collective-permute-start | bytes 393224 | tf_op jit(solution)/shard_map/ppermute | solution.py:129
  9.6 0.0 collective-permute-done.7.refs_6_
  9.6 1.2 %collective-permute-start.8 = (bf16[32,2048]{1,0:T(8,128)(2,1)S(1)}, bf16[32,2048]{1,0:T(8,128)(2,1)S(1)}, u32[]{:S(2)}, u32[]{:S(2)}) collective-permute-start(bf16[32,2048]{1,0:T(8,128)(2,1)S(1)} %collective-permute-done.7.refs_6_), channel_id=1, source_target_pairs={{0,1},{1,0},{2,3},{3,2},{4,5},{5,4},{6,7},{7,6},{8,9},{9,8},{10,11... | collective-permute-start | bytes 393224 | tf_op jit(solution)/shard_map/ppermute | solution.py:129
  10.8 0.2 count.1.count_ref
  11.0 0.0 collective-permute-done.other_ref
  11.0 0.5 %sketch.1.own_ref = bf16[32,128]{1,0:T(8,128)(2,1)S(1)} custom-call(f32[384,64]{1,0:T(8,128)S(1)} %count.1.count_ref, f32[384,128]{1,0:T(8,128)S(1)} %project.1.own_ref, f32[384,128]{1,0:T(8,128)S(1)} %collective-permute-done.other_ref), custom_call_target="tpu_custom_call" | custom-call | tf_op jit(solution)/shard_map/sketch/pallas_call | solution.py:156
  11.5 2.5 %collective-permute-start.1 = (bf16[32,128]{1,0:T(8,128)(2,1)S(1)}, bf16[32,128]{1,0:T(8,128)(2,1)S(1)}, u32[]{:S(2)}, u32[]{:S(2)}) collective-permute-start(bf16[32,128]{1,0:T(8,128)(2,1)S(1)} %sketch.1.own_ref), channel_id=1, source_target_pairs={{1,9},{3,11},{5,13},{7,15},{8,0},{10,2},{12,4},{14,6},{0,1},{2,3},... | collective-permute-start | bytes 24584 | tf_op jit(solution)/shard_map/ppermute | solution.py:166
  13.9 0.0 collective-permute-done.2.refs_1_
  13.9 0.8 %collective-permute-done.1.far_ref = bf16[32,128]{1,0:T(8,128)(2,1)S(1)} collective-permute-done((bf16[32,128]{1,0:T(8,128)(2,1)S(1)}, bf16[32,128]{1,0:T(8,128)(2,1)S(1)}, u32[]{:S(2)}, u32[]{:S(2)}) %collective-permute-start.1) | collective-permute-done | bytes 8224 | tf_op jit(solution)/shard_map/ppermute | solution.py:166
  14.7 0.0 collective-permute-done.6.refs_5_
  14.7 0.0 collective-permute-done.8.refs_7_
  14.8 0.5 %score.1 = (f32[1,128]{1,0:T(1,128)S(1)}, f32[1,128]{1,0:T(1,128)S(1)}) custom-call(bf16[32,128]{1,0:T(8,128)(2,1)S(1)} %sketch.1.own_ref, bf16[32,128]{1,0:T(8,128)(2,1)S(1)} %collective-permute-done.1.far_ref, bf16[32,2048]{1,0:T(8,128)(2,1)S(1)} %copy-done, bf16[32,2048]{1,0:T(8,128)(2,1)S(1)} %collective-permute-done.2.refs_1_, ...), custom_call_target="tpu_custom_call" | custom-call | tf_op jit(solution)/shard_map/score/pallas_call | solution.py:168
  15.2 1.3 %collective-permute-start.9 = (f32[1,128]{1,0:T(1,128)S(1)}, f32[1,128]{1,0:T(1,128)S(1)}, u32[]{:S(2)}, u32[]{:S(2)}) collective-permute-start(f32[1,128]{1,0:T(1,128)S(1)} %get-tuple-element.8), channel_id=1, source_target_pairs={{9,1},{11,3},{13,5},{15,7},{0,8},{2,10},{4,12},{6,14},{1,0},{3,2},... | collective-permute-start | bytes 1544 | tf_op jit(solution)/shard_map/ppermute | solution.py:178
  16.6 2.2 %collective-permute-done.9 = f32[1,128]{1,0:T(1,128)S(1)} collective-permute-done((f32[1,128]{1,0:T(1,128)S(1)}, f32[1,128]{1,0:T(1,128)S(1)}, u32[]{:S(2)}, u32[]{:S(2)}) %collective-permute-start.9) | collective-permute-done | bytes 544 | tf_op jit(solution)/shard_map/ppermute | solution.py:178
  18.8 0.5 %add.3 = f32[1,128]{1,0:T(1,128)} add(f32[1,128]{1,0:T(1,128)S(1)} %get-tuple-element.7, f32[1,128]{1,0:T(1,128)S(1)} %collective-permute-done.9) | non-fusion elementwise | flops 128 | bytes 1536 | tf_op jit(solution)/shard_map/add | solution.py:178
  (5 shorter events, 0.0 us)
Async XLA Ops:
  0.0 8.0 %copy-start = (bf16[32,2048]{1,0:T(8,128)(2,1)S(1)}, bf16[32,2048]{1,0:T(8,128)(2,1)}, u32[]{:S(2)}) copy-start(bf16[32,2048]{1,0:T(8,128)(2,1)} %refs_0_.1) | copy-start | bytes 393220
  0.0 10.8 %copy-start.1 = (s32[1,256]{1,0:T(1,128)S(1)}, s32[1,256]{1,0:T(1,128)}, u32[]{:S(2)}) copy-start(s32[1,256]{1,0:T(1,128)} %picks_ref.1) | copy-start | bytes 3076
  0.0 8.1 %collective-permute-start.3 = (bf16[32,2048]{1,0:T(8,128)(2,1)}, bf16[32,2048]{1,0:T(8,128)(2,1)S(1)}, u32[]{:S(2)}, u32[]{:S(2)}) collective-permute-start(bf16[32,2048]{1,0:T(8,128)(2,1)} %refs_0_.1), channel_id=1, source_target_pairs={{0,2},{2,0},{4,6},{6,4},{8,10},{10,8},{12,14},{14,12},{1,3},{3,1},... | collective-permute-start | bytes 393224 | tf_op jit(solution)/shard_map/ppermute | solution.py:128
  2.0 6.5 %collective-permute-start.5 = (bf16[32,2048]{1,0:T(8,128)(2,1)}, bf16[32,2048]{1,0:T(8,128)(2,1)S(1)}, u32[]{:S(2)}, u32[]{:S(2)}) collective-permute-start(bf16[32,2048]{1,0:T(8,128)(2,1)} %refs_0_.1), channel_id=1, source_target_pairs={{0,4},{2,6},{4,0},{6,2},{8,12},{10,14},{12,8},{14,10},{1,5},{3,7},... | collective-permute-start | bytes 393224 | tf_op jit(solution)/shard_map/ppermute | solution.py:128
  3.3 6.2 %collective-permute-start.7 = (bf16[32,2048]{1,0:T(8,128)(2,1)}, bf16[32,2048]{1,0:T(8,128)(2,1)S(1)}, u32[]{:S(2)}, u32[]{:S(2)}) collective-permute-start(bf16[32,2048]{1,0:T(8,128)(2,1)} %refs_0_.1), channel_id=1, source_target_pairs={{0,6},{2,4},{4,2},{6,0},{8,14},{10,12},{12,10},{14,8},{1,7},{3,5},... | collective-permute-start | bytes 393224 | tf_op jit(solution)/shard_map/ppermute | solution.py:128
  6.7 4.3 %collective-permute-start = (f32[384,128]{1,0:T(8,128)S(1)}, f32[384,128]{1,0:T(8,128)S(1)}, u32[]{:S(2)}, u32[]{:S(2)}) collective-permute-start(f32[384,128]{1,0:T(8,128)S(1)} %project.1.own_ref), channel_id=1, source_target_pairs={{0,1},{1,0},{2,3},{3,2},{4,5},{5,4},{6,7},{7,6},{8,9},{9,8},{10,11... | collective-permute-start | bytes 589832 | tf_op jit(solution)/shard_map/ppermute | solution.py:147
  8.0 6.0 %collective-permute-start.2 = (bf16[32,2048]{1,0:T(8,128)(2,1)S(1)}, bf16[32,2048]{1,0:T(8,128)(2,1)S(1)}, u32[]{:S(2)}, u32[]{:S(2)}) collective-permute-start(bf16[32,2048]{1,0:T(8,128)(2,1)S(1)} %copy-done), channel_id=1, source_target_pairs={{0,1},{1,0},{2,3},{3,2},{4,5},{5,4},{6,7},{7,6},{8,9},{9,8},{10,11... | collective-permute-start | bytes 393224 | tf_op jit(solution)/shard_map/ppermute | solution.py:129
  8.1 6.7 %collective-permute-start.4 = (bf16[32,2048]{1,0:T(8,128)(2,1)S(1)}, bf16[32,2048]{1,0:T(8,128)(2,1)S(1)}, u32[]{:S(2)}, u32[]{:S(2)}) collective-permute-start(bf16[32,2048]{1,0:T(8,128)(2,1)S(1)} %collective-permute-done.3.refs_2_), channel_id=1, source_target_pairs={{0,1},{1,0},{2,3},{3,2},{4,5},{5,4},{6,7},{7,6},{8,9},{9,8},{10,11... | collective-permute-start | bytes 393224 | tf_op jit(solution)/shard_map/ppermute | solution.py:129
  8.5 6.2 %collective-permute-start.6 = (bf16[32,2048]{1,0:T(8,128)(2,1)S(1)}, bf16[32,2048]{1,0:T(8,128)(2,1)S(1)}, u32[]{:S(2)}, u32[]{:S(2)}) collective-permute-start(bf16[32,2048]{1,0:T(8,128)(2,1)S(1)} %collective-permute-done.5.refs_4_), channel_id=1, source_target_pairs={{0,1},{1,0},{2,3},{3,2},{4,5},{5,4},{6,7},{7,6},{8,9},{9,8},{10,11... | collective-permute-start | bytes 393224 | tf_op jit(solution)/shard_map/ppermute | solution.py:129
  9.6 5.2 %collective-permute-start.8 = (bf16[32,2048]{1,0:T(8,128)(2,1)S(1)}, bf16[32,2048]{1,0:T(8,128)(2,1)S(1)}, u32[]{:S(2)}, u32[]{:S(2)}) collective-permute-start(bf16[32,2048]{1,0:T(8,128)(2,1)S(1)} %collective-permute-done.7.refs_6_), channel_id=1, source_target_pairs={{0,1},{1,0},{2,3},{3,2},{4,5},{5,4},{6,7},{7,6},{8,9},{9,8},{10,11... | collective-permute-start | bytes 393224 | tf_op jit(solution)/shard_map/ppermute | solution.py:129
  11.5 3.3 %collective-permute-start.1 = (bf16[32,128]{1,0:T(8,128)(2,1)S(1)}, bf16[32,128]{1,0:T(8,128)(2,1)S(1)}, u32[]{:S(2)}, u32[]{:S(2)}) collective-permute-start(bf16[32,128]{1,0:T(8,128)(2,1)S(1)} %sketch.1.own_ref), channel_id=1, source_target_pairs={{1,9},{3,11},{5,13},{7,15},{8,0},{10,2},{12,4},{14,6},{0,1},{2,3},... | collective-permute-start | bytes 24584 | tf_op jit(solution)/shard_map/ppermute | solution.py:166
  15.2 3.6 %collective-permute-start.9 = (f32[1,128]{1,0:T(1,128)S(1)}, f32[1,128]{1,0:T(1,128)S(1)}, u32[]{:S(2)}, u32[]{:S(2)}) collective-permute-start(f32[1,128]{1,0:T(1,128)S(1)} %get-tuple-element.8), channel_id=1, source_target_pairs={{9,1},{11,3},{13,5},{15,7},{0,8},{2,10},{4,12},{6,14},{1,0},{3,2},... | collective-permute-start | bytes 1544 | tf_op jit(solution)/shard_map/ppermute | solution.py:178

commit v9 on v8

--- a/solution.py
+++ b/solution.py
@@ -10,10 +10,12 @@
 F32 = jnp.float32
 BF16 = jnp.bfloat16
 LANES = 128
-CHUNK = 64
-
-
-def project_kernel(rank, acts_ref, grads_ref, proj_ref, out_ref, both, proj, sems):
+CHUNK = 128
+PIECES = 2
+
+
+def project_kernel(rank, acts_ref, grads_ref, proj_ref, *refs):
+    outs, (both, proj, sems) = refs[:-3], refs[-3:]
     chunks = both.shape[0]
     weights = pltpu.make_async_copy(proj_ref, proj, sems.at[chunks, 0])
     weights.start()
@@ -33,12 +35,19 @@
         copies.append(two)
 
     weights.wait()
+    rows = outs[0].shape[0]
     column = lax.broadcasted_iota(jnp.int32, (CHUNK, 2 * rank), 1)
     for i, two in enumerate(copies):
         for copy in two:
             copy.wait()
         term = jnp.dot(both[i], proj[...], preferred_element_type=F32)
-        out_ref[pl.ds(i * CHUNK, CHUNK), :] = jnp.where(column < rank, term[0:CHUNK], term[CHUNK:])
+        term = jnp.where(column < rank, term[0:CHUNK], term[CHUNK:])
+        done = 0
+        while done < CHUNK:
+            piece, first = divmod(i * CHUNK + done, rows)
+            size = min(CHUNK - done, rows - first)
+            outs[piece][pl.ds(first, size), :] = term[done : done + size]
+            done += size
 
 
 def count_kernel(picks_ref, out_ref):
@@ -49,8 +58,10 @@
     out_ref[...] = jnp.dot(hits, jnp.ones((samples, width), BF16), preferred_element_type=F32)
 
 
-def sketch_kernel(rank, count_ref, own_ref, other_ref, out_ref, held):
-    total = own_ref[...] + other_ref[...]
+def sketch_kernel(rank, count_ref, *refs):
+    parts, (out_ref, held) = refs[:-2], refs[-2:]
+    chunks = len(parts) // 2
+    total = jnp.concatenate([parts[i][...] + parts[chunks + i][...] for i in range(chunks)], axis=0)
     held[...] = lax.dot_general(
         total[:, rank : 2 * rank],
         total[:, 0:rank] * count_ref[...],
@@ -64,29 +75,27 @@
     out_ref[...] = jnp.concatenate([even, odd], axis=1).astype(BF16)
 
 
-def score_kernel(mates, own_ref, far_ref, *refs):
-    queries, (out_ref, back_ref, wide) = refs[: 2 * mates], refs[2 * mates :]
+def flatten_kernel(mates, own_ref, far_ref, first_ref, second_ref, wide):
     pairs = own_ref.shape[0]
+    slots = first_ref.shape[0]
+    core = lax.axis_index("tensor")
+    wide[...] = jnp.zeros_like(wide)
+    sketch = jnp.where(lax.axis_index("dp") // mates == core, far_ref[...], own_ref[...])
+    wide[pl.ds(0, pairs, stride=slots), :] = sketch.astype(F32)
+    for out_ref, half in ((first_ref, core), (second_ref, 1 - core)):
+        start = half * (slots * pairs // 2)
+        for j in range(pairs // 2):
+            rows = wide[pl.ds(pl.multiple_of(start + j * slots, slots), slots), :]
+            out_ref[:, j * LANES : (j + 1) * LANES] = rows.astype(BF16)
+
+
+def score_kernel(mates, first_ref, second_ref, *refs):
+    queries, out_ref = refs[:-1], refs[-1]
     own_queries = queries[0].shape[0]
-    slots = wide.shape[0] // pairs
-    wide[...] = jnp.zeros_like(wide)
-    wide[pl.ds(0, pairs, stride=slots), :] = own_ref[...].astype(F32)
-    wide[pl.ds(1, pairs, stride=slots), :] = far_ref[...].astype(F32)
+    slots = first_ref.shape[0]
+    flats = (first_ref[...], second_ref[...])
+    block = lax.broadcasted_iota(jnp.int32, (slots, mates * own_queries), 1) // own_queries
     spot = lax.axis_index("dp")
-    core = lax.axis_index("tensor")
-    flats = []
-    for half in (core, 1 - core):
-        start = half * (slots * pairs // 2)
-        flats.append(
-            jnp.concatenate(
-                [
-                    wide[pl.ds(pl.multiple_of(start + j * slots, slots), slots), :]
-                    for j in range(pairs // 2)
-                ],
-                axis=1,
-            ).astype(BF16)
-        )
-    block = lax.broadcasted_iota(jnp.int32, (slots, mates * own_queries), 1) // own_queries
     spread = jnp.zeros(block.shape, F32)
     for r in range(mates):
         scores = sum(
@@ -97,9 +106,7 @@
         )
         here = block == lax.rem(spot, mates) ^ r
         spread = jnp.where(here, jnp.concatenate([scores] * mates, axis=1), spread)
-    spread = jnp.where(spot // mates == core, spread, 0.0)
     out_ref[...] = spread[0:1, :]
-    back_ref[...] = spread[1:2, :]
 
 
 def on_device(activations, out_grads, projections, sample_index, queries):
@@ -123,15 +130,14 @@
     there += [(place(a, m, a), place(a, m, 1 - a)) for a, m in spots]
     back = [(dst, src) for src, dst in there]
 
-    taken = []
-    for r in range(mates):
-        half = lax.ppermute(queries, "dp", [(d, d ^ r) for d in range(clips)]) if r else queries
-        taken += [half, lax.ppermute(half, "tensor", swap)]
+    halves = [queries]
+    for r in range(1, mates):
+        halves.append(lax.ppermute(queries, "dp", [(d, d ^ r) for d in range(clips)]))
     partial = pl.pallas_call(
         functools.partial(project_kernel, rank),
         in_specs=[hbm] * 3,
-        out_specs=vmem,
-        out_shape=jax.ShapeDtypeStruct((tokens, 2 * rank), F32),
+        out_specs=[vmem] * PIECES,
+        out_shape=[jax.ShapeDtypeStruct((tokens // PIECES, 2 * rank), F32)] * PIECES,
         scratch_shapes=[
             pltpu.VMEM((tokens // CHUNK, 2 * CHUNK, units), BF16),
             pltpu.VMEM((units, 2 * rank), BF16),
@@ -144,38 +150,52 @@
         name="project",
     )(activations, out_grads, projections)
 
-    other = lax.ppermute(partial, "tensor", swap)
+    other = [lax.ppermute(part, "tensor", swap) for part in partial]
     count = pl.pallas_call(
         count_kernel,
         in_specs=[vmem],
         out_specs=vmem,
         out_shape=jax.ShapeDtypeStruct((tokens, rank), F32),
         compiler_params=pltpu.CompilerParams(vmem_limit_bytes=8 << 20),
+        cost_estimate=pl.CostEstimate(flops=1, bytes_accessed=1, transcendentals=0),
         name="count",
     )(sample_index)
     sketch = pl.pallas_call(
         functools.partial(sketch_kernel, rank),
-        in_specs=[vmem] * 3,
+        in_specs=[vmem] * (1 + 2 * len(partial)),
         out_specs=vmem,
         out_shape=jax.ShapeDtypeStruct((pairs, LANES), BF16),
         scratch_shapes=[pltpu.VMEM((rank, rank), F32)],
         compiler_params=pltpu.CompilerParams(vmem_limit_bytes=8 << 20),
+        cost_estimate=pl.CostEstimate(flops=1, bytes_accessed=1, transcendentals=0),
         name="sketch",
-    )(count, partial, other)
+    )(count, *partial, *other)
 
     far_sketch = lax.ppermute(sketch, both, there)
+    halves, sketch = lax.optimization_barrier((halves, sketch))
+    taken = []
+    for half in halves:
+        taken += [half, lax.ppermute(half, "tensor", swap)]
     width = mates * own_queries
-    near_scores, far_scores = pl.pallas_call(
+    flats = pl.pallas_call(
+        functools.partial(flatten_kernel, mates),
+        in_specs=[vmem] * 2,
+        out_specs=[vmem] * 2,
+        out_shape=[jax.ShapeDtypeStruct((slots, entries), BF16)] * 2,
+        scratch_shapes=[pltpu.VMEM((pairs * slots, LANES), F32)],
+        compiler_params=pltpu.CompilerParams(vmem_limit_bytes=8 << 20),
+        cost_estimate=pl.CostEstimate(flops=1 << 34, bytes_accessed=64 << 20, transcendentals=0),
+        name="flatten",
+    )(sketch, far_sketch)
+    scores = pl.pallas_call(
         functools.partial(score_kernel, mates),
         in_specs=[vmem] * (2 * mates + 2),
-        out_specs=[vmem] * 2,
-        out_shape=[jax.ShapeDtypeStruct((1, width), F32)] * 2,
-        scratch_shapes=[pltpu.VMEM((pairs * slots, LANES), F32)],
+        out_specs=vmem,
+        out_shape=jax.ShapeDtypeStruct((1, width), F32),
         compiler_params=pltpu.CompilerParams(vmem_limit_bytes=(16 + mates // 2) << 20),
         name="score",
-    )(sketch, far_sketch, *taken)
-
-    return near_scores + lax.ppermute(far_scores, both, back)
+    )(*flats, *taken)
+    return lax.ppermute(scores, both, back)
 
 
 def solution(mesh):

time: 19.4 us -> 18.7 us (0.964)
  starting transfers between devices: 11.2 us -> 8.88 us
  waiting for transfers between devices: 3.04 us -> 4.98 us
  other arithmetic: 0.51 us -> 0 us
  local copies, waits for them, and re-layouts: 0.01 us -> 0.52 us
  Pallas kernels: 4.45 us -> 4.18 us
    ppermute x2 -> x3, waiting for transfers between devices: 2.23 us -> 3.98 us  [the longest x1 2.97 us: on_device(): return lax.ppermute(scores, both, back)]
    ppermute x4, starting transfers between devices: 2.81 us -> 1.08 us  [on_device(): taken += [half, lax.ppermute(half, 'tensor', swap)]]
    ppermute x4, waiting for transfers between devices: 0.01 us -> 0.98 us  [on_device(): taken += [half, lax.ppermute(half, 'tensor', swap)]]
    ppermute x2 -> x3, starting transfers between devices: 2.63 us -> 1.72 us  [the longest x2 1.37 us: on_device(): other = [lax.ppermute(part, 'tensor', swap) for part in partial]]
    ppermute x1, waiting for transfers between devices: 0.79 us -> 0.01 us  [on_device(): far_sketch = lax.ppermute(sketch, both, there)]
    add x1 -> x0, other arithmetic: 0.51 us -> none  [on_device(): return near_scores + lax.ppermute(far_scores, both, back)]
    unnamed x4 -> x5, local copies, waits for them, and re-layouts: 0.01 us -> 0.52 us
    pallas_call x1, Pallas kernels: 3.34 us -> 3.04 us  [on_device(): pl.pallas_call(functools.partial(project_kernel, rank), in_specs=[hbm] *...]
  transfers between devices with their start and end apart: 10 -> 11, of which waited for: 2 -> 7; matrix products, arithmetic and copies ran while one was open for 0% -> 0% of each run, Pallas kernels for 21% -> 20%
where the time goes in v9:
time: 18.7 us; the launch traced here: 18.6 us
  starting transfers between devices  8.88 us (47%)
  waiting for transfers between devices  4.98 us (27%)
  Pallas kernels  4.18 us (22%)
  local copies, waits for them, and re-layouts  0.52 us (3%)
    ppermute x3, starting transfers between devices, on_device(): lax.ppermute(queries, 'dp', [(d, d ^ r) for d in range(clips)])  3.38 us
    pallas_call x1, Pallas kernels, on_device(): pl.pallas_call(functools.partial(project_kernel, rank), in_specs=[hbm] *...  3.04 us
    ppermute x1, waiting for transfers between devices, on_device(): return lax.ppermute(scores, both, back)  2.97 us
    ppermute x1, starting transfers between devices, on_device(): far_sketch = lax.ppermute(sketch, both, there)  2.7 us
    ppermute x2, starting transfers between devices, on_device(): other = [lax.ppermute(part, 'tensor', swap) for part in partial]  1.37 us
    ppermute x4, starting transfers between devices, on_device(): taken += [half, lax.ppermute(half, 'tensor', swap)]  1.08 us
    ppermute x2, waiting for transfers between devices, on_device(): other = [lax.ppermute(part, 'tensor', swap) for part in partial]  1.02 us
    ppermute x4, waiting for transfers between devices, on_device(): taken += [half, lax.ppermute(half, 'tensor', swap)]  0.98 us
  transfers between devices with their start and end apart: 11, of which 7 were waited for; matrix products, arithmetic and copies ran while one was open for 0% of the time, Pallas kernels for 20%

profile of v9, /device:TPU:1, one launch (start us, length us, event | category | flops | bytes accessed | tf_op | source)
XLA Modules:
  0.0 18.6 jit_solution(11657946451784979435)
XLA Ops:
  0.0 2.1 %collective-permute-start.1 = (bf16[32,2048]{1,0:T(8,128)(2,1)}, bf16[32,2048]{1,0:T(8,128)(2,1)S(1)}, u32[]{:S(2)}, u32[]{:S(2)}) collective-permute-start(bf16[32,2048]{1,0:T(8,128)(2,1)} %refs_0_), channel_id=1, source_target_pairs={{0,4},{2,6},{4,0},{6,2},{8,12},{10,14},{12,8},{14,10},{1,5},{3,7},... | collective-permute-start | bytes 393224 | tf_op jit(solution)/shard_map/ppermute | solution.py:135
  2.1 1.2 %collective-permute-start = (bf16[32,2048]{1,0:T(8,128)(2,1)}, bf16[32,2048]{1,0:T(8,128)(2,1)S(1)}, u32[]{:S(2)}, u32[]{:S(2)}) collective-permute-start(bf16[32,2048]{1,0:T(8,128)(2,1)} %refs_0_), channel_id=1, source_target_pairs={{0,2},{2,0},{4,6},{6,4},{8,10},{10,8},{12,14},{14,12},{1,3},{3,1},... | collective-permute-start | bytes 393224 | tf_op jit(solution)/shard_map/ppermute | solution.py:135
  3.3 0.0 collective-permute-start.2
  3.4 3.0 %project.1 = (f32[192,128]{1,0:T(8,128)S(1)}, f32[192,128]{1,0:T(8,128)S(1)}) custom-call(bf16[1,384,2560]{2,1,0:T(8,128)(2,1)} %acts_ref.1, bf16[1,384,2560]{2,1,0:T(8,128)(2,1)} %grads_ref.1, bf16[2560,128]{1,0:T(8,128)(2,1)} %proj_ref.1), custom_call_target="tpu_custom_call" | custom-call | flops 503316480 | bytes 3932160 | tf_op jit(solution)/shard_map/project/pallas_call | solution.py:136
  6.4 1.3 %collective-permute-start.3 = (f32[192,128]{1,0:T(8,128)S(1)}, f32[192,128]{1,0:T(8,128)S(1)}, u32[]{:S(2)}, u32[]{:S(2)}) collective-permute-start(f32[192,128]{1,0:T(8,128)S(1)} %get-tuple-element.14.refs_0_), channel_id=1, source_target_pairs={{0,1},{1,0},{2,3},{3,2},{4,5},{5,4},{6,7},{7,6},{8,9},{9,8},{10,11... | collective-permute-start | bytes 294920 | tf_op jit(solution)/shard_map/ppermute | solution.py:153
  7.7 0.1 collective-permute-start.4
  7.8 0.2 %count.1.count_ref = f32[384,64]{1,0:T(8,128)S(1)} custom-call(s32[1,256]{1,0:T(1,128)S(1)} %copy-done.1), custom_call_target="tpu_custom_call" | custom-call | flops 1 | bytes 1 | tf_op jit(solution)/shard_map/count/pallas_call | solution.py:154
  8.0 0.7 %collective-permute-done.3.refs_2_ = f32[192,128]{1,0:T(8,128)S(1)} collective-permute-done((f32[192,128]{1,0:T(8,128)S(1)}, f32[192,128]{1,0:T(8,128)S(1)}, u32[]{:S(2)}, u32[]{:S(2)}) %collective-permute-start.3) | collective-permute-done | bytes 98336 | tf_op jit(solution)/shard_map/ppermute | solution.py:153
  8.7 0.4 %collective-permute-done.4.refs_3_ = f32[192,128]{1,0:T(8,128)S(1)} collective-permute-done((f32[192,128]{1,0:T(8,128)S(1)}, f32[192,128]{1,0:T(8,128)S(1)}, u32[]{:S(2)}, u32[]{:S(2)}) %collective-permute-start.4) | collective-permute-done | bytes 98336 | tf_op jit(solution)/shard_map/ppermute | solution.py:153
  9.0 0.5 %sketch.1.own_ref = bf16[32,128]{1,0:T(8,128)(2,1)S(1)} custom-call(f32[384,64]{1,0:T(8,128)S(1)} %count.1.count_ref, f32[192,128]{1,0:T(8,128)S(1)} %get-tuple-element.14.refs_0_, f32[192,128]{1,0:T(8,128)S(1)} %get-tuple-element.15.refs_1_, f32[192,128]{1,0:T(8,128)S(1)} %collective-permute-done.3.refs_2_, f32[192,128]{1,0:T(8,128)S(1)} %collective-permute-done.4.refs_3_), custom_call_target="tpu_custom_call" | custom-call | flops 1 | bytes 1 | tf_op jit(solution)/shard_map/sketch/pallas_call | solution.py:163
  9.5 2.7 %collective-permute-start.5 = (bf16[32,128]{1,0:T(8,128)(2,1)S(1)}, bf16[32,128]{1,0:T(8,128)(2,1)S(1)}, u32[]{:S(2)}, u32[]{:S(2)}) collective-permute-start(bf16[32,128]{1,0:T(8,128)(2,1)S(1)} %sketch.1.own_ref), channel_id=1, source_target_pairs={{1,9},{3,11},{5,13},{7,15},{8,0},{10,2},{12,4},{14,6},{0,1},{2,3},... | collective-permute-start | bytes 24584 | tf_op jit(solution)/shard_map/ppermute | solution.py:174
  12.2 0.0 collective-permute-done.1.refs_4_
  12.2 0.1 collective-permute-start.6
  12.3 0.5 %collective-permute-start.7 = (bf16[32,2048]{1,0:T(8,128)(2,1)S(1)}, bf16[32,2048]{1,0:T(8,128)(2,1)S(1)}, u32[]{:S(2)}, u32[]{:S(2)}) collective-permute-start(bf16[32,2048]{1,0:T(8,128)(2,1)S(1)} %collective-permute-done.refs_2_), channel_id=1, source_target_pairs={{0,1},{1,0},{2,3},{3,2},{4,5},{5,4},{6,7},{7,6},{8,9},{9,8},{10,11... | collective-permute-start | bytes 393224 | tf_op jit(solution)/shard_map/ppermute | solution.py:178
  12.8 0.1 collective-permute-start.8
  12.9 0.4 %collective-permute-start.9 = (bf16[32,2048]{1,0:T(8,128)(2,1)S(1)}, bf16[32,2048]{1,0:T(8,128)(2,1)S(1)}, u32[]{:S(2)}, u32[]{:S(2)}) collective-permute-start(bf16[32,2048]{1,0:T(8,128)(2,1)S(1)} %collective-permute-done.2.refs_6_), channel_id=1, source_target_pairs={{0,1},{1,0},{2,3},{3,2},{4,5},{5,4},{6,7},{7,6},{8,9},{9,8},{10,11... | collective-permute-start | bytes 393224 | tf_op jit(solution)/shard_map/ppermute | solution.py:178
  13.3 0.3 %collective-permute-done.6.refs_1_ = bf16[32,2048]{1,0:T(8,128)(2,1)S(1)} collective-permute-done((bf16[32,2048]{1,0:T(8,128)(2,1)S(1)}, bf16[32,2048]{1,0:T(8,128)(2,1)S(1)}, u32[]{:S(2)}, u32[]{:S(2)}) %collective-permute-start.6) | collective-permute-done | bytes 131104 | tf_op jit(solution)/shard_map/ppermute | solution.py:178
  13.6 0.2 %collective-permute-done.7.refs_3_ = bf16[32,2048]{1,0:T(8,128)(2,1)S(1)} collective-permute-done((bf16[32,2048]{1,0:T(8,128)(2,1)S(1)}, bf16[32,2048]{1,0:T(8,128)(2,1)S(1)}, u32[]{:S(2)}, u32[]{:S(2)}) %collective-permute-start.7) | collective-permute-done | bytes 131104 | tf_op jit(solution)/shard_map/ppermute | solution.py:178
  13.8 0.3 %collective-permute-done.8.refs_5_ = bf16[32,2048]{1,0:T(8,128)(2,1)S(1)} collective-permute-done((bf16[32,2048]{1,0:T(8,128)(2,1)S(1)}, bf16[32,2048]{1,0:T(8,128)(2,1)S(1)}, u32[]{:S(2)}, u32[]{:S(2)}) %collective-permute-start.8) | collective-permute-done | bytes 131104 | tf_op jit(solution)/shard_map/ppermute | solution.py:178
  14.1 0.2 %collective-permute-done.9.refs_7_ = bf16[32,2048]{1,0:T(8,128)(2,1)S(1)} collective-permute-done((bf16[32,2048]{1,0:T(8,128)(2,1)S(1)}, bf16[32,2048]{1,0:T(8,128)(2,1)S(1)}, u32[]{:S(2)}, u32[]{:S(2)}) %collective-permute-start.9) | collective-permute-done | bytes 131104 | tf_op jit(solution)/shard_map/ppermute | solution.py:178
  14.3 0.5 %score.1 = f32[1,128]{1,0:T(1,128)S(1)} custom-call(bf16[8,2048]{1,0:T(8,128)(2,1)S(1)} %get-tuple-element.17.first_ref, bf16[8,2048]{1,0:T(8,128)(2,1)S(1)} %get-tuple-element.18.second_ref, bf16[32,2048]{1,0:T(8,128)(2,1)S(1)} %copy-done, bf16[32,2048]{1,0:T(8,128)(2,1)S(1)} %collective-permute-done.6.refs_1_, ...), custom_call_target="tpu_custom_call" | custom-call | tf_op jit(solution)/shard_map/score/pallas_call | solution.py:190
  14.8 0.4 %collective-permute-start.10 = (f32[1,128]{1,0:T(1,128)S(1)}, f32[1,128]{1,0:T(1,128)S(1)}, u32[]{:S(2)}, u32[]{:S(2)}) collective-permute-start(f32[1,128]{1,0:T(1,128)S(1)} %score.1), channel_id=1, source_target_pairs={{9,1},{11,3},{13,5},{15,7},{0,8},{2,10},{4,12},{6,14},{1,0},{3,2},... | collective-permute-start | bytes 1544 | tf_op jit(solution)/shard_map/ppermute | solution.py:198
  15.1 3.0 %collective-permute-done.10 = f32[1,128]{1,0:T(1,128)S(1)} collective-permute-done((f32[1,128]{1,0:T(1,128)S(1)}, f32[1,128]{1,0:T(1,128)S(1)}, u32[]{:S(2)}, u32[]{:S(2)}) %collective-permute-start.10) | collective-permute-done | bytes 544 | tf_op jit(solution)/shard_map/ppermute | solution.py:198
  18.1 0.5 %copy.7 = f32[1,128]{1,0:T(1,128)} copy(f32[1,128]{1,0:T(1,128)S(1)} %collective-permute-done.10) | data formatting | bytes 1024
  (8 shorter events, 0.0 us)
Async XLA Ops:
  0.0 12.2 %copy-start = (bf16[32,2048]{1,0:T(8,128)(2,1)S(1)}, bf16[32,2048]{1,0:T(8,128)(2,1)}, u32[]{:S(2)}) copy-start(bf16[32,2048]{1,0:T(8,128)(2,1)} %refs_0_) | copy-start | bytes 393220
  0.0 7.8 %copy-start.1 = (s32[1,256]{1,0:T(1,128)S(1)}, s32[1,256]{1,0:T(1,128)}, u32[]{:S(2)}) copy-start(s32[1,256]{1,0:T(1,128)} %picks_ref.1) | copy-start | bytes 3076
  0.0 12.2 %collective-permute-start.1 = (bf16[32,2048]{1,0:T(8,128)(2,1)}, bf16[32,2048]{1,0:T(8,128)(2,1)S(1)}, u32[]{:S(2)}, u32[]{:S(2)}) collective-permute-start(bf16[32,2048]{1,0:T(8,128)(2,1)} %refs_0_), channel_id=1, source_target_pairs={{0,4},{2,6},{4,0},{6,2},{8,12},{10,14},{12,8},{14,10},{1,5},{3,7},... | collective-permute-start | bytes 393224 | tf_op jit(solution)/shard_map/ppermute | solution.py:135
  2.1 10.1 %collective-permute-start = (bf16[32,2048]{1,0:T(8,128)(2,1)}, bf16[32,2048]{1,0:T(8,128)(2,1)S(1)}, u32[]{:S(2)}, u32[]{:S(2)}) collective-permute-start(bf16[32,2048]{1,0:T(8,128)(2,1)} %refs_0_), channel_id=1, source_target_pairs={{0,2},{2,0},{4,6},{6,4},{8,10},{10,8},{12,14},{14,12},{1,3},{3,1},... | collective-permute-start | bytes 393224 | tf_op jit(solution)/shard_map/ppermute | solution.py:135
  3.3 8.8 %collective-permute-start.2 = (bf16[32,2048]{1,0:T(8,128)(2,1)}, bf16[32,2048]{1,0:T(8,128)(2,1)S(1)}, u32[]{:S(2)}, u32[]{:S(2)}) collective-permute-start(bf16[32,2048]{1,0:T(8,128)(2,1)} %refs_0_), channel_id=1, source_target_pairs={{0,6},{2,4},{4,2},{6,0},{8,14},{10,12},{12,10},{14,8},{1,7},{3,5},... | collective-permute-start | bytes 393224 | tf_op jit(solution)/shard_map/ppermute | solution.py:135
  6.4 2.2 %collective-permute-start.3 = (f32[192,128]{1,0:T(8,128)S(1)}, f32[192,128]{1,0:T(8,128)S(1)}, u32[]{:S(2)}, u32[]{:S(2)}) collective-permute-start(f32[192,128]{1,0:T(8,128)S(1)} %get-tuple-element.14.refs_0_), channel_id=1, source_target_pairs={{0,1},{1,0},{2,3},{3,2},{4,5},{5,4},{6,7},{7,6},{8,9},{9,8},{10,11... | collective-permute-start | bytes 294920 | tf_op jit(solution)/shard_map/ppermute | solution.py:153
  7.7 1.3 %collective-permute-start.4 = (f32[192,128]{1,0:T(8,128)S(1)}, f32[192,128]{1,0:T(8,128)S(1)}, u32[]{:S(2)}, u32[]{:S(2)}) collective-permute-start(f32[192,128]{1,0:T(8,128)S(1)} %get-tuple-element.15.refs_1_), channel_id=1, source_target_pairs={{0,1},{1,0},{2,3},{3,2},{4,5},{5,4},{6,7},{7,6},{8,9},{9,8},{10,11... | collective-permute-start | bytes 294920 | tf_op jit(solution)/shard_map/ppermute | solution.py:153
  9.5 3.8 %collective-permute-start.5 = (bf16[32,128]{1,0:T(8,128)(2,1)S(1)}, bf16[32,128]{1,0:T(8,128)(2,1)S(1)}, u32[]{:S(2)}, u32[]{:S(2)}) collective-permute-start(bf16[32,128]{1,0:T(8,128)(2,1)S(1)} %sketch.1.own_ref), channel_id=1, source_target_pairs={{1,9},{3,11},{5,13},{7,15},{8,0},{10,2},{12,4},{14,6},{0,1},{2,3},... | collective-permute-start | bytes 24584 | tf_op jit(solution)/shard_map/ppermute | solution.py:174
  12.2 1.4 %collective-permute-start.6 = (bf16[32,2048]{1,0:T(8,128)(2,1)S(1)}, bf16[32,2048]{1,0:T(8,128)(2,1)S(1)}, u32[]{:S(2)}, u32[]{:S(2)}) collective-permute-start(bf16[32,2048]{1,0:T(8,128)(2,1)S(1)} %copy-done), channel_id=1, source_target_pairs={{0,1},{1,0},{2,3},{3,2},{4,5},{5,4},{6,7},{7,6},{8,9},{9,8},{10,11... | collective-permute-start | bytes 393224 | tf_op jit(solution)/shard_map/ppermute | solution.py:178
  12.3 1.5 %collective-permute-start.7 = (bf16[32,2048]{1,0:T(8,128)(2,1)S(1)}, bf16[32,2048]{1,0:T(8,128)(2,1)S(1)}, u32[]{:S(2)}, u32[]{:S(2)}) collective-permute-start(bf16[32,2048]{1,0:T(8,128)(2,1)S(1)} %collective-permute-done.refs_2_), channel_id=1, source_target_pairs={{0,1},{1,0},{2,3},{3,2},{4,5},{5,4},{6,7},{7,6},{8,9},{9,8},{10,11... | collective-permute-start | bytes 393224 | tf_op jit(solution)/shard_map/ppermute | solution.py:178
  12.8 1.3 %collective-permute-start.8 = (bf16[32,2048]{1,0:T(8,128)(2,1)S(1)}, bf16[32,2048]{1,0:T(8,128)(2,1)S(1)}, u32[]{:S(2)}, u32[]{:S(2)}) collective-permute-start(bf16[32,2048]{1,0:T(8,128)(2,1)S(1)} %collective-permute-done.1.refs_4_), channel_id=1, source_target_pairs={{0,1},{1,0},{2,3},{3,2},{4,5},{5,4},{6,7},{7,6},{8,9},{9,8},{10,11... | collective-permute-start | bytes 393224 | tf_op jit(solution)/shard_map/ppermute | solution.py:178
  12.9 1.5 %collective-permute-start.9 = (bf16[32,2048]{1,0:T(8,128)(2,1)S(1)}, bf16[32,2048]{1,0:T(8,128)(2,1)S(1)}, u32[]{:S(2)}, u32[]{:S(2)}) collective-permute-start(bf16[32,2048]{1,0:T(8,128)(2,1)S(1)} %collective-permute-done.2.refs_6_), channel_id=1, source_target_pairs={{0,1},{1,0},{2,3},{3,2},{4,5},{5,4},{6,7},{7,6},{8,9},{9,8},{10,11... | collective-permute-start | bytes 393224 | tf_op jit(solution)/shard_map/ppermute | solution.py:178
  14.8 3.3 %collective-permute-start.10 = (f32[1,128]{1,0:T(1,128)S(1)}, f32[1,128]{1,0:T(1,128)S(1)}, u32[]{:S(2)}, u32[]{:S(2)}) collective-permute-start(f32[1,128]{1,0:T(1,128)S(1)} %score.1), channel_id=1, source_target_pairs={{9,1},{11,3},{13,5},{15,7},{0,8},{2,10},{4,12},{6,14},{1,0},{3,2},... | collective-permute-start | bytes 1544 | tf_op jit(solution)/shard_map/ppermute | solution.py:198

commit v10 on v9

--- a/solution.py
+++ b/solution.py
@@ -10,44 +10,24 @@
 F32 = jnp.float32
 BF16 = jnp.bfloat16
 LANES = 128
-CHUNK = 128
 PIECES = 2
 
 
-def project_kernel(rank, acts_ref, grads_ref, proj_ref, *refs):
-    outs, (both, proj, sems) = refs[:-3], refs[-3:]
-    chunks = both.shape[0]
-    weights = pltpu.make_async_copy(proj_ref, proj, sems.at[chunks, 0])
-    weights.start()
-    copies = []
-    for i in range(chunks):
-        part = pl.ds(i * CHUNK, CHUNK)
-        two = (
-            pltpu.make_async_copy(
-                acts_ref.at[0, part, :], both.at[i, pl.ds(0, CHUNK), :], sems.at[i, 0]
-            ),
-            pltpu.make_async_copy(
-                grads_ref.at[0, part, :], both.at[i, pl.ds(CHUNK, CHUNK), :], sems.at[i, 1]
-            ),
+def first_kernel(out_ref):
+    out_ref[...] = jnp.zeros_like(out_ref)
+
+
+def project_kernel(rank, first_ref, acts_ref, grads_ref, proj_ref, *outs):
+    rows = outs[0].shape[0]
+    column = lax.broadcasted_iota(jnp.int32, (rows, 2 * rank), 1)
+    for i, out_ref in enumerate(outs):
+        part = slice(i * rows, (i + 1) * rows)
+        term = jnp.dot(
+            jnp.concatenate([acts_ref[0, part, :], grads_ref[0, part, :]], axis=0),
+            proj_ref[...],
+            preferred_element_type=F32,
         )
-        for copy in two:
-            copy.start()
-        copies.append(two)
-
-    weights.wait()
-    rows = outs[0].shape[0]
-    column = lax.broadcasted_iota(jnp.int32, (CHUNK, 2 * rank), 1)
-    for i, two in enumerate(copies):
-        for copy in two:
-            copy.wait()
-        term = jnp.dot(both[i], proj[...], preferred_element_type=F32)
-        term = jnp.where(column < rank, term[0:CHUNK], term[CHUNK:])
-        done = 0
-        while done < CHUNK:
-            piece, first = divmod(i * CHUNK + done, rows)
-            size = min(CHUNK - done, rows - first)
-            outs[piece][pl.ds(first, size), :] = term[done : done + size]
-            done += size
+        out_ref[...] = jnp.where(column < rank, term[0:rows], term[rows:])
 
 
 def count_kernel(picks_ref, out_ref):
@@ -92,21 +72,27 @@
 def score_kernel(mates, first_ref, second_ref, *refs):
     queries, out_ref = refs[:-1], refs[-1]
     own_queries = queries[0].shape[0]
-    slots = first_ref.shape[0]
     flats = (first_ref[...], second_ref[...])
-    block = lax.broadcasted_iota(jnp.int32, (slots, mates * own_queries), 1) // own_queries
-    spot = lax.axis_index("dp")
-    spread = jnp.zeros(block.shape, F32)
-    for r in range(mates):
-        scores = sum(
-            lax.dot_general(
-                flat, queries[2 * r + i][...], (((1,), (1,)), ((), ())), preferred_element_type=F32
-            )
-            for i, flat in enumerate(flats)
+    scores = sum(
+        lax.dot_general(
+            flat,
+            jnp.concatenate([queries[2 * r + i][...] for r in range(mates)], axis=0),
+            (((1,), (1,)), ((), ())),
+            preferred_element_type=F32,
         )
-        here = block == lax.rem(spot, mates) ^ r
-        spread = jnp.where(here, jnp.concatenate([scores] * mates, axis=1), spread)
-    out_ref[...] = spread[0:1, :]
+        for i, flat in enumerate(flats)
+    )
+    member = lax.rem(lax.axis_index("dp"), mates)
+    width = scores.shape[1]
+    block = lax.broadcasted_iota(jnp.int32, scores.shape, 1) // own_queries
+    step = 1
+    while step < mates:
+        up = pltpu.roll(scores, step * own_queries, 1)
+        down = pltpu.roll(scores, width - step * own_queries, 1)
+        swapped = jnp.where(block & step == 0, down, up)
+        scores = jnp.where(member & step == 0, scores, swapped)
+        step *= 2
+    out_ref[...] = scores[0:1, :]
 
 
 def on_device(activations, out_grads, projections, sample_index, queries):
@@ -118,7 +104,6 @@
     mates = clips // 2
     slots = 8
     vmem = pl.BlockSpec(memory_space=pltpu.VMEM)
-    hbm = pl.BlockSpec(memory_space=pl.ANY)
     swap = [(0, 1), (1, 0)]
     both = ("dp", "tensor")
 
@@ -130,25 +115,29 @@
     there += [(place(a, m, a), place(a, m, 1 - a)) for a, m in spots]
     back = [(dst, src) for src, dst in there]
 
+    first = pl.pallas_call(
+        first_kernel,
+        out_specs=vmem,
+        out_shape=jax.ShapeDtypeStruct((8, LANES), F32),
+        compiler_params=pltpu.CompilerParams(vmem_limit_bytes=1 << 20),
+        cost_estimate=pl.CostEstimate(flops=1 << 32, bytes_accessed=1, transcendentals=0),
+        name="first",
+    )()
+    queries, first = lax.optimization_barrier((queries, first))
     halves = [queries]
     for r in range(1, mates):
         halves.append(lax.ppermute(queries, "dp", [(d, d ^ r) for d in range(clips)]))
     partial = pl.pallas_call(
         functools.partial(project_kernel, rank),
-        in_specs=[hbm] * 3,
+        in_specs=[vmem] * 4,
         out_specs=[vmem] * PIECES,
         out_shape=[jax.ShapeDtypeStruct((tokens // PIECES, 2 * rank), F32)] * PIECES,
-        scratch_shapes=[
-            pltpu.VMEM((tokens // CHUNK, 2 * CHUNK, units), BF16),
-            pltpu.VMEM((units, 2 * rank), BF16),
-            pltpu.SemaphoreType.DMA((tokens // CHUNK + 1, 2)),
-        ],
-        compiler_params=pltpu.CompilerParams(vmem_limit_bytes=55000 << 10),
+        compiler_params=pltpu.CompilerParams(vmem_limit_bytes=16 << 20),
         cost_estimate=pl.CostEstimate(
             flops=8 * tokens * units * rank, bytes_accessed=4 * tokens * units, transcendentals=0
         ),
         name="project",
-    )(activations, out_grads, projections)
+    )(first, activations, out_grads, projections)
 
     other = [lax.ppermute(part, "tensor", swap) for part in partial]
     count = pl.pallas_call(

time: 18.7 us -> 18.4 us (0.984)
  the two profiles are of different devices: /device:TPU:1 before, /device:TPU:0 now
where the time goes in v10:
time: 18.4 us; the launch traced here: 18.3 us
  starting transfers between devices  8.85 us (48%)
  waiting for transfers between devices  5.62 us (31%)
  Pallas kernels  2.35 us (13%)
  local copies, waits for them, and re-layouts  1.42 us (8%)
    ppermute x3, starting transfers between devices, on_device(): lax.ppermute(queries, 'dp', [(d, d ^ r) for d in range(clips)])  4.52 us
    ppermute x3, waiting for transfers between devices, on_device(): lax.ppermute(queries, 'dp', [(d, d ^ r) for d in range(clips)])  2.38 us
    ppermute x1, starting transfers between devices, on_device(): return lax.ppermute(scores, both, back)  2.38 us
    unnamed x11, local copies, waits for them, and re-layouts  1.42 us
    ppermute x1, waiting for transfers between devices, on_device(): return lax.ppermute(scores, both, back)  1.3 us
    pallas_call x1, Pallas kernels, on_device(): pl.pallas_call(functools.partial(project_kernel, rank), in_specs=[vmem] *...  1.17 us
    ppermute x4, starting transfers between devices, on_device(): taken += [half, lax.ppermute(half, 'tensor', swap)]  1.02 us
    ppermute x1, waiting for transfers between devices, on_device(): far_sketch = lax.ppermute(sketch, both, there)  0.87 us
  transfers between devices with their start and end apart: 11, of which 7 were waited for; matrix products, arithmetic and copies ran while one was open for 0% of the time, Pallas kernels for 10%

profile of v10, /device:TPU:0, one launch (start us, length us, event | category | flops | bytes accessed | tf_op | source)
XLA Modules:
  0.0 18.3 jit_solution(9199992762071640626)
XLA Ops:
  0.0 0.9 %copy-done.3 = bf16[32,2048]{1,0:T(8,128)(2,1)S(1)} copy-done((bf16[32,2048]{1,0:T(8,128)(2,1)S(1)}, bf16[32,2048]{1,0:T(8,128)(2,1)}, u32[]{:S(2)}) %copy-start.3) | copy-done | bytes 131096
  0.9 4.0 %collective-permute-start.2 = (bf16[32,2048]{1,0:T(8,128)(2,1)S(1)}, bf16[32,2048]{1,0:T(8,128)(2,1)S(1)}, u32[]{:S(2)}, u32[]{:S(2)}) collective-permute-start(bf16[32,2048]{1,0:T(8,128)(2,1)S(1)} %copy-done.3), channel_id=1, source_target_pairs={{0,6},{2,4},{4,2},{6,0},{8,14},{10,12},{12,10},{14,8},{1,7},{3,5},... | collective-permute-start | bytes 393224 | tf_op jit(solution)/shard_map/ppermute | solution.py:129
  4.9 0.4 %collective-permute-start.1 = (bf16[32,2048]{1,0:T(8,128)(2,1)S(1)}, bf16[32,2048]{1,0:T(8,128)(2,1)S(1)}, u32[]{:S(2)}, u32[]{:S(2)}) collective-permute-start(bf16[32,2048]{1,0:T(8,128)(2,1)S(1)} %copy-done.3), channel_id=1, source_target_pairs={{0,4},{2,6},{4,0},{6,2},{8,12},{10,14},{12,8},{14,10},{1,5},{3,7},... | collective-permute-start | bytes 393224 | tf_op jit(solution)/shard_map/ppermute | solution.py:129
  5.3 0.1 collective-permute-start
  5.4 1.2 %project.1 = (f32[192,128]{1,0:T(8,128)S(1)}, f32[192,128]{1,0:T(8,128)S(1)}) custom-call(f32[8,128]{1,0:T(8,128)S(1)} %first.1.first_ref, bf16[1,384,2560]{2,1,0:T(8,128)(2,1)S(1)} %copy-done, bf16[1,384,2560]{2,1,0:T(8,128)(2,1)S(1)} %copy-done.1, bf16[2560,128]{1,0:T(8,128)(2,1)S(1)} %copy-done.2), custom_call_target="tpu_custom_call" | custom-call | flops 503316480 | bytes 3932160 | tf_op jit(solution)/shard_map/project/pallas_call | solution.py:130
  6.6 0.1 collective-permute-start.3
  6.7 0.5 %collective-permute-start.4 = (f32[192,128]{1,0:T(8,128)S(1)}, f32[192,128]{1,0:T(8,128)S(1)}, u32[]{:S(2)}, u32[]{:S(2)}) collective-permute-start(f32[192,128]{1,0:T(8,128)S(1)} %get-tuple-element.19.refs_1_), channel_id=1, source_target_pairs={{0,1},{1,0},{2,3},{3,2},{4,5},{5,4},{6,7},{7,6},{8,9},{9,8},{10,11... | collective-permute-start | bytes 294920 | tf_op jit(solution)/shard_map/ppermute | solution.py:142
  7.2 0.2 %count.1.count_ref = f32[384,64]{1,0:T(8,128)S(1)} custom-call(s32[1,256]{1,0:T(1,128)S(1)} %copy-done.4), custom_call_target="tpu_custom_call" | custom-call | flops 1 | bytes 1 | tf_op jit(solution)/shard_map/count/pallas_call | solution.py:143
  7.4 0.6 %collective-permute-done.3.refs_2_ = f32[192,128]{1,0:T(8,128)S(1)} collective-permute-done((f32[192,128]{1,0:T(8,128)S(1)}, f32[192,128]{1,0:T(8,128)S(1)}, u32[]{:S(2)}, u32[]{:S(2)}) %collective-permute-start.3) | collective-permute-done | bytes 98336 | tf_op jit(solution)/shard_map/ppermute | solution.py:142
  8.0 0.2 collective-permute-done.4.refs_3_
  8.1 0.5 %sketch.1.own_ref = bf16[32,128]{1,0:T(8,128)(2,1)S(1)} custom-call(f32[384,64]{1,0:T(8,128)S(1)} %count.1.count_ref, f32[192,128]{1,0:T(8,128)S(1)} %get-tuple-element.18.refs_0_, f32[192,128]{1,0:T(8,128)S(1)} %get-tuple-element.19.refs_1_, f32[192,128]{1,0:T(8,128)S(1)} %collective-permute-done.3.refs_2_, f32[192,128]{1,0:T(8,128)S(1)} %collective-permute-done.4.refs_3_), custom_call_target="tpu_custom_call" | custom-call | flops 1 | bytes 1 | tf_op jit(solution)/shard_map/sketch/pallas_call | solution.py:152
  8.6 0.4 %collective-permute-start.5 = (bf16[32,128]{1,0:T(8,128)(2,1)S(1)}, bf16[32,128]{1,0:T(8,128)(2,1)S(1)}, u32[]{:S(2)}, u32[]{:S(2)}) collective-permute-start(bf16[32,128]{1,0:T(8,128)(2,1)S(1)} %sketch.1.own_ref), channel_id=1, source_target_pairs={{1,9},{3,11},{5,13},{7,15},{8,0},{10,2},{12,4},{14,6},{0,1},{2,3},... | collective-permute-start | bytes 24584 | tf_op jit(solution)/shard_map/ppermute | solution.py:163
  8.9 0.2 %collective-permute-done.2.refs_6_ = bf16[32,2048]{1,0:T(8,128)(2,1)S(1)} collective-permute-done((bf16[32,2048]{1,0:T(8,128)(2,1)S(1)}, bf16[32,2048]{1,0:T(8,128)(2,1)S(1)}, u32[]{:S(2)}, u32[]{:S(2)}) %collective-permute-start.2) | collective-permute-done | bytes 131104 | tf_op jit(solution)/shard_map/ppermute | solution.py:129
  9.2 2.1 %collective-permute-done.1.refs_4_ = bf16[32,2048]{1,0:T(8,128)(2,1)S(1)} collective-permute-done((bf16[32,2048]{1,0:T(8,128)(2,1)S(1)}, bf16[32,2048]{1,0:T(8,128)(2,1)S(1)}, u32[]{:S(2)}, u32[]{:S(2)}) %collective-permute-start.1) | collective-permute-done | bytes 131104 | tf_op jit(solution)/shard_map/ppermute | solution.py:129
  11.3 0.4 %collective-permute-start.6 = (bf16[32,2048]{1,0:T(8,128)(2,1)S(1)}, bf16[32,2048]{1,0:T(8,128)(2,1)S(1)}, u32[]{:S(2)}, u32[]{:S(2)}) collective-permute-start(bf16[32,2048]{1,0:T(8,128)(2,1)S(1)} %copy-done.3), channel_id=1, source_target_pairs={{0,1},{1,0},{2,3},{3,2},{4,5},{5,4},{6,7},{7,6},{8,9},{9,8},{10,11... | collective-permute-start | bytes 393224 | tf_op jit(solution)/shard_map/ppermute | solution.py:167
  11.8 0.1 collective-permute-start.7
  11.8 0.4 %collective-permute-start.8 = (bf16[32,2048]{1,0:T(8,128)(2,1)S(1)}, bf16[32,2048]{1,0:T(8,128)(2,1)S(1)}, u32[]{:S(2)}, u32[]{:S(2)}) collective-permute-start(bf16[32,2048]{1,0:T(8,128)(2,1)S(1)} %collective-permute-done.1.refs_4_), channel_id=1, source_target_pairs={{0,1},{1,0},{2,3},{3,2},{4,5},{5,4},{6,7},{7,6},{8,9},{9,8},{10,11... | collective-permute-start | bytes 393224 | tf_op jit(solution)/shard_map/ppermute | solution.py:167
  12.3 0.1 collective-permute-start.9
  12.4 0.9 %collective-permute-done.5.far_ref = bf16[32,128]{1,0:T(8,128)(2,1)S(1)} collective-permute-done((bf16[32,128]{1,0:T(8,128)(2,1)S(1)}, bf16[32,128]{1,0:T(8,128)(2,1)S(1)}, u32[]{:S(2)}, u32[]{:S(2)}) %collective-permute-start.5) | collective-permute-done | bytes 8224 | tf_op jit(solution)/shard_map/ppermute | solution.py:163
  13.3 0.3 %collective-permute-done.9.refs_7_ = bf16[32,2048]{1,0:T(8,128)(2,1)S(1)} collective-permute-done((bf16[32,2048]{1,0:T(8,128)(2,1)S(1)}, bf16[32,2048]{1,0:T(8,128)(2,1)S(1)}, u32[]{:S(2)}, u32[]{:S(2)}) %collective-permute-start.9) | collective-permute-done | bytes 131104 | tf_op jit(solution)/shard_map/ppermute | solution.py:167
  13.6 0.5 %score.1 = f32[1,128]{1,0:T(1,128)S(1)} custom-call(bf16[8,2048]{1,0:T(8,128)(2,1)S(1)} %get-tuple-element.21.first_ref, bf16[8,2048]{1,0:T(8,128)(2,1)S(1)} %get-tuple-element.22.second_ref, bf16[32,2048]{1,0:T(8,128)(2,1)S(1)} %copy-done.3, bf16[32,2048]{1,0:T(8,128)(2,1)S(1)} %collective-permute-done.6.refs_1_, ...), custom_call_target="tpu_custom_call" | custom-call | tf_op jit(solution)/shard_map/score/pallas_call | solution.py:179
  14.1 2.4 %collective-permute-start.10 = (f32[1,128]{1,0:T(1,128)S(1)}, f32[1,128]{1,0:T(1,128)S(1)}, u32[]{:S(2)}, u32[]{:S(2)}) collective-permute-start(f32[1,128]{1,0:T(1,128)S(1)} %score.1), channel_id=1, source_target_pairs={{9,1},{11,3},{13,5},{15,7},{0,8},{2,10},{4,12},{6,14},{1,0},{3,2},... | collective-permute-start | bytes 1544 | tf_op jit(solution)/shard_map/ppermute | solution.py:187
  16.5 1.3 %collective-permute-done.10 = f32[1,128]{1,0:T(1,128)S(1)} collective-permute-done((f32[1,128]{1,0:T(1,128)S(1)}, f32[1,128]{1,0:T(1,128)S(1)}, u32[]{:S(2)}, u32[]{:S(2)}) %collective-permute-start.10) | collective-permute-done | bytes 544 | tf_op jit(solution)/shard_map/ppermute | solution.py:187
  17.8 0.5 %copy.7 = f32[1,128]{1,0:T(1,128)} copy(f32[1,128]{1,0:T(1,128)S(1)} %collective-permute-done.10) | data formatting | bytes 1024
  (15 shorter events, 0.1 us)
Async XLA Ops:
  0.0 0.9 %copy-start.3 = (bf16[32,2048]{1,0:T(8,128)(2,1)S(1)}, bf16[32,2048]{1,0:T(8,128)(2,1)}, u32[]{:S(2)}) copy-start(bf16[32,2048]{1,0:T(8,128)(2,1)} %refs_0_) | copy-start | bytes 393220
  0.0 5.4 %copy-start.2 = (bf16[2560,128]{1,0:T(8,128)(2,1)S(1)}, bf16[2560,128]{1,0:T(8,128)(2,1)}, u32[]{:S(2)}) copy-start(bf16[2560,128]{1,0:T(8,128)(2,1)} %proj_ref.1) | copy-start | bytes 1966084
  0.0 5.4 %copy-start.1 = (bf16[1,384,2560]{2,1,0:T(8,128)(2,1)S(1)}, bf16[1,384,2560]{2,1,0:T(8,128)(2,1)}, u32[]{:S(2)}) copy-start(bf16[1,384,2560]{2,1,0:T(8,128)(2,1)} %grads_ref.1) | copy-start | bytes 5898244
  0.0 5.4 %copy-start = (bf16[1,384,2560]{2,1,0:T(8,128)(2,1)S(1)}, bf16[1,384,2560]{2,1,0:T(8,128)(2,1)}, u32[]{:S(2)}) copy-start(bf16[1,384,2560]{2,1,0:T(8,128)(2,1)} %acts_ref.1) | copy-start | bytes 5898244
  0.9 6.3 %copy-start.4 = (s32[1,256]{1,0:T(1,128)S(1)}, s32[1,256]{1,0:T(1,128)}, u32[]{:S(2)}) copy-start(s32[1,256]{1,0:T(1,128)} %picks_ref.1) | copy-start | bytes 3076
  0.9 8.3 %collective-permute-start.2 = (bf16[32,2048]{1,0:T(8,128)(2,1)S(1)}, bf16[32,2048]{1,0:T(8,128)(2,1)S(1)}, u32[]{:S(2)}, u32[]{:S(2)}) collective-permute-start(bf16[32,2048]{1,0:T(8,128)(2,1)S(1)} %copy-done.3), channel_id=1, source_target_pairs={{0,6},{2,4},{4,2},{6,0},{8,14},{10,12},{12,10},{14,8},{1,7},{3,5},... | collective-permute-start | bytes 393224 | tf_op jit(solution)/shard_map/ppermute | solution.py:129
  4.9 6.5 %collective-permute-start.1 = (bf16[32,2048]{1,0:T(8,128)(2,1)S(1)}, bf16[32,2048]{1,0:T(8,128)(2,1)S(1)}, u32[]{:S(2)}, u32[]{:S(2)}) collective-permute-start(bf16[32,2048]{1,0:T(8,128)(2,1)S(1)} %copy-done.3), channel_id=1, source_target_pairs={{0,4},{2,6},{4,0},{6,2},{8,12},{10,14},{12,8},{14,10},{1,5},{3,7},... | collective-permute-start | bytes 393224 | tf_op jit(solution)/shard_map/ppermute | solution.py:129
  5.3 6.0 %collective-permute-start = (bf16[32,2048]{1,0:T(8,128)(2,1)S(1)}, bf16[32,2048]{1,0:T(8,128)(2,1)S(1)}, u32[]{:S(2)}, u32[]{:S(2)}) collective-permute-start(bf16[32,2048]{1,0:T(8,128)(2,1)S(1)} %copy-done.3), channel_id=1, source_target_pairs={{0,2},{2,0},{4,6},{6,4},{8,10},{10,8},{12,14},{14,12},{1,3},{3,1},... | collective-permute-start | bytes 393224 | tf_op jit(solution)/shard_map/ppermute | solution.py:129
  6.6 1.4 %collective-permute-start.3 = (f32[192,128]{1,0:T(8,128)S(1)}, f32[192,128]{1,0:T(8,128)S(1)}, u32[]{:S(2)}, u32[]{:S(2)}) collective-permute-start(f32[192,128]{1,0:T(8,128)S(1)} %get-tuple-element.18.refs_0_), channel_id=1, source_target_pairs={{0,1},{1,0},{2,3},{3,2},{4,5},{5,4},{6,7},{7,6},{8,9},{9,8},{10,11... | collective-permute-start | bytes 294920 | tf_op jit(solution)/shard_map/ppermute | solution.py:142
  6.7 1.4 %collective-permute-start.4 = (f32[192,128]{1,0:T(8,128)S(1)}, f32[192,128]{1,0:T(8,128)S(1)}, u32[]{:S(2)}, u32[]{:S(2)}) collective-permute-start(f32[192,128]{1,0:T(8,128)S(1)} %get-tuple-element.19.refs_1_), channel_id=1, source_target_pairs={{0,1},{1,0},{2,3},{3,2},{4,5},{5,4},{6,7},{7,6},{8,9},{9,8},{10,11... | collective-permute-start | bytes 294920 | tf_op jit(solution)/shard_map/ppermute | solution.py:142
  8.6 4.6 %collective-permute-start.5 = (bf16[32,128]{1,0:T(8,128)(2,1)S(1)}, bf16[32,128]{1,0:T(8,128)(2,1)S(1)}, u32[]{:S(2)}, u32[]{:S(2)}) collective-permute-start(bf16[32,128]{1,0:T(8,128)(2,1)S(1)} %sketch.1.own_ref), channel_id=1, source_target_pairs={{1,9},{3,11},{5,13},{7,15},{8,0},{10,2},{12,4},{14,6},{0,1},{2,3},... | collective-permute-start | bytes 24584 | tf_op jit(solution)/shard_map/ppermute | solution.py:163
  11.3 1.9 %collective-permute-start.6 = (bf16[32,2048]{1,0:T(8,128)(2,1)S(1)}, bf16[32,2048]{1,0:T(8,128)(2,1)S(1)}, u32[]{:S(2)}, u32[]{:S(2)}) collective-permute-start(bf16[32,2048]{1,0:T(8,128)(2,1)S(1)} %copy-done.3), channel_id=1, source_target_pairs={{0,1},{1,0},{2,3},{3,2},{4,5},{5,4},{6,7},{7,6},{8,9},{9,8},{10,11... | collective-permute-start | bytes 393224 | tf_op jit(solution)/shard_map/ppermute | solution.py:167
  11.8 1.5 %collective-permute-start.7 = (bf16[32,2048]{1,0:T(8,128)(2,1)S(1)}, bf16[32,2048]{1,0:T(8,128)(2,1)S(1)}, u32[]{:S(2)}, u32[]{:S(2)}) collective-permute-start(bf16[32,2048]{1,0:T(8,128)(2,1)S(1)} %collective-permute-done.refs_2_), channel_id=1, source_target_pairs={{0,1},{1,0},{2,3},{3,2},{4,5},{5,4},{6,7},{7,6},{8,9},{9,8},{10,11... | collective-permute-start | bytes 393224 | tf_op jit(solution)/shard_map/ppermute | solution.py:167
  11.8 1.4 %collective-permute-start.8 = (bf16[32,2048]{1,0:T(8,128)(2,1)S(1)}, bf16[32,2048]{1,0:T(8,128)(2,1)S(1)}, u32[]{:S(2)}, u32[]{:S(2)}) collective-permute-start(bf16[32,2048]{1,0:T(8,128)(2,1)S(1)} %collective-permute-done.1.refs_4_), channel_id=1, source_target_pairs={{0,1},{1,0},{2,3},{3,2},{4,5},{5,4},{6,7},{7,6},{8,9},{9,8},{10,11... | collective-permute-start | bytes 393224 | tf_op jit(solution)/shard_map/ppermute | solution.py:167
  12.3 1.3 %collective-permute-start.9 = (bf16[32,2048]{1,0:T(8,128)(2,1)S(1)}, bf16[32,2048]{1,0:T(8,128)(2,1)S(1)}, u32[]{:S(2)}, u32[]{:S(2)}) collective-permute-start(bf16[32,2048]{1,0:T(8,128)(2,1)S(1)} %collective-permute-done.2.refs_6_), channel_id=1, source_target_pairs={{0,1},{1,0},{2,3},{3,2},{4,5},{5,4},{6,7},{7,6},{8,9},{9,8},{10,11... | collective-permute-start | bytes 393224 | tf_op jit(solution)/shard_map/ppermute | solution.py:167
  14.1 3.7 %collective-permute-start.10 = (f32[1,128]{1,0:T(1,128)S(1)}, f32[1,128]{1,0:T(1,128)S(1)}, u32[]{:S(2)}, u32[]{:S(2)}) collective-permute-start(f32[1,128]{1,0:T(1,128)S(1)} %score.1), channel_id=1, source_target_pairs={{9,1},{11,3},{13,5},{15,7},{0,8},{2,10},{4,12},{6,14},{1,0},{3,2},... | collective-permute-start | bytes 1544 | tf_op jit(solution)/shard_map/ppermute | solution.py:187

commit v11 on v10

--- a/solution.py
+++ b/solution.py
@@ -17,7 +17,7 @@
     out_ref[...] = jnp.zeros_like(out_ref)
 
 
-def project_kernel(rank, first_ref, acts_ref, grads_ref, proj_ref, *outs):
+def project_kernel(rank, first_ref, ready_ref, acts_ref, grads_ref, proj_ref, *outs):
     rows = outs[0].shape[0]
     column = lax.broadcasted_iota(jnp.int32, (rows, 2 * rank), 1)
     for i, out_ref in enumerate(outs):
@@ -30,25 +30,30 @@
         out_ref[...] = jnp.where(column < rank, term[0:rows], term[rows:])
 
 
-def count_kernel(picks_ref, out_ref):
+def count_kernel(rank, picks_ref, out_ref):
     tokens, width = out_ref.shape
     samples = picks_ref.shape[1]
     token = lax.broadcasted_iota(jnp.int32, (tokens, samples), 0)
     hits = jnp.where(token == picks_ref[...], 1.0, 0.0).astype(BF16)
-    out_ref[...] = jnp.dot(hits, jnp.ones((samples, width), BF16), preferred_element_type=F32)
+    count = jnp.dot(hits, jnp.ones((samples, width), BF16), preferred_element_type=F32)
+    column = lax.broadcasted_iota(jnp.int32, (tokens, width), 1)
+    out_ref[...] = jnp.where(column < rank, count, 1.0)
 
 
 def sketch_kernel(rank, count_ref, *refs):
     parts, (out_ref, held) = refs[:-2], refs[-2:]
     chunks = len(parts) // 2
     total = jnp.concatenate([parts[i][...] + parts[chunks + i][...] for i in range(chunks)], axis=0)
-    held[...] = lax.dot_general(
-        total[:, rank : 2 * rank],
-        total[:, 0:rank] * count_ref[...],
+    total = total * count_ref[...]
+    high = total.astype(BF16)
+    low = (total - high.astype(F32)).astype(BF16)
+    gram = lax.dot_general(
+        jnp.concatenate([high, high, low], axis=0),
+        jnp.concatenate([high, low, high], axis=0),
         (((0,), (0,)), ((), ())),
-        precision=lax.Precision.HIGHEST,
         preferred_element_type=F32,
     )
+    held[...] = gram[rank : 2 * rank, 0:rank]
     pairs = out_ref.shape[0]
     even = held[pl.ds(0, pairs, stride=2), :]
     odd = held[pl.ds(1, pairs, stride=2), :]
@@ -72,16 +77,15 @@
 def score_kernel(mates, first_ref, second_ref, *refs):
     queries, out_ref = refs[:-1], refs[-1]
     own_queries = queries[0].shape[0]
-    flats = (first_ref[...], second_ref[...])
     scores = sum(
         lax.dot_general(
-            flat,
             jnp.concatenate([queries[2 * r + i][...] for r in range(mates)], axis=0),
+            flat_ref[...],
             (((1,), (1,)), ((), ())),
             preferred_element_type=F32,
         )
-        for i, flat in enumerate(flats)
-    )
+        for i, flat_ref in enumerate((first_ref, second_ref))
+    ).T
     member = lax.rem(lax.axis_index("dp"), mates)
     width = scores.shape[1]
     block = lax.broadcasted_iota(jnp.int32, scores.shape, 1) // own_queries
@@ -120,16 +124,17 @@
         out_specs=vmem,
         out_shape=jax.ShapeDtypeStruct((8, LANES), F32),
         compiler_params=pltpu.CompilerParams(vmem_limit_bytes=1 << 20),
-        cost_estimate=pl.CostEstimate(flops=1 << 32, bytes_accessed=1, transcendentals=0),
+        cost_estimate=pl.CostEstimate(flops=1 << 30, bytes_accessed=1, transcendentals=0),
         name="first",
     )()
-    queries, first = lax.optimization_barrier((queries, first))
+    sent, first = lax.optimization_barrier((queries, first))
+    own_swapped = lax.ppermute(sent, "tensor", swap)
     halves = [queries]
     for r in range(1, mates):
-        halves.append(lax.ppermute(queries, "dp", [(d, d ^ r) for d in range(clips)]))
+        halves.append(lax.ppermute(sent, "dp", [(d, d ^ r) for d in range(clips)]))
     partial = pl.pallas_call(
         functools.partial(project_kernel, rank),
-        in_specs=[vmem] * 4,
+        in_specs=[vmem] * 5,
         out_specs=[vmem] * PIECES,
         out_shape=[jax.ShapeDtypeStruct((tokens // PIECES, 2 * rank), F32)] * PIECES,
         compiler_params=pltpu.CompilerParams(vmem_limit_bytes=16 << 20),
@@ -137,14 +142,14 @@
             flops=8 * tokens * units * rank, bytes_accessed=4 * tokens * units, transcendentals=0
         ),
         name="project",
-    )(first, activations, out_grads, projections)
+    )(first, own_swapped, activations, out_grads, projections)
 
     other = [lax.ppermute(part, "tensor", swap) for part in partial]
     count = pl.pallas_call(
-        count_kernel,
+        functools.partial(count_kernel, rank),
         in_specs=[vmem],
         out_specs=vmem,
-        out_shape=jax.ShapeDtypeStruct((tokens, rank), F32),
+        out_shape=jax.ShapeDtypeStruct((tokens, 2 * rank), F32),
         compiler_params=pltpu.CompilerParams(vmem_limit_bytes=8 << 20),
         cost_estimate=pl.CostEstimate(flops=1, bytes_accessed=1, transcendentals=0),
         name="count",
@@ -161,9 +166,9 @@
     )(count, *partial, *other)
 
     far_sketch = lax.ppermute(sketch, both, there)
-    halves, sketch = lax.optimization_barrier((halves, sketch))
-    taken = []
-    for half in halves:
+    taken = [queries, own_swapped]
+    for half in halves[1:]:
+        half, sketch = lax.optimization_barrier((half, sketch))
         taken += [half, lax.ppermute(half, "tensor", swap)]
     width = mates * own_queries
     flats = pl.pallas_call(

time: 18.4 us -> 18.7 us (1.016)
  starting transfers between devices: 8.85 us -> 9.16 us
  waiting for transfers between devices: 5.62 us -> 5.31 us
  local copies, waits for them, and re-layouts: 1.42 us -> 1.61 us
    ppermute x4 -> x3, waiting for transfers between devices: 0.33 us -> 0.01 us  [on_device(): taken += [half, lax.ppermute(half, 'tensor', swap)]]
    unnamed x11, local copies, waits for them, and re-layouts: 1.42 us -> 1.61 us
    ppermute x3 -> x4, starting transfers between devices: 4.52 us -> 4.67 us  [the longest x3 4.15 us: on_device(): halves.append(lax.ppermute(sent, 'dp', [(d, d ^ r) for d in range(clips)]))]
    ppermute x3 -> x4, waiting for transfers between devices: 2.38 us -> 2.3 us  [the longest x3 2.3 us: on_device(): halves.append(lax.ppermute(sent, 'dp', [(d, d ^ r) for d in range(clips)]))]
    ppermute x4 -> x3, starting transfers between devices: 1.02 us -> 1 us  [on_device(): taken += [half, lax.ppermute(half, 'tensor', swap)]]
  transfers between devices with their start and end apart: 11 -> 11, of which waited for: 7 -> 6; matrix products, arithmetic and copies ran while one was open for 0% -> 0% of each run, Pallas kernels for 10% -> 10%
where the time goes in v11:
time: 18.7 us; the launch traced here: 18.5 us
  starting transfers between devices  9.16 us (49%)
  waiting for transfers between devices  5.31 us (28%)
  Pallas kernels  2.34 us (13%)
  local copies, waits for them, and re-layouts  1.61 us (9%)
    ppermute x3, starting transfers between devices, on_device(): halves.append(lax.ppermute(sent, 'dp', [(d, d ^ r) for d in range(clips)]))  4.15 us
    ppermute x1, starting transfers between devices, on_device(): return lax.ppermute(scores, both, back)  2.55 us
    ppermute x3, waiting for transfers between devices, on_device(): halves.append(lax.ppermute(sent, 'dp', [(d, d ^ r) for d in range(clips)]))  2.3 us
    unnamed x11, local copies, waits for them, and re-layouts  1.61 us
    ppermute x1, waiting for transfers between devices, on_device(): return lax.ppermute(scores, both, back)  1.3 us
    pallas_call x1, Pallas kernels, on_device(): pl.pallas_call(functools.partial(project_kernel, rank), in_specs=[vmem] *...  1.17 us
    ppermute x3, starting transfers between devices, on_device(): taken += [half, lax.ppermute(half, 'tensor', swap)]  1 us
    ppermute x1, waiting for transfers between devices, on_device(): far_sketch = lax.ppermute(sketch, both, there)  0.96 us
  transfers between devices with their start and end apart: 11, of which 6 were waited for; matrix products, arithmetic and copies ran while one was open for 0% of the time, Pallas kernels for 10%

profile of v11, /device:TPU:0, one launch (start us, length us, event | category | flops | bytes accessed | tf_op | source)
XLA Modules:
  0.0 18.5 jit_solution(2070272284124427688)
XLA Ops:
  0.0 0.5 %collective-permute-start.3 = (bf16[32,2048]{1,0:T(8,128)(2,1)}, bf16[32,2048]{1,0:T(8,128)(2,1)S(1)}, u32[]{:S(2)}, u32[]{:S(2)}) collective-permute-start(bf16[32,2048]{1,0:T(8,128)(2,1)} %refs_0_.1), channel_id=1, source_target_pairs={{0,1},{1,0},{2,3},{3,2},{4,5},{5,4},{6,7},{7,6},{8,9},{9,8},{10,11... | collective-permute-start | bytes 393224 | tf_op jit(solution)/shard_map/ppermute | solution.py:131
  0.5 2.6 %collective-permute-start.2 = (bf16[32,2048]{1,0:T(8,128)(2,1)}, bf16[32,2048]{1,0:T(8,128)(2,1)S(1)}, u32[]{:S(2)}, u32[]{:S(2)}) collective-permute-start(bf16[32,2048]{1,0:T(8,128)(2,1)} %refs_0_.1), channel_id=1, source_target_pairs={{0,2},{2,0},{4,6},{6,4},{8,10},{10,8},{12,14},{14,12},{1,3},{3,1},... | collective-permute-start | bytes 393224 | tf_op jit(solution)/shard_map/ppermute | solution.py:134
  3.1 1.6 %collective-permute-start.1 = (bf16[32,2048]{1,0:T(8,128)(2,1)}, bf16[32,2048]{1,0:T(8,128)(2,1)S(1)}, u32[]{:S(2)}, u32[]{:S(2)}) collective-permute-start(bf16[32,2048]{1,0:T(8,128)(2,1)} %refs_0_.1), channel_id=1, source_target_pairs={{0,4},{2,6},{4,0},{6,2},{8,12},{10,14},{12,8},{14,10},{1,5},{3,7},... | collective-permute-start | bytes 393224 | tf_op jit(solution)/shard_map/ppermute | solution.py:134
  4.7 0.0 copy-start.2
  4.7 1.1 %copy-done.2 = bf16[2560,128]{1,0:T(8,128)(2,1)S(1)} copy-done((bf16[2560,128]{1,0:T(8,128)(2,1)S(1)}, bf16[2560,128]{1,0:T(8,128)(2,1)}, u32[]{:S(2)}) %copy-start.2) | copy-done | bytes 655384
  5.8 1.2 %project.1 = (f32[192,128]{1,0:T(8,128)S(1)}, f32[192,128]{1,0:T(8,128)S(1)}) custom-call(f32[8,128]{1,0:T(8,128)S(1)} %first.1.first_ref, bf16[32,2048]{1,0:T(8,128)(2,1)S(1)} %collective-permute-done.3.ready_ref.refs_1_, bf16[1,384,2560]{2,1,0:T(8,128)(2,1)S(1)} %copy-done, bf16[1,384,2560]{2,1,0:T(8,128)(2,1)S(1)} %copy-done.1, ...), custom_call_target="tpu_custom_call" | custom-call | flops 503316480 | bytes 3932160 | tf_op jit(solution)/shard_map/project/pallas_call | solution.py:135
  7.0 0.1 collective-permute-start.4
  7.0 0.5 %collective-permute-start.5 = (f32[192,128]{1,0:T(8,128)S(1)}, f32[192,128]{1,0:T(8,128)S(1)}, u32[]{:S(2)}, u32[]{:S(2)}) collective-permute-start(f32[192,128]{1,0:T(8,128)S(1)} %get-tuple-element.20.refs_1_), channel_id=1, source_target_pairs={{0,1},{1,0},{2,3},{3,2},{4,5},{5,4},{6,7},{7,6},{8,9},{9,8},{10,11... | collective-permute-start | bytes 294920 | tf_op jit(solution)/shard_map/ppermute | solution.py:147
  7.5 0.2 %count.1.count_ref = f32[384,128]{1,0:T(8,128)S(1)} custom-call(s32[1,256]{1,0:T(1,128)S(1)} %copy-done.4), custom_call_target="tpu_custom_call" | custom-call | flops 1 | bytes 1 | tf_op jit(solution)/shard_map/count/pallas_call | solution.py:148
  7.8 0.6 %collective-permute-done.4.refs_2_ = f32[192,128]{1,0:T(8,128)S(1)} collective-permute-done((f32[192,128]{1,0:T(8,128)S(1)}, f32[192,128]{1,0:T(8,128)S(1)}, u32[]{:S(2)}, u32[]{:S(2)}) %collective-permute-start.4) | collective-permute-done | bytes 98336 | tf_op jit(solution)/shard_map/ppermute | solution.py:147
  8.3 0.2 collective-permute-done.5.refs_3_
  8.5 0.4 %sketch.1.own_ref = bf16[32,128]{1,0:T(8,128)(2,1)S(1)} custom-call(f32[384,128]{1,0:T(8,128)S(1)} %count.1.count_ref, f32[192,128]{1,0:T(8,128)S(1)} %get-tuple-element.19.refs_0_, f32[192,128]{1,0:T(8,128)S(1)} %get-tuple-element.20.refs_1_, f32[192,128]{1,0:T(8,128)S(1)} %collective-permute-done.4.refs_2_, f32[192,128]{1,0:T(8,128)S(1)} %collective-permute-done.5.refs_3_), custom_call_target="tpu_custom_call" | custom-call | flops 1 | bytes 1 | tf_op jit(solution)/shard_map/sketch/pallas_call | solution.py:157
  8.9 0.4 %collective-permute-start.6 = (bf16[32,128]{1,0:T(8,128)(2,1)S(1)}, bf16[32,128]{1,0:T(8,128)(2,1)S(1)}, u32[]{:S(2)}, u32[]{:S(2)}) collective-permute-start(bf16[32,128]{1,0:T(8,128)(2,1)S(1)} %sketch.1.own_ref), channel_id=1, source_target_pairs={{1,9},{3,11},{5,13},{7,15},{8,0},{10,2},{12,4},{14,6},{0,1},{2,3},... | collective-permute-start | bytes 24584 | tf_op jit(solution)/shard_map/ppermute | solution.py:168
  9.2 0.4 %collective-permute-done.1.refs_4_ = bf16[32,2048]{1,0:T(8,128)(2,1)S(1)} collective-permute-done((bf16[32,2048]{1,0:T(8,128)(2,1)}, bf16[32,2048]{1,0:T(8,128)(2,1)S(1)}, u32[]{:S(2)}, u32[]{:S(2)}) %collective-permute-start.1) | collective-permute-done | bytes 131104 | tf_op jit(solution)/shard_map/ppermute | solution.py:134
  9.7 1.9 %collective-permute-done.refs_6_ = bf16[32,2048]{1,0:T(8,128)(2,1)S(1)} collective-permute-done((bf16[32,2048]{1,0:T(8,128)(2,1)}, bf16[32,2048]{1,0:T(8,128)(2,1)S(1)}, u32[]{:S(2)}, u32[]{:S(2)}) %collective-permute-start) | collective-permute-done | bytes 131104 | tf_op jit(solution)/shard_map/ppermute | solution.py:134
  11.5 0.5 %collective-permute-start.9 = (bf16[32,2048]{1,0:T(8,128)(2,1)S(1)}, bf16[32,2048]{1,0:T(8,128)(2,1)S(1)}, u32[]{:S(2)}, u32[]{:S(2)}) collective-permute-start(bf16[32,2048]{1,0:T(8,128)(2,1)S(1)} %collective-permute-done.refs_6_), channel_id=1, source_target_pairs={{0,1},{1,0},{2,3},{3,2},{4,5},{5,4},{6,7},{7,6},{8,9},{9,8},{10,11... | collective-permute-start | bytes 393224 | tf_op jit(solution)/shard_map/ppermute | solution.py:172
  12.0 0.1 collective-permute-start.8
  12.1 0.4 %collective-permute-start.7 = (bf16[32,2048]{1,0:T(8,128)(2,1)S(1)}, bf16[32,2048]{1,0:T(8,128)(2,1)S(1)}, u32[]{:S(2)}, u32[]{:S(2)}) collective-permute-start(bf16[32,2048]{1,0:T(8,128)(2,1)S(1)} %collective-permute-done.2.refs_2_), channel_id=1, source_target_pairs={{0,1},{1,0},{2,3},{3,2},{4,5},{5,4},{6,7},{7,6},{8,9},{9,8},{10,11... | collective-permute-start | bytes 393224 | tf_op jit(solution)/shard_map/ppermute | solution.py:172
  12.5 1.0 %collective-permute-done.6.far_ref = bf16[32,128]{1,0:T(8,128)(2,1)S(1)} collective-permute-done((bf16[32,128]{1,0:T(8,128)(2,1)S(1)}, bf16[32,128]{1,0:T(8,128)(2,1)S(1)}, u32[]{:S(2)}, u32[]{:S(2)}) %collective-permute-start.6) | collective-permute-done | bytes 8224 | tf_op jit(solution)/shard_map/ppermute | solution.py:168
  13.6 0.0 collective-permute-done.7.refs_3_
  13.6 0.6 %score.1 = f32[1,128]{1,0:T(1,128)S(1)} custom-call(bf16[8,2048]{1,0:T(8,128)(2,1)S(1)} %get-tuple-element.24.first_ref, bf16[8,2048]{1,0:T(8,128)(2,1)S(1)} %get-tuple-element.25.second_ref, bf16[32,2048]{1,0:T(8,128)(2,1)S(1)} %copy-done.3, bf16[32,2048]{1,0:T(8,128)(2,1)S(1)} %collective-permute-done.3.ready_ref.refs_1_, ...), custom_call_target="tpu_custom_call" | custom-call | tf_op jit(solution)/shard_map/score/pallas_call | solution.py:184
  14.1 2.5 %collective-permute-start.10 = (f32[1,128]{1,0:T(1,128)S(1)}, f32[1,128]{1,0:T(1,128)S(1)}, u32[]{:S(2)}, u32[]{:S(2)}) collective-permute-start(f32[1,128]{1,0:T(1,128)S(1)} %score.1), channel_id=1, source_target_pairs={{9,1},{11,3},{13,5},{15,7},{0,8},{2,10},{4,12},{6,14},{1,0},{3,2},... | collective-permute-start | bytes 1544 | tf_op jit(solution)/shard_map/ppermute | solution.py:192
  16.7 1.3 %collective-permute-done.10 = f32[1,128]{1,0:T(1,128)S(1)} collective-permute-done((f32[1,128]{1,0:T(1,128)S(1)}, f32[1,128]{1,0:T(1,128)S(1)}, u32[]{:S(2)}, u32[]{:S(2)}) %collective-permute-start.10) | collective-permute-done | bytes 544 | tf_op jit(solution)/shard_map/ppermute | solution.py:192
  18.0 0.5 %copy.7 = f32[1,128]{1,0:T(1,128)} copy(f32[1,128]{1,0:T(1,128)S(1)} %collective-permute-done.10) | data formatting | bytes 1024
  (15 shorter events, 0.1 us)
Async XLA Ops:
  0.0 4.7 %copy-start = (bf16[1,384,2560]{2,1,0:T(8,128)(2,1)S(1)}, bf16[1,384,2560]{2,1,0:T(8,128)(2,1)}, u32[]{:S(2)}) copy-start(bf16[1,384,2560]{2,1,0:T(8,128)(2,1)} %acts_ref.1) | copy-start | bytes 5898244
  0.0 4.7 %copy-start.1 = (bf16[1,384,2560]{2,1,0:T(8,128)(2,1)S(1)}, bf16[1,384,2560]{2,1,0:T(8,128)(2,1)}, u32[]{:S(2)}) copy-start(bf16[1,384,2560]{2,1,0:T(8,128)(2,1)} %grads_ref.1) | copy-start | bytes 5898244
  0.0 7.5 %copy-start.4 = (s32[1,256]{1,0:T(1,128)S(1)}, s32[1,256]{1,0:T(1,128)}, u32[]{:S(2)}) copy-start(s32[1,256]{1,0:T(1,128)} %picks_ref.1) | copy-start | bytes 3076
  0.0 4.7 %collective-permute-start.3 = (bf16[32,2048]{1,0:T(8,128)(2,1)}, bf16[32,2048]{1,0:T(8,128)(2,1)S(1)}, u32[]{:S(2)}, u32[]{:S(2)}) collective-permute-start(bf16[32,2048]{1,0:T(8,128)(2,1)} %refs_0_.1), channel_id=1, source_target_pairs={{0,1},{1,0},{2,3},{3,2},{4,5},{5,4},{6,7},{7,6},{8,9},{9,8},{10,11... | collective-permute-start | bytes 393224 | tf_op jit(solution)/shard_map/ppermute | solution.py:131
  0.5 8.7 %collective-permute-start.2 = (bf16[32,2048]{1,0:T(8,128)(2,1)}, bf16[32,2048]{1,0:T(8,128)(2,1)S(1)}, u32[]{:S(2)}, u32[]{:S(2)}) collective-permute-start(bf16[32,2048]{1,0:T(8,128)(2,1)} %refs_0_.1), channel_id=1, source_target_pairs={{0,2},{2,0},{4,6},{6,4},{8,10},{10,8},{12,14},{14,12},{1,3},{3,1},... | collective-permute-start | bytes 393224 | tf_op jit(solution)/shard_map/ppermute | solution.py:134
  3.1 6.5 %collective-permute-start.1 = (bf16[32,2048]{1,0:T(8,128)(2,1)}, bf16[32,2048]{1,0:T(8,128)(2,1)S(1)}, u32[]{:S(2)}, u32[]{:S(2)}) collective-permute-start(bf16[32,2048]{1,0:T(8,128)(2,1)} %refs_0_.1), channel_id=1, source_target_pairs={{0,4},{2,6},{4,0},{6,2},{8,12},{10,14},{12,8},{14,10},{1,5},{3,7},... | collective-permute-start | bytes 393224 | tf_op jit(solution)/shard_map/ppermute | solution.py:134
  4.7 6.8 %collective-permute-start = (bf16[32,2048]{1,0:T(8,128)(2,1)}, bf16[32,2048]{1,0:T(8,128)(2,1)S(1)}, u32[]{:S(2)}, u32[]{:S(2)}) collective-permute-start(bf16[32,2048]{1,0:T(8,128)(2,1)} %refs_0_.1), channel_id=1, source_target_pairs={{0,6},{2,4},{4,2},{6,0},{8,14},{10,12},{12,10},{14,8},{1,7},{3,5},... | collective-permute-start | bytes 393224 | tf_op jit(solution)/shard_map/ppermute | solution.py:134
  4.7 1.1 %copy-start.2 = (bf16[2560,128]{1,0:T(8,128)(2,1)S(1)}, bf16[2560,128]{1,0:T(8,128)(2,1)}, u32[]{:S(2)}) copy-start(bf16[2560,128]{1,0:T(8,128)(2,1)} %proj_ref.1) | copy-start | bytes 1966084
  7.0 1.4 %collective-permute-start.4 = (f32[192,128]{1,0:T(8,128)S(1)}, f32[192,128]{1,0:T(8,128)S(1)}, u32[]{:S(2)}, u32[]{:S(2)}) collective-permute-start(f32[192,128]{1,0:T(8,128)S(1)} %get-tuple-element.19.refs_0_), channel_id=1, source_target_pairs={{0,1},{1,0},{2,3},{3,2},{4,5},{5,4},{6,7},{7,6},{8,9},{9,8},{10,11... | collective-permute-start | bytes 294920 | tf_op jit(solution)/shard_map/ppermute | solution.py:147
  7.0 1.4 %collective-permute-start.5 = (f32[192,128]{1,0:T(8,128)S(1)}, f32[192,128]{1,0:T(8,128)S(1)}, u32[]{:S(2)}, u32[]{:S(2)}) collective-permute-start(f32[192,128]{1,0:T(8,128)S(1)} %get-tuple-element.20.refs_1_), channel_id=1, source_target_pairs={{0,1},{1,0},{2,3},{3,2},{4,5},{5,4},{6,7},{7,6},{8,9},{9,8},{10,11... | collective-permute-start | bytes 294920 | tf_op jit(solution)/shard_map/ppermute | solution.py:147
  8.9 4.7 %copy-start.3 = (bf16[32,2048]{1,0:T(8,128)(2,1)S(1)}, bf16[32,2048]{1,0:T(8,128)(2,1)}, u32[]{:S(2)}) copy-start(bf16[32,2048]{1,0:T(8,128)(2,1)} %refs_0_.1) | copy-start | bytes 393220
  8.9 4.6 %collective-permute-start.6 = (bf16[32,128]{1,0:T(8,128)(2,1)S(1)}, bf16[32,128]{1,0:T(8,128)(2,1)S(1)}, u32[]{:S(2)}, u32[]{:S(2)}) collective-permute-start(bf16[32,128]{1,0:T(8,128)(2,1)S(1)} %sketch.1.own_ref), channel_id=1, source_target_pairs={{1,9},{3,11},{5,13},{7,15},{8,0},{10,2},{12,4},{14,6},{0,1},{2,3},... | collective-permute-start | bytes 24584 | tf_op jit(solution)/shard_map/ppermute | solution.py:168
  11.5 2.0 %collective-permute-start.9 = (bf16[32,2048]{1,0:T(8,128)(2,1)S(1)}, bf16[32,2048]{1,0:T(8,128)(2,1)S(1)}, u32[]{:S(2)}, u32[]{:S(2)}) collective-permute-start(bf16[32,2048]{1,0:T(8,128)(2,1)S(1)} %collective-permute-done.refs_6_), channel_id=1, source_target_pairs={{0,1},{1,0},{2,3},{3,2},{4,5},{5,4},{6,7},{7,6},{8,9},{9,8},{10,11... | collective-permute-start | bytes 393224 | tf_op jit(solution)/shard_map/ppermute | solution.py:172
  12.0 1.5 %collective-permute-start.8 = (bf16[32,2048]{1,0:T(8,128)(2,1)S(1)}, bf16[32,2048]{1,0:T(8,128)(2,1)S(1)}, u32[]{:S(2)}, u32[]{:S(2)}) collective-permute-start(bf16[32,2048]{1,0:T(8,128)(2,1)S(1)} %collective-permute-done.1.refs_4_), channel_id=1, source_target_pairs={{0,1},{1,0},{2,3},{3,2},{4,5},{5,4},{6,7},{7,6},{8,9},{9,8},{10,11... | collective-permute-start | bytes 393224 | tf_op jit(solution)/shard_map/ppermute | solution.py:172
  12.1 1.5 %collective-permute-start.7 = (bf16[32,2048]{1,0:T(8,128)(2,1)S(1)}, bf16[32,2048]{1,0:T(8,128)(2,1)S(1)}, u32[]{:S(2)}, u32[]{:S(2)}) collective-permute-start(bf16[32,2048]{1,0:T(8,128)(2,1)S(1)} %collective-permute-done.2.refs_2_), channel_id=1, source_target_pairs={{0,1},{1,0},{2,3},{3,2},{4,5},{5,4},{6,7},{7,6},{8,9},{9,8},{10,11... | collective-permute-start | bytes 393224 | tf_op jit(solution)/shard_map/ppermute | solution.py:172
  14.1 3.8 %collective-permute-start.10 = (f32[1,128]{1,0:T(1,128)S(1)}, f32[1,128]{1,0:T(1,128)S(1)}, u32[]{:S(2)}, u32[]{:S(2)}) collective-permute-start(f32[1,128]{1,0:T(1,128)S(1)} %score.1), channel_id=1, source_target_pairs={{9,1},{11,3},{13,5},{15,7},{0,8},{2,10},{4,12},{6,14},{1,0},{3,2},... | collective-permute-start | bytes 1544 | tf_op jit(solution)/shard_map/ppermute | solution.py:192

commit v12 on v11

--- a/solution.py
+++ b/solution.py
@@ -17,7 +17,7 @@
     out_ref[...] = jnp.zeros_like(out_ref)
 
 
-def project_kernel(rank, first_ref, ready_ref, acts_ref, grads_ref, proj_ref, *outs):
+def project_kernel(rank, first_ref, acts_ref, grads_ref, proj_ref, *outs):
     rows = outs[0].shape[0]
     column = lax.broadcasted_iota(jnp.int32, (rows, 2 * rank), 1)
     for i, out_ref in enumerate(outs):
@@ -55,38 +55,41 @@
     )
     held[...] = gram[rank : 2 * rank, 0:rank]
     pairs = out_ref.shape[0]
-    even = held[pl.ds(0, pairs, stride=2), :]
-    odd = held[pl.ds(1, pairs, stride=2), :]
+    start = lax.axis_index("tensor") * (2 * pairs)
+    even = held[pl.ds(start, pairs, stride=2), :]
+    odd = held[pl.ds(start + 1, pairs, stride=2), :]
     out_ref[...] = jnp.concatenate([even, odd], axis=1).astype(BF16)
 
 
-def flatten_kernel(mates, own_ref, far_ref, first_ref, second_ref, wide):
+def mark_kernel(*refs):
+    refs[-1][...] = jnp.zeros_like(refs[-1])
+
+
+def flatten_kernel(mark_ref, own_ref, far_ref, out_ref, wide):
     pairs = own_ref.shape[0]
-    slots = first_ref.shape[0]
-    core = lax.axis_index("tensor")
+    slots = out_ref.shape[0]
     wide[...] = jnp.zeros_like(wide)
-    sketch = jnp.where(lax.axis_index("dp") // mates == core, far_ref[...], own_ref[...])
-    wide[pl.ds(0, pairs, stride=slots), :] = sketch.astype(F32)
-    for out_ref, half in ((first_ref, core), (second_ref, 1 - core)):
-        start = half * (slots * pairs // 2)
-        for j in range(pairs // 2):
-            rows = wide[pl.ds(pl.multiple_of(start + j * slots, slots), slots), :]
-            out_ref[:, j * LANES : (j + 1) * LANES] = rows.astype(BF16)
-
-
-def score_kernel(mates, first_ref, second_ref, *refs):
-    queries, out_ref = refs[:-1], refs[-1]
+    wide[pl.ds(0, pairs, stride=slots), :] = own_ref[...].astype(F32)
+    wide[pl.ds(1, pairs, stride=slots), :] = far_ref[...].astype(F32)
+    for j in range(pairs):
+        out_ref[:, j * LANES : (j + 1) * LANES] = wide[j * slots : (j + 1) * slots, :].astype(BF16)
+
+
+def score_kernel(flat_ref, *refs):
+    queries, (keep_ref, send_ref) = refs[:-2], refs[-2:]
+    mates = len(queries)
     own_queries = queries[0].shape[0]
-    scores = sum(
-        lax.dot_general(
-            jnp.concatenate([queries[2 * r + i][...] for r in range(mates)], axis=0),
-            flat_ref[...],
-            (((1,), (1,)), ((), ())),
-            preferred_element_type=F32,
-        )
-        for i, flat_ref in enumerate((first_ref, second_ref))
-    ).T
-    member = lax.rem(lax.axis_index("dp"), mates)
+    scores = jnp.concatenate(
+        [
+            lax.dot_general(
+                flat_ref[...], query[...], (((1,), (1,)), ((), ())), preferred_element_type=F32
+            )
+            for query in queries
+        ],
+        axis=1,
+    )
+    spot = lax.axis_index("dp")
+    member = lax.rem(spot, mates)
     width = scores.shape[1]
     block = lax.broadcasted_iota(jnp.int32, scores.shape, 1) // own_queries
     step = 1
@@ -96,7 +99,14 @@
         swapped = jnp.where(block & step == 0, down, up)
         scores = jnp.where(member & step == 0, scores, swapped)
         step *= 2
-    out_ref[...] = scores[0:1, :]
+    worker = spot // mates == lax.axis_index("tensor")
+    own, far = scores[0:1, :], scores[1:2, :]
+    keep_ref[...] = jnp.where(worker, far, own)
+    send_ref[...] = jnp.where(worker, own, far)
+
+
+def add_kernel(one_ref, other_ref, out_ref):
+    out_ref[...] = one_ref[...] + other_ref[...]
 
 
 def on_device(activations, out_grads, projections, sample_index, queries):
@@ -104,7 +114,7 @@
     tokens, units = activations.shape[1:]
     rank = projections.shape[1] // 2
     own_queries, entries = queries.shape
-    pairs = 2 * entries // LANES
+    pairs = entries // LANES
     mates = clips // 2
     slots = 8
     vmem = pl.BlockSpec(memory_space=pltpu.VMEM)
@@ -115,9 +125,11 @@
         return (a * mates + m) * 2 + t
 
     spots = [(a, m) for a in range(2) for m in range(mates)]
-    there = [(place(a, m, 1 - a), place(1 - a, m, 1 - a)) for a, m in spots]
-    there += [(place(a, m, a), place(a, m, 1 - a)) for a, m in spots]
-    back = [(dst, src) for src, dst in there]
+    back = [(place(a, m, a), place(1 - a, m, a)) for a, m in spots]
+    back += [(place(a, m, 1 - a), place(a, m, a)) for a, m in spots]
+    across = [(d, (d + mates) % clips) for d in range(clips)]
+    small = pl.CostEstimate(flops=1, bytes_accessed=1, transcendentals=0)
+    few = pltpu.CompilerParams(vmem_limit_bytes=8 << 20)
 
     first = pl.pallas_call(
         first_kernel,
@@ -128,13 +140,12 @@
         name="first",
     )()
     sent, first = lax.optimization_barrier((queries, first))
-    own_swapped = lax.ppermute(sent, "tensor", swap)
     halves = [queries]
     for r in range(1, mates):
         halves.append(lax.ppermute(sent, "dp", [(d, d ^ r) for d in range(clips)]))
     partial = pl.pallas_call(
         functools.partial(project_kernel, rank),
-        in_specs=[vmem] * 5,
+        in_specs=[vmem] * 4,
         out_specs=[vmem] * PIECES,
         out_shape=[jax.ShapeDtypeStruct((tokens // PIECES, 2 * rank), F32)] * PIECES,
         compiler_params=pltpu.CompilerParams(vmem_limit_bytes=16 << 20),
@@ -142,7 +153,7 @@
             flops=8 * tokens * units * rank, bytes_accessed=4 * tokens * units, transcendentals=0
         ),
         name="project",
-    )(first, own_swapped, activations, out_grads, projections)
+    )(first, activations, out_grads, projections)
 
     other = [lax.ppermute(part, "tensor", swap) for part in partial]
     count = pl.pallas_call(
@@ -165,30 +176,46 @@
         name="sketch",
     )(count, *partial, *other)
 
-    far_sketch = lax.ppermute(sketch, both, there)
-    taken = [queries, own_swapped]
-    for half in halves[1:]:
-        half, sketch = lax.optimization_barrier((half, sketch))
-        taken += [half, lax.ppermute(half, "tensor", swap)]
+    far_sketch = lax.ppermute(sketch, "dp", across)
     width = mates * own_queries
-    flats = pl.pallas_call(
-        functools.partial(flatten_kernel, mates),
+    mark = pl.pallas_call(
+        mark_kernel,
+        in_specs=[vmem] * mates,
+        out_specs=vmem,
+        out_shape=jax.ShapeDtypeStruct((8, LANES), F32),
+        compiler_params=few,
+        cost_estimate=pl.CostEstimate(flops=1 << 31, bytes_accessed=1, transcendentals=0),
+        name="mark",
+    )(sketch, *halves[1:])
+    flat = pl.pallas_call(
+        flatten_kernel,
+        in_specs=[vmem] * 3,
+        out_specs=vmem,
+        out_shape=jax.ShapeDtypeStruct((slots, entries), BF16),
+        scratch_shapes=[pltpu.VMEM((pairs * slots, LANES), F32)],
+        compiler_params=few,
+        cost_estimate=small,
+        name="flatten",
+    )(mark, sketch, far_sketch)
+    row = jax.ShapeDtypeStruct((1, width), F32)
+    keep, send = pl.pallas_call(
+        score_kernel,
+        in_specs=[vmem] * (1 + mates),
+        out_specs=[vmem] * 2,
+        out_shape=[row] * 2,
+        compiler_params=pltpu.CompilerParams(vmem_limit_bytes=(8 + mates // 4) << 20),
+        cost_estimate=small,
+        name="score",
+    )(flat, *halves)
+    scores = pl.pallas_call(
+        add_kernel,
         in_specs=[vmem] * 2,
-        out_specs=[vmem] * 2,
-        out_shape=[jax.ShapeDtypeStruct((slots, entries), BF16)] * 2,
-        scratch_shapes=[pltpu.VMEM((pairs * slots, LANES), F32)],
-        compiler_params=pltpu.CompilerParams(vmem_limit_bytes=8 << 20),
-        cost_estimate=pl.CostEstimate(flops=1 << 34, bytes_accessed=64 << 20, transcendentals=0),
-        name="flatten",
-    )(sketch, far_sketch)
-    scores = pl.pallas_call(
-        functools.partial(score_kernel, mates),
-        in_specs=[vmem] * (2 * mates + 2),
-        out_specs=vmem,
-        out_shape=jax.ShapeDtypeStruct((1, width), F32),
-        compiler_params=pltpu.CompilerParams(vmem_limit_bytes=(16 + mates // 2) << 20),
-        name="score",
-    )(*flats, *taken)
+        out_specs=vmem,
+        out_shape=row,
+        compiler_params=few,
+        cost_estimate=small,
+        name="add",
+    )(keep, lax.ppermute(send, "tensor", swap))
     return lax.ppermute(scores, both, back)
 
 

time: 18.7 us -> 19.9 us (1.064)
  starting transfers between devices: 9.16 us -> 11.1 us
  waiting for transfers between devices: 5.31 us -> 4.76 us
    ppermute x3, waiting for transfers between devices: 2.3 us -> 0.01 us  [on_device(): halves.append(lax.ppermute(sent, 'dp', [(d, d ^ r) for d in range(clips)]))]
    ppermute x5 -> x2, waiting for transfers between devices: 0.98 us -> 2.72 us  [the longest x1 1.55 us: on_device(): far_sketch = lax.ppermute(sketch, 'dp', across)]
    ppermute x5 -> x2, starting transfers between devices: 1.9 us -> 3.03 us  [the longest x1 3.03 us: on_device(): far_sketch = lax.ppermute(sketch, 'dp', across)]
    ppermute x3, starting transfers between devices: 4.15 us -> 4.59 us  [on_device(): halves.append(lax.ppermute(sent, 'dp', [(d, d ^ r) for d in range(clips)]))]
    ppermute x1, starting transfers between devices: 2.55 us -> 2.93 us  [on_device(): return lax.ppermute(scores, both, back)]
    pallas_call x2 -> x4, Pallas kernels: 0.61 us -> 0.43 us  [the longest x1 0.41 us: on_device(): pl.pallas_call(score_kernel, in_specs=[vmem] * (1 + mates), out_specs=[vm...]
  transfers between devices with their start and end apart: 11 -> 8, of which waited for: 6 -> 5; matrix products, arithmetic and copies ran while one was open for 0% -> 0% of each run, Pallas kernels for 10% -> 9%
where the time goes in v12:
time: 19.9 us; the launch traced here: 19.7 us
  starting transfers between devices  11.1 us (56%)
  waiting for transfers between devices  4.76 us (24%)
  Pallas kernels  2.15 us (11%)
  local copies, waits for them, and re-layouts  1.61 us (8%)
    ppermute x3, starting transfers between devices, on_device(): halves.append(lax.ppermute(sent, 'dp', [(d, d ^ r) for d in range(clips)]))  4.59 us
    ppermute x1, starting transfers between devices, on_device(): far_sketch = lax.ppermute(sketch, 'dp', across)  3.03 us
    ppermute x1, starting transfers between devices, on_device(): return lax.ppermute(scores, both, back)  2.93 us
    unnamed x11, local copies, waits for them, and re-layouts  1.61 us
    ppermute x1, waiting for transfers between devices, on_device(): far_sketch = lax.ppermute(sketch, 'dp', across)  1.55 us
    ppermute x1, waiting for transfers between devices, on_device(): return lax.ppermute(scores, both, back)  1.3 us
    ppermute x1, waiting for transfers between devices, on_device(): lax.ppermute(send, 'tensor', swap)  1.17 us
    pallas_call x1, Pallas kernels, on_device(): pl.pallas_call(functools.partial(project_kernel, rank), in_specs=[vmem] *...  1.17 us
  transfers between devices with their start and end apart: 8, of which 5 were waited for; matrix products, arithmetic and copies ran while one was open for 0% of the time, Pallas kernels for 9%

profile of v12, /device:TPU:0, one launch (start us, length us, event | category | flops | bytes accessed | tf_op | source)
XLA Modules:
  0.0 19.7 jit_solution(11801956672796561573)
XLA Ops:
  0.0 3.0 %collective-permute-start.2 = (bf16[32,2048]{1,0:T(8,128)(2,1)}, bf16[32,2048]{1,0:T(8,128)(2,1)S(1)}, u32[]{:S(2)}, u32[]{:S(2)}) collective-permute-start(bf16[32,2048]{1,0:T(8,128)(2,1)} %refs_0_.1), channel_id=1, source_target_pairs={{0,2},{2,0},{4,6},{6,4},{8,10},{10,8},{12,14},{14,12},{1,3},{3,1},... | collective-permute-start | bytes 393224 | tf_op jit(solution)/shard_map/ppermute | solution.py:145
  3.0 1.6 %collective-permute-start.3 = (bf16[32,2048]{1,0:T(8,128)(2,1)}, bf16[32,2048]{1,0:T(8,128)(2,1)S(1)}, u32[]{:S(2)}, u32[]{:S(2)}) collective-permute-start(bf16[32,2048]{1,0:T(8,128)(2,1)} %refs_0_.1), channel_id=1, source_target_pairs={{0,4},{2,6},{4,0},{6,2},{8,12},{10,14},{12,8},{14,10},{1,5},{3,7},... | collective-permute-start | bytes 393224 | tf_op jit(solution)/shard_map/ppermute | solution.py:145
  4.6 0.0 collective-permute-start.4
  4.6 0.0 copy-done
  4.6 0.0 copy-start.2
  4.6 1.1 %copy-done.2 = bf16[2560,128]{1,0:T(8,128)(2,1)S(1)} copy-done((bf16[2560,128]{1,0:T(8,128)(2,1)S(1)}, bf16[2560,128]{1,0:T(8,128)(2,1)}, u32[]{:S(2)}) %copy-start.2) | copy-done | bytes 655384
  5.7 1.2 %project.1 = (f32[192,128]{1,0:T(8,128)S(1)}, f32[192,128]{1,0:T(8,128)S(1)}) custom-call(f32[8,128]{1,0:T(8,128)S(1)} %first.1.first_ref, bf16[1,384,2560]{2,1,0:T(8,128)(2,1)S(1)} %copy-done, bf16[1,384,2560]{2,1,0:T(8,128)(2,1)S(1)} %copy-done.1, bf16[2560,128]{1,0:T(8,128)(2,1)S(1)} %copy-done.2), custom_call_target="tpu_custom_call" | custom-call | flops 503316480 | bytes 3932160 | tf_op jit(solution)/shard_map/project/pallas_call | solution.py:146
  6.9 0.1 collective-permute-start
  7.0 0.5 %collective-permute-start.1 = (f32[192,128]{1,0:T(8,128)S(1)}, f32[192,128]{1,0:T(8,128)S(1)}, u32[]{:S(2)}, u32[]{:S(2)}) collective-permute-start(f32[192,128]{1,0:T(8,128)S(1)} %get-tuple-element.13.refs_1_), channel_id=1, source_target_pairs={{0,1},{1,0},{2,3},{3,2},{4,5},{5,4},{6,7},{7,6},{8,9},{9,8},{10,11... | collective-permute-start | bytes 294920 | tf_op jit(solution)/shard_map/ppermute | solution.py:158
  7.5 0.2 %count.1.count_ref = f32[384,128]{1,0:T(8,128)S(1)} custom-call(s32[1,256]{1,0:T(1,128)S(1)} %copy-done.4), custom_call_target="tpu_custom_call" | custom-call | flops 1 | bytes 1 | tf_op jit(solution)/shard_map/count/pallas_call | solution.py:159
  7.7 0.6 %collective-permute-done.refs_2_ = f32[192,128]{1,0:T(8,128)S(1)} collective-permute-done((f32[192,128]{1,0:T(8,128)S(1)}, f32[192,128]{1,0:T(8,128)S(1)}, u32[]{:S(2)}, u32[]{:S(2)}) %collective-permute-start) | collective-permute-done | bytes 98336 | tf_op jit(solution)/shard_map/ppermute | solution.py:158
  8.2 0.2 collective-permute-done.1.refs_3_
  8.4 0.3 %sketch.1.refs_0_.own_ref = bf16[16,128]{1,0:T(8,128)(2,1)S(1)} custom-call(f32[384,128]{1,0:T(8,128)S(1)} %count.1.count_ref, f32[192,128]{1,0:T(8,128)S(1)} %get-tuple-element.12.refs_0_, f32[192,128]{1,0:T(8,128)S(1)} %get-tuple-element.13.refs_1_, f32[192,128]{1,0:T(8,128)S(1)} %collective-permute-done.refs_2_, f32[192,128]{1,0:T(8,128)S(1)} %collective-permute-done.1.refs_3_), custom_call_target="tpu_custom_call" | custom-call | flops 1 | bytes 1 | tf_op jit(solution)/shard_map/sketch/pallas_call | solution.py:168
  8.7 3.0 %collective-permute-start.5 = (bf16[16,128]{1,0:T(8,128)(2,1)S(1)}, bf16[16,128]{1,0:T(8,128)(2,1)S(1)}, u32[]{:S(2)}, u32[]{:S(2)}) collective-permute-start(bf16[16,128]{1,0:T(8,128)(2,1)S(1)} %sketch.1.refs_0_.own_ref), channel_id=1, source_target_pairs={{0,8},{2,10},{4,12},{6,14},{8,0},{10,2},{12,4},{14,6},{1,9},{3,11}... | collective-permute-start | bytes 12296 | tf_op jit(solution)/shard_map/ppermute | solution.py:179
  11.8 0.0 collective-permute-done.2.refs_1_
  11.8 0.0 collective-permute-done.3.refs_2_
  11.8 0.0 collective-permute-done.4.refs_3_
  11.8 1.5 %collective-permute-done.5.far_ref = bf16[16,128]{1,0:T(8,128)(2,1)S(1)} collective-permute-done((bf16[16,128]{1,0:T(8,128)(2,1)S(1)}, bf16[16,128]{1,0:T(8,128)(2,1)S(1)}, u32[]{:S(2)}, u32[]{:S(2)}) %collective-permute-start.5) | collective-permute-done | bytes 4128 | tf_op jit(solution)/shard_map/ppermute | solution.py:179
  13.4 0.4 %score.1 = (f32[1,128]{1,0:T(1,128)S(1)}, f32[1,128]{1,0:T(1,128)S(1)}) custom-call(bf16[8,2048]{1,0:T(8,128)(2,1)S(1)} %flatten.1.flat_ref, bf16[32,2048]{1,0:T(8,128)(2,1)S(1)} %copy-done.3, bf16[32,2048]{1,0:T(8,128)(2,1)S(1)} %collective-permute-done.2.refs_1_, bf16[32,2048]{1,0:T(8,128)(2,1)S(1)} %collective-permute-done.3.refs_2_, ...), custom_call_target="tpu_custom_call" | custom-call | flops 1 | bytes 1 | tf_op jit(solution)/shard_map/score/pallas_call | solution.py:201
  13.8 0.0 collective-permute-start.6
  13.8 1.2 %collective-permute-done.6.other_ref = f32[1,128]{1,0:T(1,128)S(1)} collective-permute-done((f32[1,128]{1,0:T(1,128)S(1)}, f32[1,128]{1,0:T(1,128)S(1)}, u32[]{:S(2)}, u32[]{:S(2)}) %collective-permute-start.6) | collective-permute-done | bytes 544 | tf_op jit(solution)/shard_map/ppermute | solution.py:218
  15.0 2.9 %collective-permute-start.7 = (f32[1,128]{1,0:T(1,128)S(1)}, f32[1,128]{1,0:T(1,128)S(1)}, u32[]{:S(2)}, u32[]{:S(2)}) collective-permute-start(f32[1,128]{1,0:T(1,128)S(1)} %add.1), channel_id=1, source_target_pairs={{0,8},{2,10},{4,12},{6,14},{9,1},{11,3},{13,5},{15,7},{1,0},{3,2},... | collective-permute-start | bytes 1544 | tf_op jit(solution)/shard_map/ppermute | solution.py:219
  17.9 1.3 %collective-permute-done.7 = f32[1,128]{1,0:T(1,128)S(1)} collective-permute-done((f32[1,128]{1,0:T(1,128)S(1)}, f32[1,128]{1,0:T(1,128)S(1)}, u32[]{:S(2)}, u32[]{:S(2)}) %collective-permute-start.7) | collective-permute-done | bytes 544 | tf_op jit(solution)/shard_map/ppermute | solution.py:219
  19.2 0.5 %copy.7 = f32[1,128]{1,0:T(1,128)} copy(f32[1,128]{1,0:T(1,128)S(1)} %collective-permute-done.7) | data formatting | bytes 1024
  (11 shorter events, 0.0 us)
Async XLA Ops:
  0.0 4.6 %copy-start = (bf16[1,384,2560]{2,1,0:T(8,128)(2,1)S(1)}, bf16[1,384,2560]{2,1,0:T(8,128)(2,1)}, u32[]{:S(2)}) copy-start(bf16[1,384,2560]{2,1,0:T(8,128)(2,1)} %acts_ref.1) | copy-start | bytes 5898244
  0.0 4.6 %copy-start.1 = (bf16[1,384,2560]{2,1,0:T(8,128)(2,1)S(1)}, bf16[1,384,2560]{2,1,0:T(8,128)(2,1)}, u32[]{:S(2)}) copy-start(bf16[1,384,2560]{2,1,0:T(8,128)(2,1)} %grads_ref.1) | copy-start | bytes 5898244
  0.0 7.5 %copy-start.4 = (s32[1,256]{1,0:T(1,128)S(1)}, s32[1,256]{1,0:T(1,128)}, u32[]{:S(2)}) copy-start(s32[1,256]{1,0:T(1,128)} %picks_ref.1) | copy-start | bytes 3076
  0.0 11.8 %collective-permute-start.2 = (bf16[32,2048]{1,0:T(8,128)(2,1)}, bf16[32,2048]{1,0:T(8,128)(2,1)S(1)}, u32[]{:S(2)}, u32[]{:S(2)}) collective-permute-start(bf16[32,2048]{1,0:T(8,128)(2,1)} %refs_0_.1), channel_id=1, source_target_pairs={{0,2},{2,0},{4,6},{6,4},{8,10},{10,8},{12,14},{14,12},{1,3},{3,1},... | collective-permute-start | bytes 393224 | tf_op jit(solution)/shard_map/ppermute | solution.py:145
  3.0 8.8 %collective-permute-start.3 = (bf16[32,2048]{1,0:T(8,128)(2,1)}, bf16[32,2048]{1,0:T(8,128)(2,1)S(1)}, u32[]{:S(2)}, u32[]{:S(2)}) collective-permute-start(bf16[32,2048]{1,0:T(8,128)(2,1)} %refs_0_.1), channel_id=1, source_target_pairs={{0,4},{2,6},{4,0},{6,2},{8,12},{10,14},{12,8},{14,10},{1,5},{3,7},... | collective-permute-start | bytes 393224 | tf_op jit(solution)/shard_map/ppermute | solution.py:145
  4.6 7.2 %collective-permute-start.4 = (bf16[32,2048]{1,0:T(8,128)(2,1)}, bf16[32,2048]{1,0:T(8,128)(2,1)S(1)}, u32[]{:S(2)}, u32[]{:S(2)}) collective-permute-start(bf16[32,2048]{1,0:T(8,128)(2,1)} %refs_0_.1), channel_id=1, source_target_pairs={{0,6},{2,4},{4,2},{6,0},{8,14},{10,12},{12,10},{14,8},{1,7},{3,5},... | collective-permute-start | bytes 393224 | tf_op jit(solution)/shard_map/ppermute | solution.py:145
  4.6 1.1 %copy-start.2 = (bf16[2560,128]{1,0:T(8,128)(2,1)S(1)}, bf16[2560,128]{1,0:T(8,128)(2,1)}, u32[]{:S(2)}) copy-start(bf16[2560,128]{1,0:T(8,128)(2,1)} %proj_ref.1) | copy-start | bytes 1966084
  6.9 1.4 %collective-permute-start = (f32[192,128]{1,0:T(8,128)S(1)}, f32[192,128]{1,0:T(8,128)S(1)}, u32[]{:S(2)}, u32[]{:S(2)}) collective-permute-start(f32[192,128]{1,0:T(8,128)S(1)} %get-tuple-element.12.refs_0_), channel_id=1, source_target_pairs={{0,1},{1,0},{2,3},{3,2},{4,5},{5,4},{6,7},{7,6},{8,9},{9,8},{10,11... | collective-permute-start | bytes 294920 | tf_op jit(solution)/shard_map/ppermute | solution.py:158
  7.0 1.4 %collective-permute-start.1 = (f32[192,128]{1,0:T(8,128)S(1)}, f32[192,128]{1,0:T(8,128)S(1)}, u32[]{:S(2)}, u32[]{:S(2)}) collective-permute-start(f32[192,128]{1,0:T(8,128)S(1)} %get-tuple-element.13.refs_1_), channel_id=1, source_target_pairs={{0,1},{1,0},{2,3},{3,2},{4,5},{5,4},{6,7},{7,6},{8,9},{9,8},{10,11... | collective-permute-start | bytes 294920 | tf_op jit(solution)/shard_map/ppermute | solution.py:158
  8.7 4.6 %copy-start.3 = (bf16[32,2048]{1,0:T(8,128)(2,1)S(1)}, bf16[32,2048]{1,0:T(8,128)(2,1)}, u32[]{:S(2)}) copy-start(bf16[32,2048]{1,0:T(8,128)(2,1)} %refs_0_.1) | copy-start | bytes 393220
  8.7 4.6 %collective-permute-start.5 = (bf16[16,128]{1,0:T(8,128)(2,1)S(1)}, bf16[16,128]{1,0:T(8,128)(2,1)S(1)}, u32[]{:S(2)}, u32[]{:S(2)}) collective-permute-start(bf16[16,128]{1,0:T(8,128)(2,1)S(1)} %sketch.1.refs_0_.own_ref), channel_id=1, source_target_pairs={{0,8},{2,10},{4,12},{6,14},{8,0},{10,2},{12,4},{14,6},{1,9},{3,11}... | collective-permute-start | bytes 12296 | tf_op jit(solution)/shard_map/ppermute | solution.py:179
  13.8 1.2 %collective-permute-start.6 = (f32[1,128]{1,0:T(1,128)S(1)}, f32[1,128]{1,0:T(1,128)S(1)}, u32[]{:S(2)}, u32[]{:S(2)}) collective-permute-start(f32[1,128]{1,0:T(1,128)S(1)} %get-tuple-element.16), channel_id=1, source_target_pairs={{0,1},{1,0},{2,3},{3,2},{4,5},{5,4},{6,7},{7,6},{8,9},{9,8},{10,11... | collective-permute-start | bytes 1544 | tf_op jit(solution)/shard_map/ppermute | solution.py:218
  15.0 4.2 %collective-permute-start.7 = (f32[1,128]{1,0:T(1,128)S(1)}, f32[1,128]{1,0:T(1,128)S(1)}, u32[]{:S(2)}, u32[]{:S(2)}) collective-permute-start(f32[1,128]{1,0:T(1,128)S(1)} %add.1), channel_id=1, source_target_pairs={{0,8},{2,10},{4,12},{6,14},{9,1},{11,3},{13,5},{15,7},{1,0},{3,2},... | collective-permute-start | bytes 1544 | tf_op jit(solution)/shard_map/ppermute | solution.py:219

commit v13 on v11

--- a/solution.py
+++ b/solution.py
@@ -17,7 +17,7 @@
     out_ref[...] = jnp.zeros_like(out_ref)
 
 
-def project_kernel(rank, first_ref, ready_ref, acts_ref, grads_ref, proj_ref, *outs):
+def project_kernel(rank, first_ref, acts_ref, grads_ref, proj_ref, *outs):
     rows = outs[0].shape[0]
     column = lax.broadcasted_iota(jnp.int32, (rows, 2 * rank), 1)
     for i, out_ref in enumerate(outs):
@@ -74,18 +74,18 @@
             out_ref[:, j * LANES : (j + 1) * LANES] = rows.astype(BF16)
 
 
-def score_kernel(mates, first_ref, second_ref, *refs):
-    queries, out_ref = refs[:-1], refs[-1]
-    own_queries = queries[0].shape[0]
-    scores = sum(
-        lax.dot_general(
-            jnp.concatenate([queries[2 * r + i][...] for r in range(mates)], axis=0),
-            flat_ref[...],
-            (((1,), (1,)), ((), ())),
-            preferred_element_type=F32,
-        )
-        for i, flat_ref in enumerate((first_ref, second_ref))
-    ).T
+def score_kernel(first_ref, second_ref, own_ref, other_ref, out_ref):
+    contract = (((1,), (1,)), ((), ()))
+    out_ref[...] = lax.dot_general(
+        first_ref[...], own_ref[...], contract, preferred_element_type=F32
+    ) + lax.dot_general(second_ref[...], other_ref[...], contract, preferred_element_type=F32)
+
+
+def arrange_kernel(*refs):
+    parts, out_ref = refs[:-1], refs[-1]
+    mates = len(parts)
+    own_queries = parts[0].shape[1]
+    scores = jnp.concatenate([part[...] for part in parts], axis=1)
     member = lax.rem(lax.axis_index("dp"), mates)
     width = scores.shape[1]
     block = lax.broadcasted_iota(jnp.int32, scores.shape, 1) // own_queries
@@ -93,10 +93,16 @@
     while step < mates:
         up = pltpu.roll(scores, step * own_queries, 1)
         down = pltpu.roll(scores, width - step * own_queries, 1)
-        swapped = jnp.where(block & step == 0, down, up)
-        scores = jnp.where(member & step == 0, scores, swapped)
+        exchanged = jnp.where(block & step == 0, down, up)
+        scores = jnp.where(member & step == 0, scores, exchanged)
         step *= 2
     out_ref[...] = scores[0:1, :]
+
+
+def store_kernel(row_ref, out_ref, sem):
+    copy = pltpu.make_async_copy(row_ref, out_ref, sem)
+    copy.start()
+    copy.wait()
 
 
 def on_device(activations, out_grads, projections, sample_index, queries):
@@ -128,13 +134,12 @@
         name="first",
     )()
     sent, first = lax.optimization_barrier((queries, first))
-    own_swapped = lax.ppermute(sent, "tensor", swap)
     halves = [queries]
     for r in range(1, mates):
         halves.append(lax.ppermute(sent, "dp", [(d, d ^ r) for d in range(clips)]))
     partial = pl.pallas_call(
         functools.partial(project_kernel, rank),
-        in_specs=[vmem] * 5,
+        in_specs=[vmem] * 4,
         out_specs=[vmem] * PIECES,
         out_shape=[jax.ShapeDtypeStruct((tokens // PIECES, 2 * rank), F32)] * PIECES,
         compiler_params=pltpu.CompilerParams(vmem_limit_bytes=16 << 20),
@@ -142,7 +147,7 @@
             flops=8 * tokens * units * rank, bytes_accessed=4 * tokens * units, transcendentals=0
         ),
         name="project",
-    )(first, own_swapped, activations, out_grads, projections)
+    )(first, activations, out_grads, projections)
 
     other = [lax.ppermute(part, "tensor", swap) for part in partial]
     count = pl.pallas_call(
@@ -166,10 +171,11 @@
     )(count, *partial, *other)
 
     far_sketch = lax.ppermute(sketch, both, there)
-    taken = [queries, own_swapped]
-    for half in halves[1:]:
+    swapped = []
+    for half in halves:
         half, sketch = lax.optimization_barrier((half, sketch))
-        taken += [half, lax.ppermute(half, "tensor", swap)]
+        swapped.append(lax.ppermute(half, "tensor", swap))
+
     width = mates * own_queries
     flats = pl.pallas_call(
         functools.partial(flatten_kernel, mates),
@@ -181,15 +187,38 @@
         cost_estimate=pl.CostEstimate(flops=1 << 34, bytes_accessed=64 << 20, transcendentals=0),
         name="flatten",
     )(sketch, far_sketch)
+    small = pl.CostEstimate(flops=1, bytes_accessed=1, transcendentals=0)
+    few = pltpu.CompilerParams(vmem_limit_bytes=8 << 20)
+    parts = [
+        pl.pallas_call(
+            score_kernel,
+            in_specs=[vmem] * 4,
+            out_specs=vmem,
+            out_shape=jax.ShapeDtypeStruct((slots, own_queries), F32),
+            compiler_params=few,
+            cost_estimate=small,
+            name="score",
+        )(*flats, half, other)
+        for half, other in zip(halves, swapped)
+    ]
     scores = pl.pallas_call(
-        functools.partial(score_kernel, mates),
-        in_specs=[vmem] * (2 * mates + 2),
+        arrange_kernel,
+        in_specs=[vmem] * mates,
         out_specs=vmem,
         out_shape=jax.ShapeDtypeStruct((1, width), F32),
-        compiler_params=pltpu.CompilerParams(vmem_limit_bytes=(16 + mates // 2) << 20),
-        name="score",
-    )(*flats, *taken)
-    return lax.ppermute(scores, both, back)
+        compiler_params=few,
+        cost_estimate=small,
+        name="arrange",
+    )(*parts)
+    return pl.pallas_call(
+        store_kernel,
+        in_specs=[vmem],
+        out_specs=pl.BlockSpec(memory_space=pl.ANY),
+        out_shape=jax.ShapeDtypeStruct((1, width), F32),
+        scratch_shapes=[pltpu.SemaphoreType.DMA],
+        compiler_params=few,
+        name="store",
+    )(lax.ppermute(scores, both, back))
 
 
 def solution(mesh):

time: 18.7 us -> 17.9 us (0.957)
  waiting for transfers between devices: 5.31 us -> 2.93 us
  starting transfers between devices: 9.16 us -> 10.3 us
  Pallas kernels: 2.34 us -> 3.26 us
  local copies, waits for them, and re-layouts: 1.61 us -> 1.1 us
    ppermute x3, waiting for transfers between devices: 2.3 us -> 0.01 us  [on_device(): halves.append(lax.ppermute(sent, 'dp', [(d, d ^ r) for d in range(clips)]))]
    pallas_call x1 -> x6, Pallas kernels: 0.58 us -> 1.5 us  [the longest x4 0.76 us: on_device(): pl.pallas_call(score_kernel, in_specs=[vmem] * 4, out_specs=vmem, out_sha...]
    ppermute x5, starting transfers between devices: 4.08 us -> 4.78 us  [the longest x4 3.38 us: on_device(): swapped.append(lax.ppermute(half, 'tensor', swap))]
    unnamed x11 -> x10, local copies, waits for them, and re-layouts: 1.61 us -> 1.1 us
    ppermute x3, starting transfers between devices: 4.15 us -> 4.59 us  [on_device(): halves.append(lax.ppermute(sent, 'dp', [(d, d ^ r) for d in range(clips)]))]
  transfers between devices with their start and end apart: 11 -> 11, of which waited for: 6 -> 4; matrix products, arithmetic and copies ran while one was open for 0% -> 0% of each run, Pallas kernels for 10% -> 13%
where the time goes in v13:
time: 17.9 us; the launch traced here: 17.7 us
  starting transfers between devices  10.3 us (58%)
  Pallas kernels  3.26 us (18%)
  waiting for transfers between devices  2.93 us (16%)
  local copies, waits for them, and re-layouts  1.1 us (6%)
    ppermute x3, starting transfers between devices, on_device(): halves.append(lax.ppermute(sent, 'dp', [(d, d ^ r) for d in range(clips)]))  4.59 us
    ppermute x4, starting transfers between devices, on_device(): swapped.append(lax.ppermute(half, 'tensor', swap))  3.38 us
    ppermute x1, starting transfers between devices, on_device(): lax.ppermute(scores, both, back)  1.4 us
    ppermute x1, waiting for transfers between devices, on_device(): lax.ppermute(scores, both, back)  1.3 us
    pallas_call x1, Pallas kernels, on_device(): pl.pallas_call(functools.partial(project_kernel, rank), in_specs=[vmem] *...  1.17 us
    unnamed x10, local copies, waits for them, and re-layouts  1.1 us
    ppermute x1, waiting for transfers between devices, on_device(): far_sketch = lax.ppermute(sketch, both, there)  0.88 us
    pallas_call x4, Pallas kernels, on_device(): pl.pallas_call(score_kernel, in_specs=[vmem] * 4, out_specs=vmem, out_sha...  0.76 us
  transfers between devices with their start and end apart: 11, of which 4 were waited for; matrix products, arithmetic and copies ran while one was open for 0% of the time, Pallas kernels for 13%

profile of v13, /device:TPU:0, one launch (start us, length us, event | category | flops | bytes accessed | tf_op | source)
XLA Modules:
  0.0 17.7 jit_solution(6019111996661638106)
XLA Ops:
  0.0 3.0 %collective-permute-start.2 = (bf16[32,2048]{1,0:T(8,128)(2,1)}, bf16[32,2048]{1,0:T(8,128)(2,1)S(1)}, u32[]{:S(2)}, u32[]{:S(2)}) collective-permute-start(bf16[32,2048]{1,0:T(8,128)(2,1)} %own_ref.1), channel_id=1, source_target_pairs={{0,2},{2,0},{4,6},{6,4},{8,10},{10,8},{12,14},{14,12},{1,3},{3,1},... | collective-permute-start | bytes 393224 | tf_op jit(solution)/shard_map/ppermute | solution.py:139
  3.0 1.6 %collective-permute-start.1 = (bf16[32,2048]{1,0:T(8,128)(2,1)}, bf16[32,2048]{1,0:T(8,128)(2,1)S(1)}, u32[]{:S(2)}, u32[]{:S(2)}) collective-permute-start(bf16[32,2048]{1,0:T(8,128)(2,1)} %own_ref.1), channel_id=1, source_target_pairs={{0,4},{2,6},{4,0},{6,2},{8,12},{10,14},{12,8},{14,10},{1,5},{3,7},... | collective-permute-start | bytes 393224 | tf_op jit(solution)/shard_map/ppermute | solution.py:139
  4.6 1.1 %copy-done.2 = bf16[2560,128]{1,0:T(8,128)(2,1)S(1)} copy-done((bf16[2560,128]{1,0:T(8,128)(2,1)S(1)}, bf16[2560,128]{1,0:T(8,128)(2,1)}, u32[]{:S(2)}) %copy-start.2) | copy-done | bytes 655384
  5.7 1.2 %project.1 = (f32[192,128]{1,0:T(8,128)S(1)}, f32[192,128]{1,0:T(8,128)S(1)}) custom-call(f32[8,128]{1,0:T(8,128)S(1)} %first.1.first_ref, bf16[1,384,2560]{2,1,0:T(8,128)(2,1)S(1)} %copy-done, bf16[1,384,2560]{2,1,0:T(8,128)(2,1)S(1)} %copy-done.1, bf16[2560,128]{1,0:T(8,128)(2,1)S(1)} %copy-done.2), custom_call_target="tpu_custom_call" | custom-call | flops 503316480 | bytes 3932160 | tf_op jit(solution)/shard_map/project/pallas_call | solution.py:140
  6.9 0.1 collective-permute-start.3
  7.0 0.5 %collective-permute-start.4 = (f32[192,128]{1,0:T(8,128)S(1)}, f32[192,128]{1,0:T(8,128)S(1)}, u32[]{:S(2)}, u32[]{:S(2)}) collective-permute-start(f32[192,128]{1,0:T(8,128)S(1)} %get-tuple-element.22.refs_1_), channel_id=1, source_target_pairs={{0,1},{1,0},{2,3},{3,2},{4,5},{5,4},{6,7},{7,6},{8,9},{9,8},{10,11... | collective-permute-start | bytes 294920 | tf_op jit(solution)/shard_map/ppermute | solution.py:152
  7.5 0.2 %count.1.count_ref = f32[384,128]{1,0:T(8,128)S(1)} custom-call(s32[1,256]{1,0:T(1,128)S(1)} %copy-done.4), custom_call_target="tpu_custom_call" | custom-call | flops 1 | bytes 1 | tf_op jit(solution)/shard_map/count/pallas_call | solution.py:153
  7.7 0.6 %collective-permute-done.3.refs_2_ = f32[192,128]{1,0:T(8,128)S(1)} collective-permute-done((f32[192,128]{1,0:T(8,128)S(1)}, f32[192,128]{1,0:T(8,128)S(1)}, u32[]{:S(2)}, u32[]{:S(2)}) %collective-permute-start.3) | collective-permute-done | bytes 98336 | tf_op jit(solution)/shard_map/ppermute | solution.py:152
  8.2 0.2 collective-permute-done.4.refs_3_
  8.4 0.4 %sketch.1.own_ref = bf16[32,128]{1,0:T(8,128)(2,1)S(1)} custom-call(f32[384,128]{1,0:T(8,128)S(1)} %count.1.count_ref, f32[192,128]{1,0:T(8,128)S(1)} %get-tuple-element.21.refs_0_, f32[192,128]{1,0:T(8,128)S(1)} %get-tuple-element.22.refs_1_, f32[192,128]{1,0:T(8,128)S(1)} %collective-permute-done.3.refs_2_, f32[192,128]{1,0:T(8,128)S(1)} %collective-permute-done.4.refs_3_), custom_call_target="tpu_custom_call" | custom-call | flops 1 | bytes 1 | tf_op jit(solution)/shard_map/sketch/pallas_call | solution.py:162
  8.8 0.4 %collective-permute-start.5 = (bf16[32,128]{1,0:T(8,128)(2,1)S(1)}, bf16[32,128]{1,0:T(8,128)(2,1)S(1)}, u32[]{:S(2)}, u32[]{:S(2)}) collective-permute-start(bf16[32,128]{1,0:T(8,128)(2,1)S(1)} %sketch.1.own_ref), channel_id=1, source_target_pairs={{1,9},{3,11},{5,13},{7,15},{8,0},{10,2},{12,4},{14,6},{0,1},{2,3},... | collective-permute-start | bytes 24584 | tf_op jit(solution)/shard_map/ppermute | solution.py:173
  9.1 2.7 %collective-permute-start.6 = (bf16[32,2048]{1,0:T(8,128)(2,1)S(1)}, bf16[32,2048]{1,0:T(8,128)(2,1)S(1)}, u32[]{:S(2)}, u32[]{:S(2)}) collective-permute-start(bf16[32,2048]{1,0:T(8,128)(2,1)S(1)} %copy-done.3), channel_id=1, source_target_pairs={{0,1},{1,0},{2,3},{3,2},{4,5},{5,4},{6,7},{7,6},{8,9},{9,8},{10,11... | collective-permute-start | bytes 393224 | tf_op jit(solution)/shard_map/ppermute | solution.py:177
  11.9 0.1 collective-permute-start.9
  11.9 0.5 %collective-permute-start.8 = (bf16[32,2048]{1,0:T(8,128)(2,1)S(1)}, bf16[32,2048]{1,0:T(8,128)(2,1)S(1)}, u32[]{:S(2)}, u32[]{:S(2)}) collective-permute-start(bf16[32,2048]{1,0:T(8,128)(2,1)S(1)} %collective-permute-done.1.own_ref), channel_id=1, source_target_pairs={{0,1},{1,0},{2,3},{3,2},{4,5},{5,4},{6,7},{7,6},{8,9},{9,8},{10,11... | collective-permute-start | bytes 393224 | tf_op jit(solution)/shard_map/ppermute | solution.py:177
  12.4 0.1 collective-permute-start.7
  12.5 0.9 %collective-permute-done.5.far_ref = bf16[32,128]{1,0:T(8,128)(2,1)S(1)} collective-permute-done((bf16[32,128]{1,0:T(8,128)(2,1)S(1)}, bf16[32,128]{1,0:T(8,128)(2,1)S(1)}, u32[]{:S(2)}, u32[]{:S(2)}) %collective-permute-start.5) | collective-permute-done | bytes 8224 | tf_op jit(solution)/shard_map/ppermute | solution.py:173
  13.4 0.2 %score.4.refs_0_ = f32[8,32]{1,0:T(8,128)S(1)} custom-call(bf16[8,2048]{1,0:T(8,128)(2,1)S(1)} %get-tuple-element.27.first_ref, bf16[8,2048]{1,0:T(8,128)(2,1)S(1)} %get-tuple-element.28.second_ref, bf16[32,2048]{1,0:T(8,128)(2,1)S(1)} %copy-done.3, bf16[32,2048]{1,0:T(8,128)(2,1)S(1)} %collective-permute-done.6.other_ref), custom_call_target="tpu_custom_call" | custom-call | flops 1 | bytes 1 | tf_op jit(solution)/shard_map/score/pallas_call | solution.py:193
  13.6 0.2 %score.7.refs_3_ = f32[8,32]{1,0:T(8,128)S(1)} custom-call(bf16[8,2048]{1,0:T(8,128)(2,1)S(1)} %get-tuple-element.27.first_ref, bf16[8,2048]{1,0:T(8,128)(2,1)S(1)} %get-tuple-element.28.second_ref, bf16[32,2048]{1,0:T(8,128)(2,1)S(1)} %collective-permute-done.own_ref, bf16[32,2048]{1,0:T(8,128)(2,1)S(1)} %collective-permute-done.9.other_ref), custom_call_target="tpu_custom_call" | custom-call | flops 1 | bytes 1 | tf_op jit(solution)/shard_map/score/pallas_call | solution.py:193
  13.8 0.2 %score.6.refs_2_ = f32[8,32]{1,0:T(8,128)S(1)} custom-call(bf16[8,2048]{1,0:T(8,128)(2,1)S(1)} %get-tuple-element.27.first_ref, bf16[8,2048]{1,0:T(8,128)(2,1)S(1)} %get-tuple-element.28.second_ref, bf16[32,2048]{1,0:T(8,128)(2,1)S(1)} %collective-permute-done.1.own_ref, bf16[32,2048]{1,0:T(8,128)(2,1)S(1)} %collective-permute-done.8.other_ref), custom_call_target="tpu_custom_call" | custom-call | flops 1 | bytes 1 | tf_op jit(solution)/shard_map/score/pallas_call | solution.py:193
  14.0 0.2 %score.5.refs_1_ = f32[8,32]{1,0:T(8,128)S(1)} custom-call(bf16[8,2048]{1,0:T(8,128)(2,1)S(1)} %get-tuple-element.27.first_ref, bf16[8,2048]{1,0:T(8,128)(2,1)S(1)} %get-tuple-element.28.second_ref, bf16[32,2048]{1,0:T(8,128)(2,1)S(1)} %collective-permute-done.2.own_ref, bf16[32,2048]{1,0:T(8,128)(2,1)S(1)} %collective-permute-done.7.other_ref), custom_call_target="tpu_custom_call" | custom-call | flops 1 | bytes 1 | tf_op jit(solution)/shard_map/score/pallas_call | solution.py:193
  14.2 0.2 %arrange.1 = f32[1,128]{1,0:T(1,128)S(1)} custom-call(f32[8,32]{1,0:T(8,128)S(1)} %score.4.refs_0_, f32[8,32]{1,0:T(8,128)S(1)} %score.5.refs_1_, f32[8,32]{1,0:T(8,128)S(1)} %score.6.refs_2_, f32[8,32]{1,0:T(8,128)S(1)} %score.7.refs_3_), custom_call_target="tpu_custom_call" | custom-call | flops 1 | bytes 1 | tf_op jit(solution)/shard_map/arrange/pallas_call | solution.py:204
  14.4 1.4 %collective-permute-start.10 = (f32[1,128]{1,0:T(1,128)S(1)}, f32[1,128]{1,0:T(1,128)S(1)}, u32[]{:S(2)}, u32[]{:S(2)}) collective-permute-start(f32[1,128]{1,0:T(1,128)S(1)} %arrange.1), channel_id=1, source_target_pairs={{9,1},{11,3},{13,5},{15,7},{0,8},{2,10},{4,12},{6,14},{1,0},{3,2},... | collective-permute-start | bytes 1544 | tf_op jit(solution)/shard_map/ppermute | solution.py:221
  15.8 1.3 %collective-permute-done.10.row_ref = f32[1,128]{1,0:T(1,128)S(1)} collective-permute-done((f32[1,128]{1,0:T(1,128)S(1)}, f32[1,128]{1,0:T(1,128)S(1)}, u32[]{:S(2)}, u32[]{:S(2)}) %collective-permute-start.10) | collective-permute-done | bytes 544 | tf_op jit(solution)/shard_map/ppermute | solution.py:221
  17.1 0.5 %store.1 = f32[1,128]{1,0:T(1,128)} custom-call(f32[1,128]{1,0:T(1,128)S(1)} %collective-permute-done.10.row_ref), custom_call_target="tpu_custom_call" | custom-call | tf_op jit(solution)/shard_map/store/pallas_call | solution.py:213
  (19 shorter events, 0.1 us)
Async XLA Ops:
  0.0 4.6 %copy-start = (bf16[1,384,2560]{2,1,0:T(8,128)(2,1)S(1)}, bf16[1,384,2560]{2,1,0:T(8,128)(2,1)}, u32[]{:S(2)}) copy-start(bf16[1,384,2560]{2,1,0:T(8,128)(2,1)} %acts_ref.1) | copy-start | bytes 5898244
  0.0 4.6 %copy-start.1 = (bf16[1,384,2560]{2,1,0:T(8,128)(2,1)S(1)}, bf16[1,384,2560]{2,1,0:T(8,128)(2,1)}, u32[]{:S(2)}) copy-start(bf16[1,384,2560]{2,1,0:T(8,128)(2,1)} %grads_ref.1) | copy-start | bytes 5898244
  0.0 7.5 %copy-start.4 = (s32[1,256]{1,0:T(1,128)S(1)}, s32[1,256]{1,0:T(1,128)}, u32[]{:S(2)}) copy-start(s32[1,256]{1,0:T(1,128)} %picks_ref.1) | copy-start | bytes 3076
  0.0 11.8 %collective-permute-start.2 = (bf16[32,2048]{1,0:T(8,128)(2,1)}, bf16[32,2048]{1,0:T(8,128)(2,1)S(1)}, u32[]{:S(2)}, u32[]{:S(2)}) collective-permute-start(bf16[32,2048]{1,0:T(8,128)(2,1)} %own_ref.1), channel_id=1, source_target_pairs={{0,2},{2,0},{4,6},{6,4},{8,10},{10,8},{12,14},{14,12},{1,3},{3,1},... | collective-permute-start | bytes 393224 | tf_op jit(solution)/shard_map/ppermute | solution.py:139
  3.0 8.8 %collective-permute-start.1 = (bf16[32,2048]{1,0:T(8,128)(2,1)}, bf16[32,2048]{1,0:T(8,128)(2,1)S(1)}, u32[]{:S(2)}, u32[]{:S(2)}) collective-permute-start(bf16[32,2048]{1,0:T(8,128)(2,1)} %own_ref.1), channel_id=1, source_target_pairs={{0,4},{2,6},{4,0},{6,2},{8,12},{10,14},{12,8},{14,10},{1,5},{3,7},... | collective-permute-start | bytes 393224 | tf_op jit(solution)/shard_map/ppermute | solution.py:139
  4.6 7.3 %collective-permute-start = (bf16[32,2048]{1,0:T(8,128)(2,1)}, bf16[32,2048]{1,0:T(8,128)(2,1)S(1)}, u32[]{:S(2)}, u32[]{:S(2)}) collective-permute-start(bf16[32,2048]{1,0:T(8,128)(2,1)} %own_ref.1), channel_id=1, source_target_pairs={{0,6},{2,4},{4,2},{6,0},{8,14},{10,12},{12,10},{14,8},{1,7},{3,5},... | collective-permute-start | bytes 393224 | tf_op jit(solution)/shard_map/ppermute | solution.py:139
  4.6 1.1 %copy-start.2 = (bf16[2560,128]{1,0:T(8,128)(2,1)S(1)}, bf16[2560,128]{1,0:T(8,128)(2,1)}, u32[]{:S(2)}) copy-start(bf16[2560,128]{1,0:T(8,128)(2,1)} %proj_ref.1) | copy-start | bytes 1966084
  5.7 3.4 %copy-start.3 = (bf16[32,2048]{1,0:T(8,128)(2,1)S(1)}, bf16[32,2048]{1,0:T(8,128)(2,1)}, u32[]{:S(2)}) copy-start(bf16[32,2048]{1,0:T(8,128)(2,1)} %own_ref.1) | copy-start | bytes 393220
  6.9 1.4 %collective-permute-start.3 = (f32[192,128]{1,0:T(8,128)S(1)}, f32[192,128]{1,0:T(8,128)S(1)}, u32[]{:S(2)}, u32[]{:S(2)}) collective-permute-start(f32[192,128]{1,0:T(8,128)S(1)} %get-tuple-element.21.refs_0_), channel_id=1, source_target_pairs={{0,1},{1,0},{2,3},{3,2},{4,5},{5,4},{6,7},{7,6},{8,9},{9,8},{10,11... | collective-permute-start | bytes 294920 | tf_op jit(solution)/shard_map/ppermute | solution.py:152
  7.0 1.4 %collective-permute-start.4 = (f32[192,128]{1,0:T(8,128)S(1)}, f32[192,128]{1,0:T(8,128)S(1)}, u32[]{:S(2)}, u32[]{:S(2)}) collective-permute-start(f32[192,128]{1,0:T(8,128)S(1)} %get-tuple-element.22.refs_1_), channel_id=1, source_target_pairs={{0,1},{1,0},{2,3},{3,2},{4,5},{5,4},{6,7},{7,6},{8,9},{9,8},{10,11... | collective-permute-start | bytes 294920 | tf_op jit(solution)/shard_map/ppermute | solution.py:152
  8.8 4.6 %collective-permute-start.5 = (bf16[32,128]{1,0:T(8,128)(2,1)S(1)}, bf16[32,128]{1,0:T(8,128)(2,1)S(1)}, u32[]{:S(2)}, u32[]{:S(2)}) collective-permute-start(bf16[32,128]{1,0:T(8,128)(2,1)S(1)} %sketch.1.own_ref), channel_id=1, source_target_pairs={{1,9},{3,11},{5,13},{7,15},{8,0},{10,2},{12,4},{14,6},{0,1},{2,3},... | collective-permute-start | bytes 24584 | tf_op jit(solution)/shard_map/ppermute | solution.py:173
  9.1 4.3 %collective-permute-start.6 = (bf16[32,2048]{1,0:T(8,128)(2,1)S(1)}, bf16[32,2048]{1,0:T(8,128)(2,1)S(1)}, u32[]{:S(2)}, u32[]{:S(2)}) collective-permute-start(bf16[32,2048]{1,0:T(8,128)(2,1)S(1)} %copy-done.3), channel_id=1, source_target_pairs={{0,1},{1,0},{2,3},{3,2},{4,5},{5,4},{6,7},{7,6},{8,9},{9,8},{10,11... | collective-permute-start | bytes 393224 | tf_op jit(solution)/shard_map/ppermute | solution.py:177
  11.9 1.8 %collective-permute-start.9 = (bf16[32,2048]{1,0:T(8,128)(2,1)S(1)}, bf16[32,2048]{1,0:T(8,128)(2,1)S(1)}, u32[]{:S(2)}, u32[]{:S(2)}) collective-permute-start(bf16[32,2048]{1,0:T(8,128)(2,1)S(1)} %collective-permute-done.own_ref), channel_id=1, source_target_pairs={{0,1},{1,0},{2,3},{3,2},{4,5},{5,4},{6,7},{7,6},{8,9},{9,8},{10,11... | collective-permute-start | bytes 393224 | tf_op jit(solution)/shard_map/ppermute | solution.py:177
  11.9 1.9 %collective-permute-start.8 = (bf16[32,2048]{1,0:T(8,128)(2,1)S(1)}, bf16[32,2048]{1,0:T(8,128)(2,1)S(1)}, u32[]{:S(2)}, u32[]{:S(2)}) collective-permute-start(bf16[32,2048]{1,0:T(8,128)(2,1)S(1)} %collective-permute-done.1.own_ref), channel_id=1, source_target_pairs={{0,1},{1,0},{2,3},{3,2},{4,5},{5,4},{6,7},{7,6},{8,9},{9,8},{10,11... | collective-permute-start | bytes 393224 | tf_op jit(solution)/shard_map/ppermute | solution.py:177
  12.4 1.6 %collective-permute-start.7 = (bf16[32,2048]{1,0:T(8,128)(2,1)S(1)}, bf16[32,2048]{1,0:T(8,128)(2,1)S(1)}, u32[]{:S(2)}, u32[]{:S(2)}) collective-permute-start(bf16[32,2048]{1,0:T(8,128)(2,1)S(1)} %collective-permute-done.2.own_ref), channel_id=1, source_target_pairs={{0,1},{1,0},{2,3},{3,2},{4,5},{5,4},{6,7},{7,6},{8,9},{9,8},{10,11... | collective-permute-start | bytes 393224 | tf_op jit(solution)/shard_map/ppermute | solution.py:177
  14.4 2.7 %collective-permute-start.10 = (f32[1,128]{1,0:T(1,128)S(1)}, f32[1,128]{1,0:T(1,128)S(1)}, u32[]{:S(2)}, u32[]{:S(2)}) collective-permute-start(f32[1,128]{1,0:T(1,128)S(1)} %arrange.1), channel_id=1, source_target_pairs={{9,1},{11,3},{13,5},{15,7},{0,8},{2,10},{4,12},{6,14},{1,0},{3,2},... | collective-permute-start | bytes 1544 | tf_op jit(solution)/shard_map/ppermute | solution.py:221

commit v14 on v11

--- a/solution.py
+++ b/solution.py
@@ -17,17 +17,21 @@
     out_ref[...] = jnp.zeros_like(out_ref)
 
 
-def project_kernel(rank, first_ref, ready_ref, acts_ref, grads_ref, proj_ref, *outs):
+def project_kernel(rank, first_ref, acts_ref, grads_hbm, proj_ref, *refs):
+    outs, (grads, sems) = refs[:-2], refs[-2:]
     rows = outs[0].shape[0]
+    copies = []
+    for i in range(len(outs)):
+        part = pl.ds(i * rows, rows)
+        copies.append(pltpu.make_async_copy(grads_hbm.at[0, part, :], grads.at[part, :], sems.at[i]))
+        copies[-1].start()
+    left = jnp.dot(acts_ref[0], proj_ref[...], preferred_element_type=F32)
     column = lax.broadcasted_iota(jnp.int32, (rows, 2 * rank), 1)
     for i, out_ref in enumerate(outs):
         part = slice(i * rows, (i + 1) * rows)
-        term = jnp.dot(
-            jnp.concatenate([acts_ref[0, part, :], grads_ref[0, part, :]], axis=0),
-            proj_ref[...],
-            preferred_element_type=F32,
-        )
-        out_ref[...] = jnp.where(column < rank, term[0:rows], term[rows:])
+        copies[i].wait()
+        right = jnp.dot(grads[part, :], proj_ref[...], preferred_element_type=F32)
+        out_ref[...] = jnp.where(column < rank, left[part], right)
 
 
 def count_kernel(rank, picks_ref, out_ref):
@@ -71,30 +75,31 @@
         start = half * (slots * pairs // 2)
         for j in range(pairs // 2):
             rows = wide[pl.ds(pl.multiple_of(start + j * slots, slots), slots), :]
-            out_ref[:, j * LANES : (j + 1) * LANES] = rows.astype(BF16)
+            out_ref[:, j * LANES : (j + 1) * LANES] = rows
 
 
 def score_kernel(mates, first_ref, second_ref, *refs):
     queries, out_ref = refs[:-1], refs[-1]
-    own_queries = queries[0].shape[0]
-    scores = sum(
-        lax.dot_general(
-            jnp.concatenate([queries[2 * r + i][...] for r in range(mates)], axis=0),
-            flat_ref[...],
-            (((1,), (1,)), ((), ())),
-            preferred_element_type=F32,
-        )
-        for i, flat_ref in enumerate((first_ref, second_ref))
-    ).T
+    own_queries, entries = queries[0].shape
+    parts = []
+    for r in range(mates):
+        part = jnp.zeros((own_queries, LANES), F32)
+        for flat_ref, query_ref in ((first_ref, queries[2 * r]), (second_ref, queries[2 * r + 1])):
+            for j in range(entries // LANES):
+                lanes = slice(j * LANES, (j + 1) * LANES)
+                part += query_ref[:, lanes].astype(F32) * flat_ref[0:1, lanes]
+        parts.append(part)
+    width = mates * own_queries
+    scores = jnp.sum(jnp.concatenate(parts, axis=0).T, axis=0, keepdims=True)
+    scores = jnp.broadcast_to(scores, (8, width))
     member = lax.rem(lax.axis_index("dp"), mates)
-    width = scores.shape[1]
     block = lax.broadcasted_iota(jnp.int32, scores.shape, 1) // own_queries
     step = 1
     while step < mates:
         up = pltpu.roll(scores, step * own_queries, 1)
         down = pltpu.roll(scores, width - step * own_queries, 1)
-        swapped = jnp.where(block & step == 0, down, up)
-        scores = jnp.where(member & step == 0, scores, swapped)
+        exchanged = jnp.where(block & step == 0, down, up)
+        scores = jnp.where(member & step == 0, scores, exchanged)
         step *= 2
     out_ref[...] = scores[0:1, :]
 
@@ -124,25 +129,25 @@
         out_specs=vmem,
         out_shape=jax.ShapeDtypeStruct((8, LANES), F32),
         compiler_params=pltpu.CompilerParams(vmem_limit_bytes=1 << 20),
-        cost_estimate=pl.CostEstimate(flops=1 << 30, bytes_accessed=1, transcendentals=0),
+        cost_estimate=pl.CostEstimate(flops=11 << 26, bytes_accessed=1, transcendentals=0),
         name="first",
     )()
     sent, first = lax.optimization_barrier((queries, first))
-    own_swapped = lax.ppermute(sent, "tensor", swap)
     halves = [queries]
     for r in range(1, mates):
         halves.append(lax.ppermute(sent, "dp", [(d, d ^ r) for d in range(clips)]))
     partial = pl.pallas_call(
         functools.partial(project_kernel, rank),
-        in_specs=[vmem] * 5,
+        in_specs=[vmem, vmem, pl.BlockSpec(memory_space=pl.ANY), vmem],
         out_specs=[vmem] * PIECES,
         out_shape=[jax.ShapeDtypeStruct((tokens // PIECES, 2 * rank), F32)] * PIECES,
-        compiler_params=pltpu.CompilerParams(vmem_limit_bytes=16 << 20),
+        scratch_shapes=[pltpu.VMEM((tokens, units), BF16), pltpu.SemaphoreType.DMA((PIECES,))],
+        compiler_params=pltpu.CompilerParams(vmem_limit_bytes=52000 << 10),
         cost_estimate=pl.CostEstimate(
             flops=8 * tokens * units * rank, bytes_accessed=4 * tokens * units, transcendentals=0
         ),
         name="project",
-    )(first, own_swapped, activations, out_grads, projections)
+    )(first, activations, out_grads, projections)
 
     other = [lax.ppermute(part, "tensor", swap) for part in partial]
     count = pl.pallas_call(
@@ -166,21 +171,23 @@
     )(count, *partial, *other)
 
     far_sketch = lax.ppermute(sketch, both, there)
-    taken = [queries, own_swapped]
-    for half in halves[1:]:
+    swapped = []
+    for half in halves:
         half, sketch = lax.optimization_barrier((half, sketch))
-        taken += [half, lax.ppermute(half, "tensor", swap)]
+        swapped.append(lax.ppermute(half, "tensor", swap))
+
     width = mates * own_queries
     flats = pl.pallas_call(
         functools.partial(flatten_kernel, mates),
         in_specs=[vmem] * 2,
         out_specs=[vmem] * 2,
-        out_shape=[jax.ShapeDtypeStruct((slots, entries), BF16)] * 2,
+        out_shape=[jax.ShapeDtypeStruct((slots, entries), F32)] * 2,
         scratch_shapes=[pltpu.VMEM((pairs * slots, LANES), F32)],
         compiler_params=pltpu.CompilerParams(vmem_limit_bytes=8 << 20),
         cost_estimate=pl.CostEstimate(flops=1 << 34, bytes_accessed=64 << 20, transcendentals=0),
         name="flatten",
     )(sketch, far_sketch)
+    taken = [x for pair in zip(halves, swapped) for x in pair]
     scores = pl.pallas_call(
         functools.partial(score_kernel, mates),
         in_specs=[vmem] * (2 * mates + 2),

time: 18.7 us -> 19.1 us (1.021)
  the two profiles are of different devices: /device:TPU:0 before, /device:TPU:1 now
where the time goes in v14:
time: 19.1 us; the launch traced here: 19 us
  starting transfers between devices  8.91 us (47%)
  waiting for transfers between devices  4.97 us (26%)
  Pallas kernels  4.47 us (23%)
  local copies, waits for them, and re-layouts  0.53 us (3%)
    pallas_call x1, Pallas kernels, on_device(): pl.pallas_call(functools.partial(project_kernel, rank), in_specs=[vmem, v...  3.43 us
    ppermute x3, starting transfers between devices, on_device(): halves.append(lax.ppermute(sent, 'dp', [(d, d ^ r) for d in range(clips)]))  3.4 us
    ppermute x1, waiting for transfers between devices, on_device(): return lax.ppermute(scores, both, back)  2.97 us
    ppermute x1, starting transfers between devices, on_device(): far_sketch = lax.ppermute(sketch, both, there)  2.73 us
    ppermute x2, starting transfers between devices, on_device(): other = [lax.ppermute(part, 'tensor', swap) for part in partial]  1.38 us
    ppermute x4, starting transfers between devices, on_device(): swapped.append(lax.ppermute(half, 'tensor', swap))  1.07 us
    ppermute x2, waiting for transfers between devices, on_device(): other = [lax.ppermute(part, 'tensor', swap) for part in partial]  1.01 us
    ppermute x4, waiting for transfers between devices, on_device(): swapped.append(lax.ppermute(half, 'tensor', swap))  0.99 us
  transfers between devices with their start and end apart: 11, of which 7 were waited for; matrix products, arithmetic and copies ran while one was open for 0% of the time, Pallas kernels for 21%

profile of v14, /device:TPU:1, one launch (start us, length us, event | category | flops | bytes accessed | tf_op | source)
XLA Modules:
  0.0 19.0 jit_solution(11583740096163901020)
XLA Ops:
  0.0 0.0 copy-start.3
  0.0 0.0 copy-start.2
  0.0 2.1 %collective-permute-start.2 = (bf16[32,2048]{1,0:T(8,128)(2,1)}, bf16[32,2048]{1,0:T(8,128)(2,1)S(1)}, u32[]{:S(2)}, u32[]{:S(2)}) collective-permute-start(bf16[32,2048]{1,0:T(8,128)(2,1)} %refs_0_.1), channel_id=1, source_target_pairs={{0,2},{2,0},{4,6},{6,4},{8,10},{10,8},{12,14},{14,12},{1,3},{3,1},... | collective-permute-start | bytes 393224 | tf_op jit(solution)/shard_map/ppermute | solution.py:138
  2.1 1.3 %collective-permute-start.1 = (bf16[32,2048]{1,0:T(8,128)(2,1)}, bf16[32,2048]{1,0:T(8,128)(2,1)S(1)}, u32[]{:S(2)}, u32[]{:S(2)}) collective-permute-start(bf16[32,2048]{1,0:T(8,128)(2,1)} %refs_0_.1), channel_id=1, source_target_pairs={{0,4},{2,6},{4,0},{6,2},{8,12},{10,14},{12,8},{14,10},{1,5},{3,7},... | collective-permute-start | bytes 393224 | tf_op jit(solution)/shard_map/ppermute | solution.py:138
  3.4 3.4 %project.1 = (f32[192,128]{1,0:T(8,128)S(1)}, f32[192,128]{1,0:T(8,128)S(1)}) custom-call(f32[8,128]{1,0:T(8,128)S(1)} %first.1.first_ref, bf16[1,384,2560]{2,1,0:T(8,128)(2,1)S(1)} %copy-done, bf16[1,384,2560]{2,1,0:T(8,128)(2,1)} %grads_hbm.1, bf16[2560,128]{1,0:T(8,128)(2,1)S(1)} %copy-done.1), custom_call_target="tpu_custom_call" | custom-call | flops 503316480 | bytes 3932160 | tf_op jit(solution)/shard_map/project/pallas_call | solution.py:139
  6.9 1.3 %collective-permute-start.3 = (f32[192,128]{1,0:T(8,128)S(1)}, f32[192,128]{1,0:T(8,128)S(1)}, u32[]{:S(2)}, u32[]{:S(2)}) collective-permute-start(f32[192,128]{1,0:T(8,128)S(1)} %get-tuple-element.21.refs_0_), channel_id=1, source_target_pairs={{0,1},{1,0},{2,3},{3,2},{4,5},{5,4},{6,7},{7,6},{8,9},{9,8},{10,11... | collective-permute-start | bytes 294920 | tf_op jit(solution)/shard_map/ppermute | solution.py:152
  8.2 0.1 collective-permute-start.4
  8.3 0.2 %count.1.count_ref = f32[384,128]{1,0:T(8,128)S(1)} custom-call(s32[1,256]{1,0:T(1,128)S(1)} %copy-done.3), custom_call_target="tpu_custom_call" | custom-call | flops 1 | bytes 1 | tf_op jit(solution)/shard_map/count/pallas_call | solution.py:153
  8.5 0.7 %collective-permute-done.3.refs_2_ = f32[192,128]{1,0:T(8,128)S(1)} collective-permute-done((f32[192,128]{1,0:T(8,128)S(1)}, f32[192,128]{1,0:T(8,128)S(1)}, u32[]{:S(2)}, u32[]{:S(2)}) %collective-permute-start.3) | collective-permute-done | bytes 98336 | tf_op jit(solution)/shard_map/ppermute | solution.py:152
  9.1 0.4 %collective-permute-done.4.refs_3_ = f32[192,128]{1,0:T(8,128)S(1)} collective-permute-done((f32[192,128]{1,0:T(8,128)S(1)}, f32[192,128]{1,0:T(8,128)S(1)}, u32[]{:S(2)}, u32[]{:S(2)}) %collective-permute-start.4) | collective-permute-done | bytes 98336 | tf_op jit(solution)/shard_map/ppermute | solution.py:152
  9.5 0.4 %sketch.1.own_ref = bf16[32,128]{1,0:T(8,128)(2,1)S(1)} custom-call(f32[384,128]{1,0:T(8,128)S(1)} %count.1.count_ref, f32[192,128]{1,0:T(8,128)S(1)} %get-tuple-element.21.refs_0_, f32[192,128]{1,0:T(8,128)S(1)} %get-tuple-element.22.refs_1_, f32[192,128]{1,0:T(8,128)S(1)} %collective-permute-done.3.refs_2_, f32[192,128]{1,0:T(8,128)S(1)} %collective-permute-done.4.refs_3_), custom_call_target="tpu_custom_call" | custom-call | flops 1 | bytes 1 | tf_op jit(solution)/shard_map/sketch/pallas_call | solution.py:162
  9.9 2.7 %collective-permute-start.5 = (bf16[32,128]{1,0:T(8,128)(2,1)S(1)}, bf16[32,128]{1,0:T(8,128)(2,1)S(1)}, u32[]{:S(2)}, u32[]{:S(2)}) collective-permute-start(bf16[32,128]{1,0:T(8,128)(2,1)S(1)} %sketch.1.own_ref), channel_id=1, source_target_pairs={{1,9},{3,11},{5,13},{7,15},{8,0},{10,2},{12,4},{14,6},{0,1},{2,3},... | collective-permute-start | bytes 24584 | tf_op jit(solution)/shard_map/ppermute | solution.py:173
  12.6 0.0 collective-permute-start.6
  12.6 0.6 %collective-permute-start.9 = (bf16[32,2048]{1,0:T(8,128)(2,1)S(1)}, bf16[32,2048]{1,0:T(8,128)(2,1)S(1)}, u32[]{:S(2)}, u32[]{:S(2)}) collective-permute-start(bf16[32,2048]{1,0:T(8,128)(2,1)S(1)} %collective-permute-done.refs_6_), channel_id=1, source_target_pairs={{0,1},{1,0},{2,3},{3,2},{4,5},{5,4},{6,7},{7,6},{8,9},{9,8},{10,11... | collective-permute-start | bytes 393224 | tf_op jit(solution)/shard_map/ppermute | solution.py:177
  13.2 0.1 collective-permute-start.8
  13.3 0.4 %collective-permute-start.7 = (bf16[32,2048]{1,0:T(8,128)(2,1)S(1)}, bf16[32,2048]{1,0:T(8,128)(2,1)S(1)}, u32[]{:S(2)}, u32[]{:S(2)}) collective-permute-start(bf16[32,2048]{1,0:T(8,128)(2,1)S(1)} %collective-permute-done.2.refs_2_), channel_id=1, source_target_pairs={{0,1},{1,0},{2,3},{3,2},{4,5},{5,4},{6,7},{7,6},{8,9},{9,8},{10,11... | collective-permute-start | bytes 393224 | tf_op jit(solution)/shard_map/ppermute | solution.py:177
  13.7 0.2 %collective-permute-done.6.refs_1_ = bf16[32,2048]{1,0:T(8,128)(2,1)S(1)} collective-permute-done((bf16[32,2048]{1,0:T(8,128)(2,1)S(1)}, bf16[32,2048]{1,0:T(8,128)(2,1)S(1)}, u32[]{:S(2)}, u32[]{:S(2)}) %collective-permute-start.6) | collective-permute-done | bytes 131104 | tf_op jit(solution)/shard_map/ppermute | solution.py:177
  13.9 0.2 %collective-permute-done.9.refs_7_ = bf16[32,2048]{1,0:T(8,128)(2,1)S(1)} collective-permute-done((bf16[32,2048]{1,0:T(8,128)(2,1)S(1)}, bf16[32,2048]{1,0:T(8,128)(2,1)S(1)}, u32[]{:S(2)}, u32[]{:S(2)}) %collective-permute-start.9) | collective-permute-done | bytes 131104 | tf_op jit(solution)/shard_map/ppermute | solution.py:177
  14.2 0.4 %collective-permute-done.8.refs_5_ = bf16[32,2048]{1,0:T(8,128)(2,1)S(1)} collective-permute-done((bf16[32,2048]{1,0:T(8,128)(2,1)S(1)}, bf16[32,2048]{1,0:T(8,128)(2,1)S(1)}, u32[]{:S(2)}, u32[]{:S(2)}) %collective-permute-start.8) | collective-permute-done | bytes 131104 | tf_op jit(solution)/shard_map/ppermute | solution.py:177
  14.5 0.2 collective-permute-done.7.refs_3_
  14.7 0.4 %score.1 = f32[1,128]{1,0:T(1,128)S(1)} custom-call(f32[8,2048]{1,0:T(8,128)S(1)} %get-tuple-element.27.first_ref, f32[8,2048]{1,0:T(8,128)S(1)} %get-tuple-element.28.second_ref, bf16[32,2048]{1,0:T(8,128)(2,1)S(1)} %copy-done.2, bf16[32,2048]{1,0:T(8,128)(2,1)S(1)} %collective-permute-done.6.refs_1_, bf16[32,2048]{1,0:T(8,128)(2,1)S(1)} %collective-permute-done.2.refs_2_, ...), custom_call_target="tpu_custom_call" | custom-call | tf_op jit(solution)/shard_map/score/pallas_call | solution.py:191
  15.1 0.3 %collective-permute-start.10 = (f32[1,128]{1,0:T(1,128)S(1)}, f32[1,128]{1,0:T(1,128)S(1)}, u32[]{:S(2)}, u32[]{:S(2)}) collective-permute-start(f32[1,128]{1,0:T(1,128)S(1)} %score.1), channel_id=1, source_target_pairs={{9,1},{11,3},{13,5},{15,7},{0,8},{2,10},{4,12},{6,14},{1,0},{3,2},... | collective-permute-start | bytes 1544 | tf_op jit(solution)/shard_map/ppermute | solution.py:199
  15.5 3.0 %collective-permute-done.10 = f32[1,128]{1,0:T(1,128)S(1)} collective-permute-done((f32[1,128]{1,0:T(1,128)S(1)}, f32[1,128]{1,0:T(1,128)S(1)}, u32[]{:S(2)}, u32[]{:S(2)}) %collective-permute-start.10) | collective-permute-done | bytes 544 | tf_op jit(solution)/shard_map/ppermute | solution.py:199
  18.4 0.5 %copy.7 = f32[1,128]{1,0:T(1,128)} copy(f32[1,128]{1,0:T(1,128)S(1)} %collective-permute-done.10) | data formatting | bytes 1024
  (13 shorter events, 0.1 us)
Async XLA Ops:
  0.0 3.4 %copy-start.1 = (bf16[2560,128]{1,0:T(8,128)(2,1)S(1)}, bf16[2560,128]{1,0:T(8,128)(2,1)}, u32[]{:S(2)}) copy-start(bf16[2560,128]{1,0:T(8,128)(2,1)} %proj_ref.1) | copy-start | bytes 1966084
  0.0 3.4 %copy-start = (bf16[1,384,2560]{2,1,0:T(8,128)(2,1)S(1)}, bf16[1,384,2560]{2,1,0:T(8,128)(2,1)}, u32[]{:S(2)}) copy-start(bf16[1,384,2560]{2,1,0:T(8,128)(2,1)} %acts_ref.1) | copy-start | bytes 5898244
  0.0 8.3 %copy-start.3 = (s32[1,256]{1,0:T(1,128)S(1)}, s32[1,256]{1,0:T(1,128)}, u32[]{:S(2)}) copy-start(s32[1,256]{1,0:T(1,128)} %picks_ref.1) | copy-start | bytes 3076
  0.0 12.6 %copy-start.2 = (bf16[32,2048]{1,0:T(8,128)(2,1)S(1)}, bf16[32,2048]{1,0:T(8,128)(2,1)}, u32[]{:S(2)}) copy-start(bf16[32,2048]{1,0:T(8,128)(2,1)} %refs_0_.1) | copy-start | bytes 393220
  0.0 12.6 %collective-permute-start.2 = (bf16[32,2048]{1,0:T(8,128)(2,1)}, bf16[32,2048]{1,0:T(8,128)(2,1)S(1)}, u32[]{:S(2)}, u32[]{:S(2)}) collective-permute-start(bf16[32,2048]{1,0:T(8,128)(2,1)} %refs_0_.1), channel_id=1, source_target_pairs={{0,2},{2,0},{4,6},{6,4},{8,10},{10,8},{12,14},{14,12},{1,3},{3,1},... | collective-permute-start | bytes 393224 | tf_op jit(solution)/shard_map/ppermute | solution.py:138
  2.1 10.5 %collective-permute-start.1 = (bf16[32,2048]{1,0:T(8,128)(2,1)}, bf16[32,2048]{1,0:T(8,128)(2,1)S(1)}, u32[]{:S(2)}, u32[]{:S(2)}) collective-permute-start(bf16[32,2048]{1,0:T(8,128)(2,1)} %refs_0_.1), channel_id=1, source_target_pairs={{0,4},{2,6},{4,0},{6,2},{8,12},{10,14},{12,8},{14,10},{1,5},{3,7},... | collective-permute-start | bytes 393224 | tf_op jit(solution)/shard_map/ppermute | solution.py:138
  3.4 9.2 %collective-permute-start = (bf16[32,2048]{1,0:T(8,128)(2,1)}, bf16[32,2048]{1,0:T(8,128)(2,1)S(1)}, u32[]{:S(2)}, u32[]{:S(2)}) collective-permute-start(bf16[32,2048]{1,0:T(8,128)(2,1)} %refs_0_.1), channel_id=1, source_target_pairs={{0,6},{2,4},{4,2},{6,0},{8,14},{10,12},{12,10},{14,8},{1,7},{3,5},... | collective-permute-start | bytes 393224 | tf_op jit(solution)/shard_map/ppermute | solution.py:138
  6.9 2.2 %collective-permute-start.3 = (f32[192,128]{1,0:T(8,128)S(1)}, f32[192,128]{1,0:T(8,128)S(1)}, u32[]{:S(2)}, u32[]{:S(2)}) collective-permute-start(f32[192,128]{1,0:T(8,128)S(1)} %get-tuple-element.21.refs_0_), channel_id=1, source_target_pairs={{0,1},{1,0},{2,3},{3,2},{4,5},{5,4},{6,7},{7,6},{8,9},{9,8},{10,11... | collective-permute-start | bytes 294920 | tf_op jit(solution)/shard_map/ppermute | solution.py:152
  8.2 1.3 %collective-permute-start.4 = (f32[192,128]{1,0:T(8,128)S(1)}, f32[192,128]{1,0:T(8,128)S(1)}, u32[]{:S(2)}, u32[]{:S(2)}) collective-permute-start(f32[192,128]{1,0:T(8,128)S(1)} %get-tuple-element.22.refs_1_), channel_id=1, source_target_pairs={{0,1},{1,0},{2,3},{3,2},{4,5},{5,4},{6,7},{7,6},{8,9},{9,8},{10,11... | collective-permute-start | bytes 294920 | tf_op jit(solution)/shard_map/ppermute | solution.py:152
  9.9 3.8 %collective-permute-start.5 = (bf16[32,128]{1,0:T(8,128)(2,1)S(1)}, bf16[32,128]{1,0:T(8,128)(2,1)S(1)}, u32[]{:S(2)}, u32[]{:S(2)}) collective-permute-start(bf16[32,128]{1,0:T(8,128)(2,1)S(1)} %sketch.1.own_ref), channel_id=1, source_target_pairs={{1,9},{3,11},{5,13},{7,15},{8,0},{10,2},{12,4},{14,6},{0,1},{2,3},... | collective-permute-start | bytes 24584 | tf_op jit(solution)/shard_map/ppermute | solution.py:173
  12.6 1.3 %collective-permute-start.6 = (bf16[32,2048]{1,0:T(8,128)(2,1)S(1)}, bf16[32,2048]{1,0:T(8,128)(2,1)S(1)}, u32[]{:S(2)}, u32[]{:S(2)}) collective-permute-start(bf16[32,2048]{1,0:T(8,128)(2,1)S(1)} %copy-done.2), channel_id=1, source_target_pairs={{0,1},{1,0},{2,3},{3,2},{4,5},{5,4},{6,7},{7,6},{8,9},{9,8},{10,11... | collective-permute-start | bytes 393224 | tf_op jit(solution)/shard_map/ppermute | solution.py:177
  12.6 1.5 %collective-permute-start.9 = (bf16[32,2048]{1,0:T(8,128)(2,1)S(1)}, bf16[32,2048]{1,0:T(8,128)(2,1)S(1)}, u32[]{:S(2)}, u32[]{:S(2)}) collective-permute-start(bf16[32,2048]{1,0:T(8,128)(2,1)S(1)} %collective-permute-done.refs_6_), channel_id=1, source_target_pairs={{0,1},{1,0},{2,3},{3,2},{4,5},{5,4},{6,7},{7,6},{8,9},{9,8},{10,11... | collective-permute-start | bytes 393224 | tf_op jit(solution)/shard_map/ppermute | solution.py:177
  13.2 1.3 %collective-permute-start.8 = (bf16[32,2048]{1,0:T(8,128)(2,1)S(1)}, bf16[32,2048]{1,0:T(8,128)(2,1)S(1)}, u32[]{:S(2)}, u32[]{:S(2)}) collective-permute-start(bf16[32,2048]{1,0:T(8,128)(2,1)S(1)} %collective-permute-done.1.refs_4_), channel_id=1, source_target_pairs={{0,1},{1,0},{2,3},{3,2},{4,5},{5,4},{6,7},{7,6},{8,9},{9,8},{10,11... | collective-permute-start | bytes 393224 | tf_op jit(solution)/shard_map/ppermute | solution.py:177
  13.3 1.5 %collective-permute-start.7 = (bf16[32,2048]{1,0:T(8,128)(2,1)S(1)}, bf16[32,2048]{1,0:T(8,128)(2,1)S(1)}, u32[]{:S(2)}, u32[]{:S(2)}) collective-permute-start(bf16[32,2048]{1,0:T(8,128)(2,1)S(1)} %collective-permute-done.2.refs_2_), channel_id=1, source_target_pairs={{0,1},{1,0},{2,3},{3,2},{4,5},{5,4},{6,7},{7,6},{8,9},{9,8},{10,11... | collective-permute-start | bytes 393224 | tf_op jit(solution)/shard_map/ppermute | solution.py:177
  15.1 3.3 %collective-permute-start.10 = (f32[1,128]{1,0:T(1,128)S(1)}, f32[1,128]{1,0:T(1,128)S(1)}, u32[]{:S(2)}, u32[]{:S(2)}) collective-permute-start(f32[1,128]{1,0:T(1,128)S(1)} %score.1), channel_id=1, source_target_pairs={{9,1},{11,3},{13,5},{15,7},{0,8},{2,10},{4,12},{6,14},{1,0},{3,2},... | collective-permute-start | bytes 1544 | tf_op jit(solution)/shard_map/ppermute | solution.py:199

commit v15 on v14

--- a/solution.py
+++ b/solution.py
@@ -17,21 +17,17 @@
     out_ref[...] = jnp.zeros_like(out_ref)
 
 
-def project_kernel(rank, first_ref, acts_ref, grads_hbm, proj_ref, *refs):
-    outs, (grads, sems) = refs[:-2], refs[-2:]
+def project_kernel(rank, first_ref, acts_ref, grads_ref, proj_ref, *outs):
     rows = outs[0].shape[0]
-    copies = []
-    for i in range(len(outs)):
-        part = pl.ds(i * rows, rows)
-        copies.append(pltpu.make_async_copy(grads_hbm.at[0, part, :], grads.at[part, :], sems.at[i]))
-        copies[-1].start()
-    left = jnp.dot(acts_ref[0], proj_ref[...], preferred_element_type=F32)
     column = lax.broadcasted_iota(jnp.int32, (rows, 2 * rank), 1)
     for i, out_ref in enumerate(outs):
         part = slice(i * rows, (i + 1) * rows)
-        copies[i].wait()
-        right = jnp.dot(grads[part, :], proj_ref[...], preferred_element_type=F32)
-        out_ref[...] = jnp.where(column < rank, left[part], right)
+        term = jnp.dot(
+            jnp.concatenate([acts_ref[0, part, :], grads_ref[0, part, :]], axis=0),
+            proj_ref[...],
+            preferred_element_type=F32,
+        )
+        out_ref[...] = jnp.where(column < rank, term[0:rows], term[rows:])
 
 
 def count_kernel(rank, picks_ref, out_ref):
@@ -124,12 +120,13 @@
     there += [(place(a, m, a), place(a, m, 1 - a)) for a, m in spots]
     back = [(dst, src) for src, dst in there]
 
+    copied = 2 * (2 * tokens * units + units * 2 * rank)
     first = pl.pallas_call(
         first_kernel,
         out_specs=vmem,
         out_shape=jax.ShapeDtypeStruct((8, LANES), F32),
         compiler_params=pltpu.CompilerParams(vmem_limit_bytes=1 << 20),
-        cost_estimate=pl.CostEstimate(flops=11 << 26, bytes_accessed=1, transcendentals=0),
+        cost_estimate=pl.CostEstimate(flops=274 * copied, bytes_accessed=1, transcendentals=0),
         name="first",
     )()
     sent, first = lax.optimization_barrier((queries, first))
@@ -138,11 +135,10 @@
         halves.append(lax.ppermute(sent, "dp", [(d, d ^ r) for d in range(clips)]))
     partial = pl.pallas_call(
         functools.partial(project_kernel, rank),
-        in_specs=[vmem, vmem, pl.BlockSpec(memory_space=pl.ANY), vmem],
+        in_specs=[vmem] * 4,
         out_specs=[vmem] * PIECES,
         out_shape=[jax.ShapeDtypeStruct((tokens // PIECES, 2 * rank), F32)] * PIECES,
-        scratch_shapes=[pltpu.VMEM((tokens, units), BF16), pltpu.SemaphoreType.DMA((PIECES,))],
-        compiler_params=pltpu.CompilerParams(vmem_limit_bytes=52000 << 10),
+        compiler_params=pltpu.CompilerParams(vmem_limit_bytes=16 << 20),
         cost_estimate=pl.CostEstimate(
             flops=8 * tokens * units * rank, bytes_accessed=4 * tokens * units, transcendentals=0
         ),

time: 19.1 us -> 17.8 us (0.932)
  the two profiles are of different devices: /device:TPU:1 before, /device:TPU:0 now
where the time goes in v15:
time: 17.8 us; the launch traced here: 17.7 us
  starting transfers between devices  11.6 us (65%)
  waiting for transfers between devices  3.32 us (19%)
  Pallas kernels  2.2 us (12%)
  local copies, waits for them, and re-layouts  0.53 us (3%)
    ppermute x3, starting transfers between devices, on_device(): halves.append(lax.ppermute(sent, 'dp', [(d, d ^ r) for d in range(clips)]))  4.6 us
    ppermute x4, starting transfers between devices, on_device(): swapped.append(lax.ppermute(half, 'tensor', swap))  3.31 us
    ppermute x1, starting transfers between devices, on_device(): return lax.ppermute(scores, both, back)  2.73 us
    ppermute x1, waiting for transfers between devices, on_device(): return lax.ppermute(scores, both, back)  1.3 us
    pallas_call x1, Pallas kernels, on_device(): pl.pallas_call(functools.partial(project_kernel, rank), in_specs=[vmem] *...  1.17 us
    ppermute x1, waiting for transfers between devices, on_device(): far_sketch = lax.ppermute(sketch, both, there)  0.88 us
    ppermute x2, waiting for transfers between devices, on_device(): other = [lax.ppermute(part, 'tensor', swap) for part in partial]  0.73 us
    ppermute x2, starting transfers between devices, on_device(): other = [lax.ppermute(part, 'tensor', swap) for part in partial]  0.57 us
  transfers between devices with their start and end apart: 11, of which 6 were waited for; matrix products, arithmetic and copies ran while one was open for 0% of the time, Pallas kernels for 10%

profile of v15, /device:TPU:0, one launch (start us, length us, event | category | flops | bytes accessed | tf_op | source)
XLA Modules:
  0.0 17.7 jit_solution(16459875473708062745)
XLA Ops:
  0.0 0.0 copy-start.3
  0.0 3.0 %collective-permute-start.2 = (bf16[32,2048]{1,0:T(8,128)(2,1)}, bf16[32,2048]{1,0:T(8,128)(2,1)S(1)}, u32[]{:S(2)}, u32[]{:S(2)}) collective-permute-start(bf16[32,2048]{1,0:T(8,128)(2,1)} %refs_0_.1), channel_id=1, source_target_pairs={{0,2},{2,0},{4,6},{6,4},{8,10},{10,8},{12,14},{14,12},{1,3},{3,1},... | collective-permute-start | bytes 393224 | tf_op jit(solution)/shard_map/ppermute | solution.py:135
  3.0 1.6 %collective-permute-start.1 = (bf16[32,2048]{1,0:T(8,128)(2,1)}, bf16[32,2048]{1,0:T(8,128)(2,1)S(1)}, u32[]{:S(2)}, u32[]{:S(2)}) collective-permute-start(bf16[32,2048]{1,0:T(8,128)(2,1)} %refs_0_.1), channel_id=1, source_target_pairs={{0,4},{2,6},{4,0},{6,2},{8,12},{10,14},{12,8},{14,10},{1,5},{3,7},... | collective-permute-start | bytes 393224 | tf_op jit(solution)/shard_map/ppermute | solution.py:135
  4.6 0.0 collective-permute-start
  4.6 1.2 %project.1 = (f32[192,128]{1,0:T(8,128)S(1)}, f32[192,128]{1,0:T(8,128)S(1)}) custom-call(f32[8,128]{1,0:T(8,128)S(1)} %first.1.first_ref, bf16[1,384,2560]{2,1,0:T(8,128)(2,1)S(1)} %copy-done, bf16[1,384,2560]{2,1,0:T(8,128)(2,1)S(1)} %copy-done.1, bf16[2560,128]{1,0:T(8,128)(2,1)S(1)} %copy-done.2), custom_call_target="tpu_custom_call" | custom-call | flops 503316480 | bytes 3932160 | tf_op jit(solution)/shard_map/project/pallas_call | solution.py:136
  5.8 0.1 collective-permute-start.3
  5.9 0.5 %collective-permute-start.4 = (f32[192,128]{1,0:T(8,128)S(1)}, f32[192,128]{1,0:T(8,128)S(1)}, u32[]{:S(2)}, u32[]{:S(2)}) collective-permute-start(f32[192,128]{1,0:T(8,128)S(1)} %get-tuple-element.22.refs_1_), channel_id=1, source_target_pairs={{0,1},{1,0},{2,3},{3,2},{4,5},{5,4},{6,7},{7,6},{8,9},{9,8},{10,11... | collective-permute-start | bytes 294920 | tf_op jit(solution)/shard_map/ppermute | solution.py:148
  6.4 0.2 %count.1.count_ref = f32[384,128]{1,0:T(8,128)S(1)} custom-call(s32[1,256]{1,0:T(1,128)S(1)} %copy-done.4), custom_call_target="tpu_custom_call" | custom-call | flops 1 | bytes 1 | tf_op jit(solution)/shard_map/count/pallas_call | solution.py:149
  6.6 0.6 %collective-permute-done.3.refs_2_ = f32[192,128]{1,0:T(8,128)S(1)} collective-permute-done((f32[192,128]{1,0:T(8,128)S(1)}, f32[192,128]{1,0:T(8,128)S(1)}, u32[]{:S(2)}, u32[]{:S(2)}) %collective-permute-start.3) | collective-permute-done | bytes 98336 | tf_op jit(solution)/shard_map/ppermute | solution.py:148
  7.2 0.2 collective-permute-done.4.refs_3_
  7.3 0.4 %sketch.1.own_ref = bf16[32,128]{1,0:T(8,128)(2,1)S(1)} custom-call(f32[384,128]{1,0:T(8,128)S(1)} %count.1.count_ref, f32[192,128]{1,0:T(8,128)S(1)} %get-tuple-element.21.refs_0_, f32[192,128]{1,0:T(8,128)S(1)} %get-tuple-element.22.refs_1_, f32[192,128]{1,0:T(8,128)S(1)} %collective-permute-done.3.refs_2_, f32[192,128]{1,0:T(8,128)S(1)} %collective-permute-done.4.refs_3_), custom_call_target="tpu_custom_call" | custom-call | flops 1 | bytes 1 | tf_op jit(solution)/shard_map/sketch/pallas_call | solution.py:158
  7.7 0.4 %collective-permute-start.5 = (bf16[32,128]{1,0:T(8,128)(2,1)S(1)}, bf16[32,128]{1,0:T(8,128)(2,1)S(1)}, u32[]{:S(2)}, u32[]{:S(2)}) collective-permute-start(bf16[32,128]{1,0:T(8,128)(2,1)S(1)} %sketch.1.own_ref), channel_id=1, source_target_pairs={{1,9},{3,11},{5,13},{7,15},{8,0},{10,2},{12,4},{14,6},{0,1},{2,3},... | collective-permute-start | bytes 24584 | tf_op jit(solution)/shard_map/ppermute | solution.py:169
  8.1 2.7 %collective-permute-start.6 = (bf16[32,2048]{1,0:T(8,128)(2,1)S(1)}, bf16[32,2048]{1,0:T(8,128)(2,1)S(1)}, u32[]{:S(2)}, u32[]{:S(2)}) collective-permute-start(bf16[32,2048]{1,0:T(8,128)(2,1)S(1)} %copy-done.3), channel_id=1, source_target_pairs={{0,1},{1,0},{2,3},{3,2},{4,5},{5,4},{6,7},{7,6},{8,9},{9,8},{10,11... | collective-permute-start | bytes 393224 | tf_op jit(solution)/shard_map/ppermute | solution.py:173
  10.8 0.1 collective-permute-done.refs_6_
  10.9 0.0 collective-permute-start.9
  10.9 0.5 %collective-permute-start.8 = (bf16[32,2048]{1,0:T(8,128)(2,1)S(1)}, bf16[32,2048]{1,0:T(8,128)(2,1)S(1)}, u32[]{:S(2)}, u32[]{:S(2)}) collective-permute-start(bf16[32,2048]{1,0:T(8,128)(2,1)S(1)} %collective-permute-done.1.refs_4_), channel_id=1, source_target_pairs={{0,1},{1,0},{2,3},{3,2},{4,5},{5,4},{6,7},{7,6},{8,9},{9,8},{10,11... | collective-permute-start | bytes 393224 | tf_op jit(solution)/shard_map/ppermute | solution.py:173
  11.4 0.1 collective-permute-start.7
  11.5 0.9 %collective-permute-done.5.far_ref = bf16[32,128]{1,0:T(8,128)(2,1)S(1)} collective-permute-done((bf16[32,128]{1,0:T(8,128)(2,1)S(1)}, bf16[32,128]{1,0:T(8,128)(2,1)S(1)}, u32[]{:S(2)}, u32[]{:S(2)}) %collective-permute-start.5) | collective-permute-done | bytes 8224 | tf_op jit(solution)/shard_map/ppermute | solution.py:169
  12.4 0.0 collective-permute-done.8.refs_5_
  12.4 0.3 %collective-permute-done.7.refs_3_ = bf16[32,2048]{1,0:T(8,128)(2,1)S(1)} collective-permute-done((bf16[32,2048]{1,0:T(8,128)(2,1)S(1)}, bf16[32,2048]{1,0:T(8,128)(2,1)S(1)}, u32[]{:S(2)}, u32[]{:S(2)}) %collective-permute-start.7) | collective-permute-done | bytes 131104 | tf_op jit(solution)/shard_map/ppermute | solution.py:173
  12.7 0.4 %score.1 = f32[1,128]{1,0:T(1,128)S(1)} custom-call(f32[8,2048]{1,0:T(8,128)S(1)} %get-tuple-element.27.first_ref, f32[8,2048]{1,0:T(8,128)S(1)} %get-tuple-element.28.second_ref, bf16[32,2048]{1,0:T(8,128)(2,1)S(1)} %copy-done.3, bf16[32,2048]{1,0:T(8,128)(2,1)S(1)} %collective-permute-done.6.refs_1_, bf16[32,2048]{1,0:T(8,128)(2,1)S(1)} %collective-permute-done.2.refs_2_, ...), custom_call_target="tpu_custom_call" | custom-call | tf_op jit(solution)/shard_map/score/pallas_call | solution.py:187
  13.2 2.7 %collective-permute-start.10 = (f32[1,128]{1,0:T(1,128)S(1)}, f32[1,128]{1,0:T(1,128)S(1)}, u32[]{:S(2)}, u32[]{:S(2)}) collective-permute-start(f32[1,128]{1,0:T(1,128)S(1)} %score.1), channel_id=1, source_target_pairs={{9,1},{11,3},{13,5},{15,7},{0,8},{2,10},{4,12},{6,14},{1,0},{3,2},... | collective-permute-start | bytes 1544 | tf_op jit(solution)/shard_map/ppermute | solution.py:195
  15.9 1.3 %collective-permute-done.10 = f32[1,128]{1,0:T(1,128)S(1)} collective-permute-done((f32[1,128]{1,0:T(1,128)S(1)}, f32[1,128]{1,0:T(1,128)S(1)}, u32[]{:S(2)}, u32[]{:S(2)}) %collective-permute-start.10) | collective-permute-done | bytes 544 | tf_op jit(solution)/shard_map/ppermute | solution.py:195
  17.2 0.5 %copy.7 = f32[1,128]{1,0:T(1,128)} copy(f32[1,128]{1,0:T(1,128)S(1)} %collective-permute-done.10) | data formatting | bytes 1024
  (15 shorter events, 0.1 us)
Async XLA Ops:
  0.0 4.6 %copy-start.2 = (bf16[2560,128]{1,0:T(8,128)(2,1)S(1)}, bf16[2560,128]{1,0:T(8,128)(2,1)}, u32[]{:S(2)}) copy-start(bf16[2560,128]{1,0:T(8,128)(2,1)} %proj_ref.1) | copy-start | bytes 1966084
  0.0 4.6 %copy-start.1 = (bf16[1,384,2560]{2,1,0:T(8,128)(2,1)S(1)}, bf16[1,384,2560]{2,1,0:T(8,128)(2,1)}, u32[]{:S(2)}) copy-start(bf16[1,384,2560]{2,1,0:T(8,128)(2,1)} %grads_ref.1) | copy-start | bytes 5898244
  0.0 4.6 %copy-start = (bf16[1,384,2560]{2,1,0:T(8,128)(2,1)S(1)}, bf16[1,384,2560]{2,1,0:T(8,128)(2,1)}, u32[]{:S(2)}) copy-start(bf16[1,384,2560]{2,1,0:T(8,128)(2,1)} %acts_ref.1) | copy-start | bytes 5898244
  0.0 6.4 %copy-start.4 = (s32[1,256]{1,0:T(1,128)S(1)}, s32[1,256]{1,0:T(1,128)}, u32[]{:S(2)}) copy-start(s32[1,256]{1,0:T(1,128)} %picks_ref.1) | copy-start | bytes 3076
  0.0 8.1 %copy-start.3 = (bf16[32,2048]{1,0:T(8,128)(2,1)S(1)}, bf16[32,2048]{1,0:T(8,128)(2,1)}, u32[]{:S(2)}) copy-start(bf16[32,2048]{1,0:T(8,128)(2,1)} %refs_0_.1) | copy-start | bytes 393220
  0.0 10.8 %collective-permute-start.2 = (bf16[32,2048]{1,0:T(8,128)(2,1)}, bf16[32,2048]{1,0:T(8,128)(2,1)S(1)}, u32[]{:S(2)}, u32[]{:S(2)}) collective-permute-start(bf16[32,2048]{1,0:T(8,128)(2,1)} %refs_0_.1), channel_id=1, source_target_pairs={{0,2},{2,0},{4,6},{6,4},{8,10},{10,8},{12,14},{14,12},{1,3},{3,1},... | collective-permute-start | bytes 393224 | tf_op jit(solution)/shard_map/ppermute | solution.py:135
  3.0 7.7 %collective-permute-start.1 = (bf16[32,2048]{1,0:T(8,128)(2,1)}, bf16[32,2048]{1,0:T(8,128)(2,1)S(1)}, u32[]{:S(2)}, u32[]{:S(2)}) collective-permute-start(bf16[32,2048]{1,0:T(8,128)(2,1)} %refs_0_.1), channel_id=1, source_target_pairs={{0,4},{2,6},{4,0},{6,2},{8,12},{10,14},{12,8},{14,10},{1,5},{3,7},... | collective-permute-start | bytes 393224 | tf_op jit(solution)/shard_map/ppermute | solution.py:135
  4.6 6.2 %collective-permute-start = (bf16[32,2048]{1,0:T(8,128)(2,1)}, bf16[32,2048]{1,0:T(8,128)(2,1)S(1)}, u32[]{:S(2)}, u32[]{:S(2)}) collective-permute-start(bf16[32,2048]{1,0:T(8,128)(2,1)} %refs_0_.1), channel_id=1, source_target_pairs={{0,6},{2,4},{4,2},{6,0},{8,14},{10,12},{12,10},{14,8},{1,7},{3,5},... | collective-permute-start | bytes 393224 | tf_op jit(solution)/shard_map/ppermute | solution.py:135
  5.8 1.4 %collective-permute-start.3 = (f32[192,128]{1,0:T(8,128)S(1)}, f32[192,128]{1,0:T(8,128)S(1)}, u32[]{:S(2)}, u32[]{:S(2)}) collective-permute-start(f32[192,128]{1,0:T(8,128)S(1)} %get-tuple-element.21.refs_0_), channel_id=1, source_target_pairs={{0,1},{1,0},{2,3},{3,2},{4,5},{5,4},{6,7},{7,6},{8,9},{9,8},{10,11... | collective-permute-start | bytes 294920 | tf_op jit(solution)/shard_map/ppermute | solution.py:148
  5.9 1.4 %collective-permute-start.4 = (f32[192,128]{1,0:T(8,128)S(1)}, f32[192,128]{1,0:T(8,128)S(1)}, u32[]{:S(2)}, u32[]{:S(2)}) collective-permute-start(f32[192,128]{1,0:T(8,128)S(1)} %get-tuple-element.22.refs_1_), channel_id=1, source_target_pairs={{0,1},{1,0},{2,3},{3,2},{4,5},{5,4},{6,7},{7,6},{8,9},{9,8},{10,11... | collective-permute-start | bytes 294920 | tf_op jit(solution)/shard_map/ppermute | solution.py:148
  7.7 4.6 %collective-permute-start.5 = (bf16[32,128]{1,0:T(8,128)(2,1)S(1)}, bf16[32,128]{1,0:T(8,128)(2,1)S(1)}, u32[]{:S(2)}, u32[]{:S(2)}) collective-permute-start(bf16[32,128]{1,0:T(8,128)(2,1)S(1)} %sketch.1.own_ref), channel_id=1, source_target_pairs={{1,9},{3,11},{5,13},{7,15},{8,0},{10,2},{12,4},{14,6},{0,1},{2,3},... | collective-permute-start | bytes 24584 | tf_op jit(solution)/shard_map/ppermute | solution.py:169
  8.1 4.3 %collective-permute-start.6 = (bf16[32,2048]{1,0:T(8,128)(2,1)S(1)}, bf16[32,2048]{1,0:T(8,128)(2,1)S(1)}, u32[]{:S(2)}, u32[]{:S(2)}) collective-permute-start(bf16[32,2048]{1,0:T(8,128)(2,1)S(1)} %copy-done.3), channel_id=1, source_target_pairs={{0,1},{1,0},{2,3},{3,2},{4,5},{5,4},{6,7},{7,6},{8,9},{9,8},{10,11... | collective-permute-start | bytes 393224 | tf_op jit(solution)/shard_map/ppermute | solution.py:173
  10.9 1.5 %collective-permute-start.9 = (bf16[32,2048]{1,0:T(8,128)(2,1)S(1)}, bf16[32,2048]{1,0:T(8,128)(2,1)S(1)}, u32[]{:S(2)}, u32[]{:S(2)}) collective-permute-start(bf16[32,2048]{1,0:T(8,128)(2,1)S(1)} %collective-permute-done.refs_6_), channel_id=1, source_target_pairs={{0,1},{1,0},{2,3},{3,2},{4,5},{5,4},{6,7},{7,6},{8,9},{9,8},{10,11... | collective-permute-start | bytes 393224 | tf_op jit(solution)/shard_map/ppermute | solution.py:173
  10.9 1.5 %collective-permute-start.8 = (bf16[32,2048]{1,0:T(8,128)(2,1)S(1)}, bf16[32,2048]{1,0:T(8,128)(2,1)S(1)}, u32[]{:S(2)}, u32[]{:S(2)}) collective-permute-start(bf16[32,2048]{1,0:T(8,128)(2,1)S(1)} %collective-permute-done.1.refs_4_), channel_id=1, source_target_pairs={{0,1},{1,0},{2,3},{3,2},{4,5},{5,4},{6,7},{7,6},{8,9},{9,8},{10,11... | collective-permute-start | bytes 393224 | tf_op jit(solution)/shard_map/ppermute | solution.py:173
  11.4 1.3 %collective-permute-start.7 = (bf16[32,2048]{1,0:T(8,128)(2,1)S(1)}, bf16[32,2048]{1,0:T(8,128)(2,1)S(1)}, u32[]{:S(2)}, u32[]{:S(2)}) collective-permute-start(bf16[32,2048]{1,0:T(8,128)(2,1)S(1)} %collective-permute-done.2.refs_2_), channel_id=1, source_target_pairs={{0,1},{1,0},{2,3},{3,2},{4,5},{5,4},{6,7},{7,6},{8,9},{9,8},{10,11... | collective-permute-start | bytes 393224 | tf_op jit(solution)/shard_map/ppermute | solution.py:173
  13.2 4.0 %collective-permute-start.10 = (f32[1,128]{1,0:T(1,128)S(1)}, f32[1,128]{1,0:T(1,128)S(1)}, u32[]{:S(2)}, u32[]{:S(2)}) collective-permute-start(f32[1,128]{1,0:T(1,128)S(1)} %score.1), channel_id=1, source_target_pairs={{9,1},{11,3},{13,5},{15,7},{0,8},{2,10},{4,12},{6,14},{1,0},{3,2},... | collective-permute-start | bytes 1544 | tf_op jit(solution)/shard_map/ppermute | solution.py:195

commit v16 on v13

--- a/solution.py
+++ b/solution.py
@@ -71,23 +71,27 @@
         start = half * (slots * pairs // 2)
         for j in range(pairs // 2):
             rows = wide[pl.ds(pl.multiple_of(start + j * slots, slots), slots), :]
-            out_ref[:, j * LANES : (j + 1) * LANES] = rows.astype(BF16)
+            out_ref[:, j * LANES : (j + 1) * LANES] = rows
 
 
 def score_kernel(first_ref, second_ref, own_ref, other_ref, out_ref):
-    contract = (((1,), (1,)), ((), ()))
-    out_ref[...] = lax.dot_general(
-        first_ref[...], own_ref[...], contract, preferred_element_type=F32
-    ) + lax.dot_general(second_ref[...], other_ref[...], contract, preferred_element_type=F32)
+    total = None
+    for flat_ref, query_ref in ((first_ref, own_ref), (second_ref, other_ref)):
+        for j in range(query_ref.shape[1] // LANES):
+            lanes = slice(j * LANES, (j + 1) * LANES)
+            term = query_ref[:, lanes].astype(F32) * flat_ref[0:1, lanes]
+            total = term if total is None else total + term
+    out_ref[...] = total
 
 
 def arrange_kernel(*refs):
     parts, out_ref = refs[:-1], refs[-1]
     mates = len(parts)
-    own_queries = parts[0].shape[1]
-    scores = jnp.concatenate([part[...] for part in parts], axis=1)
+    own_queries = parts[0].shape[0]
+    width = mates * own_queries
+    scores = jnp.concatenate([part[...] for part in parts], axis=0).T
+    scores = jnp.broadcast_to(jnp.sum(scores, axis=0, keepdims=True), (8, width))
     member = lax.rem(lax.axis_index("dp"), mates)
-    width = scores.shape[1]
     block = lax.broadcasted_iota(jnp.int32, scores.shape, 1) // own_queries
     step = 1
     while step < mates:
@@ -97,12 +101,6 @@
         scores = jnp.where(member & step == 0, scores, exchanged)
         step *= 2
     out_ref[...] = scores[0:1, :]
-
-
-def store_kernel(row_ref, out_ref, sem):
-    copy = pltpu.make_async_copy(row_ref, out_ref, sem)
-    copy.start()
-    copy.wait()
 
 
 def on_device(activations, out_grads, projections, sample_index, queries):
@@ -125,12 +123,13 @@
     there += [(place(a, m, a), place(a, m, 1 - a)) for a, m in spots]
     back = [(dst, src) for src, dst in there]
 
+    copied = 2 * (2 * tokens * units + units * 2 * rank)
     first = pl.pallas_call(
         first_kernel,
         out_specs=vmem,
         out_shape=jax.ShapeDtypeStruct((8, LANES), F32),
         compiler_params=pltpu.CompilerParams(vmem_limit_bytes=1 << 20),
-        cost_estimate=pl.CostEstimate(flops=1 << 30, bytes_accessed=1, transcendentals=0),
+        cost_estimate=pl.CostEstimate(flops=274 * copied, bytes_accessed=1, transcendentals=0),
         name="first",
     )()
     sent, first = lax.optimization_barrier((queries, first))
@@ -181,7 +180,7 @@
         functools.partial(flatten_kernel, mates),
         in_specs=[vmem] * 2,
         out_specs=[vmem] * 2,
-        out_shape=[jax.ShapeDtypeStruct((slots, entries), BF16)] * 2,
+        out_shape=[jax.ShapeDtypeStruct((slots, entries), F32)] * 2,
         scratch_shapes=[pltpu.VMEM((pairs * slots, LANES), F32)],
         compiler_params=pltpu.CompilerParams(vmem_limit_bytes=8 << 20),
         cost_estimate=pl.CostEstimate(flops=1 << 34, bytes_accessed=64 << 20, transcendentals=0),
@@ -194,7 +193,7 @@
             score_kernel,
             in_specs=[vmem] * 4,
             out_specs=vmem,
-            out_shape=jax.ShapeDtypeStruct((slots, own_queries), F32),
+            out_shape=jax.ShapeDtypeStruct((own_queries, LANES), F32),
             compiler_params=few,
             cost_estimate=small,
             name="score",
@@ -210,15 +209,7 @@
         cost_estimate=small,
         name="arrange",
     )(*parts)
-    return pl.pallas_call(
-        store_kernel,
-        in_specs=[vmem],
-        out_specs=pl.BlockSpec(memory_space=pl.ANY),
-        out_shape=jax.ShapeDtypeStruct((1, width), F32),
-        scratch_shapes=[pltpu.SemaphoreType.DMA],
-        compiler_params=few,
-        name="store",
-    )(lax.ppermute(scores, both, back))
+    return lax.ppermute(scores, both, back)
 
 
 def solution(mesh):

time: 17.9 us -> 17.7 us (0.989)
  starting transfers between devices: 10.3 us -> 11.6 us
  Pallas kernels: 3.26 us -> 2.3 us
  local copies, waits for them, and re-layouts: 1.1 us -> 0.53 us
    ppermute x1, starting transfers between devices: 1.4 us -> 2.75 us  [on_device(): return lax.ppermute(scores, both, back)]
    unnamed x10 -> x11, local copies, waits for them, and re-layouts: 1.1 us -> 0.53 us
    pallas_call x1 -> x0, Pallas kernels: 0.52 us -> none  [on_device(): pl.pallas_call(store_kernel, in_specs=[vmem], out_specs=pl.BlockSpec(memo...]
    pallas_call x4, Pallas kernels: 0.76 us -> 0.3 us  [on_device(): pl.pallas_call(score_kernel, in_specs=[vmem] * 4, out_specs=vmem, out_sha...]
  transfers between devices with their start and end apart: 11 -> 11, of which waited for: 4 -> 6; matrix products, arithmetic and copies ran while one was open for 0% -> 0% of each run, Pallas kernels for 13% -> 11%
where the time goes in v16:
time: 17.7 us; the launch traced here: 17.6 us
  starting transfers between devices  11.6 us (66%)
  waiting for transfers between devices  3.09 us (17%)
  Pallas kernels  2.3 us (13%)
  local copies, waits for them, and re-layouts  0.53 us (3%)
    ppermute x3, starting transfers between devices, on_device(): halves.append(lax.ppermute(sent, 'dp', [(d, d ^ r) for d in range(clips)]))  4.6 us
    ppermute x4, starting transfers between devices, on_device(): swapped.append(lax.ppermute(half, 'tensor', swap))  3.31 us
    ppermute x1, starting transfers between devices, on_device(): return lax.ppermute(scores, both, back)  2.75 us
    ppermute x1, waiting for transfers between devices, on_device(): return lax.ppermute(scores, both, back)  1.3 us
    pallas_call x1, Pallas kernels, on_device(): pl.pallas_call(functools.partial(project_kernel, rank), in_specs=[vmem] *...  1.17 us
    ppermute x1, waiting for transfers between devices, on_device(): far_sketch = lax.ppermute(sketch, both, there)  0.88 us
    ppermute x2, waiting for transfers between devices, on_device(): other = [lax.ppermute(part, 'tensor', swap) for part in partial]  0.73 us
    ppermute x2, starting transfers between devices, on_device(): other = [lax.ppermute(part, 'tensor', swap) for part in partial]  0.57 us
  transfers between devices with their start and end apart: 11, of which 6 were waited for; matrix products, arithmetic and copies ran while one was open for 0% of the time, Pallas kernels for 11%

profile of v16, /device:TPU:0, one launch (start us, length us, event | category | flops | bytes accessed | tf_op | source)
XLA Modules:
  0.0 17.6 jit_solution(13523077732101486749)
XLA Ops:
  0.0 3.0 %collective-permute-start.2 = (bf16[32,2048]{1,0:T(8,128)(2,1)}, bf16[32,2048]{1,0:T(8,128)(2,1)S(1)}, u32[]{:S(2)}, u32[]{:S(2)}) collective-permute-start(bf16[32,2048]{1,0:T(8,128)(2,1)} %own_ref.1), channel_id=1, source_target_pairs={{0,2},{2,0},{4,6},{6,4},{8,10},{10,8},{12,14},{14,12},{1,3},{3,1},... | collective-permute-start | bytes 393224 | tf_op jit(solution)/shard_map/ppermute | solution.py:138
  3.0 1.6 %collective-permute-start.1 = (bf16[32,2048]{1,0:T(8,128)(2,1)}, bf16[32,2048]{1,0:T(8,128)(2,1)S(1)}, u32[]{:S(2)}, u32[]{:S(2)}) collective-permute-start(bf16[32,2048]{1,0:T(8,128)(2,1)} %own_ref.1), channel_id=1, source_target_pairs={{0,4},{2,6},{4,0},{6,2},{8,12},{10,14},{12,8},{14,10},{1,5},{3,7},... | collective-permute-start | bytes 393224 | tf_op jit(solution)/shard_map/ppermute | solution.py:138
  4.6 1.2 %project.1 = (f32[192,128]{1,0:T(8,128)S(1)}, f32[192,128]{1,0:T(8,128)S(1)}) custom-call(f32[8,128]{1,0:T(8,128)S(1)} %first.1.first_ref, bf16[1,384,2560]{2,1,0:T(8,128)(2,1)S(1)} %copy-done, bf16[1,384,2560]{2,1,0:T(8,128)(2,1)S(1)} %copy-done.1, bf16[2560,128]{1,0:T(8,128)(2,1)S(1)} %copy-done.2), custom_call_target="tpu_custom_call" | custom-call | flops 503316480 | bytes 3932160 | tf_op jit(solution)/shard_map/project/pallas_call | solution.py:139
  5.8 0.1 collective-permute-start.3
  5.9 0.5 %collective-permute-start.4 = (f32[192,128]{1,0:T(8,128)S(1)}, f32[192,128]{1,0:T(8,128)S(1)}, u32[]{:S(2)}, u32[]{:S(2)}) collective-permute-start(f32[192,128]{1,0:T(8,128)S(1)} %get-tuple-element.22.refs_1_), channel_id=1, source_target_pairs={{0,1},{1,0},{2,3},{3,2},{4,5},{5,4},{6,7},{7,6},{8,9},{9,8},{10,11... | collective-permute-start | bytes 294920 | tf_op jit(solution)/shard_map/ppermute | solution.py:151
  6.4 0.2 %count.1.count_ref = f32[384,128]{1,0:T(8,128)S(1)} custom-call(s32[1,256]{1,0:T(1,128)S(1)} %copy-done.4), custom_call_target="tpu_custom_call" | custom-call | flops 1 | bytes 1 | tf_op jit(solution)/shard_map/count/pallas_call | solution.py:152
  6.6 0.6 %collective-permute-done.3.refs_2_ = f32[192,128]{1,0:T(8,128)S(1)} collective-permute-done((f32[192,128]{1,0:T(8,128)S(1)}, f32[192,128]{1,0:T(8,128)S(1)}, u32[]{:S(2)}, u32[]{:S(2)}) %collective-permute-start.3) | collective-permute-done | bytes 98336 | tf_op jit(solution)/shard_map/ppermute | solution.py:151
  7.2 0.2 collective-permute-done.4.refs_3_
  7.3 0.4 %sketch.1.own_ref = bf16[32,128]{1,0:T(8,128)(2,1)S(1)} custom-call(f32[384,128]{1,0:T(8,128)S(1)} %count.1.count_ref, f32[192,128]{1,0:T(8,128)S(1)} %get-tuple-element.21.refs_0_, f32[192,128]{1,0:T(8,128)S(1)} %get-tuple-element.22.refs_1_, f32[192,128]{1,0:T(8,128)S(1)} %collective-permute-done.3.refs_2_, f32[192,128]{1,0:T(8,128)S(1)} %collective-permute-done.4.refs_3_), custom_call_target="tpu_custom_call" | custom-call | flops 1 | bytes 1 | tf_op jit(solution)/shard_map/sketch/pallas_call | solution.py:161
  7.7 0.4 %collective-permute-start.5 = (bf16[32,128]{1,0:T(8,128)(2,1)S(1)}, bf16[32,128]{1,0:T(8,128)(2,1)S(1)}, u32[]{:S(2)}, u32[]{:S(2)}) collective-permute-start(bf16[32,128]{1,0:T(8,128)(2,1)S(1)} %sketch.1.own_ref), channel_id=1, source_target_pairs={{1,9},{3,11},{5,13},{7,15},{8,0},{10,2},{12,4},{14,6},{0,1},{2,3},... | collective-permute-start | bytes 24584 | tf_op jit(solution)/shard_map/ppermute | solution.py:172
  8.1 2.7 %collective-permute-start.6 = (bf16[32,2048]{1,0:T(8,128)(2,1)S(1)}, bf16[32,2048]{1,0:T(8,128)(2,1)S(1)}, u32[]{:S(2)}, u32[]{:S(2)}) collective-permute-start(bf16[32,2048]{1,0:T(8,128)(2,1)S(1)} %copy-done.3), channel_id=1, source_target_pairs={{0,1},{1,0},{2,3},{3,2},{4,5},{5,4},{6,7},{7,6},{8,9},{9,8},{10,11... | collective-permute-start | bytes 393224 | tf_op jit(solution)/shard_map/ppermute | solution.py:176
  10.8 0.1 collective-permute-done.own_ref
  10.9 0.5 %collective-permute-start.8 = (bf16[32,2048]{1,0:T(8,128)(2,1)S(1)}, bf16[32,2048]{1,0:T(8,128)(2,1)S(1)}, u32[]{:S(2)}, u32[]{:S(2)}) collective-permute-start(bf16[32,2048]{1,0:T(8,128)(2,1)S(1)} %collective-permute-done.1.own_ref), channel_id=1, source_target_pairs={{0,1},{1,0},{2,3},{3,2},{4,5},{5,4},{6,7},{7,6},{8,9},{9,8},{10,11... | collective-permute-start | bytes 393224 | tf_op jit(solution)/shard_map/ppermute | solution.py:176
  11.4 0.1 collective-permute-start.7
  11.5 0.9 %collective-permute-done.5.far_ref = bf16[32,128]{1,0:T(8,128)(2,1)S(1)} collective-permute-done((bf16[32,128]{1,0:T(8,128)(2,1)S(1)}, bf16[32,128]{1,0:T(8,128)(2,1)S(1)}, u32[]{:S(2)}, u32[]{:S(2)}) %collective-permute-start.5) | collective-permute-done | bytes 8224 | tf_op jit(solution)/shard_map/ppermute | solution.py:172
  12.4 0.1 score.4.refs_0_
  12.5 0.1 score.7.refs_3_
  12.5 0.1 score.6.refs_2_
  12.6 0.1 collective-permute-done.7.other_ref
  12.7 0.1 score.5.refs_1_
  12.8 0.2 %arrange.1 = f32[1,128]{1,0:T(1,128)S(1)} custom-call(f32[32,128]{1,0:T(8,128)S(1)} %score.4.refs_0_, f32[32,128]{1,0:T(8,128)S(1)} %score.5.refs_1_, f32[32,128]{1,0:T(8,128)S(1)} %score.6.refs_2_, f32[32,128]{1,0:T(8,128)S(1)} %score.7.refs_3_), custom_call_target="tpu_custom_call" | custom-call | flops 1 | bytes 1 | tf_op jit(solution)/shard_map/arrange/pallas_call | solution.py:203
  13.0 2.7 %collective-permute-start.10 = (f32[1,128]{1,0:T(1,128)S(1)}, f32[1,128]{1,0:T(1,128)S(1)}, u32[]{:S(2)}, u32[]{:S(2)}) collective-permute-start(f32[1,128]{1,0:T(1,128)S(1)} %arrange.1), channel_id=1, source_target_pairs={{9,1},{11,3},{13,5},{15,7},{0,8},{2,10},{4,12},{6,14},{1,0},{3,2},... | collective-permute-start | bytes 1544 | tf_op jit(solution)/shard_map/ppermute | solution.py:212
  15.8 1.3 %collective-permute-done.10 = f32[1,128]{1,0:T(1,128)S(1)} collective-permute-done((f32[1,128]{1,0:T(1,128)S(1)}, f32[1,128]{1,0:T(1,128)S(1)}, u32[]{:S(2)}, u32[]{:S(2)}) %collective-permute-start.10) | collective-permute-done | bytes 544 | tf_op jit(solution)/shard_map/ppermute | solution.py:212
  17.1 0.5 %copy.7 = f32[1,128]{1,0:T(1,128)} copy(f32[1,128]{1,0:T(1,128)S(1)} %collective-permute-done.10) | data formatting | bytes 1024
  (19 shorter events, 0.1 us)
Async XLA Ops:
  0.0 4.6 %copy-start = (bf16[1,384,2560]{2,1,0:T(8,128)(2,1)S(1)}, bf16[1,384,2560]{2,1,0:T(8,128)(2,1)}, u32[]{:S(2)}) copy-start(bf16[1,384,2560]{2,1,0:T(8,128)(2,1)} %acts_ref.1) | copy-start | bytes 5898244
  0.0 4.6 %copy-start.1 = (bf16[1,384,2560]{2,1,0:T(8,128)(2,1)S(1)}, bf16[1,384,2560]{2,1,0:T(8,128)(2,1)}, u32[]{:S(2)}) copy-start(bf16[1,384,2560]{2,1,0:T(8,128)(2,1)} %grads_ref.1) | copy-start | bytes 5898244
  0.0 4.6 %copy-start.2 = (bf16[2560,128]{1,0:T(8,128)(2,1)S(1)}, bf16[2560,128]{1,0:T(8,128)(2,1)}, u32[]{:S(2)}) copy-start(bf16[2560,128]{1,0:T(8,128)(2,1)} %proj_ref.1) | copy-start | bytes 1966084
  0.0 6.4 %copy-start.4 = (s32[1,256]{1,0:T(1,128)S(1)}, s32[1,256]{1,0:T(1,128)}, u32[]{:S(2)}) copy-start(s32[1,256]{1,0:T(1,128)} %picks_ref.1) | copy-start | bytes 3076
  0.0 8.1 %copy-start.3 = (bf16[32,2048]{1,0:T(8,128)(2,1)S(1)}, bf16[32,2048]{1,0:T(8,128)(2,1)}, u32[]{:S(2)}) copy-start(bf16[32,2048]{1,0:T(8,128)(2,1)} %own_ref.1) | copy-start | bytes 393220
  0.0 10.8 %collective-permute-start.2 = (bf16[32,2048]{1,0:T(8,128)(2,1)}, bf16[32,2048]{1,0:T(8,128)(2,1)S(1)}, u32[]{:S(2)}, u32[]{:S(2)}) collective-permute-start(bf16[32,2048]{1,0:T(8,128)(2,1)} %own_ref.1), channel_id=1, source_target_pairs={{0,2},{2,0},{4,6},{6,4},{8,10},{10,8},{12,14},{14,12},{1,3},{3,1},... | collective-permute-start | bytes 393224 | tf_op jit(solution)/shard_map/ppermute | solution.py:138
  3.0 7.7 %collective-permute-start.1 = (bf16[32,2048]{1,0:T(8,128)(2,1)}, bf16[32,2048]{1,0:T(8,128)(2,1)S(1)}, u32[]{:S(2)}, u32[]{:S(2)}) collective-permute-start(bf16[32,2048]{1,0:T(8,128)(2,1)} %own_ref.1), channel_id=1, source_target_pairs={{0,4},{2,6},{4,0},{6,2},{8,12},{10,14},{12,8},{14,10},{1,5},{3,7},... | collective-permute-start | bytes 393224 | tf_op jit(solution)/shard_map/ppermute | solution.py:138
  4.6 6.2 %collective-permute-start = (bf16[32,2048]{1,0:T(8,128)(2,1)}, bf16[32,2048]{1,0:T(8,128)(2,1)S(1)}, u32[]{:S(2)}, u32[]{:S(2)}) collective-permute-start(bf16[32,2048]{1,0:T(8,128)(2,1)} %own_ref.1), channel_id=1, source_target_pairs={{0,6},{2,4},{4,2},{6,0},{8,14},{10,12},{12,10},{14,8},{1,7},{3,5},... | collective-permute-start | bytes 393224 | tf_op jit(solution)/shard_map/ppermute | solution.py:138
  5.8 1.4 %collective-permute-start.3 = (f32[192,128]{1,0:T(8,128)S(1)}, f32[192,128]{1,0:T(8,128)S(1)}, u32[]{:S(2)}, u32[]{:S(2)}) collective-permute-start(f32[192,128]{1,0:T(8,128)S(1)} %get-tuple-element.21.refs_0_), channel_id=1, source_target_pairs={{0,1},{1,0},{2,3},{3,2},{4,5},{5,4},{6,7},{7,6},{8,9},{9,8},{10,11... | collective-permute-start | bytes 294920 | tf_op jit(solution)/shard_map/ppermute | solution.py:151
  5.9 1.4 %collective-permute-start.4 = (f32[192,128]{1,0:T(8,128)S(1)}, f32[192,128]{1,0:T(8,128)S(1)}, u32[]{:S(2)}, u32[]{:S(2)}) collective-permute-start(f32[192,128]{1,0:T(8,128)S(1)} %get-tuple-element.22.refs_1_), channel_id=1, source_target_pairs={{0,1},{1,0},{2,3},{3,2},{4,5},{5,4},{6,7},{7,6},{8,9},{9,8},{10,11... | collective-permute-start | bytes 294920 | tf_op jit(solution)/shard_map/ppermute | solution.py:151
  7.7 4.6 %collective-permute-start.5 = (bf16[32,128]{1,0:T(8,128)(2,1)S(1)}, bf16[32,128]{1,0:T(8,128)(2,1)S(1)}, u32[]{:S(2)}, u32[]{:S(2)}) collective-permute-start(bf16[32,128]{1,0:T(8,128)(2,1)S(1)} %sketch.1.own_ref), channel_id=1, source_target_pairs={{1,9},{3,11},{5,13},{7,15},{8,0},{10,2},{12,4},{14,6},{0,1},{2,3},... | collective-permute-start | bytes 24584 | tf_op jit(solution)/shard_map/ppermute | solution.py:172
  8.1 4.3 %collective-permute-start.6 = (bf16[32,2048]{1,0:T(8,128)(2,1)S(1)}, bf16[32,2048]{1,0:T(8,128)(2,1)S(1)}, u32[]{:S(2)}, u32[]{:S(2)}) collective-permute-start(bf16[32,2048]{1,0:T(8,128)(2,1)S(1)} %copy-done.3), channel_id=1, source_target_pairs={{0,1},{1,0},{2,3},{3,2},{4,5},{5,4},{6,7},{7,6},{8,9},{9,8},{10,11... | collective-permute-start | bytes 393224 | tf_op jit(solution)/shard_map/ppermute | solution.py:176
  10.9 1.6 %collective-permute-start.9 = (bf16[32,2048]{1,0:T(8,128)(2,1)S(1)}, bf16[32,2048]{1,0:T(8,128)(2,1)S(1)}, u32[]{:S(2)}, u32[]{:S(2)}) collective-permute-start(bf16[32,2048]{1,0:T(8,128)(2,1)S(1)} %collective-permute-done.own_ref), channel_id=1, source_target_pairs={{0,1},{1,0},{2,3},{3,2},{4,5},{5,4},{6,7},{7,6},{8,9},{9,8},{10,11... | collective-permute-start | bytes 393224 | tf_op jit(solution)/shard_map/ppermute | solution.py:176
  10.9 1.7 %collective-permute-start.8 = (bf16[32,2048]{1,0:T(8,128)(2,1)S(1)}, bf16[32,2048]{1,0:T(8,128)(2,1)S(1)}, u32[]{:S(2)}, u32[]{:S(2)}) collective-permute-start(bf16[32,2048]{1,0:T(8,128)(2,1)S(1)} %collective-permute-done.1.own_ref), channel_id=1, source_target_pairs={{0,1},{1,0},{2,3},{3,2},{4,5},{5,4},{6,7},{7,6},{8,9},{9,8},{10,11... | collective-permute-start | bytes 393224 | tf_op jit(solution)/shard_map/ppermute | solution.py:176
  11.4 1.3 %collective-permute-start.7 = (bf16[32,2048]{1,0:T(8,128)(2,1)S(1)}, bf16[32,2048]{1,0:T(8,128)(2,1)S(1)}, u32[]{:S(2)}, u32[]{:S(2)}) collective-permute-start(bf16[32,2048]{1,0:T(8,128)(2,1)S(1)} %collective-permute-done.2.own_ref), channel_id=1, source_target_pairs={{0,1},{1,0},{2,3},{3,2},{4,5},{5,4},{6,7},{7,6},{8,9},{9,8},{10,11... | collective-permute-start | bytes 393224 | tf_op jit(solution)/shard_map/ppermute | solution.py:176
  13.0 4.0 %collective-permute-start.10 = (f32[1,128]{1,0:T(1,128)S(1)}, f32[1,128]{1,0:T(1,128)S(1)}, u32[]{:S(2)}, u32[]{:S(2)}) collective-permute-start(f32[1,128]{1,0:T(1,128)S(1)} %arrange.1), channel_id=1, source_target_pairs={{9,1},{11,3},{13,5},{15,7},{0,8},{2,10},{4,12},{6,14},{1,0},{3,2},... | collective-permute-start | bytes 1544 | tf_op jit(solution)/shard_map/ppermute | solution.py:212

commit v17 on v16

--- a/solution.py
+++ b/solution.py
@@ -74,7 +74,8 @@
             out_ref[:, j * LANES : (j + 1) * LANES] = rows
 
 
-def score_kernel(first_ref, second_ref, own_ref, other_ref, out_ref):
+def score_kernel(first_ref, second_ref, own_ref, other_ref, *refs):
+    out_ref = refs[-1]
     total = None
     for flat_ref, query_ref in ((first_ref, own_ref), (second_ref, other_ref)):
         for j in range(query_ref.shape[1] // LANES):
@@ -134,7 +135,7 @@
     )()
     sent, first = lax.optimization_barrier((queries, first))
     halves = [queries]
-    for r in range(1, mates):
+    for r in range(mates - 1, 0, -1):
         halves.append(lax.ppermute(sent, "dp", [(d, d ^ r) for d in range(clips)]))
     partial = pl.pallas_call(
         functools.partial(project_kernel, rank),
@@ -188,18 +189,20 @@
     )(sketch, far_sketch)
     small = pl.CostEstimate(flops=1, bytes_accessed=1, transcendentals=0)
     few = pltpu.CompilerParams(vmem_limit_bytes=8 << 20)
-    parts = [
-        pl.pallas_call(
-            score_kernel,
-            in_specs=[vmem] * 4,
-            out_specs=vmem,
-            out_shape=jax.ShapeDtypeStruct((own_queries, LANES), F32),
-            compiler_params=few,
-            cost_estimate=small,
-            name="score",
-        )(*flats, half, other)
-        for half, other in zip(halves, swapped)
-    ]
+    parts = []
+    for half, other in zip(halves, swapped):
+        before = parts[-1:]
+        parts.append(
+            pl.pallas_call(
+                score_kernel,
+                in_specs=[vmem] * (4 + len(before)),
+                out_specs=vmem,
+                out_shape=jax.ShapeDtypeStruct((own_queries, LANES), F32),
+                compiler_params=few,
+                cost_estimate=small,
+                name="score",
+            )(*flats, half, other, *before)
+        )
     scores = pl.pallas_call(
         arrange_kernel,
         in_specs=[vmem] * mates,
@@ -208,7 +211,7 @@
         compiler_params=few,
         cost_estimate=small,
         name="arrange",
-    )(*parts)
+    )(parts[0], *parts[:0:-1])
     return lax.ppermute(scores, both, back)
 
 

time: 17.7 us -> 17.5 us (0.989)
  starting transfers between devices: 11.6 us -> 11.4 us
    ppermute x1, starting transfers between devices: 2.75 us -> 2.48 us  [on_device(): return lax.ppermute(scores, both, back)]
  transfers between devices with their start and end apart: 11 -> 11, of which waited for: 6 -> 5; matrix products, arithmetic and copies ran while one was open for 0% -> 0% of each run, Pallas kernels for 11% -> 12%
where the time goes in v17:
time: 17.5 us; the launch traced here: 17.3 us
  starting transfers between devices  11.4 us (65%)
  waiting for transfers between devices  3.03 us (17%)
  Pallas kernels  2.3 us (13%)
  local copies, waits for them, and re-layouts  0.53 us (3%)
    ppermute x3, starting transfers between devices, on_device(): halves.append(lax.ppermute(sent, 'dp', [(d, d ^ r) for d in range(clips)]))  4.67 us
    ppermute x4, starting transfers between devices, on_device(): swapped.append(lax.ppermute(half, 'tensor', swap))  3.31 us
    ppermute x1, starting transfers between devices, on_device(): return lax.ppermute(scores, both, back)  2.48 us
    ppermute x1, waiting for transfers between devices, on_device(): return lax.ppermute(scores, both, back)  1.3 us
    pallas_call x1, Pallas kernels, on_device(): pl.pallas_call(functools.partial(project_kernel, rank), in_specs=[vmem] *...  1.17 us
    ppermute x1, waiting for transfers between devices, on_device(): far_sketch = lax.ppermute(sketch, both, there)  0.88 us
    ppermute x2, waiting for transfers between devices, on_device(): other = [lax.ppermute(part, 'tensor', swap) for part in partial]  0.74 us
    ppermute x2, starting transfers between devices, on_device(): other = [lax.ppermute(part, 'tensor', swap) for part in partial]  0.57 us
  transfers between devices with their start and end apart: 11, of which 5 were waited for; matrix products, arithmetic and copies ran while one was open for 0% of the time, Pallas kernels for 12%

profile of v17, /device:TPU:0, one launch (start us, length us, event | category | flops | bytes accessed | tf_op | source)
XLA Modules:
  0.0 17.3 jit_solution(475511133583339320)
XLA Ops:
  0.0 4.0 %collective-permute-start.2 = (bf16[32,2048]{1,0:T(8,128)(2,1)}, bf16[32,2048]{1,0:T(8,128)(2,1)S(1)}, u32[]{:S(2)}, u32[]{:S(2)}) collective-permute-start(bf16[32,2048]{1,0:T(8,128)(2,1)} %own_ref.1), channel_id=1, source_target_pairs={{0,6},{2,4},{4,2},{6,0},{8,14},{10,12},{12,10},{14,8},{1,7},{3,5},... | collective-permute-start | bytes 393224 | tf_op jit(solution)/shard_map/ppermute | solution.py:139
  4.1 0.4 %collective-permute-start.1 = (bf16[32,2048]{1,0:T(8,128)(2,1)}, bf16[32,2048]{1,0:T(8,128)(2,1)S(1)}, u32[]{:S(2)}, u32[]{:S(2)}) collective-permute-start(bf16[32,2048]{1,0:T(8,128)(2,1)} %own_ref.1), channel_id=1, source_target_pairs={{0,4},{2,6},{4,0},{6,2},{8,12},{10,14},{12,8},{14,10},{1,5},{3,7},... | collective-permute-start | bytes 393224 | tf_op jit(solution)/shard_map/ppermute | solution.py:139
  4.5 0.2 %collective-permute-start = (bf16[32,2048]{1,0:T(8,128)(2,1)}, bf16[32,2048]{1,0:T(8,128)(2,1)S(1)}, u32[]{:S(2)}, u32[]{:S(2)}) collective-permute-start(bf16[32,2048]{1,0:T(8,128)(2,1)} %own_ref.1), channel_id=1, source_target_pairs={{0,2},{2,0},{4,6},{6,4},{8,10},{10,8},{12,14},{14,12},{1,3},{3,1},... | collective-permute-start | bytes 393224 | tf_op jit(solution)/shard_map/ppermute | solution.py:139
  4.7 1.2 %project.1 = (f32[192,128]{1,0:T(8,128)S(1)}, f32[192,128]{1,0:T(8,128)S(1)}) custom-call(f32[8,128]{1,0:T(8,128)S(1)} %first.1.first_ref, bf16[1,384,2560]{2,1,0:T(8,128)(2,1)S(1)} %copy-done, bf16[1,384,2560]{2,1,0:T(8,128)(2,1)S(1)} %copy-done.1, bf16[2560,128]{1,0:T(8,128)(2,1)S(1)} %copy-done.2), custom_call_target="tpu_custom_call" | custom-call | flops 503316480 | bytes 3932160 | tf_op jit(solution)/shard_map/project/pallas_call | solution.py:140
  6.0 0.5 %collective-permute-start.4 = (f32[192,128]{1,0:T(8,128)S(1)}, f32[192,128]{1,0:T(8,128)S(1)}, u32[]{:S(2)}, u32[]{:S(2)}) collective-permute-start(f32[192,128]{1,0:T(8,128)S(1)} %get-tuple-element.22.refs_1_), channel_id=1, source_target_pairs={{0,1},{1,0},{2,3},{3,2},{4,5},{5,4},{6,7},{7,6},{8,9},{9,8},{10,11... | collective-permute-start | bytes 294920 | tf_op jit(solution)/shard_map/ppermute | solution.py:152
  6.5 0.2 %count.1.count_ref = f32[384,128]{1,0:T(8,128)S(1)} custom-call(s32[1,256]{1,0:T(1,128)S(1)} %copy-done.4), custom_call_target="tpu_custom_call" | custom-call | flops 1 | bytes 1 | tf_op jit(solution)/shard_map/count/pallas_call | solution.py:153
  6.7 0.6 %collective-permute-done.3.refs_2_ = f32[192,128]{1,0:T(8,128)S(1)} collective-permute-done((f32[192,128]{1,0:T(8,128)S(1)}, f32[192,128]{1,0:T(8,128)S(1)}, u32[]{:S(2)}, u32[]{:S(2)}) %collective-permute-start.3) | collective-permute-done | bytes 98336 | tf_op jit(solution)/shard_map/ppermute | solution.py:152
  7.3 0.2 collective-permute-done.4.refs_3_
  7.4 0.4 %sketch.1.own_ref = bf16[32,128]{1,0:T(8,128)(2,1)S(1)} custom-call(f32[384,128]{1,0:T(8,128)S(1)} %count.1.count_ref, f32[192,128]{1,0:T(8,128)S(1)} %get-tuple-element.21.refs_0_, f32[192,128]{1,0:T(8,128)S(1)} %get-tuple-element.22.refs_1_, f32[192,128]{1,0:T(8,128)S(1)} %collective-permute-done.3.refs_2_, f32[192,128]{1,0:T(8,128)S(1)} %collective-permute-done.4.refs_3_), custom_call_target="tpu_custom_call" | custom-call | flops 1 | bytes 1 | tf_op jit(solution)/shard_map/sketch/pallas_call | solution.py:162
  7.8 0.4 %collective-permute-start.5 = (bf16[32,128]{1,0:T(8,128)(2,1)S(1)}, bf16[32,128]{1,0:T(8,128)(2,1)S(1)}, u32[]{:S(2)}, u32[]{:S(2)}) collective-permute-start(bf16[32,128]{1,0:T(8,128)(2,1)S(1)} %sketch.1.own_ref), channel_id=1, source_target_pairs={{1,9},{3,11},{5,13},{7,15},{8,0},{10,2},{12,4},{14,6},{0,1},{2,3},... | collective-permute-start | bytes 24584 | tf_op jit(solution)/shard_map/ppermute | solution.py:173
  8.1 2.7 %collective-permute-start.6 = (bf16[32,2048]{1,0:T(8,128)(2,1)S(1)}, bf16[32,2048]{1,0:T(8,128)(2,1)S(1)}, u32[]{:S(2)}, u32[]{:S(2)}) collective-permute-start(bf16[32,2048]{1,0:T(8,128)(2,1)S(1)} %copy-done.3), channel_id=1, source_target_pairs={{0,1},{1,0},{2,3},{3,2},{4,5},{5,4},{6,7},{7,6},{8,9},{9,8},{10,11... | collective-permute-start | bytes 393224 | tf_op jit(solution)/shard_map/ppermute | solution.py:177
  10.8 0.1 collective-permute-start.9
  10.9 0.5 %collective-permute-start.8 = (bf16[32,2048]{1,0:T(8,128)(2,1)S(1)}, bf16[32,2048]{1,0:T(8,128)(2,1)S(1)}, u32[]{:S(2)}, u32[]{:S(2)}) collective-permute-start(bf16[32,2048]{1,0:T(8,128)(2,1)S(1)} %collective-permute-done.1.own_ref), channel_id=1, source_target_pairs={{0,1},{1,0},{2,3},{3,2},{4,5},{5,4},{6,7},{7,6},{8,9},{9,8},{10,11... | collective-permute-start | bytes 393224 | tf_op jit(solution)/shard_map/ppermute | solution.py:177
  11.4 0.1 collective-permute-start.7
  11.5 0.9 %collective-permute-done.5.far_ref = bf16[32,128]{1,0:T(8,128)(2,1)S(1)} collective-permute-done((bf16[32,128]{1,0:T(8,128)(2,1)S(1)}, bf16[32,128]{1,0:T(8,128)(2,1)S(1)}, u32[]{:S(2)}, u32[]{:S(2)}) %collective-permute-start.5) | collective-permute-done | bytes 8224 | tf_op jit(solution)/shard_map/ppermute | solution.py:173
  12.4 0.1 score.4.refs_0_
  12.5 0.1 score.5.refs_0_.refs_3_
  12.6 0.1 score.6.refs_0_.refs_2_
  12.6 0.1 collective-permute-done.7.other_ref
  12.7 0.1 score.7.refs_1_
  12.8 0.2 %arrange.1 = f32[1,128]{1,0:T(1,128)S(1)} custom-call(f32[32,128]{1,0:T(8,128)S(1)} %score.4.refs_0_, f32[32,128]{1,0:T(8,128)S(1)} %score.7.refs_1_, f32[32,128]{1,0:T(8,128)S(1)} %score.6.refs_0_.refs_2_, f32[32,128]{1,0:T(8,128)S(1)} %score.5.refs_0_.refs_3_), custom_call_target="tpu_custom_call" | custom-call | flops 1 | bytes 1 | tf_op jit(solution)/shard_map/arrange/pallas_call | solution.py:206
  13.0 2.5 %collective-permute-start.10 = (f32[1,128]{1,0:T(1,128)S(1)}, f32[1,128]{1,0:T(1,128)S(1)}, u32[]{:S(2)}, u32[]{:S(2)}) collective-permute-start(f32[1,128]{1,0:T(1,128)S(1)} %arrange.1), channel_id=1, source_target_pairs={{9,1},{11,3},{13,5},{15,7},{0,8},{2,10},{4,12},{6,14},{1,0},{3,2},... | collective-permute-start | bytes 1544 | tf_op jit(solution)/shard_map/ppermute | solution.py:215
  15.5 1.3 %collective-permute-done.10 = f32[1,128]{1,0:T(1,128)S(1)} collective-permute-done((f32[1,128]{1,0:T(1,128)S(1)}, f32[1,128]{1,0:T(1,128)S(1)}, u32[]{:S(2)}, u32[]{:S(2)}) %collective-permute-start.10) | collective-permute-done | bytes 544 | tf_op jit(solution)/shard_map/ppermute | solution.py:215
  16.8 0.5 %copy.7 = f32[1,128]{1,0:T(1,128)} copy(f32[1,128]{1,0:T(1,128)S(1)} %collective-permute-done.10) | data formatting | bytes 1024
  (19 shorter events, 0.1 us)
Async XLA Ops:
  0.0 4.7 %copy-start = (bf16[1,384,2560]{2,1,0:T(8,128)(2,1)S(1)}, bf16[1,384,2560]{2,1,0:T(8,128)(2,1)}, u32[]{:S(2)}) copy-start(bf16[1,384,2560]{2,1,0:T(8,128)(2,1)} %acts_ref.1) | copy-start | bytes 5898244
  0.0 4.7 %copy-start.1 = (bf16[1,384,2560]{2,1,0:T(8,128)(2,1)S(1)}, bf16[1,384,2560]{2,1,0:T(8,128)(2,1)}, u32[]{:S(2)}) copy-start(bf16[1,384,2560]{2,1,0:T(8,128)(2,1)} %grads_ref.1) | copy-start | bytes 5898244
  0.0 4.7 %copy-start.2 = (bf16[2560,128]{1,0:T(8,128)(2,1)S(1)}, bf16[2560,128]{1,0:T(8,128)(2,1)}, u32[]{:S(2)}) copy-start(bf16[2560,128]{1,0:T(8,128)(2,1)} %proj_ref.1) | copy-start | bytes 1966084
  0.0 6.5 %copy-start.4 = (s32[1,256]{1,0:T(1,128)S(1)}, s32[1,256]{1,0:T(1,128)}, u32[]{:S(2)}) copy-start(s32[1,256]{1,0:T(1,128)} %picks_ref.1) | copy-start | bytes 3076
  0.0 8.1 %copy-start.3 = (bf16[32,2048]{1,0:T(8,128)(2,1)S(1)}, bf16[32,2048]{1,0:T(8,128)(2,1)}, u32[]{:S(2)}) copy-start(bf16[32,2048]{1,0:T(8,128)(2,1)} %own_ref.1) | copy-start | bytes 393220
  0.0 10.8 %collective-permute-start.2 = (bf16[32,2048]{1,0:T(8,128)(2,1)}, bf16[32,2048]{1,0:T(8,128)(2,1)S(1)}, u32[]{:S(2)}, u32[]{:S(2)}) collective-permute-start(bf16[32,2048]{1,0:T(8,128)(2,1)} %own_ref.1), channel_id=1, source_target_pairs={{0,6},{2,4},{4,2},{6,0},{8,14},{10,12},{12,10},{14,8},{1,7},{3,5},... | collective-permute-start | bytes 393224 | tf_op jit(solution)/shard_map/ppermute | solution.py:139
  4.1 6.7 %collective-permute-start.1 = (bf16[32,2048]{1,0:T(8,128)(2,1)}, bf16[32,2048]{1,0:T(8,128)(2,1)S(1)}, u32[]{:S(2)}, u32[]{:S(2)}) collective-permute-start(bf16[32,2048]{1,0:T(8,128)(2,1)} %own_ref.1), channel_id=1, source_target_pairs={{0,4},{2,6},{4,0},{6,2},{8,12},{10,14},{12,8},{14,10},{1,5},{3,7},... | collective-permute-start | bytes 393224 | tf_op jit(solution)/shard_map/ppermute | solution.py:139
  4.5 6.3 %collective-permute-start = (bf16[32,2048]{1,0:T(8,128)(2,1)}, bf16[32,2048]{1,0:T(8,128)(2,1)S(1)}, u32[]{:S(2)}, u32[]{:S(2)}) collective-permute-start(bf16[32,2048]{1,0:T(8,128)(2,1)} %own_ref.1), channel_id=1, source_target_pairs={{0,2},{2,0},{4,6},{6,4},{8,10},{10,8},{12,14},{14,12},{1,3},{3,1},... | collective-permute-start | bytes 393224 | tf_op jit(solution)/shard_map/ppermute | solution.py:139
  5.9 1.4 %collective-permute-start.3 = (f32[192,128]{1,0:T(8,128)S(1)}, f32[192,128]{1,0:T(8,128)S(1)}, u32[]{:S(2)}, u32[]{:S(2)}) collective-permute-start(f32[192,128]{1,0:T(8,128)S(1)} %get-tuple-element.21.refs_0_), channel_id=1, source_target_pairs={{0,1},{1,0},{2,3},{3,2},{4,5},{5,4},{6,7},{7,6},{8,9},{9,8},{10,11... | collective-permute-start | bytes 294920 | tf_op jit(solution)/shard_map/ppermute | solution.py:152
  6.0 1.4 %collective-permute-start.4 = (f32[192,128]{1,0:T(8,128)S(1)}, f32[192,128]{1,0:T(8,128)S(1)}, u32[]{:S(2)}, u32[]{:S(2)}) collective-permute-start(f32[192,128]{1,0:T(8,128)S(1)} %get-tuple-element.22.refs_1_), channel_id=1, source_target_pairs={{0,1},{1,0},{2,3},{3,2},{4,5},{5,4},{6,7},{7,6},{8,9},{9,8},{10,11... | collective-permute-start | bytes 294920 | tf_op jit(solution)/shard_map/ppermute | solution.py:152
  7.8 4.6 %collective-permute-start.5 = (bf16[32,128]{1,0:T(8,128)(2,1)S(1)}, bf16[32,128]{1,0:T(8,128)(2,1)S(1)}, u32[]{:S(2)}, u32[]{:S(2)}) collective-permute-start(bf16[32,128]{1,0:T(8,128)(2,1)S(1)} %sketch.1.own_ref), channel_id=1, source_target_pairs={{1,9},{3,11},{5,13},{7,15},{8,0},{10,2},{12,4},{14,6},{0,1},{2,3},... | collective-permute-start | bytes 24584 | tf_op jit(solution)/shard_map/ppermute | solution.py:173
  8.1 4.2 %collective-permute-start.6 = (bf16[32,2048]{1,0:T(8,128)(2,1)S(1)}, bf16[32,2048]{1,0:T(8,128)(2,1)S(1)}, u32[]{:S(2)}, u32[]{:S(2)}) collective-permute-start(bf16[32,2048]{1,0:T(8,128)(2,1)S(1)} %copy-done.3), channel_id=1, source_target_pairs={{0,1},{1,0},{2,3},{3,2},{4,5},{5,4},{6,7},{7,6},{8,9},{9,8},{10,11... | collective-permute-start | bytes 393224 | tf_op jit(solution)/shard_map/ppermute | solution.py:177
  10.8 1.7 %collective-permute-start.9 = (bf16[32,2048]{1,0:T(8,128)(2,1)S(1)}, bf16[32,2048]{1,0:T(8,128)(2,1)S(1)}, u32[]{:S(2)}, u32[]{:S(2)}) collective-permute-start(bf16[32,2048]{1,0:T(8,128)(2,1)S(1)} %collective-permute-done.2.own_ref), channel_id=1, source_target_pairs={{0,1},{1,0},{2,3},{3,2},{4,5},{5,4},{6,7},{7,6},{8,9},{9,8},{10,11... | collective-permute-start | bytes 393224 | tf_op jit(solution)/shard_map/ppermute | solution.py:177
  10.9 1.7 %collective-permute-start.8 = (bf16[32,2048]{1,0:T(8,128)(2,1)S(1)}, bf16[32,2048]{1,0:T(8,128)(2,1)S(1)}, u32[]{:S(2)}, u32[]{:S(2)}) collective-permute-start(bf16[32,2048]{1,0:T(8,128)(2,1)S(1)} %collective-permute-done.1.own_ref), channel_id=1, source_target_pairs={{0,1},{1,0},{2,3},{3,2},{4,5},{5,4},{6,7},{7,6},{8,9},{9,8},{10,11... | collective-permute-start | bytes 393224 | tf_op jit(solution)/shard_map/ppermute | solution.py:177
  11.4 1.3 %collective-permute-start.7 = (bf16[32,2048]{1,0:T(8,128)(2,1)S(1)}, bf16[32,2048]{1,0:T(8,128)(2,1)S(1)}, u32[]{:S(2)}, u32[]{:S(2)}) collective-permute-start(bf16[32,2048]{1,0:T(8,128)(2,1)S(1)} %collective-permute-done.own_ref), channel_id=1, source_target_pairs={{0,1},{1,0},{2,3},{3,2},{4,5},{5,4},{6,7},{7,6},{8,9},{9,8},{10,11... | collective-permute-start | bytes 393224 | tf_op jit(solution)/shard_map/ppermute | solution.py:177
  13.0 3.8 %collective-permute-start.10 = (f32[1,128]{1,0:T(1,128)S(1)}, f32[1,128]{1,0:T(1,128)S(1)}, u32[]{:S(2)}, u32[]{:S(2)}) collective-permute-start(f32[1,128]{1,0:T(1,128)S(1)} %arrange.1), channel_id=1, source_target_pairs={{9,1},{11,3},{13,5},{15,7},{0,8},{2,10},{4,12},{6,14},{1,0},{3,2},... | collective-permute-start | bytes 1544 | tf_op jit(solution)/shard_map/ppermute | solution.py:215

commit v18 on v17

--- a/solution.py
+++ b/solution.py
@@ -86,22 +86,14 @@
 
 
 def arrange_kernel(*refs):
-    parts, out_ref = refs[:-1], refs[-1]
+    parts, out_ref, held = refs[:-2], refs[-2], refs[-1]
     mates = len(parts)
     own_queries = parts[0].shape[0]
-    width = mates * own_queries
-    scores = jnp.concatenate([part[...] for part in parts], axis=0).T
-    scores = jnp.broadcast_to(jnp.sum(scores, axis=0, keepdims=True), (8, width))
     member = lax.rem(lax.axis_index("dp"), mates)
-    block = lax.broadcasted_iota(jnp.int32, scores.shape, 1) // own_queries
-    step = 1
-    while step < mates:
-        up = pltpu.roll(scores, step * own_queries, 1)
-        down = pltpu.roll(scores, width - step * own_queries, 1)
-        exchanged = jnp.where(block & step == 0, down, up)
-        scores = jnp.where(member & step == 0, scores, exchanged)
-        step *= 2
-    out_ref[...] = scores[0:1, :]
+    for r, part in enumerate(parts):
+        start = pl.multiple_of((member ^ r) * own_queries, own_queries)
+        held[pl.ds(start, own_queries), :] = part[...]
+    out_ref[...] = jnp.sum(held[...].T, axis=0, keepdims=True)
 
 
 def on_device(activations, out_grads, projections, sample_index, queries):
@@ -208,6 +200,7 @@
         in_specs=[vmem] * mates,
         out_specs=vmem,
         out_shape=jax.ShapeDtypeStruct((1, width), F32),
+        scratch_shapes=[pltpu.VMEM((width, LANES), F32)],
         compiler_params=few,
         cost_estimate=small,
         name="arrange",

time: 17.5 us -> 17.4 us (level)
  no operation moved by 1% of the time
where the time goes in v18:
time: 17.4 us; the launch traced here: 17.3 us
  starting transfers between devices  11.4 us (66%)
  waiting for transfers between devices  3.03 us (17%)
  Pallas kernels  2.18 us (13%)
  local copies, waits for them, and re-layouts  0.53 us (3%)
    ppermute x3, starting transfers between devices, on_device(): halves.append(lax.ppermute(sent, 'dp', [(d, d ^ r) for d in range(clips)]))  4.67 us
    ppermute x4, starting transfers between devices, on_device(): swapped.append(lax.ppermute(half, 'tensor', swap))  3.31 us
    ppermute x1, starting transfers between devices, on_device(): return lax.ppermute(scores, both, back)  2.53 us
    ppermute x1, waiting for transfers between devices, on_device(): return lax.ppermute(scores, both, back)  1.3 us
    pallas_call x1, Pallas kernels, on_device(): pl.pallas_call(functools.partial(project_kernel, rank), in_specs=[vmem] *...  1.17 us
    ppermute x1, waiting for transfers between devices, on_device(): far_sketch = lax.ppermute(sketch, both, there)  0.88 us
    ppermute x2, waiting for transfers between devices, on_device(): other = [lax.ppermute(part, 'tensor', swap) for part in partial]  0.74 us
    ppermute x2, starting transfers between devices, on_device(): other = [lax.ppermute(part, 'tensor', swap) for part in partial]  0.57 us
  transfers between devices with their start and end apart: 11, of which 5 were waited for; matrix products, arithmetic and copies ran while one was open for 0% of the time, Pallas kernels for 12%

profile of v18, /device:TPU:0, one launch (start us, length us, event | category | flops | bytes accessed | tf_op | source)
XLA Modules:
  0.0 17.3 jit_solution(17105060889914537831)
XLA Ops:
  0.0 4.0 %collective-permute-start.2 = (bf16[32,2048]{1,0:T(8,128)(2,1)}, bf16[32,2048]{1,0:T(8,128)(2,1)S(1)}, u32[]{:S(2)}, u32[]{:S(2)}) collective-permute-start(bf16[32,2048]{1,0:T(8,128)(2,1)} %own_ref.1), channel_id=1, source_target_pairs={{0,6},{2,4},{4,2},{6,0},{8,14},{10,12},{12,10},{14,8},{1,7},{3,5},... | collective-permute-start | bytes 393224 | tf_op jit(solution)/shard_map/ppermute | solution.py:131
  4.1 0.4 %collective-permute-start.1 = (bf16[32,2048]{1,0:T(8,128)(2,1)}, bf16[32,2048]{1,0:T(8,128)(2,1)S(1)}, u32[]{:S(2)}, u32[]{:S(2)}) collective-permute-start(bf16[32,2048]{1,0:T(8,128)(2,1)} %own_ref.1), channel_id=1, source_target_pairs={{0,4},{2,6},{4,0},{6,2},{8,12},{10,14},{12,8},{14,10},{1,5},{3,7},... | collective-permute-start | bytes 393224 | tf_op jit(solution)/shard_map/ppermute | solution.py:131
  4.5 0.2 %collective-permute-start = (bf16[32,2048]{1,0:T(8,128)(2,1)}, bf16[32,2048]{1,0:T(8,128)(2,1)S(1)}, u32[]{:S(2)}, u32[]{:S(2)}) collective-permute-start(bf16[32,2048]{1,0:T(8,128)(2,1)} %own_ref.1), channel_id=1, source_target_pairs={{0,2},{2,0},{4,6},{6,4},{8,10},{10,8},{12,14},{14,12},{1,3},{3,1},... | collective-permute-start | bytes 393224 | tf_op jit(solution)/shard_map/ppermute | solution.py:131
  4.7 1.2 %project.1 = (f32[192,128]{1,0:T(8,128)S(1)}, f32[192,128]{1,0:T(8,128)S(1)}) custom-call(f32[8,128]{1,0:T(8,128)S(1)} %first.1.first_ref, bf16[1,384,2560]{2,1,0:T(8,128)(2,1)S(1)} %copy-done, bf16[1,384,2560]{2,1,0:T(8,128)(2,1)S(1)} %copy-done.1, bf16[2560,128]{1,0:T(8,128)(2,1)S(1)} %copy-done.2), custom_call_target="tpu_custom_call" | custom-call | flops 503316480 | bytes 3932160 | tf_op jit(solution)/shard_map/project/pallas_call | solution.py:132
  6.0 0.5 %collective-permute-start.4 = (f32[192,128]{1,0:T(8,128)S(1)}, f32[192,128]{1,0:T(8,128)S(1)}, u32[]{:S(2)}, u32[]{:S(2)}) collective-permute-start(f32[192,128]{1,0:T(8,128)S(1)} %get-tuple-element.22.refs_1_), channel_id=1, source_target_pairs={{0,1},{1,0},{2,3},{3,2},{4,5},{5,4},{6,7},{7,6},{8,9},{9,8},{10,11... | collective-permute-start | bytes 294920 | tf_op jit(solution)/shard_map/ppermute | solution.py:144
  6.5 0.2 %count.1.count_ref = f32[384,128]{1,0:T(8,128)S(1)} custom-call(s32[1,256]{1,0:T(1,128)S(1)} %copy-done.4), custom_call_target="tpu_custom_call" | custom-call | flops 1 | bytes 1 | tf_op jit(solution)/shard_map/count/pallas_call | solution.py:145
  6.7 0.6 %collective-permute-done.3.refs_2_ = f32[192,128]{1,0:T(8,128)S(1)} collective-permute-done((f32[192,128]{1,0:T(8,128)S(1)}, f32[192,128]{1,0:T(8,128)S(1)}, u32[]{:S(2)}, u32[]{:S(2)}) %collective-permute-start.3) | collective-permute-done | bytes 98336 | tf_op jit(solution)/shard_map/ppermute | solution.py:144
  7.3 0.2 collective-permute-done.4.refs_3_
  7.4 0.4 %sketch.1.own_ref = bf16[32,128]{1,0:T(8,128)(2,1)S(1)} custom-call(f32[384,128]{1,0:T(8,128)S(1)} %count.1.count_ref, f32[192,128]{1,0:T(8,128)S(1)} %get-tuple-element.21.refs_0_, f32[192,128]{1,0:T(8,128)S(1)} %get-tuple-element.22.refs_1_, f32[192,128]{1,0:T(8,128)S(1)} %collective-permute-done.3.refs_2_, f32[192,128]{1,0:T(8,128)S(1)} %collective-permute-done.4.refs_3_), custom_call_target="tpu_custom_call" | custom-call | flops 1 | bytes 1 | tf_op jit(solution)/shard_map/sketch/pallas_call | solution.py:154
  7.8 0.4 %collective-permute-start.5 = (bf16[32,128]{1,0:T(8,128)(2,1)S(1)}, bf16[32,128]{1,0:T(8,128)(2,1)S(1)}, u32[]{:S(2)}, u32[]{:S(2)}) collective-permute-start(bf16[32,128]{1,0:T(8,128)(2,1)S(1)} %sketch.1.own_ref), channel_id=1, source_target_pairs={{1,9},{3,11},{5,13},{7,15},{8,0},{10,2},{12,4},{14,6},{0,1},{2,3},... | collective-permute-start | bytes 24584 | tf_op jit(solution)/shard_map/ppermute | solution.py:165
  8.1 2.7 %collective-permute-start.6 = (bf16[32,2048]{1,0:T(8,128)(2,1)S(1)}, bf16[32,2048]{1,0:T(8,128)(2,1)S(1)}, u32[]{:S(2)}, u32[]{:S(2)}) collective-permute-start(bf16[32,2048]{1,0:T(8,128)(2,1)S(1)} %copy-done.3), channel_id=1, source_target_pairs={{0,1},{1,0},{2,3},{3,2},{4,5},{5,4},{6,7},{7,6},{8,9},{9,8},{10,11... | collective-permute-start | bytes 393224 | tf_op jit(solution)/shard_map/ppermute | solution.py:169
  10.8 0.1 collective-permute-start.9
  10.9 0.5 %collective-permute-start.8 = (bf16[32,2048]{1,0:T(8,128)(2,1)S(1)}, bf16[32,2048]{1,0:T(8,128)(2,1)S(1)}, u32[]{:S(2)}, u32[]{:S(2)}) collective-permute-start(bf16[32,2048]{1,0:T(8,128)(2,1)S(1)} %collective-permute-done.1.own_ref), channel_id=1, source_target_pairs={{0,1},{1,0},{2,3},{3,2},{4,5},{5,4},{6,7},{7,6},{8,9},{9,8},{10,11... | collective-permute-start | bytes 393224 | tf_op jit(solution)/shard_map/ppermute | solution.py:169
  11.4 0.1 collective-permute-start.7
  11.5 0.9 %collective-permute-done.5.far_ref = bf16[32,128]{1,0:T(8,128)(2,1)S(1)} collective-permute-done((bf16[32,128]{1,0:T(8,128)(2,1)S(1)}, bf16[32,128]{1,0:T(8,128)(2,1)S(1)}, u32[]{:S(2)}, u32[]{:S(2)}) %collective-permute-start.5) | collective-permute-done | bytes 8224 | tf_op jit(solution)/shard_map/ppermute | solution.py:165
  12.4 0.1 score.4.refs_0_
  12.5 0.1 score.5.refs_0_.refs_3_
  12.6 0.1 score.6.refs_0_.refs_2_
  12.6 0.1 collective-permute-done.7.other_ref
  12.7 0.1 score.7.refs_1_
  12.8 0.1 arrange.1
  12.9 2.5 %collective-permute-start.10 = (f32[1,128]{1,0:T(1,128)S(1)}, f32[1,128]{1,0:T(1,128)S(1)}, u32[]{:S(2)}, u32[]{:S(2)}) collective-permute-start(f32[1,128]{1,0:T(1,128)S(1)} %arrange.1), channel_id=1, source_target_pairs={{9,1},{11,3},{13,5},{15,7},{0,8},{2,10},{4,12},{6,14},{1,0},{3,2},... | collective-permute-start | bytes 1544 | tf_op jit(solution)/shard_map/ppermute | solution.py:208
  15.5 1.3 %collective-permute-done.10 = f32[1,128]{1,0:T(1,128)S(1)} collective-permute-done((f32[1,128]{1,0:T(1,128)S(1)}, f32[1,128]{1,0:T(1,128)S(1)}, u32[]{:S(2)}, u32[]{:S(2)}) %collective-permute-start.10) | collective-permute-done | bytes 544 | tf_op jit(solution)/shard_map/ppermute | solution.py:208
  16.7 0.5 %copy.7 = f32[1,128]{1,0:T(1,128)} copy(f32[1,128]{1,0:T(1,128)S(1)} %collective-permute-done.10) | data formatting | bytes 1024
  (19 shorter events, 0.1 us)
Async XLA Ops:
  0.0 4.7 %copy-start = (bf16[1,384,2560]{2,1,0:T(8,128)(2,1)S(1)}, bf16[1,384,2560]{2,1,0:T(8,128)(2,1)}, u32[]{:S(2)}) copy-start(bf16[1,384,2560]{2,1,0:T(8,128)(2,1)} %acts_ref.1) | copy-start | bytes 5898244
  0.0 4.7 %copy-start.1 = (bf16[1,384,2560]{2,1,0:T(8,128)(2,1)S(1)}, bf16[1,384,2560]{2,1,0:T(8,128)(2,1)}, u32[]{:S(2)}) copy-start(bf16[1,384,2560]{2,1,0:T(8,128)(2,1)} %grads_ref.1) | copy-start | bytes 5898244
  0.0 4.7 %copy-start.2 = (bf16[2560,128]{1,0:T(8,128)(2,1)S(1)}, bf16[2560,128]{1,0:T(8,128)(2,1)}, u32[]{:S(2)}) copy-start(bf16[2560,128]{1,0:T(8,128)(2,1)} %proj_ref.1) | copy-start | bytes 1966084
  0.0 6.5 %copy-start.4 = (s32[1,256]{1,0:T(1,128)S(1)}, s32[1,256]{1,0:T(1,128)}, u32[]{:S(2)}) copy-start(s32[1,256]{1,0:T(1,128)} %picks_ref.1) | copy-start | bytes 3076
  0.0 8.1 %copy-start.3 = (bf16[32,2048]{1,0:T(8,128)(2,1)S(1)}, bf16[32,2048]{1,0:T(8,128)(2,1)}, u32[]{:S(2)}) copy-start(bf16[32,2048]{1,0:T(8,128)(2,1)} %own_ref.1) | copy-start | bytes 393220
  0.0 10.8 %collective-permute-start.2 = (bf16[32,2048]{1,0:T(8,128)(2,1)}, bf16[32,2048]{1,0:T(8,128)(2,1)S(1)}, u32[]{:S(2)}, u32[]{:S(2)}) collective-permute-start(bf16[32,2048]{1,0:T(8,128)(2,1)} %own_ref.1), channel_id=1, source_target_pairs={{0,6},{2,4},{4,2},{6,0},{8,14},{10,12},{12,10},{14,8},{1,7},{3,5},... | collective-permute-start | bytes 393224 | tf_op jit(solution)/shard_map/ppermute | solution.py:131
  4.1 6.7 %collective-permute-start.1 = (bf16[32,2048]{1,0:T(8,128)(2,1)}, bf16[32,2048]{1,0:T(8,128)(2,1)S(1)}, u32[]{:S(2)}, u32[]{:S(2)}) collective-permute-start(bf16[32,2048]{1,0:T(8,128)(2,1)} %own_ref.1), channel_id=1, source_target_pairs={{0,4},{2,6},{4,0},{6,2},{8,12},{10,14},{12,8},{14,10},{1,5},{3,7},... | collective-permute-start | bytes 393224 | tf_op jit(solution)/shard_map/ppermute | solution.py:131
  4.5 6.3 %collective-permute-start = (bf16[32,2048]{1,0:T(8,128)(2,1)}, bf16[32,2048]{1,0:T(8,128)(2,1)S(1)}, u32[]{:S(2)}, u32[]{:S(2)}) collective-permute-start(bf16[32,2048]{1,0:T(8,128)(2,1)} %own_ref.1), channel_id=1, source_target_pairs={{0,2},{2,0},{4,6},{6,4},{8,10},{10,8},{12,14},{14,12},{1,3},{3,1},... | collective-permute-start | bytes 393224 | tf_op jit(solution)/shard_map/ppermute | solution.py:131
  5.9 1.4 %collective-permute-start.3 = (f32[192,128]{1,0:T(8,128)S(1)}, f32[192,128]{1,0:T(8,128)S(1)}, u32[]{:S(2)}, u32[]{:S(2)}) collective-permute-start(f32[192,128]{1,0:T(8,128)S(1)} %get-tuple-element.21.refs_0_), channel_id=1, source_target_pairs={{0,1},{1,0},{2,3},{3,2},{4,5},{5,4},{6,7},{7,6},{8,9},{9,8},{10,11... | collective-permute-start | bytes 294920 | tf_op jit(solution)/shard_map/ppermute | solution.py:144
  6.0 1.4 %collective-permute-start.4 = (f32[192,128]{1,0:T(8,128)S(1)}, f32[192,128]{1,0:T(8,128)S(1)}, u32[]{:S(2)}, u32[]{:S(2)}) collective-permute-start(f32[192,128]{1,0:T(8,128)S(1)} %get-tuple-element.22.refs_1_), channel_id=1, source_target_pairs={{0,1},{1,0},{2,3},{3,2},{4,5},{5,4},{6,7},{7,6},{8,9},{9,8},{10,11... | collective-permute-start | bytes 294920 | tf_op jit(solution)/shard_map/ppermute | solution.py:144
  7.8 4.6 %collective-permute-start.5 = (bf16[32,128]{1,0:T(8,128)(2,1)S(1)}, bf16[32,128]{1,0:T(8,128)(2,1)S(1)}, u32[]{:S(2)}, u32[]{:S(2)}) collective-permute-start(bf16[32,128]{1,0:T(8,128)(2,1)S(1)} %sketch.1.own_ref), channel_id=1, source_target_pairs={{1,9},{3,11},{5,13},{7,15},{8,0},{10,2},{12,4},{14,6},{0,1},{2,3},... | collective-permute-start | bytes 24584 | tf_op jit(solution)/shard_map/ppermute | solution.py:165
  8.1 4.2 %collective-permute-start.6 = (bf16[32,2048]{1,0:T(8,128)(2,1)S(1)}, bf16[32,2048]{1,0:T(8,128)(2,1)S(1)}, u32[]{:S(2)}, u32[]{:S(2)}) collective-permute-start(bf16[32,2048]{1,0:T(8,128)(2,1)S(1)} %copy-done.3), channel_id=1, source_target_pairs={{0,1},{1,0},{2,3},{3,2},{4,5},{5,4},{6,7},{7,6},{8,9},{9,8},{10,11... | collective-permute-start | bytes 393224 | tf_op jit(solution)/shard_map/ppermute | solution.py:169
  10.8 1.7 %collective-permute-start.9 = (bf16[32,2048]{1,0:T(8,128)(2,1)S(1)}, bf16[32,2048]{1,0:T(8,128)(2,1)S(1)}, u32[]{:S(2)}, u32[]{:S(2)}) collective-permute-start(bf16[32,2048]{1,0:T(8,128)(2,1)S(1)} %collective-permute-done.2.own_ref), channel_id=1, source_target_pairs={{0,1},{1,0},{2,3},{3,2},{4,5},{5,4},{6,7},{7,6},{8,9},{9,8},{10,11... | collective-permute-start | bytes 393224 | tf_op jit(solution)/shard_map/ppermute | solution.py:169
  10.9 1.7 %collective-permute-start.8 = (bf16[32,2048]{1,0:T(8,128)(2,1)S(1)}, bf16[32,2048]{1,0:T(8,128)(2,1)S(1)}, u32[]{:S(2)}, u32[]{:S(2)}) collective-permute-start(bf16[32,2048]{1,0:T(8,128)(2,1)S(1)} %collective-permute-done.1.own_ref), channel_id=1, source_target_pairs={{0,1},{1,0},{2,3},{3,2},{4,5},{5,4},{6,7},{7,6},{8,9},{9,8},{10,11... | collective-permute-start | bytes 393224 | tf_op jit(solution)/shard_map/ppermute | solution.py:169
  11.4 1.3 %collective-permute-start.7 = (bf16[32,2048]{1,0:T(8,128)(2,1)S(1)}, bf16[32,2048]{1,0:T(8,128)(2,1)S(1)}, u32[]{:S(2)}, u32[]{:S(2)}) collective-permute-start(bf16[32,2048]{1,0:T(8,128)(2,1)S(1)} %collective-permute-done.own_ref), channel_id=1, source_target_pairs={{0,1},{1,0},{2,3},{3,2},{4,5},{5,4},{6,7},{7,6},{8,9},{9,8},{10,11... | collective-permute-start | bytes 393224 | tf_op jit(solution)/shard_map/ppermute | solution.py:169
  12.9 3.8 %collective-permute-start.10 = (f32[1,128]{1,0:T(1,128)S(1)}, f32[1,128]{1,0:T(1,128)S(1)}, u32[]{:S(2)}, u32[]{:S(2)}) collective-permute-start(f32[1,128]{1,0:T(1,128)S(1)} %arrange.1), channel_id=1, source_target_pairs={{9,1},{11,3},{13,5},{15,7},{0,8},{2,10},{4,12},{6,14},{1,0},{3,2},... | collective-permute-start | bytes 1544 | tf_op jit(solution)/shard_map/ppermute | solution.py:208

commit v19 on v18

--- a/solution.py
+++ b/solution.py
@@ -58,6 +58,10 @@
     even = held[pl.ds(0, pairs, stride=2), :]
     odd = held[pl.ds(1, pairs, stride=2), :]
     out_ref[...] = jnp.concatenate([even, odd], axis=1).astype(BF16)
+
+
+def hold_kernel(*refs):
+    pass
 
 
 def flatten_kernel(mates, own_ref, far_ref, first_ref, second_ref, wide):
@@ -163,11 +167,24 @@
     )(count, *partial, *other)
 
     far_sketch = lax.ppermute(sketch, both, there)
-    swapped = []
-    for half in halves:
-        half, sketch = lax.optimization_barrier((half, sketch))
-        swapped.append(lax.ppermute(half, "tensor", swap))
-
+    def hold(half, *ended):
+        return pl.pallas_call(
+            hold_kernel,
+            in_specs=[vmem] * (1 + len(ended)),
+            out_specs=vmem,
+            out_shape=jax.ShapeDtypeStruct(half.shape, BF16),
+            input_output_aliases={0: 0},
+            compiler_params=pltpu.CompilerParams(vmem_limit_bytes=8 << 20),
+            cost_estimate=pl.CostEstimate(flops=1, bytes_accessed=1, transcendentals=0),
+            name="hold",
+        )(half, *ended)
+
+    last = mates // 2
+    sequence = [k for k in range(mates) if k != last] + [last]
+    for k in sequence[1:-1]:
+        halves[k] = hold(halves[k], sketch)
+    halves[last] = hold(halves[last], *[halves[k] for k in sequence[1:-1]])
+    swapped = [lax.ppermute(half, "tensor", swap) for half in halves]
     width = mates * own_queries
     flats = pl.pallas_call(
         functools.partial(flatten_kernel, mates),
@@ -182,7 +199,8 @@
     small = pl.CostEstimate(flops=1, bytes_accessed=1, transcendentals=0)
     few = pltpu.CompilerParams(vmem_limit_bytes=8 << 20)
     parts = []
-    for half, other in zip(halves, swapped):
+    for k in sequence:
+        half, other = halves[k], swapped[k]
         before = parts[-1:]
         parts.append(
             pl.pallas_call(
@@ -204,7 +222,7 @@
         compiler_params=few,
         cost_estimate=small,
         name="arrange",
-    )(parts[0], *parts[:0:-1])
+    )(*[parts[sequence.index(-r % mates)] for r in range(mates)])
     return lax.ppermute(scores, both, back)
 
 

time: 17.4 us -> 17 us (0.977)
  starting transfers between devices: 11.4 us -> 11.1 us
    ppermute x1, starting transfers between devices: 2.53 us -> 2.24 us  [on_device(): return lax.ppermute(scores, both, back)]
  transfers between devices with their start and end apart: 11 -> 11, of which waited for: 5 -> 4; matrix products, arithmetic and copies ran while one was open for 0% -> 0% of each run, Pallas kernels for 12% -> 12%
where the time goes in v19:
time: 17 us; the launch traced here: 16.9 us
  starting transfers between devices  11.1 us (65%)
  waiting for transfers between devices  3.03 us (18%)
  Pallas kernels  2.18 us (13%)
  local copies, waits for them, and re-layouts  0.53 us (3%)
    ppermute x3, starting transfers between devices, on_device(): halves.append(lax.ppermute(sent, 'dp', [(d, d ^ r) for d in range(clips)]))  4.67 us
    ppermute x4, starting transfers between devices, on_device(): swapped = [lax.ppermute(half, 'tensor', swap) for half in halves]  3.24 us
    ppermute x1, starting transfers between devices, on_device(): return lax.ppermute(scores, both, back)  2.24 us
    ppermute x1, waiting for transfers between devices, on_device(): return lax.ppermute(scores, both, back)  1.3 us
    pallas_call x1, Pallas kernels, on_device(): pl.pallas_call(functools.partial(project_kernel, rank), in_specs=[vmem] *...  1.17 us
    ppermute x1, waiting for transfers between devices, on_device(): far_sketch = lax.ppermute(sketch, both, there)  0.94 us
    ppermute x2, waiting for transfers between devices, on_device(): other = [lax.ppermute(part, 'tensor', swap) for part in partial]  0.74 us
    ppermute x2, starting transfers between devices, on_device(): other = [lax.ppermute(part, 'tensor', swap) for part in partial]  0.57 us
  transfers between devices with their start and end apart: 11, of which 4 were waited for; matrix products, arithmetic and copies ran while one was open for 0% of the time, Pallas kernels for 12%

profile of v19, /device:TPU:0, one launch (start us, length us, event | category | flops | bytes accessed | tf_op | source)
XLA Modules:
  0.0 16.9 jit_solution(16549043480139301644)
XLA Ops:
  0.0 4.0 %collective-permute-start.6 = (bf16[32,2048]{1,0:T(8,128)(2,1)}, bf16[32,2048]{1,0:T(8,128)(2,1)S(1)}, u32[]{:S(2)}, u32[]{:S(2)}) collective-permute-start(bf16[32,2048]{1,0:T(8,128)(2,1)} %own_ref.1), channel_id=1, source_target_pairs={{0,6},{2,4},{4,2},{6,0},{8,14},{10,12},{12,10},{14,8},{1,7},{3,5},... | collective-permute-start | bytes 393224 | tf_op jit(solution)/shard_map/ppermute | solution.py:135
  4.1 0.5 %collective-permute-start.4 = (bf16[32,2048]{1,0:T(8,128)(2,1)}, bf16[32,2048]{1,0:T(8,128)(2,1)S(1)}, u32[]{:S(2)}, u32[]{:S(2)}) collective-permute-start(bf16[32,2048]{1,0:T(8,128)(2,1)} %own_ref.1), channel_id=1, source_target_pairs={{0,2},{2,0},{4,6},{6,4},{8,10},{10,8},{12,14},{14,12},{1,3},{3,1},... | collective-permute-start | bytes 393224 | tf_op jit(solution)/shard_map/ppermute | solution.py:135
  4.6 0.1 collective-permute-start.8
  4.7 1.2 %project.1 = (f32[192,128]{1,0:T(8,128)S(1)}, f32[192,128]{1,0:T(8,128)S(1)}) custom-call(f32[8,128]{1,0:T(8,128)S(1)} %first.1.first_ref, bf16[1,384,2560]{2,1,0:T(8,128)(2,1)S(1)} %copy-done, bf16[1,384,2560]{2,1,0:T(8,128)(2,1)S(1)} %copy-done.1, bf16[2560,128]{1,0:T(8,128)(2,1)S(1)} %copy-done.2), custom_call_target="tpu_custom_call" | custom-call | flops 503316480 | bytes 3932160 | tf_op jit(solution)/shard_map/project/pallas_call | solution.py:136
  5.9 0.1 collective-permute-start
  6.0 0.5 %collective-permute-start.1 = (f32[192,128]{1,0:T(8,128)S(1)}, f32[192,128]{1,0:T(8,128)S(1)}, u32[]{:S(2)}, u32[]{:S(2)}) collective-permute-start(f32[192,128]{1,0:T(8,128)S(1)} %get-tuple-element.13.refs_1_), channel_id=1, source_target_pairs={{0,1},{1,0},{2,3},{3,2},{4,5},{5,4},{6,7},{7,6},{8,9},{9,8},{10,11... | collective-permute-start | bytes 294920 | tf_op jit(solution)/shard_map/ppermute | solution.py:148
  6.5 0.2 %count.1.count_ref = f32[384,128]{1,0:T(8,128)S(1)} custom-call(s32[1,256]{1,0:T(1,128)S(1)} %copy-done.4), custom_call_target="tpu_custom_call" | custom-call | flops 1 | bytes 1 | tf_op jit(solution)/shard_map/count/pallas_call | solution.py:149
  6.7 0.6 %collective-permute-done.refs_2_ = f32[192,128]{1,0:T(8,128)S(1)} collective-permute-done((f32[192,128]{1,0:T(8,128)S(1)}, f32[192,128]{1,0:T(8,128)S(1)}, u32[]{:S(2)}, u32[]{:S(2)}) %collective-permute-start) | collective-permute-done | bytes 98336 | tf_op jit(solution)/shard_map/ppermute | solution.py:148
  7.3 0.2 collective-permute-done.1.refs_3_
  7.4 0.4 %sketch.1.own_ref.refs_1_ = bf16[32,128]{1,0:T(8,128)(2,1)S(1)} custom-call(f32[384,128]{1,0:T(8,128)S(1)} %count.1.count_ref, f32[192,128]{1,0:T(8,128)S(1)} %get-tuple-element.12.refs_0_, f32[192,128]{1,0:T(8,128)S(1)} %get-tuple-element.13.refs_1_, f32[192,128]{1,0:T(8,128)S(1)} %collective-permute-done.refs_2_, f32[192,128]{1,0:T(8,128)S(1)} %collective-permute-done.1.refs_3_), custom_call_target="tpu_custom_call" | custom-call | flops 1 | bytes 1 | tf_op jit(solution)/shard_map/sketch/pallas_call | solution.py:158
  7.8 0.4 %collective-permute-start.2 = (bf16[32,128]{1,0:T(8,128)(2,1)S(1)}, bf16[32,128]{1,0:T(8,128)(2,1)S(1)}, u32[]{:S(2)}, u32[]{:S(2)}) collective-permute-start(bf16[32,128]{1,0:T(8,128)(2,1)S(1)} %sketch.1.own_ref.refs_1_), channel_id=1, source_target_pairs={{1,9},{3,11},{5,13},{7,15},{8,0},{10,2},{12,4},{14,6},{0,1},{2,3},... | collective-permute-start | bytes 24584 | tf_op jit(solution)/shard_map/ppermute | solution.py:169
  8.1 2.7 %collective-permute-start.3 = (bf16[32,2048]{1,0:T(8,128)(2,1)S(1)}, bf16[32,2048]{1,0:T(8,128)(2,1)S(1)}, u32[]{:S(2)}, u32[]{:S(2)}) collective-permute-start(bf16[32,2048]{1,0:T(8,128)(2,1)S(1)} %copy-done.3), channel_id=1, source_target_pairs={{0,1},{1,0},{2,3},{3,2},{4,5},{5,4},{6,7},{7,6},{8,9},{9,8},{10,11... | collective-permute-start | bytes 393224 | tf_op jit(solution)/shard_map/ppermute | solution.py:187
  10.8 0.1 collective-permute-start.7
  10.9 0.4 %collective-permute-start.5 = (bf16[32,2048]{1,0:T(8,128)(2,1)S(1)}, bf16[32,2048]{1,0:T(8,128)(2,1)S(1)}, u32[]{:S(2)}, u32[]{:S(2)}) collective-permute-start(bf16[32,2048]{1,0:T(8,128)(2,1)S(1)} %hold.3.own_ref.refs_2_), channel_id=1, source_target_pairs={{0,1},{1,0},{2,3},{3,2},{4,5},{5,4},{6,7},{7,6},{8,9},{9,8},{10,11... | collective-permute-start | bytes 393224 | tf_op jit(solution)/shard_map/ppermute | solution.py:187
  11.3 0.1 collective-permute-start.9
  11.4 0.9 %collective-permute-done.2.far_ref = bf16[32,128]{1,0:T(8,128)(2,1)S(1)} collective-permute-done((bf16[32,128]{1,0:T(8,128)(2,1)S(1)}, bf16[32,128]{1,0:T(8,128)(2,1)S(1)}, u32[]{:S(2)}, u32[]{:S(2)}) %collective-permute-start.2) | collective-permute-done | bytes 8224 | tf_op jit(solution)/shard_map/ppermute | solution.py:169
  12.4 0.1 score.4.refs_0_
  12.5 0.1 score.5.refs_0_.refs_3_
  12.6 0.1 score.6.refs_0_.refs_1_
  12.7 0.1 score.7.refs_2_
  12.7 0.1 arrange.1
  12.9 2.2 %collective-permute-start.10 = (f32[1,128]{1,0:T(1,128)S(1)}, f32[1,128]{1,0:T(1,128)S(1)}, u32[]{:S(2)}, u32[]{:S(2)}) collective-permute-start(f32[1,128]{1,0:T(1,128)S(1)} %arrange.1), channel_id=1, source_target_pairs={{9,1},{11,3},{13,5},{15,7},{0,8},{2,10},{4,12},{6,14},{1,0},{3,2},... | collective-permute-start | bytes 1544 | tf_op jit(solution)/shard_map/ppermute | solution.py:226
  15.1 1.3 %collective-permute-done.10 = f32[1,128]{1,0:T(1,128)S(1)} collective-permute-done((f32[1,128]{1,0:T(1,128)S(1)}, f32[1,128]{1,0:T(1,128)S(1)}, u32[]{:S(2)}, u32[]{:S(2)}) %collective-permute-start.10) | collective-permute-done | bytes 544 | tf_op jit(solution)/shard_map/ppermute | solution.py:226
  16.4 0.5 %copy.13 = f32[1,128]{1,0:T(1,128)} copy(f32[1,128]{1,0:T(1,128)S(1)} %collective-permute-done.10) | data formatting | bytes 1024
  (22 shorter events, 0.1 us)
Async XLA Ops:
  0.0 4.7 %copy-start = (bf16[1,384,2560]{2,1,0:T(8,128)(2,1)S(1)}, bf16[1,384,2560]{2,1,0:T(8,128)(2,1)}, u32[]{:S(2)}) copy-start(bf16[1,384,2560]{2,1,0:T(8,128)(2,1)} %acts_ref.1) | copy-start | bytes 5898244
  0.0 4.7 %copy-start.1 = (bf16[1,384,2560]{2,1,0:T(8,128)(2,1)S(1)}, bf16[1,384,2560]{2,1,0:T(8,128)(2,1)}, u32[]{:S(2)}) copy-start(bf16[1,384,2560]{2,1,0:T(8,128)(2,1)} %grads_ref.1) | copy-start | bytes 5898244
  0.0 4.7 %copy-start.2 = (bf16[2560,128]{1,0:T(8,128)(2,1)S(1)}, bf16[2560,128]{1,0:T(8,128)(2,1)}, u32[]{:S(2)}) copy-start(bf16[2560,128]{1,0:T(8,128)(2,1)} %proj_ref.1) | copy-start | bytes 1966084
  0.0 6.5 %copy-start.4 = (s32[1,256]{1,0:T(1,128)S(1)}, s32[1,256]{1,0:T(1,128)}, u32[]{:S(2)}) copy-start(s32[1,256]{1,0:T(1,128)} %picks_ref.1) | copy-start | bytes 3076
  0.0 8.1 %copy-start.3 = (bf16[32,2048]{1,0:T(8,128)(2,1)S(1)}, bf16[32,2048]{1,0:T(8,128)(2,1)}, u32[]{:S(2)}) copy-start(bf16[32,2048]{1,0:T(8,128)(2,1)} %own_ref.1) | copy-start | bytes 393220
  0.0 10.8 %collective-permute-start.6 = (bf16[32,2048]{1,0:T(8,128)(2,1)}, bf16[32,2048]{1,0:T(8,128)(2,1)S(1)}, u32[]{:S(2)}, u32[]{:S(2)}) collective-permute-start(bf16[32,2048]{1,0:T(8,128)(2,1)} %own_ref.1), channel_id=1, source_target_pairs={{0,6},{2,4},{4,2},{6,0},{8,14},{10,12},{12,10},{14,8},{1,7},{3,5},... | collective-permute-start | bytes 393224 | tf_op jit(solution)/shard_map/ppermute | solution.py:135
  4.1 6.8 %collective-permute-start.4 = (bf16[32,2048]{1,0:T(8,128)(2,1)}, bf16[32,2048]{1,0:T(8,128)(2,1)S(1)}, u32[]{:S(2)}, u32[]{:S(2)}) collective-permute-start(bf16[32,2048]{1,0:T(8,128)(2,1)} %own_ref.1), channel_id=1, source_target_pairs={{0,2},{2,0},{4,6},{6,4},{8,10},{10,8},{12,14},{14,12},{1,3},{3,1},... | collective-permute-start | bytes 393224 | tf_op jit(solution)/shard_map/ppermute | solution.py:135
  4.6 6.7 %collective-permute-start.8 = (bf16[32,2048]{1,0:T(8,128)(2,1)}, bf16[32,2048]{1,0:T(8,128)(2,1)S(1)}, u32[]{:S(2)}, u32[]{:S(2)}) collective-permute-start(bf16[32,2048]{1,0:T(8,128)(2,1)} %own_ref.1), channel_id=1, source_target_pairs={{0,4},{2,6},{4,0},{6,2},{8,12},{10,14},{12,8},{14,10},{1,5},{3,7},... | collective-permute-start | bytes 393224 | tf_op jit(solution)/shard_map/ppermute | solution.py:135
  5.9 1.4 %collective-permute-start = (f32[192,128]{1,0:T(8,128)S(1)}, f32[192,128]{1,0:T(8,128)S(1)}, u32[]{:S(2)}, u32[]{:S(2)}) collective-permute-start(f32[192,128]{1,0:T(8,128)S(1)} %get-tuple-element.12.refs_0_), channel_id=1, source_target_pairs={{0,1},{1,0},{2,3},{3,2},{4,5},{5,4},{6,7},{7,6},{8,9},{9,8},{10,11... | collective-permute-start | bytes 294920 | tf_op jit(solution)/shard_map/ppermute | solution.py:148
  6.0 1.4 %collective-permute-start.1 = (f32[192,128]{1,0:T(8,128)S(1)}, f32[192,128]{1,0:T(8,128)S(1)}, u32[]{:S(2)}, u32[]{:S(2)}) collective-permute-start(f32[192,128]{1,0:T(8,128)S(1)} %get-tuple-element.13.refs_1_), channel_id=1, source_target_pairs={{0,1},{1,0},{2,3},{3,2},{4,5},{5,4},{6,7},{7,6},{8,9},{9,8},{10,11... | collective-permute-start | bytes 294920 | tf_op jit(solution)/shard_map/ppermute | solution.py:148
  7.8 4.6 %collective-permute-start.2 = (bf16[32,128]{1,0:T(8,128)(2,1)S(1)}, bf16[32,128]{1,0:T(8,128)(2,1)S(1)}, u32[]{:S(2)}, u32[]{:S(2)}) collective-permute-start(bf16[32,128]{1,0:T(8,128)(2,1)S(1)} %sketch.1.own_ref.refs_1_), channel_id=1, source_target_pairs={{1,9},{3,11},{5,13},{7,15},{8,0},{10,2},{12,4},{14,6},{0,1},{2,3},... | collective-permute-start | bytes 24584 | tf_op jit(solution)/shard_map/ppermute | solution.py:169
  8.1 4.2 %collective-permute-start.3 = (bf16[32,2048]{1,0:T(8,128)(2,1)S(1)}, bf16[32,2048]{1,0:T(8,128)(2,1)S(1)}, u32[]{:S(2)}, u32[]{:S(2)}) collective-permute-start(bf16[32,2048]{1,0:T(8,128)(2,1)S(1)} %copy-done.3), channel_id=1, source_target_pairs={{0,1},{1,0},{2,3},{3,2},{4,5},{5,4},{6,7},{7,6},{8,9},{9,8},{10,11... | collective-permute-start | bytes 393224 | tf_op jit(solution)/shard_map/ppermute | solution.py:187
  10.8 1.7 %collective-permute-start.7 = (bf16[32,2048]{1,0:T(8,128)(2,1)S(1)}, bf16[32,2048]{1,0:T(8,128)(2,1)S(1)}, u32[]{:S(2)}, u32[]{:S(2)}) collective-permute-start(bf16[32,2048]{1,0:T(8,128)(2,1)S(1)} %hold.4.own_ref.refs_1_), channel_id=1, source_target_pairs={{0,1},{1,0},{2,3},{3,2},{4,5},{5,4},{6,7},{7,6},{8,9},{9,8},{10,11... | collective-permute-start | bytes 393224 | tf_op jit(solution)/shard_map/ppermute | solution.py:187
  10.9 1.7 %collective-permute-start.5 = (bf16[32,2048]{1,0:T(8,128)(2,1)S(1)}, bf16[32,2048]{1,0:T(8,128)(2,1)S(1)}, u32[]{:S(2)}, u32[]{:S(2)}) collective-permute-start(bf16[32,2048]{1,0:T(8,128)(2,1)S(1)} %hold.3.own_ref.refs_2_), channel_id=1, source_target_pairs={{0,1},{1,0},{2,3},{3,2},{4,5},{5,4},{6,7},{7,6},{8,9},{9,8},{10,11... | collective-permute-start | bytes 393224 | tf_op jit(solution)/shard_map/ppermute | solution.py:187
  11.3 1.3 %collective-permute-start.9 = (bf16[32,2048]{1,0:T(8,128)(2,1)S(1)}, bf16[32,2048]{1,0:T(8,128)(2,1)S(1)}, u32[]{:S(2)}, u32[]{:S(2)}) collective-permute-start(bf16[32,2048]{1,0:T(8,128)(2,1)S(1)} %hold.5.own_ref), channel_id=1, source_target_pairs={{0,1},{1,0},{2,3},{3,2},{4,5},{5,4},{6,7},{7,6},{8,9},{9,8},{10,11... | collective-permute-start | bytes 393224 | tf_op jit(solution)/shard_map/ppermute | solution.py:187
  12.9 3.5 %collective-permute-start.10 = (f32[1,128]{1,0:T(1,128)S(1)}, f32[1,128]{1,0:T(1,128)S(1)}, u32[]{:S(2)}, u32[]{:S(2)}) collective-permute-start(f32[1,128]{1,0:T(1,128)S(1)} %arrange.1), channel_id=1, source_target_pairs={{9,1},{11,3},{13,5},{15,7},{0,8},{2,10},{4,12},{6,14},{1,0},{3,2},... | collective-permute-start | bytes 1544 | tf_op jit(solution)/shard_map/ppermute | solution.py:226

commit v20 on v19

--- a/solution.py
+++ b/solution.py
@@ -179,11 +179,9 @@
             name="hold",
         )(half, *ended)
 
-    last = mates // 2
-    sequence = [k for k in range(mates) if k != last] + [last]
-    for k in sequence[1:-1]:
+    for k in range(1, mates - 1):
         halves[k] = hold(halves[k], sketch)
-    halves[last] = hold(halves[last], *[halves[k] for k in sequence[1:-1]])
+    halves[-1] = hold(halves[-1], *halves[1:-1])
     swapped = [lax.ppermute(half, "tensor", swap) for half in halves]
     width = mates * own_queries
     flats = pl.pallas_call(
@@ -199,8 +197,7 @@
     small = pl.CostEstimate(flops=1, bytes_accessed=1, transcendentals=0)
     few = pltpu.CompilerParams(vmem_limit_bytes=8 << 20)
     parts = []
-    for k in sequence:
-        half, other = halves[k], swapped[k]
+    for half, other in zip(halves, swapped):
         before = parts[-1:]
         parts.append(
             pl.pallas_call(
@@ -222,7 +219,7 @@
         compiler_params=few,
         cost_estimate=small,
         name="arrange",
-    )(*[parts[sequence.index(-r % mates)] for r in range(mates)])
+    )(parts[0], *parts[:0:-1])
     return lax.ppermute(scores, both, back)
 
 

time: 17 us -> 17.1 us (level)
  no operation moved by 1% of the time
where the time goes in v20:
time: 17.1 us; the launch traced here: 16.9 us
  starting transfers between devices  11.1 us (65%)
  waiting for transfers between devices  3.03 us (18%)
  Pallas kernels  2.18 us (13%)
  local copies, waits for them, and re-layouts  0.53 us (3%)
    ppermute x3, starting transfers between devices, on_device(): halves.append(lax.ppermute(sent, 'dp', [(d, d ^ r) for d in range(clips)]))  4.67 us
    ppermute x4, starting transfers between devices, on_device(): swapped = [lax.ppermute(half, 'tensor', swap) for half in halves]  3.24 us
    ppermute x1, starting transfers between devices, on_device(): return lax.ppermute(scores, both, back)  2.26 us
    ppermute x1, waiting for transfers between devices, on_device(): return lax.ppermute(scores, both, back)  1.3 us
    pallas_call x1, Pallas kernels, on_device(): pl.pallas_call(functools.partial(project_kernel, rank), in_specs=[vmem] *...  1.17 us
    ppermute x1, waiting for transfers between devices, on_device(): far_sketch = lax.ppermute(sketch, both, there)  0.94 us
    ppermute x2, waiting for transfers between devices, on_device(): other = [lax.ppermute(part, 'tensor', swap) for part in partial]  0.74 us
    ppermute x2, starting transfers between devices, on_device(): other = [lax.ppermute(part, 'tensor', swap) for part in partial]  0.57 us
  transfers between devices with their start and end apart: 11, of which 4 were waited for; matrix products, arithmetic and copies ran while one was open for 0% of the time, Pallas kernels for 12%

profile of v20, /device:TPU:0, one launch (start us, length us, event | category | flops | bytes accessed | tf_op | source)
XLA Modules:
  0.0 16.9 jit_solution(2337013009830806278)
XLA Ops:
  0.0 4.0 %collective-permute-start.5 = (bf16[32,2048]{1,0:T(8,128)(2,1)}, bf16[32,2048]{1,0:T(8,128)(2,1)S(1)}, u32[]{:S(2)}, u32[]{:S(2)}) collective-permute-start(bf16[32,2048]{1,0:T(8,128)(2,1)} %own_ref.1), channel_id=1, source_target_pairs={{0,6},{2,4},{4,2},{6,0},{8,14},{10,12},{12,10},{14,8},{1,7},{3,5},... | collective-permute-start | bytes 393224 | tf_op jit(solution)/shard_map/ppermute | solution.py:135
  4.1 0.4 %collective-permute-start.6 = (bf16[32,2048]{1,0:T(8,128)(2,1)}, bf16[32,2048]{1,0:T(8,128)(2,1)S(1)}, u32[]{:S(2)}, u32[]{:S(2)}) collective-permute-start(bf16[32,2048]{1,0:T(8,128)(2,1)} %own_ref.1), channel_id=1, source_target_pairs={{0,4},{2,6},{4,0},{6,2},{8,12},{10,14},{12,8},{14,10},{1,5},{3,7},... | collective-permute-start | bytes 393224 | tf_op jit(solution)/shard_map/ppermute | solution.py:135
  4.5 0.2 %collective-permute-start.4 = (bf16[32,2048]{1,0:T(8,128)(2,1)}, bf16[32,2048]{1,0:T(8,128)(2,1)S(1)}, u32[]{:S(2)}, u32[]{:S(2)}) collective-permute-start(bf16[32,2048]{1,0:T(8,128)(2,1)} %own_ref.1), channel_id=1, source_target_pairs={{0,2},{2,0},{4,6},{6,4},{8,10},{10,8},{12,14},{14,12},{1,3},{3,1},... | collective-permute-start | bytes 393224 | tf_op jit(solution)/shard_map/ppermute | solution.py:135
  4.7 1.2 %project.1 = (f32[192,128]{1,0:T(8,128)S(1)}, f32[192,128]{1,0:T(8,128)S(1)}) custom-call(f32[8,128]{1,0:T(8,128)S(1)} %first.1.first_ref, bf16[1,384,2560]{2,1,0:T(8,128)(2,1)S(1)} %copy-done, bf16[1,384,2560]{2,1,0:T(8,128)(2,1)S(1)} %copy-done.1, bf16[2560,128]{1,0:T(8,128)(2,1)S(1)} %copy-done.2), custom_call_target="tpu_custom_call" | custom-call | flops 503316480 | bytes 3932160 | tf_op jit(solution)/shard_map/project/pallas_call | solution.py:136
  5.9 0.1 collective-permute-start
  6.0 0.5 %collective-permute-start.1 = (f32[192,128]{1,0:T(8,128)S(1)}, f32[192,128]{1,0:T(8,128)S(1)}, u32[]{:S(2)}, u32[]{:S(2)}) collective-permute-start(f32[192,128]{1,0:T(8,128)S(1)} %get-tuple-element.13.refs_1_), channel_id=1, source_target_pairs={{0,1},{1,0},{2,3},{3,2},{4,5},{5,4},{6,7},{7,6},{8,9},{9,8},{10,11... | collective-permute-start | bytes 294920 | tf_op jit(solution)/shard_map/ppermute | solution.py:148
  6.5 0.2 %count.1.count_ref = f32[384,128]{1,0:T(8,128)S(1)} custom-call(s32[1,256]{1,0:T(1,128)S(1)} %copy-done.4), custom_call_target="tpu_custom_call" | custom-call | flops 1 | bytes 1 | tf_op jit(solution)/shard_map/count/pallas_call | solution.py:149
  6.7 0.6 %collective-permute-done.refs_2_ = f32[192,128]{1,0:T(8,128)S(1)} collective-permute-done((f32[192,128]{1,0:T(8,128)S(1)}, f32[192,128]{1,0:T(8,128)S(1)}, u32[]{:S(2)}, u32[]{:S(2)}) %collective-permute-start) | collective-permute-done | bytes 98336 | tf_op jit(solution)/shard_map/ppermute | solution.py:148
  7.3 0.2 collective-permute-done.1.refs_3_
  7.4 0.4 %sketch.1.own_ref.refs_1_ = bf16[32,128]{1,0:T(8,128)(2,1)S(1)} custom-call(f32[384,128]{1,0:T(8,128)S(1)} %count.1.count_ref, f32[192,128]{1,0:T(8,128)S(1)} %get-tuple-element.12.refs_0_, f32[192,128]{1,0:T(8,128)S(1)} %get-tuple-element.13.refs_1_, f32[192,128]{1,0:T(8,128)S(1)} %collective-permute-done.refs_2_, f32[192,128]{1,0:T(8,128)S(1)} %collective-permute-done.1.refs_3_), custom_call_target="tpu_custom_call" | custom-call | flops 1 | bytes 1 | tf_op jit(solution)/shard_map/sketch/pallas_call | solution.py:158
  7.8 0.4 %collective-permute-start.2 = (bf16[32,128]{1,0:T(8,128)(2,1)S(1)}, bf16[32,128]{1,0:T(8,128)(2,1)S(1)}, u32[]{:S(2)}, u32[]{:S(2)}) collective-permute-start(bf16[32,128]{1,0:T(8,128)(2,1)S(1)} %sketch.1.own_ref.refs_1_), channel_id=1, source_target_pairs={{1,9},{3,11},{5,13},{7,15},{8,0},{10,2},{12,4},{14,6},{0,1},{2,3},... | collective-permute-start | bytes 24584 | tf_op jit(solution)/shard_map/ppermute | solution.py:169
  8.1 2.7 %collective-permute-start.3 = (bf16[32,2048]{1,0:T(8,128)(2,1)S(1)}, bf16[32,2048]{1,0:T(8,128)(2,1)S(1)}, u32[]{:S(2)}, u32[]{:S(2)}) collective-permute-start(bf16[32,2048]{1,0:T(8,128)(2,1)S(1)} %copy-done.3), channel_id=1, source_target_pairs={{0,1},{1,0},{2,3},{3,2},{4,5},{5,4},{6,7},{7,6},{8,9},{9,8},{10,11... | collective-permute-start | bytes 393224 | tf_op jit(solution)/shard_map/ppermute | solution.py:185
  10.8 0.1 collective-permute-start.9
  10.9 0.4 %collective-permute-start.8 = (bf16[32,2048]{1,0:T(8,128)(2,1)S(1)}, bf16[32,2048]{1,0:T(8,128)(2,1)S(1)}, u32[]{:S(2)}, u32[]{:S(2)}) collective-permute-start(bf16[32,2048]{1,0:T(8,128)(2,1)S(1)} %hold.4.refs_2_.own_ref), channel_id=1, source_target_pairs={{0,1},{1,0},{2,3},{3,2},{4,5},{5,4},{6,7},{7,6},{8,9},{9,8},{10,11... | collective-permute-start | bytes 393224 | tf_op jit(solution)/shard_map/ppermute | solution.py:185
  11.3 0.1 collective-permute-start.7
  11.4 0.9 %collective-permute-done.2.far_ref = bf16[32,128]{1,0:T(8,128)(2,1)S(1)} collective-permute-done((bf16[32,128]{1,0:T(8,128)(2,1)S(1)}, bf16[32,128]{1,0:T(8,128)(2,1)S(1)}, u32[]{:S(2)}, u32[]{:S(2)}) %collective-permute-start.2) | collective-permute-done | bytes 8224 | tf_op jit(solution)/shard_map/ppermute | solution.py:169
  12.4 0.1 score.4.refs_0_
  12.5 0.1 score.5.refs_0_.refs_3_
  12.6 0.1 score.6.refs_0_.refs_2_
  12.7 0.1 score.7.refs_1_
  12.7 0.1 arrange.1
  12.9 2.3 %collective-permute-start.10 = (f32[1,128]{1,0:T(1,128)S(1)}, f32[1,128]{1,0:T(1,128)S(1)}, u32[]{:S(2)}, u32[]{:S(2)}) collective-permute-start(f32[1,128]{1,0:T(1,128)S(1)} %arrange.1), channel_id=1, source_target_pairs={{9,1},{11,3},{13,5},{15,7},{0,8},{2,10},{4,12},{6,14},{1,0},{3,2},... | collective-permute-start | bytes 1544 | tf_op jit(solution)/shard_map/ppermute | solution.py:223
  15.1 1.3 %collective-permute-done.10 = f32[1,128]{1,0:T(1,128)S(1)} collective-permute-done((f32[1,128]{1,0:T(1,128)S(1)}, f32[1,128]{1,0:T(1,128)S(1)}, u32[]{:S(2)}, u32[]{:S(2)}) %collective-permute-start.10) | collective-permute-done | bytes 544 | tf_op jit(solution)/shard_map/ppermute | solution.py:223
  16.4 0.5 %copy.13 = f32[1,128]{1,0:T(1,128)} copy(f32[1,128]{1,0:T(1,128)S(1)} %collective-permute-done.10) | data formatting | bytes 1024
  (22 shorter events, 0.1 us)
Async XLA Ops:
  0.0 4.7 %copy-start = (bf16[1,384,2560]{2,1,0:T(8,128)(2,1)S(1)}, bf16[1,384,2560]{2,1,0:T(8,128)(2,1)}, u32[]{:S(2)}) copy-start(bf16[1,384,2560]{2,1,0:T(8,128)(2,1)} %acts_ref.1) | copy-start | bytes 5898244
  0.0 4.7 %copy-start.1 = (bf16[1,384,2560]{2,1,0:T(8,128)(2,1)S(1)}, bf16[1,384,2560]{2,1,0:T(8,128)(2,1)}, u32[]{:S(2)}) copy-start(bf16[1,384,2560]{2,1,0:T(8,128)(2,1)} %grads_ref.1) | copy-start | bytes 5898244
  0.0 4.7 %copy-start.2 = (bf16[2560,128]{1,0:T(8,128)(2,1)S(1)}, bf16[2560,128]{1,0:T(8,128)(2,1)}, u32[]{:S(2)}) copy-start(bf16[2560,128]{1,0:T(8,128)(2,1)} %proj_ref.1) | copy-start | bytes 1966084
  0.0 6.5 %copy-start.4 = (s32[1,256]{1,0:T(1,128)S(1)}, s32[1,256]{1,0:T(1,128)}, u32[]{:S(2)}) copy-start(s32[1,256]{1,0:T(1,128)} %picks_ref.1) | copy-start | bytes 3076
  0.0 8.1 %copy-start.3 = (bf16[32,2048]{1,0:T(8,128)(2,1)S(1)}, bf16[32,2048]{1,0:T(8,128)(2,1)}, u32[]{:S(2)}) copy-start(bf16[32,2048]{1,0:T(8,128)(2,1)} %own_ref.1) | copy-start | bytes 393220
  0.0 10.8 %collective-permute-start.5 = (bf16[32,2048]{1,0:T(8,128)(2,1)}, bf16[32,2048]{1,0:T(8,128)(2,1)S(1)}, u32[]{:S(2)}, u32[]{:S(2)}) collective-permute-start(bf16[32,2048]{1,0:T(8,128)(2,1)} %own_ref.1), channel_id=1, source_target_pairs={{0,6},{2,4},{4,2},{6,0},{8,14},{10,12},{12,10},{14,8},{1,7},{3,5},... | collective-permute-start | bytes 393224 | tf_op jit(solution)/shard_map/ppermute | solution.py:135
  4.1 6.8 %collective-permute-start.6 = (bf16[32,2048]{1,0:T(8,128)(2,1)}, bf16[32,2048]{1,0:T(8,128)(2,1)S(1)}, u32[]{:S(2)}, u32[]{:S(2)}) collective-permute-start(bf16[32,2048]{1,0:T(8,128)(2,1)} %own_ref.1), channel_id=1, source_target_pairs={{0,4},{2,6},{4,0},{6,2},{8,12},{10,14},{12,8},{14,10},{1,5},{3,7},... | collective-permute-start | bytes 393224 | tf_op jit(solution)/shard_map/ppermute | solution.py:135
  4.5 6.8 %collective-permute-start.4 = (bf16[32,2048]{1,0:T(8,128)(2,1)}, bf16[32,2048]{1,0:T(8,128)(2,1)S(1)}, u32[]{:S(2)}, u32[]{:S(2)}) collective-permute-start(bf16[32,2048]{1,0:T(8,128)(2,1)} %own_ref.1), channel_id=1, source_target_pairs={{0,2},{2,0},{4,6},{6,4},{8,10},{10,8},{12,14},{14,12},{1,3},{3,1},... | collective-permute-start | bytes 393224 | tf_op jit(solution)/shard_map/ppermute | solution.py:135
  5.9 1.4 %collective-permute-start = (f32[192,128]{1,0:T(8,128)S(1)}, f32[192,128]{1,0:T(8,128)S(1)}, u32[]{:S(2)}, u32[]{:S(2)}) collective-permute-start(f32[192,128]{1,0:T(8,128)S(1)} %get-tuple-element.12.refs_0_), channel_id=1, source_target_pairs={{0,1},{1,0},{2,3},{3,2},{4,5},{5,4},{6,7},{7,6},{8,9},{9,8},{10,11... | collective-permute-start | bytes 294920 | tf_op jit(solution)/shard_map/ppermute | solution.py:148
  6.0 1.4 %collective-permute-start.1 = (f32[192,128]{1,0:T(8,128)S(1)}, f32[192,128]{1,0:T(8,128)S(1)}, u32[]{:S(2)}, u32[]{:S(2)}) collective-permute-start(f32[192,128]{1,0:T(8,128)S(1)} %get-tuple-element.13.refs_1_), channel_id=1, source_target_pairs={{0,1},{1,0},{2,3},{3,2},{4,5},{5,4},{6,7},{7,6},{8,9},{9,8},{10,11... | collective-permute-start | bytes 294920 | tf_op jit(solution)/shard_map/ppermute | solution.py:148
  7.8 4.6 %collective-permute-start.2 = (bf16[32,128]{1,0:T(8,128)(2,1)S(1)}, bf16[32,128]{1,0:T(8,128)(2,1)S(1)}, u32[]{:S(2)}, u32[]{:S(2)}) collective-permute-start(bf16[32,128]{1,0:T(8,128)(2,1)S(1)} %sketch.1.own_ref.refs_1_), channel_id=1, source_target_pairs={{1,9},{3,11},{5,13},{7,15},{8,0},{10,2},{12,4},{14,6},{0,1},{2,3},... | collective-permute-start | bytes 24584 | tf_op jit(solution)/shard_map/ppermute | solution.py:169
  8.1 4.2 %collective-permute-start.3 = (bf16[32,2048]{1,0:T(8,128)(2,1)S(1)}, bf16[32,2048]{1,0:T(8,128)(2,1)S(1)}, u32[]{:S(2)}, u32[]{:S(2)}) collective-permute-start(bf16[32,2048]{1,0:T(8,128)(2,1)S(1)} %copy-done.3), channel_id=1, source_target_pairs={{0,1},{1,0},{2,3},{3,2},{4,5},{5,4},{6,7},{7,6},{8,9},{9,8},{10,11... | collective-permute-start | bytes 393224 | tf_op jit(solution)/shard_map/ppermute | solution.py:185
  10.8 1.7 %collective-permute-start.9 = (bf16[32,2048]{1,0:T(8,128)(2,1)S(1)}, bf16[32,2048]{1,0:T(8,128)(2,1)S(1)}, u32[]{:S(2)}, u32[]{:S(2)}) collective-permute-start(bf16[32,2048]{1,0:T(8,128)(2,1)S(1)} %hold.3.refs_1_.own_ref), channel_id=1, source_target_pairs={{0,1},{1,0},{2,3},{3,2},{4,5},{5,4},{6,7},{7,6},{8,9},{9,8},{10,11... | collective-permute-start | bytes 393224 | tf_op jit(solution)/shard_map/ppermute | solution.py:185
  10.9 1.7 %collective-permute-start.8 = (bf16[32,2048]{1,0:T(8,128)(2,1)S(1)}, bf16[32,2048]{1,0:T(8,128)(2,1)S(1)}, u32[]{:S(2)}, u32[]{:S(2)}) collective-permute-start(bf16[32,2048]{1,0:T(8,128)(2,1)S(1)} %hold.4.refs_2_.own_ref), channel_id=1, source_target_pairs={{0,1},{1,0},{2,3},{3,2},{4,5},{5,4},{6,7},{7,6},{8,9},{9,8},{10,11... | collective-permute-start | bytes 393224 | tf_op jit(solution)/shard_map/ppermute | solution.py:185
  11.3 1.3 %collective-permute-start.7 = (bf16[32,2048]{1,0:T(8,128)(2,1)S(1)}, bf16[32,2048]{1,0:T(8,128)(2,1)S(1)}, u32[]{:S(2)}, u32[]{:S(2)}) collective-permute-start(bf16[32,2048]{1,0:T(8,128)(2,1)S(1)} %hold.5.own_ref), channel_id=1, source_target_pairs={{0,1},{1,0},{2,3},{3,2},{4,5},{5,4},{6,7},{7,6},{8,9},{9,8},{10,11... | collective-permute-start | bytes 393224 | tf_op jit(solution)/shard_map/ppermute | solution.py:185
  12.9 3.6 %collective-permute-start.10 = (f32[1,128]{1,0:T(1,128)S(1)}, f32[1,128]{1,0:T(1,128)S(1)}, u32[]{:S(2)}, u32[]{:S(2)}) collective-permute-start(f32[1,128]{1,0:T(1,128)S(1)} %arrange.1), channel_id=1, source_target_pairs={{9,1},{11,3},{13,5},{15,7},{0,8},{2,10},{4,12},{6,14},{1,0},{3,2},... | collective-permute-start | bytes 1544 | tf_op jit(solution)/shard_map/ppermute | solution.py:223

commit v21 on v20

--- a/solution.py
+++ b/solution.py
@@ -45,15 +45,13 @@
     chunks = len(parts) // 2
     total = jnp.concatenate([parts[i][...] + parts[chunks + i][...] for i in range(chunks)], axis=0)
     total = total * count_ref[...]
-    high = total.astype(BF16)
-    low = (total - high.astype(F32)).astype(BF16)
-    gram = lax.dot_general(
-        jnp.concatenate([high, high, low], axis=0),
-        jnp.concatenate([high, low, high], axis=0),
+    held[...] = lax.dot_general(
+        total[:, rank : 2 * rank],
+        total[:, 0:rank],
         (((0,), (0,)), ((), ())),
+        precision=lax.Precision.HIGHEST,
         preferred_element_type=F32,
     )
-    held[...] = gram[rank : 2 * rank, 0:rank]
     pairs = out_ref.shape[0]
     even = held[pl.ds(0, pairs, stride=2), :]
     odd = held[pl.ds(1, pairs, stride=2), :]
@@ -78,25 +76,29 @@
             out_ref[:, j * LANES : (j + 1) * LANES] = rows
 
 
-def score_kernel(first_ref, second_ref, own_ref, other_ref, *refs):
-    out_ref = refs[-1]
+def products(first_ref, second_ref, own_ref, other_ref):
     total = None
     for flat_ref, query_ref in ((first_ref, own_ref), (second_ref, other_ref)):
         for j in range(query_ref.shape[1] // LANES):
             lanes = slice(j * LANES, (j + 1) * LANES)
             term = query_ref[:, lanes].astype(F32) * flat_ref[0:1, lanes]
             total = term if total is None else total + term
-    out_ref[...] = total
-
-
-def arrange_kernel(*refs):
-    parts, out_ref, held = refs[:-2], refs[-2], refs[-1]
-    mates = len(parts)
+    return total
+
+
+def score_kernel(first_ref, second_ref, own_ref, other_ref, *refs):
+    refs[-1][...] = products(first_ref, second_ref, own_ref, other_ref)
+
+
+def arrange_kernel(rounds, *refs):
+    parts, out_ref, held = refs[4:-2], refs[-2], refs[-1]
+    mates = len(rounds)
     own_queries = parts[0].shape[0]
     member = lax.rem(lax.axis_index("dp"), mates)
-    for r, part in enumerate(parts):
+    sums = [part[...] for part in parts] + [products(*refs[:4])]
+    for r, part in zip(rounds, sums):
         start = pl.multiple_of((member ^ r) * own_queries, own_queries)
-        held[pl.ds(start, own_queries), :] = part[...]
+        held[pl.ds(start, own_queries), :] = part
     out_ref[...] = jnp.sum(held[...].T, axis=0, keepdims=True)
 
 
@@ -197,7 +199,7 @@
     small = pl.CostEstimate(flops=1, bytes_accessed=1, transcendentals=0)
     few = pltpu.CompilerParams(vmem_limit_bytes=8 << 20)
     parts = []
-    for half, other in zip(halves, swapped):
+    for half, other in zip(halves[:-1], swapped[:-1]):
         before = parts[-1:]
         parts.append(
             pl.pallas_call(
@@ -211,15 +213,15 @@
             )(*flats, half, other, *before)
         )
     scores = pl.pallas_call(
-        arrange_kernel,
-        in_specs=[vmem] * mates,
+        functools.partial(arrange_kernel, [-k % mates for k in range(mates)]),
+        in_specs=[vmem] * (mates + 3),
         out_specs=vmem,
         out_shape=jax.ShapeDtypeStruct((1, width), F32),
         scratch_shapes=[pltpu.VMEM((width, LANES), F32)],
         compiler_params=few,
         cost_estimate=small,
         name="arrange",
-    )(parts[0], *parts[:0:-1])
+    )(*flats, halves[-1], swapped[-1], *parts)
     return lax.ppermute(scores, both, back)
 
 

time: 17.1 us -> 17 us (level)
  no operation moved by 1% of the time
where the time goes in v21:
time: 17 us; the launch traced here: 16.9 us
  starting transfers between devices  11 us (65%)
  waiting for transfers between devices  3.03 us (18%)
  Pallas kernels  2.23 us (13%)
  local copies, waits for them, and re-layouts  0.53 us (3%)
    ppermute x3, starting transfers between devices, on_device(): halves.append(lax.ppermute(sent, 'dp', [(d, d ^ r) for d in range(clips)]))  4.67 us
    ppermute x4, starting transfers between devices, on_device(): swapped = [lax.ppermute(half, 'tensor', swap) for half in halves]  3.24 us
    ppermute x1, starting transfers between devices, on_device(): return lax.ppermute(scores, both, back)  2.17 us
    ppermute x1, waiting for transfers between devices, on_device(): return lax.ppermute(scores, both, back)  1.3 us
    pallas_call x1, Pallas kernels, on_device(): pl.pallas_call(functools.partial(project_kernel, rank), in_specs=[vmem] *...  1.17 us
    ppermute x1, waiting for transfers between devices, on_device(): far_sketch = lax.ppermute(sketch, both, there)  0.94 us
    ppermute x2, waiting for transfers between devices, on_device(): other = [lax.ppermute(part, 'tensor', swap) for part in partial]  0.74 us
    ppermute x2, starting transfers between devices, on_device(): other = [lax.ppermute(part, 'tensor', swap) for part in partial]  0.57 us
  transfers between devices with their start and end apart: 11, of which 4 were waited for; matrix products, arithmetic and copies ran while one was open for 0% of the time, Pallas kernels for 12%

profile of v21, /device:TPU:0, one launch (start us, length us, event | category | flops | bytes accessed | tf_op | source)
XLA Modules:
  0.0 16.9 jit_solution(9376977806487507388)
XLA Ops:
  0.0 4.0 %collective-permute-start.4 = (bf16[32,2048]{1,0:T(8,128)(2,1)}, bf16[32,2048]{1,0:T(8,128)(2,1)S(1)}, u32[]{:S(2)}, u32[]{:S(2)}) collective-permute-start(bf16[32,2048]{1,0:T(8,128)(2,1)} %own_ref.1), channel_id=1, source_target_pairs={{0,6},{2,4},{4,2},{6,0},{8,14},{10,12},{12,10},{14,8},{1,7},{3,5},... | collective-permute-start | bytes 393224 | tf_op jit(solution)/shard_map/ppermute | solution.py:137
  4.1 0.4 %collective-permute-start.5 = (bf16[32,2048]{1,0:T(8,128)(2,1)}, bf16[32,2048]{1,0:T(8,128)(2,1)S(1)}, u32[]{:S(2)}, u32[]{:S(2)}) collective-permute-start(bf16[32,2048]{1,0:T(8,128)(2,1)} %own_ref.1), channel_id=1, source_target_pairs={{0,4},{2,6},{4,0},{6,2},{8,12},{10,14},{12,8},{14,10},{1,5},{3,7},... | collective-permute-start | bytes 393224 | tf_op jit(solution)/shard_map/ppermute | solution.py:137
  4.5 0.2 %collective-permute-start.3 = (bf16[32,2048]{1,0:T(8,128)(2,1)}, bf16[32,2048]{1,0:T(8,128)(2,1)S(1)}, u32[]{:S(2)}, u32[]{:S(2)}) collective-permute-start(bf16[32,2048]{1,0:T(8,128)(2,1)} %own_ref.1), channel_id=1, source_target_pairs={{0,2},{2,0},{4,6},{6,4},{8,10},{10,8},{12,14},{14,12},{1,3},{3,1},... | collective-permute-start | bytes 393224 | tf_op jit(solution)/shard_map/ppermute | solution.py:137
  4.7 1.2 %project.1 = (f32[192,128]{1,0:T(8,128)S(1)}, f32[192,128]{1,0:T(8,128)S(1)}) custom-call(f32[8,128]{1,0:T(8,128)S(1)} %first.1.first_ref, bf16[1,384,2560]{2,1,0:T(8,128)(2,1)S(1)} %copy-done, bf16[1,384,2560]{2,1,0:T(8,128)(2,1)S(1)} %copy-done.1, bf16[2560,128]{1,0:T(8,128)(2,1)S(1)} %copy-done.2), custom_call_target="tpu_custom_call" | custom-call | flops 503316480 | bytes 3932160 | tf_op jit(solution)/shard_map/project/pallas_call | solution.py:138
  5.9 0.1 collective-permute-start
  6.0 0.5 %collective-permute-start.1 = (f32[192,128]{1,0:T(8,128)S(1)}, f32[192,128]{1,0:T(8,128)S(1)}, u32[]{:S(2)}, u32[]{:S(2)}) collective-permute-start(f32[192,128]{1,0:T(8,128)S(1)} %get-tuple-element.13.refs_1_), channel_id=1, source_target_pairs={{0,1},{1,0},{2,3},{3,2},{4,5},{5,4},{6,7},{7,6},{8,9},{9,8},{10,11... | collective-permute-start | bytes 294920 | tf_op jit(solution)/shard_map/ppermute | solution.py:150
  6.5 0.2 %count.1.count_ref = f32[384,128]{1,0:T(8,128)S(1)} custom-call(s32[1,256]{1,0:T(1,128)S(1)} %copy-done.4), custom_call_target="tpu_custom_call" | custom-call | flops 1 | bytes 1 | tf_op jit(solution)/shard_map/count/pallas_call | solution.py:151
  6.7 0.6 %collective-permute-done.refs_2_ = f32[192,128]{1,0:T(8,128)S(1)} collective-permute-done((f32[192,128]{1,0:T(8,128)S(1)}, f32[192,128]{1,0:T(8,128)S(1)}, u32[]{:S(2)}, u32[]{:S(2)}) %collective-permute-start) | collective-permute-done | bytes 98336 | tf_op jit(solution)/shard_map/ppermute | solution.py:150
  7.3 0.2 collective-permute-done.1.refs_3_
  7.4 0.5 %sketch.1.own_ref.refs_1_ = bf16[32,128]{1,0:T(8,128)(2,1)S(1)} custom-call(f32[384,128]{1,0:T(8,128)S(1)} %count.1.count_ref, f32[192,128]{1,0:T(8,128)S(1)} %get-tuple-element.12.refs_0_, f32[192,128]{1,0:T(8,128)S(1)} %get-tuple-element.13.refs_1_, f32[192,128]{1,0:T(8,128)S(1)} %collective-permute-done.refs_2_, f32[192,128]{1,0:T(8,128)S(1)} %collective-permute-done.1.refs_3_), custom_call_target="tpu_custom_call" | custom-call | flops 1 | bytes 1 | tf_op jit(solution)/shard_map/sketch/pallas_call | solution.py:160
  7.9 0.4 %collective-permute-start.2 = (bf16[32,128]{1,0:T(8,128)(2,1)S(1)}, bf16[32,128]{1,0:T(8,128)(2,1)S(1)}, u32[]{:S(2)}, u32[]{:S(2)}) collective-permute-start(bf16[32,128]{1,0:T(8,128)(2,1)S(1)} %sketch.1.own_ref.refs_1_), channel_id=1, source_target_pairs={{1,9},{3,11},{5,13},{7,15},{8,0},{10,2},{12,4},{14,6},{0,1},{2,3},... | collective-permute-start | bytes 24584 | tf_op jit(solution)/shard_map/ppermute | solution.py:171
  8.2 2.7 %collective-permute-start.7 = (bf16[32,2048]{1,0:T(8,128)(2,1)S(1)}, bf16[32,2048]{1,0:T(8,128)(2,1)S(1)}, u32[]{:S(2)}, u32[]{:S(2)}) collective-permute-start(bf16[32,2048]{1,0:T(8,128)(2,1)S(1)} %copy-done.3), channel_id=1, source_target_pairs={{0,1},{1,0},{2,3},{3,2},{4,5},{5,4},{6,7},{7,6},{8,9},{9,8},{10,11... | collective-permute-start | bytes 393224 | tf_op jit(solution)/shard_map/ppermute | solution.py:187
  10.9 0.1 collective-permute-start.8
  11.0 0.4 %collective-permute-start.9 = (bf16[32,2048]{1,0:T(8,128)(2,1)S(1)}, bf16[32,2048]{1,0:T(8,128)(2,1)S(1)}, u32[]{:S(2)}, u32[]{:S(2)}) collective-permute-start(bf16[32,2048]{1,0:T(8,128)(2,1)S(1)} %hold.4.refs_2_.own_ref), channel_id=1, source_target_pairs={{0,1},{1,0},{2,3},{3,2},{4,5},{5,4},{6,7},{7,6},{8,9},{9,8},{10,11... | collective-permute-start | bytes 393224 | tf_op jit(solution)/shard_map/ppermute | solution.py:187
  11.4 0.1 collective-permute-start.6
  11.5 0.9 %collective-permute-done.2.far_ref = bf16[32,128]{1,0:T(8,128)(2,1)S(1)} collective-permute-done((bf16[32,128]{1,0:T(8,128)(2,1)S(1)}, bf16[32,128]{1,0:T(8,128)(2,1)S(1)}, u32[]{:S(2)}, u32[]{:S(2)}) %collective-permute-start.2) | collective-permute-done | bytes 8224 | tf_op jit(solution)/shard_map/ppermute | solution.py:171
  12.5 0.1 score.3.refs_0_.refs_4_
  12.6 0.1 score.4.refs_0_.refs_5_
  12.6 0.1 score.5.refs_6_
  12.7 0.0 collective-permute-done.6.refs_3_
  12.8 0.2 arrange.1
  12.9 2.2 %collective-permute-start.10 = (f32[1,128]{1,0:T(1,128)S(1)}, f32[1,128]{1,0:T(1,128)S(1)}, u32[]{:S(2)}, u32[]{:S(2)}) collective-permute-start(f32[1,128]{1,0:T(1,128)S(1)} %arrange.1), channel_id=1, source_target_pairs={{9,1},{11,3},{13,5},{15,7},{0,8},{2,10},{4,12},{6,14},{1,0},{3,2},... | collective-permute-start | bytes 1544 | tf_op jit(solution)/shard_map/ppermute | solution.py:225
  15.1 1.3 %collective-permute-done.10 = f32[1,128]{1,0:T(1,128)S(1)} collective-permute-done((f32[1,128]{1,0:T(1,128)S(1)}, f32[1,128]{1,0:T(1,128)S(1)}, u32[]{:S(2)}, u32[]{:S(2)}) %collective-permute-start.10) | collective-permute-done | bytes 544 | tf_op jit(solution)/shard_map/ppermute | solution.py:225
  16.4 0.5 %copy.13 = f32[1,128]{1,0:T(1,128)} copy(f32[1,128]{1,0:T(1,128)S(1)} %collective-permute-done.10) | data formatting | bytes 1024
  (21 shorter events, 0.1 us)
Async XLA Ops:
  0.0 4.7 %copy-start = (bf16[1,384,2560]{2,1,0:T(8,128)(2,1)S(1)}, bf16[1,384,2560]{2,1,0:T(8,128)(2,1)}, u32[]{:S(2)}) copy-start(bf16[1,384,2560]{2,1,0:T(8,128)(2,1)} %acts_ref.1) | copy-start | bytes 5898244
  0.0 4.7 %copy-start.1 = (bf16[1,384,2560]{2,1,0:T(8,128)(2,1)S(1)}, bf16[1,384,2560]{2,1,0:T(8,128)(2,1)}, u32[]{:S(2)}) copy-start(bf16[1,384,2560]{2,1,0:T(8,128)(2,1)} %grads_ref.1) | copy-start | bytes 5898244
  0.0 4.7 %copy-start.2 = (bf16[2560,128]{1,0:T(8,128)(2,1)S(1)}, bf16[2560,128]{1,0:T(8,128)(2,1)}, u32[]{:S(2)}) copy-start(bf16[2560,128]{1,0:T(8,128)(2,1)} %proj_ref.1) | copy-start | bytes 1966084
  0.0 6.5 %copy-start.4 = (s32[1,256]{1,0:T(1,128)S(1)}, s32[1,256]{1,0:T(1,128)}, u32[]{:S(2)}) copy-start(s32[1,256]{1,0:T(1,128)} %picks_ref.1) | copy-start | bytes 3076
  0.0 8.2 %copy-start.3 = (bf16[32,2048]{1,0:T(8,128)(2,1)S(1)}, bf16[32,2048]{1,0:T(8,128)(2,1)}, u32[]{:S(2)}) copy-start(bf16[32,2048]{1,0:T(8,128)(2,1)} %own_ref.1) | copy-start | bytes 393220
  0.0 10.9 %collective-permute-start.4 = (bf16[32,2048]{1,0:T(8,128)(2,1)}, bf16[32,2048]{1,0:T(8,128)(2,1)S(1)}, u32[]{:S(2)}, u32[]{:S(2)}) collective-permute-start(bf16[32,2048]{1,0:T(8,128)(2,1)} %own_ref.1), channel_id=1, source_target_pairs={{0,6},{2,4},{4,2},{6,0},{8,14},{10,12},{12,10},{14,8},{1,7},{3,5},... | collective-permute-start | bytes 393224 | tf_op jit(solution)/shard_map/ppermute | solution.py:137
  4.1 6.9 %collective-permute-start.5 = (bf16[32,2048]{1,0:T(8,128)(2,1)}, bf16[32,2048]{1,0:T(8,128)(2,1)S(1)}, u32[]{:S(2)}, u32[]{:S(2)}) collective-permute-start(bf16[32,2048]{1,0:T(8,128)(2,1)} %own_ref.1), channel_id=1, source_target_pairs={{0,4},{2,6},{4,0},{6,2},{8,12},{10,14},{12,8},{14,10},{1,5},{3,7},... | collective-permute-start | bytes 393224 | tf_op jit(solution)/shard_map/ppermute | solution.py:137
  4.5 6.9 %collective-permute-start.3 = (bf16[32,2048]{1,0:T(8,128)(2,1)}, bf16[32,2048]{1,0:T(8,128)(2,1)S(1)}, u32[]{:S(2)}, u32[]{:S(2)}) collective-permute-start(bf16[32,2048]{1,0:T(8,128)(2,1)} %own_ref.1), channel_id=1, source_target_pairs={{0,2},{2,0},{4,6},{6,4},{8,10},{10,8},{12,14},{14,12},{1,3},{3,1},... | collective-permute-start | bytes 393224 | tf_op jit(solution)/shard_map/ppermute | solution.py:137
  5.9 1.4 %collective-permute-start = (f32[192,128]{1,0:T(8,128)S(1)}, f32[192,128]{1,0:T(8,128)S(1)}, u32[]{:S(2)}, u32[]{:S(2)}) collective-permute-start(f32[192,128]{1,0:T(8,128)S(1)} %get-tuple-element.12.refs_0_), channel_id=1, source_target_pairs={{0,1},{1,0},{2,3},{3,2},{4,5},{5,4},{6,7},{7,6},{8,9},{9,8},{10,11... | collective-permute-start | bytes 294920 | tf_op jit(solution)/shard_map/ppermute | solution.py:150
  6.0 1.4 %collective-permute-start.1 = (f32[192,128]{1,0:T(8,128)S(1)}, f32[192,128]{1,0:T(8,128)S(1)}, u32[]{:S(2)}, u32[]{:S(2)}) collective-permute-start(f32[192,128]{1,0:T(8,128)S(1)} %get-tuple-element.13.refs_1_), channel_id=1, source_target_pairs={{0,1},{1,0},{2,3},{3,2},{4,5},{5,4},{6,7},{7,6},{8,9},{9,8},{10,11... | collective-permute-start | bytes 294920 | tf_op jit(solution)/shard_map/ppermute | solution.py:150
  7.9 4.6 %collective-permute-start.2 = (bf16[32,128]{1,0:T(8,128)(2,1)S(1)}, bf16[32,128]{1,0:T(8,128)(2,1)S(1)}, u32[]{:S(2)}, u32[]{:S(2)}) collective-permute-start(bf16[32,128]{1,0:T(8,128)(2,1)S(1)} %sketch.1.own_ref.refs_1_), channel_id=1, source_target_pairs={{1,9},{3,11},{5,13},{7,15},{8,0},{10,2},{12,4},{14,6},{0,1},{2,3},... | collective-permute-start | bytes 24584 | tf_op jit(solution)/shard_map/ppermute | solution.py:171
  8.2 4.2 %collective-permute-start.7 = (bf16[32,2048]{1,0:T(8,128)(2,1)S(1)}, bf16[32,2048]{1,0:T(8,128)(2,1)S(1)}, u32[]{:S(2)}, u32[]{:S(2)}) collective-permute-start(bf16[32,2048]{1,0:T(8,128)(2,1)S(1)} %copy-done.3), channel_id=1, source_target_pairs={{0,1},{1,0},{2,3},{3,2},{4,5},{5,4},{6,7},{7,6},{8,9},{9,8},{10,11... | collective-permute-start | bytes 393224 | tf_op jit(solution)/shard_map/ppermute | solution.py:187
  10.9 1.7 %collective-permute-start.8 = (bf16[32,2048]{1,0:T(8,128)(2,1)S(1)}, bf16[32,2048]{1,0:T(8,128)(2,1)S(1)}, u32[]{:S(2)}, u32[]{:S(2)}) collective-permute-start(bf16[32,2048]{1,0:T(8,128)(2,1)S(1)} %hold.3.refs_1_.own_ref), channel_id=1, source_target_pairs={{0,1},{1,0},{2,3},{3,2},{4,5},{5,4},{6,7},{7,6},{8,9},{9,8},{10,11... | collective-permute-start | bytes 393224 | tf_op jit(solution)/shard_map/ppermute | solution.py:187
  11.0 1.7 %collective-permute-start.9 = (bf16[32,2048]{1,0:T(8,128)(2,1)S(1)}, bf16[32,2048]{1,0:T(8,128)(2,1)S(1)}, u32[]{:S(2)}, u32[]{:S(2)}) collective-permute-start(bf16[32,2048]{1,0:T(8,128)(2,1)S(1)} %hold.4.refs_2_.own_ref), channel_id=1, source_target_pairs={{0,1},{1,0},{2,3},{3,2},{4,5},{5,4},{6,7},{7,6},{8,9},{9,8},{10,11... | collective-permute-start | bytes 393224 | tf_op jit(solution)/shard_map/ppermute | solution.py:187
  11.4 1.3 %collective-permute-start.6 = (bf16[32,2048]{1,0:T(8,128)(2,1)S(1)}, bf16[32,2048]{1,0:T(8,128)(2,1)S(1)}, u32[]{:S(2)}, u32[]{:S(2)}) collective-permute-start(bf16[32,2048]{1,0:T(8,128)(2,1)S(1)} %hold.5.refs_2_), channel_id=1, source_target_pairs={{0,1},{1,0},{2,3},{3,2},{4,5},{5,4},{6,7},{7,6},{8,9},{9,8},{10,11... | collective-permute-start | bytes 393224 | tf_op jit(solution)/shard_map/ppermute | solution.py:187
  12.9 3.5 %collective-permute-start.10 = (f32[1,128]{1,0:T(1,128)S(1)}, f32[1,128]{1,0:T(1,128)S(1)}, u32[]{:S(2)}, u32[]{:S(2)}) collective-permute-start(f32[1,128]{1,0:T(1,128)S(1)} %arrange.1), channel_id=1, source_target_pairs={{9,1},{11,3},{13,5},{15,7},{0,8},{2,10},{4,12},{6,14},{1,0},{3,2},... | collective-permute-start | bytes 1544 | tf_op jit(solution)/shard_map/ppermute | solution.py:225

commit v22 on v20

--- a/solution.py
+++ b/solution.py
@@ -45,15 +45,13 @@
     chunks = len(parts) // 2
     total = jnp.concatenate([parts[i][...] + parts[chunks + i][...] for i in range(chunks)], axis=0)
     total = total * count_ref[...]
-    high = total.astype(BF16)
-    low = (total - high.astype(F32)).astype(BF16)
-    gram = lax.dot_general(
-        jnp.concatenate([high, high, low], axis=0),
-        jnp.concatenate([high, low, high], axis=0),
+    held[...] = lax.dot_general(
+        total[:, rank : 2 * rank],
+        total[:, 0:rank],
         (((0,), (0,)), ((), ())),
+        precision=lax.Precision.HIGHEST,
         preferred_element_type=F32,
     )
-    held[...] = gram[rank : 2 * rank, 0:rank]
     pairs = out_ref.shape[0]
     even = held[pl.ds(0, pairs, stride=2), :]
     odd = held[pl.ds(1, pairs, stride=2), :]

time: 17.1 us -> 17.1 us (level)
  no operation moved by 1% of the time
where the time goes in v22:
time: 17.1 us; the launch traced here: 16.9 us
  starting transfers between devices  11 us (64%)
  waiting for transfers between devices  3.03 us (18%)
  Pallas kernels  2.28 us (13%)
  local copies, waits for them, and re-layouts  0.53 us (3%)
    ppermute x3, starting transfers between devices, on_device(): halves.append(lax.ppermute(sent, 'dp', [(d, d ^ r) for d in range(clips)]))  4.67 us
    ppermute x4, starting transfers between devices, on_device(): swapped = [lax.ppermute(half, 'tensor', swap) for half in halves]  3.24 us
    ppermute x1, starting transfers between devices, on_device(): return lax.ppermute(scores, both, back)  2.17 us
    ppermute x1, waiting for transfers between devices, on_device(): return lax.ppermute(scores, both, back)  1.3 us
    pallas_call x1, Pallas kernels, on_device(): pl.pallas_call(functools.partial(project_kernel, rank), in_specs=[vmem] *...  1.17 us
    ppermute x1, waiting for transfers between devices, on_device(): far_sketch = lax.ppermute(sketch, both, there)  0.94 us
    ppermute x2, waiting for transfers between devices, on_device(): other = [lax.ppermute(part, 'tensor', swap) for part in partial]  0.74 us
    ppermute x2, starting transfers between devices, on_device(): other = [lax.ppermute(part, 'tensor', swap) for part in partial]  0.57 us
  transfers between devices with their start and end apart: 11, of which 4 were waited for; matrix products, arithmetic and copies ran while one was open for 0% of the time, Pallas kernels for 12%

profile of v22, /device:TPU:0, one launch (start us, length us, event | category | flops | bytes accessed | tf_op | source)
XLA Modules:
  0.0 16.9 jit_solution(4439031342564145773)
XLA Ops:
  0.0 4.0 %collective-permute-start.5 = (bf16[32,2048]{1,0:T(8,128)(2,1)}, bf16[32,2048]{1,0:T(8,128)(2,1)S(1)}, u32[]{:S(2)}, u32[]{:S(2)}) collective-permute-start(bf16[32,2048]{1,0:T(8,128)(2,1)} %own_ref.1), channel_id=1, source_target_pairs={{0,6},{2,4},{4,2},{6,0},{8,14},{10,12},{12,10},{14,8},{1,7},{3,5},... | collective-permute-start | bytes 393224 | tf_op jit(solution)/shard_map/ppermute | solution.py:133
  4.1 0.4 %collective-permute-start.6 = (bf16[32,2048]{1,0:T(8,128)(2,1)}, bf16[32,2048]{1,0:T(8,128)(2,1)S(1)}, u32[]{:S(2)}, u32[]{:S(2)}) collective-permute-start(bf16[32,2048]{1,0:T(8,128)(2,1)} %own_ref.1), channel_id=1, source_target_pairs={{0,4},{2,6},{4,0},{6,2},{8,12},{10,14},{12,8},{14,10},{1,5},{3,7},... | collective-permute-start | bytes 393224 | tf_op jit(solution)/shard_map/ppermute | solution.py:133
  4.5 0.2 %collective-permute-start.4 = (bf16[32,2048]{1,0:T(8,128)(2,1)}, bf16[32,2048]{1,0:T(8,128)(2,1)S(1)}, u32[]{:S(2)}, u32[]{:S(2)}) collective-permute-start(bf16[32,2048]{1,0:T(8,128)(2,1)} %own_ref.1), channel_id=1, source_target_pairs={{0,2},{2,0},{4,6},{6,4},{8,10},{10,8},{12,14},{14,12},{1,3},{3,1},... | collective-permute-start | bytes 393224 | tf_op jit(solution)/shard_map/ppermute | solution.py:133
  4.7 1.2 %project.1 = (f32[192,128]{1,0:T(8,128)S(1)}, f32[192,128]{1,0:T(8,128)S(1)}) custom-call(f32[8,128]{1,0:T(8,128)S(1)} %first.1.first_ref, bf16[1,384,2560]{2,1,0:T(8,128)(2,1)S(1)} %copy-done, bf16[1,384,2560]{2,1,0:T(8,128)(2,1)S(1)} %copy-done.1, bf16[2560,128]{1,0:T(8,128)(2,1)S(1)} %copy-done.2), custom_call_target="tpu_custom_call" | custom-call | flops 503316480 | bytes 3932160 | tf_op jit(solution)/shard_map/project/pallas_call | solution.py:134
  5.9 0.1 collective-permute-start
  6.0 0.5 %collective-permute-start.1 = (f32[192,128]{1,0:T(8,128)S(1)}, f32[192,128]{1,0:T(8,128)S(1)}, u32[]{:S(2)}, u32[]{:S(2)}) collective-permute-start(f32[192,128]{1,0:T(8,128)S(1)} %get-tuple-element.13.refs_1_), channel_id=1, source_target_pairs={{0,1},{1,0},{2,3},{3,2},{4,5},{5,4},{6,7},{7,6},{8,9},{9,8},{10,11... | collective-permute-start | bytes 294920 | tf_op jit(solution)/shard_map/ppermute | solution.py:146
  6.5 0.2 %count.1.count_ref = f32[384,128]{1,0:T(8,128)S(1)} custom-call(s32[1,256]{1,0:T(1,128)S(1)} %copy-done.4), custom_call_target="tpu_custom_call" | custom-call | flops 1 | bytes 1 | tf_op jit(solution)/shard_map/count/pallas_call | solution.py:147
  6.7 0.6 %collective-permute-done.refs_2_ = f32[192,128]{1,0:T(8,128)S(1)} collective-permute-done((f32[192,128]{1,0:T(8,128)S(1)}, f32[192,128]{1,0:T(8,128)S(1)}, u32[]{:S(2)}, u32[]{:S(2)}) %collective-permute-start) | collective-permute-done | bytes 98336 | tf_op jit(solution)/shard_map/ppermute | solution.py:146
  7.3 0.2 collective-permute-done.1.refs_3_
  7.4 0.5 %sketch.1.own_ref.refs_1_ = bf16[32,128]{1,0:T(8,128)(2,1)S(1)} custom-call(f32[384,128]{1,0:T(8,128)S(1)} %count.1.count_ref, f32[192,128]{1,0:T(8,128)S(1)} %get-tuple-element.12.refs_0_, f32[192,128]{1,0:T(8,128)S(1)} %get-tuple-element.13.refs_1_, f32[192,128]{1,0:T(8,128)S(1)} %collective-permute-done.refs_2_, f32[192,128]{1,0:T(8,128)S(1)} %collective-permute-done.1.refs_3_), custom_call_target="tpu_custom_call" | custom-call | flops 1 | bytes 1 | tf_op jit(solution)/shard_map/sketch/pallas_call | solution.py:156
  7.9 0.4 %collective-permute-start.2 = (bf16[32,128]{1,0:T(8,128)(2,1)S(1)}, bf16[32,128]{1,0:T(8,128)(2,1)S(1)}, u32[]{:S(2)}, u32[]{:S(2)}) collective-permute-start(bf16[32,128]{1,0:T(8,128)(2,1)S(1)} %sketch.1.own_ref.refs_1_), channel_id=1, source_target_pairs={{1,9},{3,11},{5,13},{7,15},{8,0},{10,2},{12,4},{14,6},{0,1},{2,3},... | collective-permute-start | bytes 24584 | tf_op jit(solution)/shard_map/ppermute | solution.py:167
  8.2 2.7 %collective-permute-start.3 = (bf16[32,2048]{1,0:T(8,128)(2,1)S(1)}, bf16[32,2048]{1,0:T(8,128)(2,1)S(1)}, u32[]{:S(2)}, u32[]{:S(2)}) collective-permute-start(bf16[32,2048]{1,0:T(8,128)(2,1)S(1)} %copy-done.3), channel_id=1, source_target_pairs={{0,1},{1,0},{2,3},{3,2},{4,5},{5,4},{6,7},{7,6},{8,9},{9,8},{10,11... | collective-permute-start | bytes 393224 | tf_op jit(solution)/shard_map/ppermute | solution.py:183
  10.9 0.1 collective-permute-start.9
  11.0 0.4 %collective-permute-start.8 = (bf16[32,2048]{1,0:T(8,128)(2,1)S(1)}, bf16[32,2048]{1,0:T(8,128)(2,1)S(1)}, u32[]{:S(2)}, u32[]{:S(2)}) collective-permute-start(bf16[32,2048]{1,0:T(8,128)(2,1)S(1)} %hold.4.refs_2_.own_ref), channel_id=1, source_target_pairs={{0,1},{1,0},{2,3},{3,2},{4,5},{5,4},{6,7},{7,6},{8,9},{9,8},{10,11... | collective-permute-start | bytes 393224 | tf_op jit(solution)/shard_map/ppermute | solution.py:183
  11.4 0.1 collective-permute-start.7
  11.5 0.9 %collective-permute-done.2.far_ref = bf16[32,128]{1,0:T(8,128)(2,1)S(1)} collective-permute-done((bf16[32,128]{1,0:T(8,128)(2,1)S(1)}, bf16[32,128]{1,0:T(8,128)(2,1)S(1)}, u32[]{:S(2)}, u32[]{:S(2)}) %collective-permute-start.2) | collective-permute-done | bytes 8224 | tf_op jit(solution)/shard_map/ppermute | solution.py:167
  12.5 0.1 score.4.refs_0_
  12.6 0.1 score.5.refs_0_.refs_3_
  12.7 0.1 score.6.refs_0_.refs_2_
  12.8 0.1 score.7.refs_1_
  12.8 0.1 arrange.1
  13.0 2.2 %collective-permute-start.10 = (f32[1,128]{1,0:T(1,128)S(1)}, f32[1,128]{1,0:T(1,128)S(1)}, u32[]{:S(2)}, u32[]{:S(2)}) collective-permute-start(f32[1,128]{1,0:T(1,128)S(1)} %arrange.1), channel_id=1, source_target_pairs={{9,1},{11,3},{13,5},{15,7},{0,8},{2,10},{4,12},{6,14},{1,0},{3,2},... | collective-permute-start | bytes 1544 | tf_op jit(solution)/shard_map/ppermute | solution.py:221
  15.1 1.3 %collective-permute-done.10 = f32[1,128]{1,0:T(1,128)S(1)} collective-permute-done((f32[1,128]{1,0:T(1,128)S(1)}, f32[1,128]{1,0:T(1,128)S(1)}, u32[]{:S(2)}, u32[]{:S(2)}) %collective-permute-start.10) | collective-permute-done | bytes 544 | tf_op jit(solution)/shard_map/ppermute | solution.py:221
  16.4 0.5 %copy.13 = f32[1,128]{1,0:T(1,128)} copy(f32[1,128]{1,0:T(1,128)S(1)} %collective-permute-done.10) | data formatting | bytes 1024
  (22 shorter events, 0.1 us)
Async XLA Ops:
  0.0 4.7 %copy-start = (bf16[1,384,2560]{2,1,0:T(8,128)(2,1)S(1)}, bf16[1,384,2560]{2,1,0:T(8,128)(2,1)}, u32[]{:S(2)}) copy-start(bf16[1,384,2560]{2,1,0:T(8,128)(2,1)} %acts_ref.1) | copy-start | bytes 5898244
  0.0 4.7 %copy-start.1 = (bf16[1,384,2560]{2,1,0:T(8,128)(2,1)S(1)}, bf16[1,384,2560]{2,1,0:T(8,128)(2,1)}, u32[]{:S(2)}) copy-start(bf16[1,384,2560]{2,1,0:T(8,128)(2,1)} %grads_ref.1) | copy-start | bytes 5898244
  0.0 4.7 %copy-start.2 = (bf16[2560,128]{1,0:T(8,128)(2,1)S(1)}, bf16[2560,128]{1,0:T(8,128)(2,1)}, u32[]{:S(2)}) copy-start(bf16[2560,128]{1,0:T(8,128)(2,1)} %proj_ref.1) | copy-start | bytes 1966084
  0.0 6.5 %copy-start.4 = (s32[1,256]{1,0:T(1,128)S(1)}, s32[1,256]{1,0:T(1,128)}, u32[]{:S(2)}) copy-start(s32[1,256]{1,0:T(1,128)} %picks_ref.1) | copy-start | bytes 3076
  0.0 8.2 %copy-start.3 = (bf16[32,2048]{1,0:T(8,128)(2,1)S(1)}, bf16[32,2048]{1,0:T(8,128)(2,1)}, u32[]{:S(2)}) copy-start(bf16[32,2048]{1,0:T(8,128)(2,1)} %own_ref.1) | copy-start | bytes 393220
  0.0 10.9 %collective-permute-start.5 = (bf16[32,2048]{1,0:T(8,128)(2,1)}, bf16[32,2048]{1,0:T(8,128)(2,1)S(1)}, u32[]{:S(2)}, u32[]{:S(2)}) collective-permute-start(bf16[32,2048]{1,0:T(8,128)(2,1)} %own_ref.1), channel_id=1, source_target_pairs={{0,6},{2,4},{4,2},{6,0},{8,14},{10,12},{12,10},{14,8},{1,7},{3,5},... | collective-permute-start | bytes 393224 | tf_op jit(solution)/shard_map/ppermute | solution.py:133
  4.1 6.9 %collective-permute-start.6 = (bf16[32,2048]{1,0:T(8,128)(2,1)}, bf16[32,2048]{1,0:T(8,128)(2,1)S(1)}, u32[]{:S(2)}, u32[]{:S(2)}) collective-permute-start(bf16[32,2048]{1,0:T(8,128)(2,1)} %own_ref.1), channel_id=1, source_target_pairs={{0,4},{2,6},{4,0},{6,2},{8,12},{10,14},{12,8},{14,10},{1,5},{3,7},... | collective-permute-start | bytes 393224 | tf_op jit(solution)/shard_map/ppermute | solution.py:133
  4.5 6.9 %collective-permute-start.4 = (bf16[32,2048]{1,0:T(8,128)(2,1)}, bf16[32,2048]{1,0:T(8,128)(2,1)S(1)}, u32[]{:S(2)}, u32[]{:S(2)}) collective-permute-start(bf16[32,2048]{1,0:T(8,128)(2,1)} %own_ref.1), channel_id=1, source_target_pairs={{0,2},{2,0},{4,6},{6,4},{8,10},{10,8},{12,14},{14,12},{1,3},{3,1},... | collective-permute-start | bytes 393224 | tf_op jit(solution)/shard_map/ppermute | solution.py:133
  5.9 1.4 %collective-permute-start = (f32[192,128]{1,0:T(8,128)S(1)}, f32[192,128]{1,0:T(8,128)S(1)}, u32[]{:S(2)}, u32[]{:S(2)}) collective-permute-start(f32[192,128]{1,0:T(8,128)S(1)} %get-tuple-element.12.refs_0_), channel_id=1, source_target_pairs={{0,1},{1,0},{2,3},{3,2},{4,5},{5,4},{6,7},{7,6},{8,9},{9,8},{10,11... | collective-permute-start | bytes 294920 | tf_op jit(solution)/shard_map/ppermute | solution.py:146
  6.0 1.4 %collective-permute-start.1 = (f32[192,128]{1,0:T(8,128)S(1)}, f32[192,128]{1,0:T(8,128)S(1)}, u32[]{:S(2)}, u32[]{:S(2)}) collective-permute-start(f32[192,128]{1,0:T(8,128)S(1)} %get-tuple-element.13.refs_1_), channel_id=1, source_target_pairs={{0,1},{1,0},{2,3},{3,2},{4,5},{5,4},{6,7},{7,6},{8,9},{9,8},{10,11... | collective-permute-start | bytes 294920 | tf_op jit(solution)/shard_map/ppermute | solution.py:146
  7.9 4.6 %collective-permute-start.2 = (bf16[32,128]{1,0:T(8,128)(2,1)S(1)}, bf16[32,128]{1,0:T(8,128)(2,1)S(1)}, u32[]{:S(2)}, u32[]{:S(2)}) collective-permute-start(bf16[32,128]{1,0:T(8,128)(2,1)S(1)} %sketch.1.own_ref.refs_1_), channel_id=1, source_target_pairs={{1,9},{3,11},{5,13},{7,15},{8,0},{10,2},{12,4},{14,6},{0,1},{2,3},... | collective-permute-start | bytes 24584 | tf_op jit(solution)/shard_map/ppermute | solution.py:167
  8.2 4.2 %collective-permute-start.3 = (bf16[32,2048]{1,0:T(8,128)(2,1)S(1)}, bf16[32,2048]{1,0:T(8,128)(2,1)S(1)}, u32[]{:S(2)}, u32[]{:S(2)}) collective-permute-start(bf16[32,2048]{1,0:T(8,128)(2,1)S(1)} %copy-done.3), channel_id=1, source_target_pairs={{0,1},{1,0},{2,3},{3,2},{4,5},{5,4},{6,7},{7,6},{8,9},{9,8},{10,11... | collective-permute-start | bytes 393224 | tf_op jit(solution)/shard_map/ppermute | solution.py:183
  10.9 1.7 %collective-permute-start.9 = (bf16[32,2048]{1,0:T(8,128)(2,1)S(1)}, bf16[32,2048]{1,0:T(8,128)(2,1)S(1)}, u32[]{:S(2)}, u32[]{:S(2)}) collective-permute-start(bf16[32,2048]{1,0:T(8,128)(2,1)S(1)} %hold.3.refs_1_.own_ref), channel_id=1, source_target_pairs={{0,1},{1,0},{2,3},{3,2},{4,5},{5,4},{6,7},{7,6},{8,9},{9,8},{10,11... | collective-permute-start | bytes 393224 | tf_op jit(solution)/shard_map/ppermute | solution.py:183
  11.0 1.7 %collective-permute-start.8 = (bf16[32,2048]{1,0:T(8,128)(2,1)S(1)}, bf16[32,2048]{1,0:T(8,128)(2,1)S(1)}, u32[]{:S(2)}, u32[]{:S(2)}) collective-permute-start(bf16[32,2048]{1,0:T(8,128)(2,1)S(1)} %hold.4.refs_2_.own_ref), channel_id=1, source_target_pairs={{0,1},{1,0},{2,3},{3,2},{4,5},{5,4},{6,7},{7,6},{8,9},{9,8},{10,11... | collective-permute-start | bytes 393224 | tf_op jit(solution)/shard_map/ppermute | solution.py:183
  11.4 1.3 %collective-permute-start.7 = (bf16[32,2048]{1,0:T(8,128)(2,1)S(1)}, bf16[32,2048]{1,0:T(8,128)(2,1)S(1)}, u32[]{:S(2)}, u32[]{:S(2)}) collective-permute-start(bf16[32,2048]{1,0:T(8,128)(2,1)S(1)} %hold.5.own_ref), channel_id=1, source_target_pairs={{0,1},{1,0},{2,3},{3,2},{4,5},{5,4},{6,7},{7,6},{8,9},{9,8},{10,11... | collective-permute-start | bytes 393224 | tf_op jit(solution)/shard_map/ppermute | solution.py:183
  13.0 3.5 %collective-permute-start.10 = (f32[1,128]{1,0:T(1,128)S(1)}, f32[1,128]{1,0:T(1,128)S(1)}, u32[]{:S(2)}, u32[]{:S(2)}) collective-permute-start(f32[1,128]{1,0:T(1,128)S(1)} %arrange.1), channel_id=1, source_target_pairs={{9,1},{11,3},{13,5},{15,7},{0,8},{2,10},{4,12},{6,14},{1,0},{3,2},... | collective-permute-start | bytes 1544 | tf_op jit(solution)/shard_map/ppermute | solution.py:221

commit v23 on v20

--- a/solution.py
+++ b/solution.py
@@ -97,7 +97,14 @@
     for r, part in enumerate(parts):
         start = pl.multiple_of((member ^ r) * own_queries, own_queries)
         held[pl.ds(start, own_queries), :] = part[...]
-    out_ref[...] = jnp.sum(held[...].T, axis=0, keepdims=True)
+    row = lax.dot_general(
+        jnp.ones((8, LANES), F32),
+        held[...],
+        (((1,), (1,)), ((), ())),
+        precision=lax.Precision.HIGHEST,
+        preferred_element_type=F32,
+    )
+    out_ref[...] = row[0:1, :]
 
 
 def on_device(activations, out_grads, projections, sample_index, queries):

time: 17.1 us -> 17.1 us (level)
  no operation moved by 1% of the time
where the time goes in v23:
time: 17.1 us; the launch traced here: 17 us
  starting transfers between devices  11.1 us (65%)
  waiting for transfers between devices  3.03 us (18%)
  Pallas kernels  2.27 us (13%)
  local copies, waits for them, and re-layouts  0.53 us (3%)
    ppermute x3, starting transfers between devices, on_device(): halves.append(lax.ppermute(sent, 'dp', [(d, d ^ r) for d in range(clips)]))  4.67 us
    ppermute x4, starting transfers between devices, on_device(): swapped = [lax.ppermute(half, 'tensor', swap) for half in halves]  3.24 us
    ppermute x1, starting transfers between devices, on_device(): return lax.ppermute(scores, both, back)  2.23 us
    ppermute x1, waiting for transfers between devices, on_device(): return lax.ppermute(scores, both, back)  1.3 us
    pallas_call x1, Pallas kernels, on_device(): pl.pallas_call(functools.partial(project_kernel, rank), in_specs=[vmem] *...  1.17 us
    ppermute x1, waiting for transfers between devices, on_device(): far_sketch = lax.ppermute(sketch, both, there)  0.94 us
    ppermute x2, waiting for transfers between devices, on_device(): other = [lax.ppermute(part, 'tensor', swap) for part in partial]  0.74 us
    ppermute x2, starting transfers between devices, on_device(): other = [lax.ppermute(part, 'tensor', swap) for part in partial]  0.57 us
  transfers between devices with their start and end apart: 11, of which 4 were waited for; matrix products, arithmetic and copies ran while one was open for 0% of the time, Pallas kernels for 12%

profile of v23, /device:TPU:0, one launch (start us, length us, event | category | flops | bytes accessed | tf_op | source)
XLA Modules:
  0.0 17.0 jit_solution(11736940626573205680)
XLA Ops:
  0.0 4.0 %collective-permute-start.5 = (bf16[32,2048]{1,0:T(8,128)(2,1)}, bf16[32,2048]{1,0:T(8,128)(2,1)S(1)}, u32[]{:S(2)}, u32[]{:S(2)}) collective-permute-start(bf16[32,2048]{1,0:T(8,128)(2,1)} %own_ref.1), channel_id=1, source_target_pairs={{0,6},{2,4},{4,2},{6,0},{8,14},{10,12},{12,10},{14,8},{1,7},{3,5},... | collective-permute-start | bytes 393224 | tf_op jit(solution)/shard_map/ppermute | solution.py:142
  4.1 0.4 %collective-permute-start.6 = (bf16[32,2048]{1,0:T(8,128)(2,1)}, bf16[32,2048]{1,0:T(8,128)(2,1)S(1)}, u32[]{:S(2)}, u32[]{:S(2)}) collective-permute-start(bf16[32,2048]{1,0:T(8,128)(2,1)} %own_ref.1), channel_id=1, source_target_pairs={{0,4},{2,6},{4,0},{6,2},{8,12},{10,14},{12,8},{14,10},{1,5},{3,7},... | collective-permute-start | bytes 393224 | tf_op jit(solution)/shard_map/ppermute | solution.py:142
  4.5 0.2 %collective-permute-start.4 = (bf16[32,2048]{1,0:T(8,128)(2,1)}, bf16[32,2048]{1,0:T(8,128)(2,1)S(1)}, u32[]{:S(2)}, u32[]{:S(2)}) collective-permute-start(bf16[32,2048]{1,0:T(8,128)(2,1)} %own_ref.1), channel_id=1, source_target_pairs={{0,2},{2,0},{4,6},{6,4},{8,10},{10,8},{12,14},{14,12},{1,3},{3,1},... | collective-permute-start | bytes 393224 | tf_op jit(solution)/shard_map/ppermute | solution.py:142
  4.7 1.2 %project.1 = (f32[192,128]{1,0:T(8,128)S(1)}, f32[192,128]{1,0:T(8,128)S(1)}) custom-call(f32[8,128]{1,0:T(8,128)S(1)} %first.1.first_ref, bf16[1,384,2560]{2,1,0:T(8,128)(2,1)S(1)} %copy-done, bf16[1,384,2560]{2,1,0:T(8,128)(2,1)S(1)} %copy-done.1, bf16[2560,128]{1,0:T(8,128)(2,1)S(1)} %copy-done.2), custom_call_target="tpu_custom_call" | custom-call | flops 503316480 | bytes 3932160 | tf_op jit(solution)/shard_map/project/pallas_call | solution.py:143
  5.9 0.1 collective-permute-start
  6.0 0.5 %collective-permute-start.1 = (f32[192,128]{1,0:T(8,128)S(1)}, f32[192,128]{1,0:T(8,128)S(1)}, u32[]{:S(2)}, u32[]{:S(2)}) collective-permute-start(f32[192,128]{1,0:T(8,128)S(1)} %get-tuple-element.13.refs_1_), channel_id=1, source_target_pairs={{0,1},{1,0},{2,3},{3,2},{4,5},{5,4},{6,7},{7,6},{8,9},{9,8},{10,11... | collective-permute-start | bytes 294920 | tf_op jit(solution)/shard_map/ppermute | solution.py:155
  6.5 0.2 %count.1.count_ref = f32[384,128]{1,0:T(8,128)S(1)} custom-call(s32[1,256]{1,0:T(1,128)S(1)} %copy-done.4), custom_call_target="tpu_custom_call" | custom-call | flops 1 | bytes 1 | tf_op jit(solution)/shard_map/count/pallas_call | solution.py:156
  6.7 0.6 %collective-permute-done.refs_2_ = f32[192,128]{1,0:T(8,128)S(1)} collective-permute-done((f32[192,128]{1,0:T(8,128)S(1)}, f32[192,128]{1,0:T(8,128)S(1)}, u32[]{:S(2)}, u32[]{:S(2)}) %collective-permute-start) | collective-permute-done | bytes 98336 | tf_op jit(solution)/shard_map/ppermute | solution.py:155
  7.3 0.2 collective-permute-done.1.refs_3_
  7.4 0.4 %sketch.1.own_ref.refs_1_ = bf16[32,128]{1,0:T(8,128)(2,1)S(1)} custom-call(f32[384,128]{1,0:T(8,128)S(1)} %count.1.count_ref, f32[192,128]{1,0:T(8,128)S(1)} %get-tuple-element.12.refs_0_, f32[192,128]{1,0:T(8,128)S(1)} %get-tuple-element.13.refs_1_, f32[192,128]{1,0:T(8,128)S(1)} %collective-permute-done.refs_2_, f32[192,128]{1,0:T(8,128)S(1)} %collective-permute-done.1.refs_3_), custom_call_target="tpu_custom_call" | custom-call | flops 1 | bytes 1 | tf_op jit(solution)/shard_map/sketch/pallas_call | solution.py:165
  7.8 0.4 %collective-permute-start.2 = (bf16[32,128]{1,0:T(8,128)(2,1)S(1)}, bf16[32,128]{1,0:T(8,128)(2,1)S(1)}, u32[]{:S(2)}, u32[]{:S(2)}) collective-permute-start(bf16[32,128]{1,0:T(8,128)(2,1)S(1)} %sketch.1.own_ref.refs_1_), channel_id=1, source_target_pairs={{1,9},{3,11},{5,13},{7,15},{8,0},{10,2},{12,4},{14,6},{0,1},{2,3},... | collective-permute-start | bytes 24584 | tf_op jit(solution)/shard_map/ppermute | solution.py:176
  8.1 2.7 %collective-permute-start.3 = (bf16[32,2048]{1,0:T(8,128)(2,1)S(1)}, bf16[32,2048]{1,0:T(8,128)(2,1)S(1)}, u32[]{:S(2)}, u32[]{:S(2)}) collective-permute-start(bf16[32,2048]{1,0:T(8,128)(2,1)S(1)} %copy-done.3), channel_id=1, source_target_pairs={{0,1},{1,0},{2,3},{3,2},{4,5},{5,4},{6,7},{7,6},{8,9},{9,8},{10,11... | collective-permute-start | bytes 393224 | tf_op jit(solution)/shard_map/ppermute | solution.py:192
  10.8 0.1 collective-permute-start.9
  10.9 0.4 %collective-permute-start.8 = (bf16[32,2048]{1,0:T(8,128)(2,1)S(1)}, bf16[32,2048]{1,0:T(8,128)(2,1)S(1)}, u32[]{:S(2)}, u32[]{:S(2)}) collective-permute-start(bf16[32,2048]{1,0:T(8,128)(2,1)S(1)} %hold.4.refs_2_.own_ref), channel_id=1, source_target_pairs={{0,1},{1,0},{2,3},{3,2},{4,5},{5,4},{6,7},{7,6},{8,9},{9,8},{10,11... | collective-permute-start | bytes 393224 | tf_op jit(solution)/shard_map/ppermute | solution.py:192
  11.3 0.1 collective-permute-start.7
  11.4 0.9 %collective-permute-done.2.far_ref = bf16[32,128]{1,0:T(8,128)(2,1)S(1)} collective-permute-done((bf16[32,128]{1,0:T(8,128)(2,1)S(1)}, bf16[32,128]{1,0:T(8,128)(2,1)S(1)}, u32[]{:S(2)}, u32[]{:S(2)}) %collective-permute-start.2) | collective-permute-done | bytes 8224 | tf_op jit(solution)/shard_map/ppermute | solution.py:176
  12.4 0.1 score.4.refs_0_
  12.5 0.1 score.5.refs_0_.refs_3_
  12.6 0.1 score.6.refs_0_.refs_2_
  12.7 0.1 score.7.refs_1_
  12.7 0.2 %arrange.1 = f32[1,128]{1,0:T(1,128)S(1)} custom-call(f32[32,128]{1,0:T(8,128)S(1)} %score.4.refs_0_, f32[32,128]{1,0:T(8,128)S(1)} %score.7.refs_1_, f32[32,128]{1,0:T(8,128)S(1)} %score.6.refs_0_.refs_2_, f32[32,128]{1,0:T(8,128)S(1)} %score.5.refs_0_.refs_3_), custom_call_target="tpu_custom_call" | custom-call | flops 1 | bytes 1 | tf_op jit(solution)/shard_map/arrange/pallas_call | solution.py:220
  12.9 2.2 %collective-permute-start.10 = (f32[1,128]{1,0:T(1,128)S(1)}, f32[1,128]{1,0:T(1,128)S(1)}, u32[]{:S(2)}, u32[]{:S(2)}) collective-permute-start(f32[1,128]{1,0:T(1,128)S(1)} %arrange.1), channel_id=1, source_target_pairs={{9,1},{11,3},{13,5},{15,7},{0,8},{2,10},{4,12},{6,14},{1,0},{3,2},... | collective-permute-start | bytes 1544 | tf_op jit(solution)/shard_map/ppermute | solution.py:230
  15.2 1.3 %collective-permute-done.10 = f32[1,128]{1,0:T(1,128)S(1)} collective-permute-done((f32[1,128]{1,0:T(1,128)S(1)}, f32[1,128]{1,0:T(1,128)S(1)}, u32[]{:S(2)}, u32[]{:S(2)}) %collective-permute-start.10) | collective-permute-done | bytes 544 | tf_op jit(solution)/shard_map/ppermute | solution.py:230
  16.5 0.5 %copy.13 = f32[1,128]{1,0:T(1,128)} copy(f32[1,128]{1,0:T(1,128)S(1)} %collective-permute-done.10) | data formatting | bytes 1024
  (22 shorter events, 0.1 us)
Async XLA Ops:
  0.0 4.7 %copy-start = (bf16[1,384,2560]{2,1,0:T(8,128)(2,1)S(1)}, bf16[1,384,2560]{2,1,0:T(8,128)(2,1)}, u32[]{:S(2)}) copy-start(bf16[1,384,2560]{2,1,0:T(8,128)(2,1)} %acts_ref.1) | copy-start | bytes 5898244
  0.0 4.7 %copy-start.1 = (bf16[1,384,2560]{2,1,0:T(8,128)(2,1)S(1)}, bf16[1,384,2560]{2,1,0:T(8,128)(2,1)}, u32[]{:S(2)}) copy-start(bf16[1,384,2560]{2,1,0:T(8,128)(2,1)} %grads_ref.1) | copy-start | bytes 5898244
  0.0 4.7 %copy-start.2 = (bf16[2560,128]{1,0:T(8,128)(2,1)S(1)}, bf16[2560,128]{1,0:T(8,128)(2,1)}, u32[]{:S(2)}) copy-start(bf16[2560,128]{1,0:T(8,128)(2,1)} %proj_ref.1) | copy-start | bytes 1966084
  0.0 6.5 %copy-start.4 = (s32[1,256]{1,0:T(1,128)S(1)}, s32[1,256]{1,0:T(1,128)}, u32[]{:S(2)}) copy-start(s32[1,256]{1,0:T(1,128)} %picks_ref.1) | copy-start | bytes 3076
  0.0 8.1 %copy-start.3 = (bf16[32,2048]{1,0:T(8,128)(2,1)S(1)}, bf16[32,2048]{1,0:T(8,128)(2,1)}, u32[]{:S(2)}) copy-start(bf16[32,2048]{1,0:T(8,128)(2,1)} %own_ref.1) | copy-start | bytes 393220
  0.0 10.8 %collective-permute-start.5 = (bf16[32,2048]{1,0:T(8,128)(2,1)}, bf16[32,2048]{1,0:T(8,128)(2,1)S(1)}, u32[]{:S(2)}, u32[]{:S(2)}) collective-permute-start(bf16[32,2048]{1,0:T(8,128)(2,1)} %own_ref.1), channel_id=1, source_target_pairs={{0,6},{2,4},{4,2},{6,0},{8,14},{10,12},{12,10},{14,8},{1,7},{3,5},... | collective-permute-start | bytes 393224 | tf_op jit(solution)/shard_map/ppermute | solution.py:142
  4.1 6.8 %collective-permute-start.6 = (bf16[32,2048]{1,0:T(8,128)(2,1)}, bf16[32,2048]{1,0:T(8,128)(2,1)S(1)}, u32[]{:S(2)}, u32[]{:S(2)}) collective-permute-start(bf16[32,2048]{1,0:T(8,128)(2,1)} %own_ref.1), channel_id=1, source_target_pairs={{0,4},{2,6},{4,0},{6,2},{8,12},{10,14},{12,8},{14,10},{1,5},{3,7},... | collective-permute-start | bytes 393224 | tf_op jit(solution)/shard_map/ppermute | solution.py:142
  4.5 6.8 %collective-permute-start.4 = (bf16[32,2048]{1,0:T(8,128)(2,1)}, bf16[32,2048]{1,0:T(8,128)(2,1)S(1)}, u32[]{:S(2)}, u32[]{:S(2)}) collective-permute-start(bf16[32,2048]{1,0:T(8,128)(2,1)} %own_ref.1), channel_id=1, source_target_pairs={{0,2},{2,0},{4,6},{6,4},{8,10},{10,8},{12,14},{14,12},{1,3},{3,1},... | collective-permute-start | bytes 393224 | tf_op jit(solution)/shard_map/ppermute | solution.py:142
  5.9 1.4 %collective-permute-start = (f32[192,128]{1,0:T(8,128)S(1)}, f32[192,128]{1,0:T(8,128)S(1)}, u32[]{:S(2)}, u32[]{:S(2)}) collective-permute-start(f32[192,128]{1,0:T(8,128)S(1)} %get-tuple-element.12.refs_0_), channel_id=1, source_target_pairs={{0,1},{1,0},{2,3},{3,2},{4,5},{5,4},{6,7},{7,6},{8,9},{9,8},{10,11... | collective-permute-start | bytes 294920 | tf_op jit(solution)/shard_map/ppermute | solution.py:155
  6.0 1.4 %collective-permute-start.1 = (f32[192,128]{1,0:T(8,128)S(1)}, f32[192,128]{1,0:T(8,128)S(1)}, u32[]{:S(2)}, u32[]{:S(2)}) collective-permute-start(f32[192,128]{1,0:T(8,128)S(1)} %get-tuple-element.13.refs_1_), channel_id=1, source_target_pairs={{0,1},{1,0},{2,3},{3,2},{4,5},{5,4},{6,7},{7,6},{8,9},{9,8},{10,11... | collective-permute-start | bytes 294920 | tf_op jit(solution)/shard_map/ppermute | solution.py:155
  7.8 4.6 %collective-permute-start.2 = (bf16[32,128]{1,0:T(8,128)(2,1)S(1)}, bf16[32,128]{1,0:T(8,128)(2,1)S(1)}, u32[]{:S(2)}, u32[]{:S(2)}) collective-permute-start(bf16[32,128]{1,0:T(8,128)(2,1)S(1)} %sketch.1.own_ref.refs_1_), channel_id=1, source_target_pairs={{1,9},{3,11},{5,13},{7,15},{8,0},{10,2},{12,4},{14,6},{0,1},{2,3},... | collective-permute-start | bytes 24584 | tf_op jit(solution)/shard_map/ppermute | solution.py:176
  8.1 4.2 %collective-permute-start.3 = (bf16[32,2048]{1,0:T(8,128)(2,1)S(1)}, bf16[32,2048]{1,0:T(8,128)(2,1)S(1)}, u32[]{:S(2)}, u32[]{:S(2)}) collective-permute-start(bf16[32,2048]{1,0:T(8,128)(2,1)S(1)} %copy-done.3), channel_id=1, source_target_pairs={{0,1},{1,0},{2,3},{3,2},{4,5},{5,4},{6,7},{7,6},{8,9},{9,8},{10,11... | collective-permute-start | bytes 393224 | tf_op jit(solution)/shard_map/ppermute | solution.py:192
  10.8 1.7 %collective-permute-start.9 = (bf16[32,2048]{1,0:T(8,128)(2,1)S(1)}, bf16[32,2048]{1,0:T(8,128)(2,1)S(1)}, u32[]{:S(2)}, u32[]{:S(2)}) collective-permute-start(bf16[32,2048]{1,0:T(8,128)(2,1)S(1)} %hold.3.refs_1_.own_ref), channel_id=1, source_target_pairs={{0,1},{1,0},{2,3},{3,2},{4,5},{5,4},{6,7},{7,6},{8,9},{9,8},{10,11... | collective-permute-start | bytes 393224 | tf_op jit(solution)/shard_map/ppermute | solution.py:192
  10.9 1.7 %collective-permute-start.8 = (bf16[32,2048]{1,0:T(8,128)(2,1)S(1)}, bf16[32,2048]{1,0:T(8,128)(2,1)S(1)}, u32[]{:S(2)}, u32[]{:S(2)}) collective-permute-start(bf16[32,2048]{1,0:T(8,128)(2,1)S(1)} %hold.4.refs_2_.own_ref), channel_id=1, source_target_pairs={{0,1},{1,0},{2,3},{3,2},{4,5},{5,4},{6,7},{7,6},{8,9},{9,8},{10,11... | collective-permute-start | bytes 393224 | tf_op jit(solution)/shard_map/ppermute | solution.py:192
  11.3 1.3 %collective-permute-start.7 = (bf16[32,2048]{1,0:T(8,128)(2,1)S(1)}, bf16[32,2048]{1,0:T(8,128)(2,1)S(1)}, u32[]{:S(2)}, u32[]{:S(2)}) collective-permute-start(bf16[32,2048]{1,0:T(8,128)(2,1)S(1)} %hold.5.own_ref), channel_id=1, source_target_pairs={{0,1},{1,0},{2,3},{3,2},{4,5},{5,4},{6,7},{7,6},{8,9},{9,8},{10,11... | collective-permute-start | bytes 393224 | tf_op jit(solution)/shard_map/ppermute | solution.py:192
  12.9 3.5 %collective-permute-start.10 = (f32[1,128]{1,0:T(1,128)S(1)}, f32[1,128]{1,0:T(1,128)S(1)}, u32[]{:S(2)}, u32[]{:S(2)}) collective-permute-start(f32[1,128]{1,0:T(1,128)S(1)} %arrange.1), channel_id=1, source_target_pairs={{9,1},{11,3},{13,5},{15,7},{0,8},{2,10},{4,12},{6,14},{1,0},{3,2},... | collective-permute-start | bytes 1544 | tf_op jit(solution)/shard_map/ppermute | solution.py:230

commit v24 on v20

--- a/solution.py
+++ b/solution.py
@@ -80,12 +80,14 @@
 
 def score_kernel(first_ref, second_ref, own_ref, other_ref, *refs):
     out_ref = refs[-1]
-    total = None
-    for flat_ref, query_ref in ((first_ref, own_ref), (second_ref, other_ref)):
+    totals = [None] * 4
+    for i, (flat_ref, query_ref) in enumerate(((first_ref, own_ref), (second_ref, other_ref))):
         for j in range(query_ref.shape[1] // LANES):
             lanes = slice(j * LANES, (j + 1) * LANES)
             term = query_ref[:, lanes].astype(F32) * flat_ref[0:1, lanes]
-            total = term if total is None else total + term
+            at = 2 * i + j % 2
+            totals[at] = term if totals[at] is None else totals[at] + term
+    total = (totals[0] + totals[1]) + (totals[2] + totals[3])
     out_ref[...] = total
 
 

time: 17.1 us -> 17.1 us (level)
  transfers between devices with their start and end apart: 11 -> 11, of which waited for: 4 -> 5; matrix products, arithmetic and copies ran while one was open for 0% -> 0% of each run, Pallas kernels for 12% -> 12%
where the time goes in v24:
time: 17.1 us; the launch traced here: 16.9 us
  starting transfers between devices  11.1 us (65%)
  waiting for transfers between devices  3.05 us (18%)
  Pallas kernels  2.12 us (12%)
  local copies, waits for them, and re-layouts  0.53 us (3%)
    ppermute x3, starting transfers between devices, on_device(): halves.append(lax.ppermute(sent, 'dp', [(d, d ^ r) for d in range(clips)]))  4.67 us
    ppermute x4, starting transfers between devices, on_device(): swapped = [lax.ppermute(half, 'tensor', swap) for half in halves]  3.24 us
    ppermute x1, starting transfers between devices, on_device(): return lax.ppermute(scores, both, back)  2.26 us
    ppermute x1, waiting for transfers between devices, on_device(): return lax.ppermute(scores, both, back)  1.3 us
    pallas_call x1, Pallas kernels, on_device(): pl.pallas_call(functools.partial(project_kernel, rank), in_specs=[vmem] *...  1.17 us
    ppermute x1, waiting for transfers between devices, on_device(): far_sketch = lax.ppermute(sketch, both, there)  0.94 us
    ppermute x2, waiting for transfers between devices, on_device(): other = [lax.ppermute(part, 'tensor', swap) for part in partial]  0.74 us
    ppermute x2, starting transfers between devices, on_device(): other = [lax.ppermute(part, 'tensor', swap) for part in partial]  0.57 us
  transfers between devices with their start and end apart: 11, of which 5 were waited for; matrix products, arithmetic and copies ran while one was open for 0% of the time, Pallas kernels for 12%

profile of v24, /device:TPU:0, one launch (start us, length us, event | category | flops | bytes accessed | tf_op | source)
XLA Modules:
  0.0 16.9 jit_solution(536880991176597640)
XLA Ops:
  0.0 4.0 %collective-permute-start.5 = (bf16[32,2048]{1,0:T(8,128)(2,1)}, bf16[32,2048]{1,0:T(8,128)(2,1)S(1)}, u32[]{:S(2)}, u32[]{:S(2)}) collective-permute-start(bf16[32,2048]{1,0:T(8,128)(2,1)} %own_ref.1), channel_id=1, source_target_pairs={{0,6},{2,4},{4,2},{6,0},{8,14},{10,12},{12,10},{14,8},{1,7},{3,5},... | collective-permute-start | bytes 393224 | tf_op jit(solution)/shard_map/ppermute | solution.py:137
  4.1 0.4 %collective-permute-start.6 = (bf16[32,2048]{1,0:T(8,128)(2,1)}, bf16[32,2048]{1,0:T(8,128)(2,1)S(1)}, u32[]{:S(2)}, u32[]{:S(2)}) collective-permute-start(bf16[32,2048]{1,0:T(8,128)(2,1)} %own_ref.1), channel_id=1, source_target_pairs={{0,4},{2,6},{4,0},{6,2},{8,12},{10,14},{12,8},{14,10},{1,5},{3,7},... | collective-permute-start | bytes 393224 | tf_op jit(solution)/shard_map/ppermute | solution.py:137
  4.5 0.2 %collective-permute-start.4 = (bf16[32,2048]{1,0:T(8,128)(2,1)}, bf16[32,2048]{1,0:T(8,128)(2,1)S(1)}, u32[]{:S(2)}, u32[]{:S(2)}) collective-permute-start(bf16[32,2048]{1,0:T(8,128)(2,1)} %own_ref.1), channel_id=1, source_target_pairs={{0,2},{2,0},{4,6},{6,4},{8,10},{10,8},{12,14},{14,12},{1,3},{3,1},... | collective-permute-start | bytes 393224 | tf_op jit(solution)/shard_map/ppermute | solution.py:137
  4.7 1.2 %project.1 = (f32[192,128]{1,0:T(8,128)S(1)}, f32[192,128]{1,0:T(8,128)S(1)}) custom-call(f32[8,128]{1,0:T(8,128)S(1)} %first.1.first_ref, bf16[1,384,2560]{2,1,0:T(8,128)(2,1)S(1)} %copy-done, bf16[1,384,2560]{2,1,0:T(8,128)(2,1)S(1)} %copy-done.1, bf16[2560,128]{1,0:T(8,128)(2,1)S(1)} %copy-done.2), custom_call_target="tpu_custom_call" | custom-call | flops 503316480 | bytes 3932160 | tf_op jit(solution)/shard_map/project/pallas_call | solution.py:138
  5.9 0.1 collective-permute-start
  6.0 0.5 %collective-permute-start.1 = (f32[192,128]{1,0:T(8,128)S(1)}, f32[192,128]{1,0:T(8,128)S(1)}, u32[]{:S(2)}, u32[]{:S(2)}) collective-permute-start(f32[192,128]{1,0:T(8,128)S(1)} %get-tuple-element.13.refs_1_), channel_id=1, source_target_pairs={{0,1},{1,0},{2,3},{3,2},{4,5},{5,4},{6,7},{7,6},{8,9},{9,8},{10,11... | collective-permute-start | bytes 294920 | tf_op jit(solution)/shard_map/ppermute | solution.py:150
  6.5 0.2 %count.1.count_ref = f32[384,128]{1,0:T(8,128)S(1)} custom-call(s32[1,256]{1,0:T(1,128)S(1)} %copy-done.4), custom_call_target="tpu_custom_call" | custom-call | flops 1 | bytes 1 | tf_op jit(solution)/shard_map/count/pallas_call | solution.py:151
  6.7 0.6 %collective-permute-done.refs_2_ = f32[192,128]{1,0:T(8,128)S(1)} collective-permute-done((f32[192,128]{1,0:T(8,128)S(1)}, f32[192,128]{1,0:T(8,128)S(1)}, u32[]{:S(2)}, u32[]{:S(2)}) %collective-permute-start) | collective-permute-done | bytes 98336 | tf_op jit(solution)/shard_map/ppermute | solution.py:150
  7.3 0.2 collective-permute-done.1.refs_3_
  7.4 0.4 %sketch.1.own_ref.refs_1_ = bf16[32,128]{1,0:T(8,128)(2,1)S(1)} custom-call(f32[384,128]{1,0:T(8,128)S(1)} %count.1.count_ref, f32[192,128]{1,0:T(8,128)S(1)} %get-tuple-element.12.refs_0_, f32[192,128]{1,0:T(8,128)S(1)} %get-tuple-element.13.refs_1_, f32[192,128]{1,0:T(8,128)S(1)} %collective-permute-done.refs_2_, f32[192,128]{1,0:T(8,128)S(1)} %collective-permute-done.1.refs_3_), custom_call_target="tpu_custom_call" | custom-call | flops 1 | bytes 1 | tf_op jit(solution)/shard_map/sketch/pallas_call | solution.py:160
  7.8 0.4 %collective-permute-start.2 = (bf16[32,128]{1,0:T(8,128)(2,1)S(1)}, bf16[32,128]{1,0:T(8,128)(2,1)S(1)}, u32[]{:S(2)}, u32[]{:S(2)}) collective-permute-start(bf16[32,128]{1,0:T(8,128)(2,1)S(1)} %sketch.1.own_ref.refs_1_), channel_id=1, source_target_pairs={{1,9},{3,11},{5,13},{7,15},{8,0},{10,2},{12,4},{14,6},{0,1},{2,3},... | collective-permute-start | bytes 24584 | tf_op jit(solution)/shard_map/ppermute | solution.py:171
  8.1 2.7 %collective-permute-start.3 = (bf16[32,2048]{1,0:T(8,128)(2,1)S(1)}, bf16[32,2048]{1,0:T(8,128)(2,1)S(1)}, u32[]{:S(2)}, u32[]{:S(2)}) collective-permute-start(bf16[32,2048]{1,0:T(8,128)(2,1)S(1)} %copy-done.3), channel_id=1, source_target_pairs={{0,1},{1,0},{2,3},{3,2},{4,5},{5,4},{6,7},{7,6},{8,9},{9,8},{10,11... | collective-permute-start | bytes 393224 | tf_op jit(solution)/shard_map/ppermute | solution.py:187
  10.8 0.1 collective-permute-start.9
  10.9 0.4 %collective-permute-start.8 = (bf16[32,2048]{1,0:T(8,128)(2,1)S(1)}, bf16[32,2048]{1,0:T(8,128)(2,1)S(1)}, u32[]{:S(2)}, u32[]{:S(2)}) collective-permute-start(bf16[32,2048]{1,0:T(8,128)(2,1)S(1)} %hold.4.refs_2_.own_ref), channel_id=1, source_target_pairs={{0,1},{1,0},{2,3},{3,2},{4,5},{5,4},{6,7},{7,6},{8,9},{9,8},{10,11... | collective-permute-start | bytes 393224 | tf_op jit(solution)/shard_map/ppermute | solution.py:187
  11.3 0.1 collective-permute-start.7
  11.4 0.9 %collective-permute-done.2.far_ref = bf16[32,128]{1,0:T(8,128)(2,1)S(1)} collective-permute-done((bf16[32,128]{1,0:T(8,128)(2,1)S(1)}, bf16[32,128]{1,0:T(8,128)(2,1)S(1)}, u32[]{:S(2)}, u32[]{:S(2)}) %collective-permute-start.2) | collective-permute-done | bytes 8224 | tf_op jit(solution)/shard_map/ppermute | solution.py:171
  12.4 0.1 score.4.refs_0_
  12.5 0.1 score.5.refs_0_.refs_3_
  12.5 0.1 score.6.refs_0_.refs_2_
  12.6 0.1 collective-permute-done.7.other_ref
  12.7 0.1 arrange.1
  12.8 2.3 %collective-permute-start.10 = (f32[1,128]{1,0:T(1,128)S(1)}, f32[1,128]{1,0:T(1,128)S(1)}, u32[]{:S(2)}, u32[]{:S(2)}) collective-permute-start(f32[1,128]{1,0:T(1,128)S(1)} %arrange.1), channel_id=1, source_target_pairs={{9,1},{11,3},{13,5},{15,7},{0,8},{2,10},{4,12},{6,14},{1,0},{3,2},... | collective-permute-start | bytes 1544 | tf_op jit(solution)/shard_map/ppermute | solution.py:225
  15.1 1.3 %collective-permute-done.10 = f32[1,128]{1,0:T(1,128)S(1)} collective-permute-done((f32[1,128]{1,0:T(1,128)S(1)}, f32[1,128]{1,0:T(1,128)S(1)}, u32[]{:S(2)}, u32[]{:S(2)}) %collective-permute-start.10) | collective-permute-done | bytes 544 | tf_op jit(solution)/shard_map/ppermute | solution.py:225
  16.4 0.5 %copy.13 = f32[1,128]{1,0:T(1,128)} copy(f32[1,128]{1,0:T(1,128)S(1)} %collective-permute-done.10) | data formatting | bytes 1024
  (22 shorter events, 0.1 us)
Async XLA Ops:
  0.0 4.7 %copy-start = (bf16[1,384,2560]{2,1,0:T(8,128)(2,1)S(1)}, bf16[1,384,2560]{2,1,0:T(8,128)(2,1)}, u32[]{:S(2)}) copy-start(bf16[1,384,2560]{2,1,0:T(8,128)(2,1)} %acts_ref.1) | copy-start | bytes 5898244
  0.0 4.7 %copy-start.1 = (bf16[1,384,2560]{2,1,0:T(8,128)(2,1)S(1)}, bf16[1,384,2560]{2,1,0:T(8,128)(2,1)}, u32[]{:S(2)}) copy-start(bf16[1,384,2560]{2,1,0:T(8,128)(2,1)} %grads_ref.1) | copy-start | bytes 5898244
  0.0 4.7 %copy-start.2 = (bf16[2560,128]{1,0:T(8,128)(2,1)S(1)}, bf16[2560,128]{1,0:T(8,128)(2,1)}, u32[]{:S(2)}) copy-start(bf16[2560,128]{1,0:T(8,128)(2,1)} %proj_ref.1) | copy-start | bytes 1966084
  0.0 6.5 %copy-start.4 = (s32[1,256]{1,0:T(1,128)S(1)}, s32[1,256]{1,0:T(1,128)}, u32[]{:S(2)}) copy-start(s32[1,256]{1,0:T(1,128)} %picks_ref.1) | copy-start | bytes 3076
  0.0 8.1 %copy-start.3 = (bf16[32,2048]{1,0:T(8,128)(2,1)S(1)}, bf16[32,2048]{1,0:T(8,128)(2,1)}, u32[]{:S(2)}) copy-start(bf16[32,2048]{1,0:T(8,128)(2,1)} %own_ref.1) | copy-start | bytes 393220
  0.0 10.8 %collective-permute-start.5 = (bf16[32,2048]{1,0:T(8,128)(2,1)}, bf16[32,2048]{1,0:T(8,128)(2,1)S(1)}, u32[]{:S(2)}, u32[]{:S(2)}) collective-permute-start(bf16[32,2048]{1,0:T(8,128)(2,1)} %own_ref.1), channel_id=1, source_target_pairs={{0,6},{2,4},{4,2},{6,0},{8,14},{10,12},{12,10},{14,8},{1,7},{3,5},... | collective-permute-start | bytes 393224 | tf_op jit(solution)/shard_map/ppermute | solution.py:137
  4.1 6.8 %collective-permute-start.6 = (bf16[32,2048]{1,0:T(8,128)(2,1)}, bf16[32,2048]{1,0:T(8,128)(2,1)S(1)}, u32[]{:S(2)}, u32[]{:S(2)}) collective-permute-start(bf16[32,2048]{1,0:T(8,128)(2,1)} %own_ref.1), channel_id=1, source_target_pairs={{0,4},{2,6},{4,0},{6,2},{8,12},{10,14},{12,8},{14,10},{1,5},{3,7},... | collective-permute-start | bytes 393224 | tf_op jit(solution)/shard_map/ppermute | solution.py:137
  4.5 6.8 %collective-permute-start.4 = (bf16[32,2048]{1,0:T(8,128)(2,1)}, bf16[32,2048]{1,0:T(8,128)(2,1)S(1)}, u32[]{:S(2)}, u32[]{:S(2)}) collective-permute-start(bf16[32,2048]{1,0:T(8,128)(2,1)} %own_ref.1), channel_id=1, source_target_pairs={{0,2},{2,0},{4,6},{6,4},{8,10},{10,8},{12,14},{14,12},{1,3},{3,1},... | collective-permute-start | bytes 393224 | tf_op jit(solution)/shard_map/ppermute | solution.py:137
  5.9 1.4 %collective-permute-start = (f32[192,128]{1,0:T(8,128)S(1)}, f32[192,128]{1,0:T(8,128)S(1)}, u32[]{:S(2)}, u32[]{:S(2)}) collective-permute-start(f32[192,128]{1,0:T(8,128)S(1)} %get-tuple-element.12.refs_0_), channel_id=1, source_target_pairs={{0,1},{1,0},{2,3},{3,2},{4,5},{5,4},{6,7},{7,6},{8,9},{9,8},{10,11... | collective-permute-start | bytes 294920 | tf_op jit(solution)/shard_map/ppermute | solution.py:150
  6.0 1.4 %collective-permute-start.1 = (f32[192,128]{1,0:T(8,128)S(1)}, f32[192,128]{1,0:T(8,128)S(1)}, u32[]{:S(2)}, u32[]{:S(2)}) collective-permute-start(f32[192,128]{1,0:T(8,128)S(1)} %get-tuple-element.13.refs_1_), channel_id=1, source_target_pairs={{0,1},{1,0},{2,3},{3,2},{4,5},{5,4},{6,7},{7,6},{8,9},{9,8},{10,11... | collective-permute-start | bytes 294920 | tf_op jit(solution)/shard_map/ppermute | solution.py:150
  7.8 4.6 %collective-permute-start.2 = (bf16[32,128]{1,0:T(8,128)(2,1)S(1)}, bf16[32,128]{1,0:T(8,128)(2,1)S(1)}, u32[]{:S(2)}, u32[]{:S(2)}) collective-permute-start(bf16[32,128]{1,0:T(8,128)(2,1)S(1)} %sketch.1.own_ref.refs_1_), channel_id=1, source_target_pairs={{1,9},{3,11},{5,13},{7,15},{8,0},{10,2},{12,4},{14,6},{0,1},{2,3},... | collective-permute-start | bytes 24584 | tf_op jit(solution)/shard_map/ppermute | solution.py:171
  8.1 4.2 %collective-permute-start.3 = (bf16[32,2048]{1,0:T(8,128)(2,1)S(1)}, bf16[32,2048]{1,0:T(8,128)(2,1)S(1)}, u32[]{:S(2)}, u32[]{:S(2)}) collective-permute-start(bf16[32,2048]{1,0:T(8,128)(2,1)S(1)} %copy-done.3), channel_id=1, source_target_pairs={{0,1},{1,0},{2,3},{3,2},{4,5},{5,4},{6,7},{7,6},{8,9},{9,8},{10,11... | collective-permute-start | bytes 393224 | tf_op jit(solution)/shard_map/ppermute | solution.py:187
  10.8 1.7 %collective-permute-start.9 = (bf16[32,2048]{1,0:T(8,128)(2,1)S(1)}, bf16[32,2048]{1,0:T(8,128)(2,1)S(1)}, u32[]{:S(2)}, u32[]{:S(2)}) collective-permute-start(bf16[32,2048]{1,0:T(8,128)(2,1)S(1)} %hold.3.refs_1_.own_ref), channel_id=1, source_target_pairs={{0,1},{1,0},{2,3},{3,2},{4,5},{5,4},{6,7},{7,6},{8,9},{9,8},{10,11... | collective-permute-start | bytes 393224 | tf_op jit(solution)/shard_map/ppermute | solution.py:187
  10.9 1.6 %collective-permute-start.8 = (bf16[32,2048]{1,0:T(8,128)(2,1)S(1)}, bf16[32,2048]{1,0:T(8,128)(2,1)S(1)}, u32[]{:S(2)}, u32[]{:S(2)}) collective-permute-start(bf16[32,2048]{1,0:T(8,128)(2,1)S(1)} %hold.4.refs_2_.own_ref), channel_id=1, source_target_pairs={{0,1},{1,0},{2,3},{3,2},{4,5},{5,4},{6,7},{7,6},{8,9},{9,8},{10,11... | collective-permute-start | bytes 393224 | tf_op jit(solution)/shard_map/ppermute | solution.py:187
  11.3 1.3 %collective-permute-start.7 = (bf16[32,2048]{1,0:T(8,128)(2,1)S(1)}, bf16[32,2048]{1,0:T(8,128)(2,1)S(1)}, u32[]{:S(2)}, u32[]{:S(2)}) collective-permute-start(bf16[32,2048]{1,0:T(8,128)(2,1)S(1)} %hold.5.own_ref), channel_id=1, source_target_pairs={{0,1},{1,0},{2,3},{3,2},{4,5},{5,4},{6,7},{7,6},{8,9},{9,8},{10,11... | collective-permute-start | bytes 393224 | tf_op jit(solution)/shard_map/ppermute | solution.py:187
  12.8 3.6 %collective-permute-start.10 = (f32[1,128]{1,0:T(1,128)S(1)}, f32[1,128]{1,0:T(1,128)S(1)}, u32[]{:S(2)}, u32[]{:S(2)}) collective-permute-start(f32[1,128]{1,0:T(1,128)S(1)} %arrange.1), channel_id=1, source_target_pairs={{9,1},{11,3},{13,5},{15,7},{0,8},{2,10},{4,12},{6,14},{1,0},{3,2},... | collective-permute-start | bytes 1544 | tf_op jit(solution)/shard_map/ppermute | solution.py:225
